TPU v7x, 32 devices: a whole 2x2x4 slice. The times are simulated.
32 devices in a mesh: seq: 4 (over y, x), fsdp: 8 (over z, core).
Axes of the slice: x: 2, y: 2, z: 4, core: 2. Of those that a mesh axis runs over, the one named last changes fastest.
Arguments:
- inputs: bfloat16 [2, 8, 1024, 2048], P(None, 'fsdp', 'seq'), may hold values from -6 to 6
- cotangent: bfloat16 [2, 8, 1024, 2048], P(None, 'fsdp', 'seq'), may hold values from -6 to 6
- segments: int32 [2, 8, 1024], P(None, 'fsdp'), may hold values from 0 to 3, as said below
- norm_in: bfloat16 [2048], P(('seq', 'fsdp')), may hold values from 0.25 to 1.75
- ssm_in: bfloat16 [2048, 6704], P(('seq', 'fsdp')), may hold values from -0.125 to 0.125
- attn_in: bfloat16 [2048, 1536], P(('seq', 'fsdp')), may hold values from -0.125 to 0.125
- conv_w: bfloat16 [4, 3584], P(None, ('seq', 'fsdp')), may hold values from -3 to 3
- conv_b: bfloat16 [3584], P(('seq', 'fsdp')), may hold values from -0.5 to 0.5
- a_log: bfloat16 [48], replicated, may hold values from 0 to 2.765625
- dt_bias: bfloat16 [48], replicated, may hold values from -4 to -1
- d_skip: bfloat16 [48], replicated, may hold values from 0.5 to 1.5
- ssm_out: bfloat16 [3072, 2048], P(('seq', 'fsdp')), may hold values from -0.109375 to 0.109375
- attn_out: bfloat16 [1024, 2048], P(('seq', 'fsdp')), may hold values from -1.5 to 1.5
- norm_ffn: bfloat16 [2048], P(('seq', 'fsdp')), may hold values from 0.25 to 1.75
- w_gate: bfloat16 [2048, 4096], P(('seq', 'fsdp')), may hold values from -0.125 to 0.125
- w_up: bfloat16 [2048, 4096], P(('seq', 'fsdp')), may hold values from -0.125 to 0.125
- w_down: bfloat16 [4096, 2048], P(('seq', 'fsdp')), may hold values from -0.09375 to 0.09375
Outputs:
- outputs: bfloat16 [2, 8, 1024, 2048], P(None, 'fsdp', 'seq')
- input_grad: bfloat16 [2, 8, 1024, 2048], P(None, 'fsdp', 'seq')
- norm_in_grad: float32 [2048], P(('seq', 'fsdp'))
- ssm_in_grad: float32 [2048, 6704], P(('seq', 'fsdp'))
- attn_in_grad: float32 [2048, 1536], P(('seq', 'fsdp'))
- conv_w_grad: float32 [4, 3584], P(None, ('seq', 'fsdp'))
- conv_b_grad: float32 [3584], P(('seq', 'fsdp'))
- a_log_grad: float32 [48], replicated
- dt_bias_grad: float32 [48], replicated
- d_skip_grad: float32 [48], replicated
- ssm_out_grad: float32 [3072, 2048], P(('seq', 'fsdp'))
- attn_out_grad: float32 [1024, 2048], P(('seq', 'fsdp'))
- norm_ffn_grad: float32 [2048], P(('seq', 'fsdp'))
- w_gate_grad: float32 [2048, 4096], P(('seq', 'fsdp'))
- w_up_grad: float32 [2048, 4096], P(('seq', 'fsdp'))
- w_down_grad: float32 [4096, 2048], P(('seq', 'fsdp'))
Inputs may be any that keep to these rules, and one draw needn't show every extreme that they name: `segments`: segment numbers never fall along a sequence.
All inputs are finite; a program needn't handle non-finite values.
Results may differ from a plain program's by a relative error of at most 0.013.
The roundings to bfloat16 on the way count: a program that leaves them out, or rounds other values in their place, can miss the bound.
Values may be sent and summed in bfloat16 or wider, within the bound.
No kernel may reach another device: no remote copies, remote signals or barrier semaphores. Data moves between devices by JAX's collectives and lax.ppermute only.
A program may use at most 512 MiB of HBM per device.

v0:
```python
import jax
import jax.numpy as jnp
from jax import lax
from jax.sharding import PartitionSpec as P

SSM_HEADS = 48
SSM_DIM = 64
STATE = 256
CONV = 4
Q_HEADS = 8
KV_HEADS = 2
HEAD_DIM = 128
MICRO = 2
SPAN = 128
ATT_BLOCK = 512
SSM_INNER = 3072
CONV_CH = 3584


PRECISE = lax.Precision.HIGHEST
EPSILON = 1e-05
ROPE_BASE = 10000.0


def round_plain(value):
    return lax.optimization_barrier(value.astype(jnp.bfloat16)).astype(jnp.float32)


def round_keep(value):
    return (round_plain(value), None)


def round_pass(kept, grad):
    return (grad,)


def make_rounder():
    rounder = jax.custom_vjp(round_plain)
    rounder.defvjp(round_keep, round_pass)
    return rounder


def rotate(head_rows, positions):
    half_width = head_rows.shape[-1] // 2
    frequency = ROPE_BASE ** (-jnp.arange(half_width).astype(jnp.float32) / half_width)
    angles = positions.astype(jnp.float32)[:, None] * frequency[None, :]
    cosine = jnp.cos(angles)[:, None, :]
    sine_part = jnp.sin(angles)[:, None, :]
    lead_half = head_rows[..., :half_width]
    tail_half = head_rows[..., half_width:]
    return jnp.concatenate(
        [lead_half * cosine - tail_half * sine_part, tail_half * cosine + lead_half * sine_part],
        axis=-1,
    )


def causal_conv(channels, segment, conv_weight, conv_bias):
    length = channels.shape[0]
    summed = jnp.broadcast_to(conv_bias[None, :], channels.shape)
    for offset in range(CONV):
        shifted = jnp.pad(channels, ((offset, 0), (0, 0)))[:length]
        earlier = jnp.pad(segment, (offset, 0), constant_values=-1)[:length]
        keep_mask = (earlier == segment).astype(jnp.float32)
        summed = summed + conv_weight[CONV - 1 - offset][None, :] * shifted * keep_mask[:, None]
    return jax.nn.silu(summed)


def ssd_scan(x_heads, log_decay, step_size, b_rows, c_rows, segment):
    length, head_count, head_width = x_heads.shape
    block_count = length // SPAN
    seq_items = (
        x_heads.reshape(block_count, SPAN, head_count, head_width),
        log_decay.reshape(block_count, SPAN, head_count),
        step_size.reshape(block_count, SPAN, head_count),
        b_rows.reshape(block_count, SPAN, STATE),
        c_rows.reshape(block_count, SPAN, STATE),
        segment.reshape(block_count, SPAN),
    )
    lower_mask = jnp.tril(jnp.ones((SPAN, SPAN), dtype=bool))

    def block_step(block_carry, block_items):
        ssm_state, last_segment = block_carry
        x_block, decay_block, step_block, b_block, c_block, seg_block = block_items
        cumulative = jnp.cumsum(decay_block, axis=0)
        same_doc = ((seg_block[:, None] == seg_block[None, :]) & lower_mask)[:, :, None]
        decay_gap = cumulative[:, None, :] - cumulative[None, :, :]
        inner_weight = jnp.where(same_doc, jnp.exp(jnp.where(same_doc, decay_gap, 0.0)), 0.0)
        block_scores = jnp.dot(c_block, b_block.T, precision=PRECISE)
        mixing = inner_weight * block_scores[:, :, None] * step_block[None, :, :]
        y_inner = jnp.einsum("tsh,shp->thp", mixing, x_block, precision=PRECISE)
        carry_keep = (seg_block == last_segment).astype(jnp.float32)
        state_weight = jnp.exp(cumulative) * carry_keep[:, None]
        from_state = (
            jnp.einsum("tn,hpn->thp", c_block, ssm_state, precision=PRECISE)
            * state_weight[:, :, None]
        )
        end_keep = (seg_block == seg_block[-1]).astype(jnp.float32)
        input_weight = (
            jnp.exp(cumulative[-1][None, :] - cumulative) * step_block * end_keep[:, None]
        )
        state_keep = jnp.exp(cumulative[-1]) * (seg_block[-1] == last_segment).astype(jnp.float32)
        new_state = ssm_state * state_keep[:, None, None] + jnp.einsum(
            "sh,shp,sn->hpn", input_weight, x_block, b_block, precision=PRECISE
        )
        return ((new_state, seg_block[-1]), y_inner + from_state)

    start_carry = (
        jnp.zeros((head_count, head_width, STATE), jnp.float32),
        jnp.array(-1, jnp.int32),
    )
    unused, y_blocks = lax.scan(jax.checkpoint(block_step), start_carry, seq_items)
    return y_blocks.reshape(length, head_count, head_width)


def attend(q_rot, k_rot, value_heads, segment):
    length, head_count, head_width = q_rot.shape
    block_count = length // ATT_BLOCK
    positions = jnp.arange(length, dtype=jnp.int32)
    rounder = make_rounder()

    def one_block(block_index):
        first_row = block_index * ATT_BLOCK
        q_block = lax.dynamic_slice_in_dim(q_rot, first_row, ATT_BLOCK, 0)
        seg_query = lax.dynamic_slice_in_dim(segment, first_row, ATT_BLOCK, 0)
        pos_query = first_row + jnp.arange(ATT_BLOCK, dtype=jnp.int32)
        scores = jnp.einsum("qhe,khe->hqk", q_block, k_rot, precision=PRECISE) * head_width ** (
            -0.5
        )
        allowed = (pos_query[:, None] >= positions[None, :]) & (
            seg_query[:, None] == segment[None, :]
        )
        scores = jnp.where(allowed[None, :, :], scores, -1e30)
        attn_probs = rounder(jax.nn.softmax(scores, axis=-1))
        return jnp.einsum("hqk,khe->qhe", attn_probs, value_heads, precision=PRECISE)

    blocks = lax.map(jax.checkpoint(one_block), jnp.arange(block_count, dtype=jnp.int32))
    return blocks.reshape(length, head_count, head_width)


def mixer_heads(
    x_part,
    dt_part,
    query_rows,
    key_rep,
    value_rep,
    bc_part,
    segment,
    conv_weight,
    conv_bias,
    log_rate,
    step_bias,
    skip_gain,
):
    rounder = make_rounder()
    length = x_part.shape[0]
    inner_width = x_part.shape[1]
    head_count = dt_part.shape[1]
    conv_out = rounder(
        causal_conv(jnp.concatenate([x_part, bc_part], axis=1), segment, conv_weight, conv_bias)
    )
    x_heads = conv_out[:, :inner_width].reshape(length, head_count, inner_width // head_count)
    b_rows = conv_out[:, inner_width : inner_width + STATE]
    c_rows = conv_out[:, inner_width + STATE :]
    step_size = jax.nn.softplus(dt_part + step_bias[None, :])
    log_decay = -jnp.exp(log_rate)[None, :] * step_size
    y_heads = (
        ssd_scan(x_heads, log_decay, step_size, b_rows, c_rows, segment)
        + skip_gain[None, :, None] * x_heads
    )
    y_rows = rounder(y_heads.reshape(length, inner_width))
    positions = jnp.arange(length, dtype=jnp.int32)
    query_heads = query_rows.shape[1] // HEAD_DIM
    q_rot = rounder(rotate(query_rows.reshape(length, query_heads, HEAD_DIM), positions))
    k_rot = rounder(rotate(key_rep.reshape(length, query_heads, HEAD_DIM), positions))
    attended = attend(q_rot, k_rot, value_rep.reshape(length, query_heads, HEAD_DIM), segment)
    attended = rounder(attended.reshape(length, query_heads * HEAD_DIM))
    return (y_rows, attended)


def norm_forward(token_rows, gain_vec):
    inv_scale = lax.rsqrt(jnp.mean(token_rows * token_rows, axis=-1, keepdims=True) + EPSILON)
    return (token_rows * inv_scale * gain_vec, inv_scale)


def norm_backward(token_rows, inv_scale, gain_vec, grad_rows):
    normed = token_rows * inv_scale
    gain_grad = jnp.sum(normed * grad_rows, axis=0)
    weighted = grad_rows * gain_vec
    row_grad = inv_scale * (weighted - normed * jnp.mean(weighted * normed, axis=-1, keepdims=True))
    return (row_grad, gain_grad)


def repeat_heads(kv_rows, groups):
    length = kv_rows.shape[0]
    shaped = kv_rows.reshape(length, -1, 1, HEAD_DIM)
    return jnp.broadcast_to(shaped, (length, shaped.shape[1], groups, HEAD_DIM)).reshape(length, -1)


def fold_heads(rep_rows, groups):
    length = rep_rows.shape[0]
    summed = jnp.sum(rep_rows.astype(jnp.float32).reshape(length, -1, groups, HEAD_DIM), axis=2)
    return summed.reshape(length, -1).astype(jnp.bfloat16)


def fetch_mixer(norm_in, ssm_in, attn_in, conv_w, conv_b, ssm_out, attn_out):
    return (
        lax.all_gather(norm_in, ("seq", "fsdp"), axis=0, tiled=True),
        lax.all_gather(ssm_in, ("seq", "fsdp"), axis=0, tiled=True),
        lax.all_gather(attn_in, ("seq", "fsdp"), axis=0, tiled=True),
        lax.all_gather(conv_w, ("seq", "fsdp"), axis=1, tiled=True),
        lax.all_gather(conv_b, ("seq", "fsdp"), axis=0, tiled=True),
        lax.all_gather(ssm_out, ("seq", "fsdp"), axis=0, tiled=True),
        lax.all_gather(attn_out, ("seq", "fsdp"), axis=0, tiled=True),
    )


def fetch_ffn(norm_ffn, w_gate, w_up, w_down):
    return (
        lax.all_gather(norm_ffn, ("seq", "fsdp"), axis=0, tiled=True),
        lax.all_gather(w_gate, ("seq", "fsdp"), axis=0, tiled=True),
        lax.all_gather(w_up, ("seq", "fsdp"), axis=0, tiled=True),
        lax.all_gather(w_down, ("seq", "fsdp"), axis=0, tiled=True),
    )


def spread_ffn(local_grads):
    return (
        lax.psum_scatter(local_grads[0], ("seq", "fsdp"), scatter_dimension=0, tiled=True),
        lax.psum_scatter(local_grads[1], ("seq", "fsdp"), scatter_dimension=0, tiled=True),
        lax.psum_scatter(local_grads[2], ("seq", "fsdp"), scatter_dimension=0, tiled=True),
        lax.psum_scatter(local_grads[3], ("seq", "fsdp"), scatter_dimension=0, tiled=True),
    )


def spread_mixer(local_grads):
    return (
        lax.psum_scatter(local_grads[0], ("seq", "fsdp"), scatter_dimension=0, tiled=True),
        lax.psum_scatter(local_grads[1], ("seq", "fsdp"), scatter_dimension=0, tiled=True),
        lax.psum_scatter(local_grads[2], ("seq", "fsdp"), scatter_dimension=0, tiled=True),
        lax.psum_scatter(local_grads[3], ("seq", "fsdp"), scatter_dimension=1, tiled=True),
        lax.psum_scatter(local_grads[4], ("seq", "fsdp"), scatter_dimension=0, tiled=True),
        lax.psum_scatter(local_grads[5], ("seq", "fsdp"), scatter_dimension=0, tiled=True),
        lax.psum_scatter(local_grads[6], ("seq", "fsdp"), scatter_dimension=0, tiled=True),
    )


def matmul_rows(left, right):
    return jnp.einsum("tc,cd->td", left, right, preferred_element_type=jnp.float32)


def matmul_back(left, right):
    return jnp.einsum("td,cd->tc", left, right, preferred_element_type=jnp.float32)


def weight_grad(left, right):
    return jnp.einsum("tc,td->cd", left, right, preferred_element_type=jnp.float32)


def add_sums(old_sums, new_sums):
    return new_sums if old_sums is None else jax.tree.map(jnp.add, old_sums, new_sums)


def on_device(
    inputs,
    cotangent,
    segments,
    norm_in,
    ssm_in,
    attn_in,
    conv_w,
    conv_b,
    a_log,
    dt_bias,
    d_skip,
    ssm_out,
    attn_out,
    norm_ffn,
    w_gate,
    w_up,
    w_down,
):
    seq_count = lax.axis_size("seq")
    seq_index = lax.axis_index("seq")
    local_heads = SSM_HEADS // seq_count
    local_inner = local_heads * SSM_DIM
    head_start = seq_index * local_heads
    inner_start = seq_index * local_inner
    groups = Q_HEADS // KV_HEADS
    q_width = Q_HEADS * HEAD_DIM
    k_width = KV_HEADS * HEAD_DIM
    rate_local = lax.dynamic_slice_in_dim(a_log.astype(jnp.float32), head_start, local_heads)
    bias_local = lax.dynamic_slice_in_dim(dt_bias.astype(jnp.float32), head_start, local_heads)
    skip_local = lax.dynamic_slice_in_dim(d_skip.astype(jnp.float32), head_start, local_heads)
    mixer_shards = (norm_in, ssm_in, attn_in, conv_w, conv_b, ssm_out, attn_out)
    ffn_shards = (norm_ffn, w_gate, w_up, w_down)
    outputs_list = []
    input_grads = []
    mixer_sums = None
    ffn_sums = None
    rate_sum = jnp.zeros((SSM_HEADS,), jnp.float32)
    bias_sum = jnp.zeros((SSM_HEADS,), jnp.float32)
    skip_sum = jnp.zeros((SSM_HEADS,), jnp.float32)
    for batch_index in range(MICRO):
        whole_mixer = fetch_mixer(*mixer_shards)
        (
            gain_in,
            whole_ssm_in,
            whole_attn_in,
            whole_conv_w,
            whole_conv_b,
            whole_ssm_out,
            whole_attn_out,
        ) = whole_mixer
        token_rows = inputs[batch_index, 0].astype(jnp.float32)
        segment = segments[batch_index, 0]
        normed_in, scale_in = norm_forward(token_rows, gain_in.astype(jnp.float32))
        hidden_in = normed_in.astype(jnp.bfloat16)
        projected = matmul_rows(hidden_in, whole_ssm_in)
        gate_z = projected[:, :SSM_INNER]
        x_rows = projected[:, SSM_INNER : 2 * SSM_INNER].astype(jnp.bfloat16)
        bc_rows = projected[:, 2 * SSM_INNER : 2 * SSM_INNER + 2 * STATE].astype(jnp.bfloat16)
        dt_rows = projected[:, 2 * SSM_INNER + 2 * STATE :].astype(jnp.bfloat16)
        attn_rows = matmul_rows(hidden_in, whole_attn_in)
        query_rows = attn_rows[:, :q_width].astype(jnp.bfloat16)
        key_rows = attn_rows[:, q_width : q_width + k_width].astype(jnp.bfloat16)
        value_rows = attn_rows[:, q_width + k_width :].astype(jnp.bfloat16)
        head_x, head_dt, head_query, head_key, head_value = (
            lax.all_to_all(x_rows, "seq", split_axis=1, concat_axis=0, tiled=True),
            lax.all_to_all(dt_rows, "seq", split_axis=1, concat_axis=0, tiled=True),
            lax.all_to_all(query_rows, "seq", split_axis=1, concat_axis=0, tiled=True),
            lax.all_to_all(
                repeat_heads(key_rows, groups), "seq", split_axis=1, concat_axis=0, tiled=True
            ),
            lax.all_to_all(
                repeat_heads(value_rows, groups), "seq", split_axis=1, concat_axis=0, tiled=True
            ),
        )
        bc_whole = lax.all_gather(bc_rows, "seq", axis=0, tiled=True)
        conv_local_w = jnp.concatenate(
            [
                lax.dynamic_slice_in_dim(whole_conv_w, inner_start, local_inner, 1),
                whole_conv_w[:, SSM_INNER:],
            ],
            axis=1,
        ).astype(jnp.float32)
        conv_local_b = jnp.concatenate(
            [
                lax.dynamic_slice_in_dim(whole_conv_b, inner_start, local_inner, 0),
                whole_conv_b[SSM_INNER:],
            ],
            axis=0,
        ).astype(jnp.float32)

        def local_mixer(
            x_part,
            dt_part,
            query_part,
            key_part,
            value_part,
            bc_part,
            conv_weight,
            conv_bias,
            log_rate,
            step_bias,
            skip_gain,
        ):
            return mixer_heads(
                x_part,
                dt_part,
                query_part,
                key_part,
                value_part,
                bc_part,
                segment,
                conv_weight,
                conv_bias,
                log_rate,
                step_bias,
                skip_gain,
            )

        (head_y, head_attended), pullback = jax.vjp(
            local_mixer,
            head_x.astype(jnp.float32),
            head_dt.astype(jnp.float32),
            head_query.astype(jnp.float32),
            head_key.astype(jnp.float32),
            head_value.astype(jnp.float32),
            bc_whole.astype(jnp.float32),
            conv_local_w,
            conv_local_b,
            rate_local,
            bias_local,
            skip_local,
        )
        y_rows, attended = (
            lax.all_to_all(
                head_y.astype(jnp.bfloat16), "seq", split_axis=0, concat_axis=1, tiled=True
            ),
            lax.all_to_all(
                head_attended.astype(jnp.bfloat16), "seq", split_axis=0, concat_axis=1, tiled=True
            ),
        )
        gate_sig = jax.nn.sigmoid(gate_z)
        gate_silu = gate_z * gate_sig
        y_float = y_rows.astype(jnp.float32)
        gated_rows = (y_float * gate_silu).astype(jnp.bfloat16)
        mixed_rows = matmul_rows(gated_rows, whole_ssm_out) + matmul_rows(attended, whole_attn_out)
        middle = token_rows + mixed_rows
        whole_ffn = fetch_ffn(*ffn_shards)
        gain_ffn, whole_gate, whole_up, whole_down = whole_ffn
        normed_ffn, scale_ffn = norm_forward(middle, gain_ffn.astype(jnp.float32))
        hidden_ffn = normed_ffn.astype(jnp.bfloat16)
        gate_pre = matmul_rows(hidden_ffn, whole_gate)
        up_pre = matmul_rows(hidden_ffn, whole_up)
        up_sig = jax.nn.sigmoid(gate_pre)
        activated = (gate_pre * up_sig * up_pre).astype(jnp.bfloat16)
        outputs_list.append((middle + matmul_rows(activated, whole_down)).astype(jnp.bfloat16))
        back_ffn = fetch_ffn(*ffn_shards)
        gain_ffn_back, back_gate, back_up, back_down = back_ffn
        grad_out = cotangent[batch_index, 0]
        grad_down = weight_grad(activated, grad_out)
        grad_act = matmul_back(grad_out, back_down)
        grad_up = (grad_act * gate_pre * up_sig).astype(jnp.bfloat16)
        grad_gate = (grad_act * up_pre * up_sig * (1.0 + gate_pre * (1.0 - up_sig))).astype(
            jnp.bfloat16
        )
        grad_w_gate = weight_grad(hidden_ffn, grad_gate)
        grad_w_up = weight_grad(hidden_ffn, grad_up)
        grad_hidden_ffn = matmul_back(grad_gate, back_gate) + matmul_back(grad_up, back_up)
        grad_middle_norm, grad_gain_ffn = norm_backward(
            middle, scale_ffn, gain_ffn_back.astype(jnp.float32), grad_hidden_ffn
        )
        ffn_sums = add_sums(
            ffn_sums, spread_ffn((grad_gain_ffn, grad_w_gate, grad_w_up, grad_down))
        )
        grad_middle = grad_out.astype(jnp.float32) + grad_middle_norm
        grad_mixed = grad_middle.astype(jnp.bfloat16)
        back_mixer = fetch_mixer(*mixer_shards)
        (
            gain_in_back,
            back_ssm_in,
            back_attn_in,
            unused_conv_w,
            unused_conv_b,
            back_ssm_out,
            back_attn_out,
        ) = back_mixer
        grad_w_ssm_out = weight_grad(gated_rows, grad_mixed)
        grad_w_attn_out = weight_grad(attended, grad_mixed)
        grad_gated = matmul_back(grad_mixed, back_ssm_out)
        grad_attended = matmul_back(grad_mixed, back_attn_out).astype(jnp.bfloat16)
        grad_y = (grad_gated * gate_silu).astype(jnp.bfloat16)
        grad_z = (grad_gated * y_float * gate_sig * (1.0 + gate_z * (1.0 - gate_sig))).astype(
            jnp.bfloat16
        )
        head_grad_y, head_grad_attended = (
            lax.all_to_all(grad_y, "seq", split_axis=1, concat_axis=0, tiled=True),
            lax.all_to_all(grad_attended, "seq", split_axis=1, concat_axis=0, tiled=True),
        )
        (
            grad_head_x,
            grad_head_dt,
            grad_head_query,
            grad_head_key,
            grad_head_value,
            grad_bc_part,
            grad_conv_local_w,
            grad_conv_local_b,
            grad_rate,
            grad_bias,
            grad_skip,
        ) = pullback((head_grad_y.astype(jnp.float32), head_grad_attended.astype(jnp.float32)))
        back_x, back_dt, back_query, back_key, back_value = (
            lax.all_to_all(
                grad_head_x.astype(jnp.bfloat16), "seq", split_axis=0, concat_axis=1, tiled=True
            ),
            lax.all_to_all(
                grad_head_dt.astype(jnp.bfloat16), "seq", split_axis=0, concat_axis=1, tiled=True
            ),
            lax.all_to_all(
                grad_head_query.astype(jnp.bfloat16), "seq", split_axis=0, concat_axis=1, tiled=True
            ),
            lax.all_to_all(
                grad_head_key.astype(jnp.bfloat16), "seq", split_axis=0, concat_axis=1, tiled=True
            ),
            lax.all_to_all(
                grad_head_value.astype(jnp.bfloat16), "seq", split_axis=0, concat_axis=1, tiled=True
            ),
        )
        grad_bc = lax.psum_scatter(
            grad_bc_part.astype(jnp.bfloat16), "seq", scatter_dimension=0, tiled=True
        )
        grad_keys = fold_heads(back_key, groups)
        grad_values = fold_heads(back_value, groups)
        grad_projected = jnp.concatenate([grad_z, back_x, grad_bc, back_dt], axis=1)
        grad_attn_rows = jnp.concatenate([back_query, grad_keys, grad_values], axis=1)
        grad_w_ssm_in = weight_grad(hidden_in, grad_projected)
        grad_w_attn_in = weight_grad(hidden_in, grad_attn_rows)
        grad_hidden_in = matmul_back(grad_projected, back_ssm_in) + matmul_back(
            grad_attn_rows, back_attn_in
        )
        grad_rows_norm, grad_gain_in = norm_backward(
            token_rows, scale_in, gain_in_back.astype(jnp.float32), grad_hidden_in
        )
        input_grads.append((grad_middle + grad_rows_norm).astype(jnp.bfloat16))
        conv_w_full = jnp.zeros((CONV, CONV_CH), jnp.float32)
        conv_w_full = lax.dynamic_update_slice_in_dim(
            conv_w_full, grad_conv_local_w[:, :local_inner], inner_start, 1
        )
        conv_w_full = lax.dynamic_update_slice_in_dim(
            conv_w_full, grad_conv_local_w[:, local_inner:], SSM_INNER, 1
        )
        conv_b_full = jnp.zeros((CONV_CH,), jnp.float32)
        conv_b_full = lax.dynamic_update_slice_in_dim(
            conv_b_full, grad_conv_local_b[:local_inner], inner_start, 0
        )
        conv_b_full = lax.dynamic_update_slice_in_dim(
            conv_b_full, grad_conv_local_b[local_inner:], SSM_INNER, 0
        )
        head_zeros = jnp.zeros((SSM_HEADS,), jnp.float32)
        rate_sum = rate_sum + lax.dynamic_update_slice_in_dim(head_zeros, grad_rate, head_start, 0)
        bias_sum = bias_sum + lax.dynamic_update_slice_in_dim(head_zeros, grad_bias, head_start, 0)
        skip_sum = skip_sum + lax.dynamic_update_slice_in_dim(head_zeros, grad_skip, head_start, 0)
        mixer_sums = add_sums(
            mixer_sums,
            spread_mixer(
                (
                    grad_gain_in,
                    grad_w_ssm_in,
                    grad_w_attn_in,
                    conv_w_full,
                    conv_b_full,
                    grad_w_ssm_out,
                    grad_w_attn_out,
                )
            ),
        )
    rate_total, bias_total, skip_total = lax.psum((rate_sum, bias_sum, skip_sum), ("seq", "fsdp"))
    (
        gain_in_grad,
        ssm_in_grad,
        attn_in_grad,
        conv_w_grad,
        conv_b_grad,
        ssm_out_grad,
        attn_out_grad,
    ) = mixer_sums
    gain_ffn_grad, gate_grad, up_grad, down_grad = ffn_sums
    return (
        jnp.stack(outputs_list)[:, None],
        jnp.stack(input_grads)[:, None],
        gain_in_grad,
        ssm_in_grad,
        attn_in_grad,
        conv_w_grad,
        conv_b_grad,
        rate_total,
        bias_total,
        skip_total,
        ssm_out_grad,
        attn_out_grad,
        gain_ffn_grad,
        gate_grad,
        up_grad,
        down_grad,
    )


def solution(mesh):
    return jax.shard_map(
        on_device,
        mesh=mesh,
        in_specs=(
            P(None, "fsdp", "seq", None),
            P(None, "fsdp", "seq", None),
            P(None, "fsdp", None),
            P(("seq", "fsdp")),
            P(("seq", "fsdp"), None),
            P(("seq", "fsdp"), None),
            P(None, ("seq", "fsdp")),
            P(("seq", "fsdp")),
            P(),
            P(),
            P(),
            P(("seq", "fsdp"), None),
            P(("seq", "fsdp"), None),
            P(("seq", "fsdp")),
            P(("seq", "fsdp"), None),
            P(("seq", "fsdp"), None),
            P(("seq", "fsdp"), None),
        ),
        out_specs=(
            P(None, "fsdp", "seq", None),
            P(None, "fsdp", "seq", None),
            P(("seq", "fsdp")),
            P(("seq", "fsdp"), None),
            P(("seq", "fsdp"), None),
            P(None, ("seq", "fsdp")),
            P(("seq", "fsdp")),
            P(),
            P(),
            P(),
            P(("seq", "fsdp"), None),
            P(("seq", "fsdp"), None),
            P(("seq", "fsdp")),
            P(("seq", "fsdp"), None),
            P(("seq", "fsdp"), None),
            P(("seq", "fsdp"), None),
        ),
        check_vma=False,
    )
```

profile of v0, /device:TPU:0, one launch (start us, length us, event | category | flops | bytes accessed | tf_op | source)
XLA Modules:
  0.0 4392.6 jit_solution(17702187349503270403)
XLA Ops:
  11.3 43.5 all-reduce.51
  56.9 125.2 %all-gather.11.cloned.1.call-done = bf16[2048,6704]{1,0:T(8,128)(2,1)} async-done(((bf16[64,6704]{1,0:T(8,128)(2,1)}), bf16[2048,6704]{1,0:T(8,128)(2,1)}) %all-gather.11.cloned.1.call-update) | async-done | bytes 27459600 | tf_op jit(solution)/shard_map/all_gather | solution.py:208
  182.0 20.2 fusion.341
  204.8 17.8 fusion.340
  228.6 24.1 all-gather.17.cloned.1.call-done
  277.1 12.6 all-to-all-done.10
  294.2 42.3 all-gather
  498.0 200.1 %while.156 = (s32[]{:T(128)}, f32[12,64,256]{2,1,0:T(8,128)S(1)}, s32[]{:T(128)}, f32[8,128,12,64]{1,0,3,2:T(8,128)}, f32[8,12,64,256]{3,2,1,0:T(8,128)}, /*inde...) while((s32[]{:T(128)}, f32[12,64,256]{2,1,0:T(8,128)S(1)}, ...), condition=%wide.region_3.5_spmd.clone, body=%wide.region_1.4_spmd.clone.sunk | while | flops 807818240 | bytes 7521302 | solution.py:111
  713.6 199.8 %while.157 = (s32[]{:T(128)}, f32[12,64,256]{2,1,0:T(8,128)S(1)}, s32[]{:T(128)}, f32[8,128,12,64]{1,0,3,2:T(8,128)}, f32[8,12,64,256]{3,2,1,0:T(8,128)}, /*inde...) while((s32[]{:T(128)}, f32[12,64,256]{2,1,0:T(8,128)S(1)}, ...), condition=%wide.region_12.14_spmd.clone, body=%wide.region_10.13_spmd.clone.sunk | while | flops 807818240 | bytes 7521302 | solution.py:111
  926.7 21.9 while.155
  968.2 21.8 while.154
  1059.3 13.3 multiply_convert_fusion.4
  1072.6 12.4 fusion.350
  1085.1 14.4 multiply_reduce_fusion.21
  1120.2 13.9 multiply_convert_fusion.2
  1146.3 14.3 multiply_reduce_fusion.20
  1165.4 13.2 fusion.235
  1182.2 12.4 fusion.239
  1216.7 305.4 %while.160 = (s32[]{:T(128)}, f32[12,64,256]{2,1,0:T(8,128)}, f32[8,128,12,64]{1,0,3,2:T(8,128)}, f32[8,128,12]{2,1,0:T(8,128)}, f32[8,128,12]{2,1,0:T(8,128)}, ...) while((s32[]{:T(128)}, f32[12,64,256]{2,1,0:T(8,128)}, ...), condition=%wide.region_50.52_spmd.clone, body=%wide.region_40.51_spmd.clone.sunk | while | flops 1969253888 | bytes 19313112 | solution.py:111
  1536.5 310.1 %while.158 = (s32[]{:T(128)}, f32[12,64,256]{2,1,0:T(8,128)}, f32[8,128,12,64]{1,0,3,2:T(8,128)}, f32[8,128,12]{2,1,0:T(8,128)}, f32[8,128,12]{2,1,0:T(8,128)}, ...) while((s32[]{:T(128)}, f32[12,64,256]{2,1,0:T(8,128)}, ...), condition=%wide.region_29.31_spmd.clone, body=%wide.region_19.30_spmd.clone.sunk | while | flops 1969253888 | bytes 19313112 | solution.py:111
  1871.8 15.9 multiply_reduce_fusion.13
  1887.8 12.5 multiply_reduce_fusion.17
  1900.4 14.4 multiply_multiply_fusion.6
  1914.8 17.8 fusion.221
  1967.5 91.2 %while.161 = (s32[]{:T(128)}, f32[1024,2,128]{2,1,0:T(2,128)}, f32[1024,2,128]{2,0,1:T(8,128)}, f32[1024,2,128]{0,2,1:T(8,128)}, s32[2]{0:T(128)S(1)}, /*index=5...) while((s32[]{:T(128)}, f32[1024,2,128]{2,1,0:T(2,128)}, ...), condition=%wide.region_56.58_spmd.clone, body=%wide.region_52.57_spmd.clone.sunk | while | flops 8077839872 | bytes 111221216 | solution.py:136
  1989.8 12.3 fusion.678
  2026.4 12.4 fusion.678
  2069.5 81.0 %while.159 = (s32[]{:T(128)}, f32[1024,2,128]{2,1,0:T(2,128)}, f32[1024,2,128]{2,0,1:T(8,128)}, f32[1024,2,128]{0,2,1:T(8,128)}, s32[2]{0:T(128)S(1)}, /*index=5...) while((s32[]{:T(128)}, f32[1024,2,128]{2,1,0:T(2,128)}, ...), condition=%wide.region_35.37_spmd.clone, body=%wide.region_31.36_spmd.clone.sunk | while | flops 8077839872 | bytes 111221216 | solution.py:136
  2128.2 12.4 fusion.640
  2264.1 17.3 convolution_add_fusion.12
  2282.7 15.0 fusion.354
  2297.6 26.7 convolution_add_fusion.11
  2324.4 16.4 fusion.355
  2340.8 25.1 convolution_add_fusion.10
  2367.5 15.5 fusion.275
  2383.0 25.3 convolution_add_fusion.9
  2437.0 16.7 all-to-all-done.15
  2458.4 25.1 fusion.283
  2483.5 42.7 convolution_add_fusion.8
  2526.9 12.7 fusion.252
  2560.2 22.3 convolution_add_fusion.15
  2582.5 16.7 fusion.260
  2599.2 39.1 all-reduce.50
  2648.4 63.0 %reduce-scatter.21.cloned.1.call-done = f32[96,2048]{1,0:T(8,128)} async-done(((f32[3072,2048]{1,0:T(8,128)}), f32[96,2048]{1,0:T(8,128)}) %reduce-scatter.21.cloned.1.call-update) | async-done | bytes 786448 | tf_op jit(solution)/shard_map/reduce_scatter | solution.py:242
  2711.4 363.5 %reduce-scatter.25.cloned.1.call-done = f32[64,4096]{1,0:T(8,128)} async-done(((f32[2048,4096]{1,0:T(8,128)}), f32[64,4096]{1,0:T(8,128)}) %reduce-scatter.25.cloned.1.call-update) | async-done | bytes 1048592 | tf_op jit(solution)/shard_map/reduce_scatter | solution.py:229
  3075.0 360.5 %reduce-scatter.27.cloned.1.call-done = f32[64,4096]{1,0:T(8,128)} async-done(((f32[2048,4096]{1,0:T(8,128)}), f32[64,4096]{1,0:T(8,128)}) %reduce-scatter.27.cloned.1.call-update) | async-done | bytes 1048592 | tf_op jit(solution)/shard_map/reduce_scatter | solution.py:230
  3435.5 360.5 %reduce-scatter.29.cloned.1.call-done = f32[128,2048]{1,0:T(8,128)} async-done(((f32[4096,2048]{1,0:T(8,128)}), f32[128,2048]{1,0:T(8,128)}) %reduce-scatter.29.cloned.1.call-update) | async-done | bytes 1048592 | tf_op jit(solution)/shard_map/reduce_scatter | solution.py:231
  3795.9 589.6 %reduce-scatter.17.cloned.1.call-done = f32[64,6704]{1,0:T(8,128)} async-done(((f32[2048,6704]{1,0:T(8,128)}), f32[64,6704]{1,0:T(8,128)}) %reduce-scatter.17.cloned.1.call-update) | async-done | bytes 1716240 | tf_op jit(solution)/shard_map/reduce_scatter | solution.py:238
  (1894 shorter events, 1767.4 us)
Async XLA Ops:
  7.2 174.9 %all-gather.11.cloned.1.call-start = ((), (), s32[]{:S(2)}) async-start(), calls=%async_computation.38 | async-start | bytes 28655616 | tf_op jit(solution)/shard_map/all_gather | solution.py:208
  7.9 244.8 %all-gather.17.cloned.1.call-start = ((), (), s32[]{:S(2)}) async-start(), calls=%async_computation.41 | async-start | bytes 6488064 | tf_op jit(solution)/shard_map/all_gather | solution.py:209
  8.7 449.1 %all-gather.13.cloned.1.call-start = ((), (), s32[]{:S(2)}) async-start(), calls=%async_computation.39 | async-start | bytes 1310720 | tf_op jit(solution)/shard_map/all_gather | solution.py:338
  204.7 257.7 %all-gather.27.cloned.1.call-start = ((), (), s32[]{:S(2)}) async-start(), calls=%async_computation.46 | async-start | bytes 1310720 | tf_op jit(solution)/shard_map/all_gather | solution.py:338
  225.2 782.4 %all-gather.15.cloned.1.call-start = ((), (), s32[]{:S(2)}) async-start(), calls=%async_computation.40 | async-start | bytes 12976128 | tf_op jit(solution)/shard_map/all_gather | solution.py:212
  225.8 799.9 %all-gather.19.cloned.1.call-start = ((), (), s32[]{:S(2)}) async-start(), calls=%async_computation.42 | async-start | bytes 4325376 | tf_op jit(solution)/shard_map/all_gather | solution.py:213
  226.3 812.1 %all-gather.21.cloned.1.call-start = ((), (), s32[]{:S(2)}) async-start(), calls=%async_computation.43 | async-start | bytes 17301504 | tf_op jit(solution)/shard_map/all_gather | solution.py:220
  227.1 822.0 %all-gather.23.cloned.1.call-start = ((), (), s32[]{:S(2)}) async-start(), calls=%async_computation.44 | async-start | bytes 17301504 | tf_op jit(solution)/shard_map/all_gather | solution.py:221
  227.8 831.5 %all-gather.25.cloned.1.call-start = ((), (), s32[]{:S(2)}) async-start(), calls=%async_computation.45 | async-start | bytes 17301504 | tf_op jit(solution)/shard_map/all_gather | solution.py:222
  258.9 13.3 all-to-all-start.4
  272.3 17.5 all-to-all-start.10
  290.7 47.0 %all-to-all-start.11 = ((bf16[256,4,256]{0,2,1:T(8,128)(2,1)}), bf16[256,4,256]{0,2,1:T(8,128)(2,1)S(1)}, u32[]{:S(2)}, u32[]{:S(2)}) async-start(bf16[256,4,256]{0,2,1:T(8,128)(2,1)} %bitcast.37), calls=%async_computation.11 | async-start | bytes 1048576 | tf_op jit(solution)/shard_map/all_to_all | solution.py:331
  337.6 12.2 all-to-all-start.3
  350.8 17.9 all-to-all-start.12
  355.8 557.6 %copy-start.127 = (f32[768]{0:T(1024)}, f32[768]{0:T(1024)S(1)}, u32[]{:S(2)}) copy-start(f32[768]{0:T(1024)S(1)} %mul.2213) | copy-start | bytes 9220
  368.7 8.0 all-to-all-start.7
  376.7 8.5 all-to-all-start
  385.2 38.2 all-to-all-start.1
  423.4 26.4 all-to-all-start.8
  450.7 471.2 %all-to-all-start.5 = ((bf16[256,4,256]{0,2,1:T(8,128)(2,1)}), bf16[256,4,256]{0,2,1:T(8,128)(2,1)}, u32[]{:S(2)}, u32[]{:S(2)}) async-start(bf16[256,4,256]{0,2,1:T(8,128)(2,1)} %bitcast.19), calls=%async_computation.5 | async-start | bytes 1048576 | tf_op jit(solution)/shard_map/all_to_all | solution.py:334
  921.8 41.7 all-to-all-start.9
  963.5 34.5 all-to-all-start.2
  998.0 23.4 all-to-all-start.6
  1021.4 10.9 all-to-all-start.13
  1178.6 20.5 all-to-all-start.21
  1199.1 323.0 %all-to-all-start.14 = ((bf16[256,4,768]{0,2,1:T(8,128)(2,1)}), bf16[256,4,768]{0,2,1:T(8,128)(2,1)}, u32[]{:S(2)}, u32[]{:S(2)}) async-start(bf16[256,4,768]{0,2,1:T(8,128)(2,1)} %bitcast.1047), calls=%async_computation.14 | async-start | bytes 3145728 | tf_op jit(solution)/shard_map/all_to_all | solution.py:458
  1203.5 1254.9 %reduce-scatter.13.cloned.1.call-start = ((), (), s32[]{:S(2)}) async-start(), calls=%async_computation.47 | async-start | bytes 1310720 | tf_op jit(solution)/shard_map/reduce_scatter | solution.py:491
  1939.2 20.1 all-to-all-start.24
  1943.4 540.1 %reduce-scatter.15.cloned.1.call-start = ((), (), s32[]{:S(2)}) async-start(), calls=%async_computation.48 | async-start | bytes 1310720 | tf_op jit(solution)/shard_map/reduce_scatter | solution.py:491
  1945.8 612.9 %reduce-scatter.31.cloned.1.call-start = ((), (), s32[]{:S(2)}) async-start(), calls=%async_computation.56 | async-start | bytes 1892352
  1954.9 693.5 %reduce-scatter.23.cloned.1.call-start = ((), (), s32[]{:S(2)}) async-start(), calls=%async_computation.52 | async-start | bytes 8650752 | tf_op jit(solution)/shard_map/reduce_scatter | solution.py:243
  1959.3 102.2 %all-to-all-start.17 = ((bf16[256,4,256]{2,0,1:T(8,128)(2,1)}), bf16[256,4,256]{2,0,1:T(8,128)(2,1)}, u32[]{:S(2)}, u32[]{:S(2)}) async-start(bf16[256,4,256]{2,0,1:T(8,128)(2,1)} %bitcast.693), calls=%async_computation.18 | async-start | bytes 1048576 | tf_op jit(solution)/shard_map/all_to_all | solution.py:459
  2061.5 105.2 %all-to-all-start.27 = ((bf16[4,256,256]{2,1,0:T(8,128)(2,1)}), bf16[4,256,256]{2,1,0:T(8,128)(2,1)}, u32[]{:S(2)}, u32[]{:S(2)}) async-start(bf16[4,256,256]{2,1,0:T(8,128)(2,1)} %copy.624), calls=%async_computation.29 | async-start | bytes 1048576 | tf_op jit(solution)/shard_map/all_to_all | solution.py:487
  2166.7 14.5 all-to-all-start.26
  2181.1 13.5 all-to-all-start.25
  2194.7 14.3 all-to-all-start.20
  2208.9 12.5 all-to-all-start.19
  2221.5 13.5 all-to-all-start.18
  2224.9 423.5 %reduce-scatter.19.cloned.1.call-start = ((), (), s32[]{:S(2)}) async-start(), calls=%async_computation.50 | async-start | bytes 12976128 | tf_op jit(solution)/shard_map/reduce_scatter | solution.py:239
  2251.1 460.3 %reduce-scatter.21.cloned.1.call-start = ((), (), s32[]{:S(2)}) async-start(), calls=%async_computation.51 | async-start | bytes 25952256 | tf_op jit(solution)/shard_map/reduce_scatter | solution.py:242
  2281.5 793.5 %reduce-scatter.25.cloned.1.call-start = ((), (), s32[]{:S(2)}) async-start(), calls=%async_computation.53 | async-start | bytes 34603008 | tf_op jit(solution)/shard_map/reduce_scatter | solution.py:229
  2324.4 1111.1 %reduce-scatter.27.cloned.1.call-start = ((), (), s32[]{:S(2)}) async-start(), calls=%async_computation.54 | async-start | bytes 34603008 | tf_op jit(solution)/shard_map/reduce_scatter | solution.py:230
  2365.9 1430.0 %reduce-scatter.29.cloned.1.call-start = ((), (), s32[]{:S(2)}) async-start(), calls=%async_computation.55 | async-start | bytes 34603008 | tf_op jit(solution)/shard_map/reduce_scatter | solution.py:231
  2414.3 8.9 all-to-all-start.23
  2423.2 8.0 all-to-all-start.16
  2431.2 22.6 all-to-all-start.15
  2453.8 29.7 all-to-all-start.22
  2458.1 1927.4 %reduce-scatter.17.cloned.1.call-start = ((), (), s32[]{:S(2)}) async-start(), calls=%async_computation.49 | async-start | bytes 57311232 | tf_op jit(solution)/shard_map/reduce_scatter | solution.py:238
  (198 other events, 4634.6 us)
Sparse Core Ops, SparseCore 0:
  10.9 171.1 all-gather.10
  185.0 67.5 all-gather.16
  255.1 34.8 all-gather.12
  292.3 26.7 all-gather.26
  321.9 117.9 all-gather.14
  442.7 67.2 all-gather.18
  513.0 113.5 all-gather.20
  629.6 113.0 all-gather.22
  745.7 113.1 all-gather.24
  1935.0 29.8 reduce-scatter.12
  1968.0 28.8 reduce-scatter.14
  1999.0 136.7 reduce-scatter.30
  2138.8 148.9 reduce-scatter.22
  2295.3 165.4 reduce-scatter.18
  2467.6 243.7 reduce-scatter.20
  2714.3 360.6 reduce-scatter.24
  3077.8 357.6 reduce-scatter.26
  3438.3 357.6 reduce-scatter.28
  3798.9 586.5 reduce-scatter.16
where the time goes:
time: 4420 us; the launch traced here: 4390 us
  waiting for transfers between devices  1980 us (45%)
  matrix products  981 us (22%)
  local copies, waits for them, and re-layouts  759 us (17%)
  other arithmetic  340 us (8%)
  blocking collectives  125 us (3%)
  starting transfers between devices  114 us (3%)
  loops' own time  77 us (2%)
    reduce_scatter x1, waiting for transfers between devices, spread_mixer(): lax.psum_scatter(local_grads[1], ('seq', 'fsdp'), scatter_dimension=0, ti...  590 us
    reduce_scatter x1, waiting for transfers between devices, spread_ffn(): lax.psum_scatter(local_grads[1], ('seq', 'fsdp'), scatter_dimension=0, ti...  364 us
    dynamic_update_slice x64, local copies, waits for them, and re-layouts, ssd_scan(): lax.scan(jax.checkpoint(block_step), start_carry, seq_items)  363 us
    reduce_scatter x1, waiting for transfers between devices, spread_ffn(): lax.psum_scatter(local_grads[2], ('seq', 'fsdp'), scatter_dimension=0, ti...  360 us
    reduce_scatter x1, waiting for transfers between devices, spread_ffn(): lax.psum_scatter(local_grads[3], ('seq', 'fsdp'), scatter_dimension=0, ti...  360 us
    dot_general x14, matrix products, weight_grad(): jnp.einsum('tc,td->cd', left, right, preferred_element_type=jnp.float32)  236 us
    dot_general x14, matrix products, matmul_back(): jnp.einsum('td,cd->tc', left, right, preferred_element_type=jnp.float32)  158 us
    dot_general x14, matrix products, matmul_rows(): jnp.einsum('tc,cd->td', left, right, preferred_element_type=jnp.float32)  136 us
  transfers between devices with their start and end apart: 47, of which 22 were waited for; matrix products, arithmetic and copies ran while one was open for 35% of the time, Pallas kernels for 0%

commit v1 on v0

v1 whole, which is shorter than its diff:
```python
import jax
import jax.numpy as jnp
from jax import lax
from jax.sharding import PartitionSpec as P

SSM_HEADS = 48
SSM_DIM = 64
STATE = 256
CONV = 4
Q_HEADS = 8
KV_HEADS = 2
HEAD_DIM = 128
MICRO = 2
SPAN = 128
ATT_BLOCK = 512
SSM_INNER = 3072
CONV_CH = 3584


PRECISE = lax.Precision.HIGHEST
EPSILON = 1e-05
ROPE_BASE = 10000.0


def round_plain(value):
    return lax.optimization_barrier(value.astype(jnp.bfloat16)).astype(jnp.float32)


def round_keep(value):
    return (round_plain(value), None)


def round_pass(kept, grad):
    return (grad,)


def make_rounder():
    rounder = jax.custom_vjp(round_plain)
    rounder.defvjp(round_keep, round_pass)
    return rounder


def rotate(head_rows, positions):
    half_width = head_rows.shape[-1] // 2
    frequency = ROPE_BASE ** (-jnp.arange(half_width).astype(jnp.float32) / half_width)
    angles = positions.astype(jnp.float32)[:, None] * frequency[None, :]
    cosine = jnp.cos(angles)[:, None, :]
    sine_part = jnp.sin(angles)[:, None, :]
    lead_half = head_rows[..., :half_width]
    tail_half = head_rows[..., half_width:]
    return jnp.concatenate(
        [lead_half * cosine - tail_half * sine_part, tail_half * cosine + lead_half * sine_part],
        axis=-1,
    )


def causal_conv(channels, segment, conv_weight, conv_bias):
    length = channels.shape[0]
    summed = jnp.broadcast_to(conv_bias[None, :], channels.shape)
    for offset in range(CONV):
        shifted = jnp.pad(channels, ((offset, 0), (0, 0)))[:length]
        earlier = jnp.pad(segment, (offset, 0), constant_values=-1)[:length]
        keep_mask = (earlier == segment).astype(jnp.float32)
        summed = summed + conv_weight[CONV - 1 - offset][None, :] * shifted * keep_mask[:, None]
    return jax.nn.silu(summed)


def ssd_scan(x_heads, log_decay, step_size, b_rows, c_rows, segment):
    length, head_count, head_width = x_heads.shape
    block_count = length // SPAN
    seq_items = (
        x_heads.reshape(block_count, SPAN, head_count, head_width),
        log_decay.reshape(block_count, SPAN, head_count),
        step_size.reshape(block_count, SPAN, head_count),
        b_rows.reshape(block_count, SPAN, STATE),
        c_rows.reshape(block_count, SPAN, STATE),
        segment.reshape(block_count, SPAN),
    )
    lower_mask = jnp.tril(jnp.ones((SPAN, SPAN), dtype=bool))

    def block_step(block_carry, block_items):
        ssm_state, last_segment = block_carry
        x_block, decay_block, step_block, b_block, c_block, seg_block = block_items
        cumulative = jnp.cumsum(decay_block, axis=0)
        same_doc = ((seg_block[:, None] == seg_block[None, :]) & lower_mask)[:, :, None]
        decay_gap = cumulative[:, None, :] - cumulative[None, :, :]
        inner_weight = jnp.where(same_doc, jnp.exp(jnp.where(same_doc, decay_gap, 0.0)), 0.0)
        block_scores = jnp.dot(c_block, b_block.T, precision=PRECISE)
        mixing = inner_weight * block_scores[:, :, None] * step_block[None, :, :]
        y_inner = jnp.einsum("tsh,shp->thp", mixing, x_block, precision=PRECISE)
        carry_keep = (seg_block == last_segment).astype(jnp.float32)
        state_weight = jnp.exp(cumulative) * carry_keep[:, None]
        from_state = (
            jnp.einsum("tn,hpn->thp", c_block, ssm_state, precision=PRECISE)
            * state_weight[:, :, None]
        )
        end_keep = (seg_block == seg_block[-1]).astype(jnp.float32)
        input_weight = (
            jnp.exp(cumulative[-1][None, :] - cumulative) * step_block * end_keep[:, None]
        )
        state_keep = jnp.exp(cumulative[-1]) * (seg_block[-1] == last_segment).astype(jnp.float32)
        new_state = ssm_state * state_keep[:, None, None] + jnp.einsum(
            "sh,shp,sn->hpn", input_weight, x_block, b_block, precision=PRECISE
        )
        return ((new_state, seg_block[-1]), y_inner + from_state)

    start_carry = (
        jnp.zeros((head_count, head_width, STATE), jnp.float32),
        jnp.array(-1, jnp.int32),
    )
    unused, y_blocks = lax.scan(jax.checkpoint(block_step), start_carry, seq_items)
    return y_blocks.reshape(length, head_count, head_width)


def attend(q_rot, k_rot, value_heads, segment):
    length, head_count, head_width = q_rot.shape
    block_count = length // ATT_BLOCK
    positions = jnp.arange(length, dtype=jnp.int32)
    rounder = make_rounder()

    def one_block(block_index):
        first_row = block_index * ATT_BLOCK
        q_block = lax.dynamic_slice_in_dim(q_rot, first_row, ATT_BLOCK, 0)
        seg_query = lax.dynamic_slice_in_dim(segment, first_row, ATT_BLOCK, 0)
        pos_query = first_row + jnp.arange(ATT_BLOCK, dtype=jnp.int32)
        scores = jnp.einsum("qhe,khe->hqk", q_block, k_rot, precision=PRECISE) * head_width ** (
            -0.5
        )
        allowed = (pos_query[:, None] >= positions[None, :]) & (
            seg_query[:, None] == segment[None, :]
        )
        scores = jnp.where(allowed[None, :, :], scores, -1e30)
        attn_probs = rounder(jax.nn.softmax(scores, axis=-1))
        return jnp.einsum("hqk,khe->qhe", attn_probs, value_heads, precision=PRECISE)

    blocks = lax.map(jax.checkpoint(one_block), jnp.arange(block_count, dtype=jnp.int32))
    return blocks.reshape(length, head_count, head_width)


def mixer_heads(
    x_part,
    dt_part,
    query_rows,
    key_rep,
    value_rep,
    bc_part,
    segment,
    conv_weight,
    conv_bias,
    log_rate,
    step_bias,
    skip_gain,
):
    rounder = make_rounder()
    length = x_part.shape[0]
    inner_width = x_part.shape[1]
    head_count = dt_part.shape[1]
    conv_out = rounder(
        causal_conv(jnp.concatenate([x_part, bc_part], axis=1), segment, conv_weight, conv_bias)
    )
    x_heads = conv_out[:, :inner_width].reshape(length, head_count, inner_width // head_count)
    b_rows = conv_out[:, inner_width : inner_width + STATE]
    c_rows = conv_out[:, inner_width + STATE :]
    step_size = jax.nn.softplus(dt_part + step_bias[None, :])
    log_decay = -jnp.exp(log_rate)[None, :] * step_size
    y_heads = (
        ssd_scan(x_heads, log_decay, step_size, b_rows, c_rows, segment)
        + skip_gain[None, :, None] * x_heads
    )
    y_rows = rounder(y_heads.reshape(length, inner_width))
    positions = jnp.arange(length, dtype=jnp.int32)
    query_heads = query_rows.shape[1] // HEAD_DIM
    q_rot = rounder(rotate(query_rows.reshape(length, query_heads, HEAD_DIM), positions))
    k_rot = rounder(rotate(key_rep.reshape(length, query_heads, HEAD_DIM), positions))
    attended = attend(q_rot, k_rot, value_rep.reshape(length, query_heads, HEAD_DIM), segment)
    attended = rounder(attended.reshape(length, query_heads * HEAD_DIM))
    return (y_rows, attended)


def norm_forward(token_rows, gain_vec):
    inv_scale = lax.rsqrt(jnp.mean(token_rows * token_rows, axis=-1, keepdims=True) + EPSILON)
    return (token_rows * inv_scale * gain_vec, inv_scale)


def norm_backward(token_rows, inv_scale, gain_vec, grad_rows):
    normed = token_rows * inv_scale
    gain_grad = jnp.sum(normed * grad_rows, axis=0)
    weighted = grad_rows * gain_vec
    row_grad = inv_scale * (weighted - normed * jnp.mean(weighted * normed, axis=-1, keepdims=True))
    return (row_grad, gain_grad)


def repeat_heads(kv_rows, groups):
    length = kv_rows.shape[0]
    shaped = kv_rows.reshape(length, -1, 1, HEAD_DIM)
    return jnp.broadcast_to(shaped, (length, shaped.shape[1], groups, HEAD_DIM)).reshape(length, -1)


def fold_heads(rep_rows, groups):
    length = rep_rows.shape[0]
    summed = jnp.sum(rep_rows.astype(jnp.float32).reshape(length, -1, groups, HEAD_DIM), axis=2)
    return summed.reshape(length, -1).astype(jnp.bfloat16)


def matmul_rows(left, right):
    return jnp.einsum("tc,cd->td", left, right, preferred_element_type=jnp.float32)


def matmul_back(left, right):
    return jnp.einsum("td,cd->tc", left, right, preferred_element_type=jnp.float32)


def weight_grad(left, right):
    return jnp.einsum("tc,td->cd", left, right, preferred_element_type=jnp.float32)


def peers(count, flip):
    return [(i, i ^ flip) for i in range(count)]


def gather_tokens(rows):
    count = lax.axis_size("seq")
    index = lax.axis_index("seq")
    tokens = rows.shape[0]
    whole = jnp.zeros((count * tokens, rows.shape[1]), rows.dtype)
    for flip in range(count):
        part = rows if flip == 0 else lax.ppermute(rows, "seq", peers(count, flip))
        whole = lax.dynamic_update_slice_in_dim(whole, part, (index ^ flip) * tokens, 0)
    return whole


def scatter_tokens(product):
    count = lax.axis_size("seq")
    index = lax.axis_index("seq")
    arrived = []
    for flip in range(count - 1, 0, -1):
        part = product(index ^ flip).astype(jnp.bfloat16)
        arrived.append(lax.ppermute(part, "seq", peers(count, flip)))
    total = product(index)
    for part in arrived:
        total = total + part.astype(jnp.float32)
    return total


def add_small(vector):
    for axis in ("fsdp", "seq"):
        count = lax.axis_size(axis)
        flip = 1
        while flip < count:
            vector = vector + lax.ppermute(vector, axis, peers(count, flip))
            flip *= 2
    return vector


def spread_columns(stacked):
    mine = lax.all_to_all(stacked, "seq", split_axis=0, concat_axis=0, tiled=True)
    whole = lax.all_gather(mine.reshape(-1, mine.shape[-1]), "fsdp", axis=0, tiled=True)
    return whole


def collect_columns(grad):
    count = lax.axis_size("seq")
    part = lax.psum_scatter(grad.astype(jnp.bfloat16), "fsdp", scatter_dimension=0, tiled=True)
    part = part.reshape(count, -1, part.shape[-1])
    return lax.all_to_all(part, "seq", split_axis=0, concat_axis=0, tiled=True)


def collect_rows(grad):
    return lax.psum_scatter(
        grad.astype(jnp.bfloat16), "fsdp", scatter_dimension=0, tiled=True
    ).astype(jnp.float32)


def to_gathered(rows):
    seq, fsdp = lax.axis_size("seq"), lax.axis_size("fsdp")
    shape = rows.shape
    split = rows.reshape(shape[:-1] + (seq, fsdp, -1))
    return jnp.swapaxes(split, -3, -2).reshape(shape)


def from_gathered(rows):
    seq, fsdp = lax.axis_size("seq"), lax.axis_size("fsdp")
    shape = rows.shape
    split = rows.reshape(shape[:-1] + (fsdp, seq, -1))
    return jnp.swapaxes(split, -3, -2).reshape(shape)


def inv_rms(token_rows):
    return lax.rsqrt(jnp.mean(token_rows * token_rows, axis=-1, keepdims=True) + EPSILON)


def on_device(
    inputs,
    cotangent,
    segments,
    norm_in,
    ssm_in,
    attn_in,
    conv_w,
    conv_b,
    a_log,
    dt_bias,
    d_skip,
    ssm_out,
    attn_out,
    norm_ffn,
    w_gate,
    w_up,
    w_down,
):
    f32, bf16 = jnp.float32, jnp.bfloat16
    seq = lax.axis_size("seq")
    fsdp = lax.axis_size("fsdp")
    index = lax.axis_index("seq")
    rows = ssm_in.shape[0]
    tokens = inputs.shape[2]
    heads = SSM_HEADS // seq
    inner = heads * SSM_DIM
    query_heads = Q_HEADS // seq
    q_width = query_heads * HEAD_DIM
    groups = Q_HEADS // KV_HEADS
    kv_of = [(s * query_heads) // groups for s in range(seq)]
    head_start = index * heads
    inner_start = index * inner
    rate_local = lax.dynamic_slice_in_dim(a_log.astype(f32), head_start, heads)
    bias_local = lax.dynamic_slice_in_dim(dt_bias.astype(f32), head_start, heads)
    skip_local = lax.dynamic_slice_in_dim(d_skip.astype(f32), head_start, heads)

    def by_seq(block):
        return jnp.swapaxes(block.reshape(rows, seq, -1), 0, 1)

    def for_all(block):
        return jnp.broadcast_to(block[None], (seq,) + block.shape)

    channels = conv_b.shape[0]
    conv_pack = jnp.concatenate([conv_w, conv_b[None]], axis=0).reshape(-1)
    conv_cols = -(-conv_pack.shape[0] // rows)
    conv_pack = jnp.pad(conv_pack, (0, conv_cols * rows - conv_pack.shape[0]))
    misc = jnp.concatenate([norm_in[:, None], norm_ffn[:, None], conv_pack.reshape(rows, conv_cols)], axis=1)
    misc_pad = -(heads + misc.shape[1]) % 128
    z_end, x_end, bc_end = SSM_INNER, 2 * SSM_INNER, 2 * SSM_INNER + 2 * STATE
    first_send = jnp.concatenate(
        [
            by_seq(ssm_in[:, z_end:x_end]),
            for_all(ssm_in[:, x_end:bc_end]),
            by_seq(ssm_in[:, bc_end:]),
            for_all(jnp.pad(misc, ((0, 0), (0, misc_pad)))),
        ],
        axis=2,
    )
    q_end = Q_HEADS * HEAD_DIM
    kv_end = q_end + KV_HEADS * HEAD_DIM

    def by_kv(block):
        return jnp.stack([block[:, h * HEAD_DIM : (h + 1) * HEAD_DIM] for h in kv_of])

    second_send = jnp.concatenate(
        [
            by_seq(ssm_in[:, :z_end]),
            by_seq(attn_in[:, :q_end]),
            by_kv(attn_in[:, q_end:kv_end]),
            by_kv(attn_in[:, kv_end:]),
        ],
        axis=2,
    )
    ffn_send = jnp.concatenate([by_seq(w_gate), by_seq(w_up)], axis=2)
    first_w = spread_columns(first_send)
    second_w = spread_columns(second_send)
    whole_ssm_out = lax.all_gather(ssm_out, "fsdp", axis=0, tiled=True)
    whole_attn_out = lax.all_gather(attn_out, "fsdp", axis=0, tiled=True)
    gate_up_w = spread_columns(ffn_send)
    down_w = lax.all_gather(w_down, "fsdp", axis=0, tiled=True)
    units = down_w.shape[0]

    misc_at = inner + 2 * STATE + heads
    small = first_w[:, misc_at : misc_at + misc.shape[1]]
    gain_in = small[:, 0].astype(f32)
    gain_ffn = from_gathered(small[:, 1].astype(f32))
    conv_all = small[:, 2:].reshape(fsdp, seq, -1)[:, :, : (CONV + 1) * channels]
    conv_all = conv_all.reshape(fsdp, seq, CONV + 1, channels).transpose(2, 1, 0, 3)
    conv_all = conv_all.reshape(CONV + 1, CONV_CH).astype(f32)
    conv_local = jnp.concatenate(
        [lax.dynamic_slice_in_dim(conv_all, inner_start, inner, 1), conv_all[:, SSM_INNER:]], axis=1
    )

    micro = range(MICRO)
    token_rows = [inputs[m, 0].astype(f32) for m in micro]
    rows_all = [gather_tokens(to_gathered(inputs[m, 0])) for m in micro]
    cot_all = [gather_tokens(cotangent[m, 0]) for m in micro]
    hidden_all, normed_all = [], []
    mixer_out, pullbacks, gate_zs, middles, dts = [], [], [], [], []
    for m in micro:
        segment = segments[m, 0]
        wide = rows_all[m].astype(f32)
        normed = wide * inv_rms(wide)
        hidden = (normed * gain_in).astype(bf16)
        hidden_all.append(hidden)
        first = matmul_rows(hidden, first_w).astype(bf16)
        second = matmul_rows(hidden, second_w)
        gate_z = second[:, :inner]
        attn_rows = second[:, inner:].astype(bf16).astype(f32)

        def local_mixer(x_part, dt_part, query, key, value, bc_part, weight, bias, rate, step_bias, skip):
            key_rep = jnp.tile(key, (1, query_heads))
            value_rep = jnp.tile(value, (1, query_heads))
            return mixer_heads(
                x_part, dt_part, query, key_rep, value_rep, bc_part, segment, weight, bias, rate, step_bias, skip
            )

        (y_rows, attended), pullback = jax.vjp(
            local_mixer,
            first[:, :inner].astype(f32),
            first[:, inner + 2 * STATE : inner + 2 * STATE + heads].astype(f32),
            attn_rows[:, :q_width],
            attn_rows[:, q_width : q_width + HEAD_DIM],
            attn_rows[:, q_width + HEAD_DIM :],
            first[:, inner : inner + 2 * STATE].astype(f32),
            conv_local[:CONV],
            conv_local[CONV],
            rate_local,
            bias_local,
            skip_local,
        )
        gate_zs.append(gate_z)
        pullbacks.append(pullback)
        gated = (y_rows * jax.nn.silu(gate_z)).astype(bf16)
        attended = attended.astype(bf16)
        mixer_out.append((y_rows, gated, attended))

        def mixed_rows(block):
            g = lax.dynamic_slice_in_dim(gated, block * tokens, tokens, 0)
            a = lax.dynamic_slice_in_dim(attended, block * tokens, tokens, 0)
            return matmul_rows(g, whole_ssm_out) + matmul_rows(a, whole_attn_out)

        middles.append(token_rows[m] + scatter_tokens(mixed_rows))

    outputs, grad_middles, ffn_grads = [], [], []
    gain_ffn_grad = 0.0
    for m in micro:
        middle = middles[m]
        scale = inv_rms(middle)
        normed = middle * scale
        hidden = gather_tokens(to_gathered((normed * gain_ffn).astype(bf16)))
        gate_up = matmul_rows(hidden, gate_up_w)
        gate_pre, up_pre = gate_up[:, :units], gate_up[:, units:]
        sig = jax.nn.sigmoid(gate_pre)
        activated = (gate_pre * sig * up_pre).astype(bf16)

        def out_rows(block):
            return matmul_rows(lax.dynamic_slice_in_dim(activated, block * tokens, tokens, 0), down_w)

        outputs.append((middle + scatter_tokens(out_rows)).astype(bf16))
        grad_act = matmul_back(cot_all[m], down_w)
        grad_up = grad_act * gate_pre * sig
        grad_gate = grad_act * up_pre * sig * (1.0 + gate_pre * (1.0 - sig))
        grad_gu = jnp.concatenate([grad_gate, grad_up], axis=1).astype(bf16)

        def hidden_rows(block):
            return matmul_back(lax.dynamic_slice_in_dim(grad_gu, block * tokens, tokens, 0), gate_up_w)

        grad_hidden = from_gathered(scatter_tokens(hidden_rows))
        gain_ffn_grad = gain_ffn_grad + jnp.sum(normed * grad_hidden, axis=0)
        weighted = grad_hidden * gain_ffn
        grad_norm = scale * (weighted - normed * jnp.mean(weighted * normed, axis=-1, keepdims=True))
        grad_middles.append(cotangent[m, 0].astype(f32) + grad_norm)
        ffn_grads.append((weight_grad(hidden, grad_gu), weight_grad(activated, cot_all[m])))
    gate_up_grad = collect_columns(ffn_grads[0][0] + ffn_grads[1][0])
    down_grad = collect_rows(ffn_grads[0][1] + ffn_grads[1][1])

    input_grads, mixer_grads = [], []
    conv_grad = rate_sum = bias_sum = skip_sum = gain_in_grad = 0.0
    for m in micro:
        y_rows, gated, attended = mixer_out[m]
        grad_mixed = gather_tokens(grad_middles[m].astype(bf16))
        grad_gated = matmul_back(grad_mixed, whole_ssm_out)
        grad_attended = matmul_back(grad_mixed, whole_attn_out).astype(bf16)
        gate_z = gate_zs[m]
        sig = jax.nn.sigmoid(gate_z)
        grad_y = (grad_gated * gate_z * sig).astype(bf16)
        grad_z = (grad_gated * y_rows * sig * (1.0 + gate_z * (1.0 - sig))).astype(bf16)
        (g_x, g_dt, g_query, g_key, g_value, g_bc, g_w, g_b, g_rate, g_bias, g_skip) = pullbacks[m](
            (grad_y.astype(f32), grad_attended.astype(f32))
        )
        conv_grad = conv_grad + jnp.concatenate([g_w, g_b[None]], axis=0)
        rate_sum, bias_sum, skip_sum = rate_sum + g_rate, bias_sum + g_bias, skip_sum + g_skip
        first_grad = jnp.concatenate([g_x, g_bc, g_dt], axis=1).astype(bf16)
        first_grad = jnp.pad(first_grad, ((0, 0), (0, first_w.shape[1] - first_grad.shape[1])))
        second_grad = jnp.concatenate(
            [grad_z, g_query.astype(bf16), g_key.astype(bf16), g_value.astype(bf16)], axis=1
        )

        def in_rows(block):
            one = lax.dynamic_slice_in_dim(first_grad, block * tokens, tokens, 0)
            two = lax.dynamic_slice_in_dim(second_grad, block * tokens, tokens, 0)
            return matmul_back(one, first_w) + matmul_back(two, second_w)

        grad_hidden = from_gathered(scatter_tokens(in_rows))
        gain_row = from_gathered(gain_in)
        scale = inv_rms(token_rows[m])
        normed = token_rows[m] * scale
        gain_in_grad = gain_in_grad + jnp.sum(normed * grad_hidden, axis=0)
        weighted = grad_hidden * gain_row
        grad_norm = scale * (weighted - normed * jnp.mean(weighted * normed, axis=-1, keepdims=True))
        input_grads.append((grad_middles[m] + grad_norm).astype(bf16))
        mixer_grads.append(
            (
                weight_grad(hidden_all[m], first_grad),
                weight_grad(hidden_all[m], second_grad),
                weight_grad(gated, grad_mixed),
                weight_grad(attended, grad_mixed),
            )
        )
    first_sum, second_sum, ssm_out_sum, attn_out_sum = (a + b for a, b in zip(*mixer_grads))
    ssm_out_grad = collect_rows(ssm_out_sum)
    attn_out_grad = collect_rows(attn_out_sum)
    second_back = collect_columns(second_sum).astype(f32)
    first_back = collect_columns(first_sum).astype(f32)

    def own_columns(block):
        return jnp.swapaxes(block, 0, 1).reshape(rows, -1)

    ssm_in_grad = jnp.concatenate(
        [
            own_columns(second_back[:, :, :inner]),
            own_columns(first_back[:, :, :inner]),
            jnp.sum(first_back[:, :, inner : inner + 2 * STATE], axis=0),
            own_columns(first_back[:, :, inner + 2 * STATE : inner + 2 * STATE + heads]),
        ],
        axis=1,
    )

    def kv_columns(block):
        return jnp.concatenate(
            [sum(block[s] for s in range(seq) if kv_of[s] == h) for h in range(KV_HEADS)], axis=1
        )

    attn_in_grad = jnp.concatenate(
        [
            own_columns(second_back[:, :, inner : inner + q_width]),
            kv_columns(second_back[:, :, inner + q_width : inner + q_width + HEAD_DIM]),
            kv_columns(second_back[:, :, inner + q_width + HEAD_DIM :]),
        ],
        axis=1,
    )
    gate_up_grad = gate_up_grad.astype(f32)
    gate_grad = own_columns(gate_up_grad[:, :, :units])
    up_grad = own_columns(gate_up_grad[:, :, units:])

    conv_whole = jnp.zeros((CONV + 1, CONV_CH), f32)
    conv_whole = lax.dynamic_update_slice_in_dim(conv_whole, conv_grad[:, :inner], inner_start, 1)
    conv_whole = lax.dynamic_update_slice_in_dim(conv_whole, conv_grad[:, inner:], SSM_INNER, 1)
    head_sums = lax.dynamic_update_slice_in_dim(
        jnp.zeros((3, SSM_HEADS), f32), jnp.stack([rate_sum, bias_sum, skip_sum]), head_start, 1
    )
    pieces = [conv_whole.reshape(-1), head_sums.reshape(-1), gain_in_grad, gain_ffn_grad]
    ends = [0]
    for piece in pieces:
        ends.append(ends[-1] + piece.shape[0])
    total = add_small(jnp.concatenate(pieces))
    conv_total, head_total, gain_in_total, gain_ffn_total = (
        total[a:b] for a, b in zip(ends[:-1], ends[1:])
    )
    place = index * fsdp + lax.axis_index("fsdp")
    conv_total = lax.dynamic_slice_in_dim(conv_total.reshape(CONV + 1, CONV_CH), place * channels, channels, 1)
    head_total = head_total.reshape(3, SSM_HEADS)
    return (
        jnp.stack(outputs)[:, None],
        jnp.stack(input_grads)[:, None],
        lax.dynamic_slice_in_dim(gain_in_total, place * rows, rows),
        ssm_in_grad,
        attn_in_grad,
        conv_total[:CONV],
        conv_total[CONV],
        head_total[0],
        head_total[1],
        head_total[2],
        ssm_out_grad,
        attn_out_grad,
        lax.dynamic_slice_in_dim(gain_ffn_total, place * rows, rows),
        gate_grad,
        up_grad,
        down_grad,
    )


def solution(mesh):
    return jax.shard_map(
        on_device,
        mesh=mesh,
        in_specs=(
            P(None, "fsdp", "seq", None),
            P(None, "fsdp", "seq", None),
            P(None, "fsdp", None),
            P(("seq", "fsdp")),
            P(("seq", "fsdp"), None),
            P(("seq", "fsdp"), None),
            P(None, ("seq", "fsdp")),
            P(("seq", "fsdp")),
            P(),
            P(),
            P(),
            P(("seq", "fsdp"), None),
            P(("seq", "fsdp"), None),
            P(("seq", "fsdp")),
            P(("seq", "fsdp"), None),
            P(("seq", "fsdp"), None),
            P(("seq", "fsdp"), None),
        ),
        out_specs=(
            P(None, "fsdp", "seq", None),
            P(None, "fsdp", "seq", None),
            P(("seq", "fsdp")),
            P(("seq", "fsdp"), None),
            P(("seq", "fsdp"), None),
            P(None, ("seq", "fsdp")),
            P(("seq", "fsdp")),
            P(),
            P(),
            P(),
            P(("seq", "fsdp"), None),
            P(("seq", "fsdp"), None),
            P(("seq", "fsdp")),
            P(("seq", "fsdp"), None),
            P(("seq", "fsdp"), None),
            P(("seq", "fsdp"), None),
        ),
        check_vma=False,
    )
```

time: 4420 us -> 2750 us (0.62)
  waiting for transfers between devices: 1980 us -> 406 us
  matrix products: 981 us -> 841 us
  local copies, waits for them, and re-layouts: 759 us -> 889 us
  blocking collectives: 125 us -> 42.7 us
  other arithmetic: 340 us -> 395 us
    reduce_scatter x9 -> x6, waiting for transfers between devices: 1740 us -> 0.05 us  [the longest x3 0.04 us: collect_columns(): lax.psum_scatter(grad.astype(jnp.bfloat16), 'fsdp', scatter_dimension=0,...]
    ppermute x0 -> x53, waiting for transfers between devices: none -> 385 us  [the longest x24 201 us: scatter_tokens(): arrived.append(lax.ppermute(part, 'seq', peers(count, flip)))]
    all_gather x9 -> x6, waiting for transfers between devices: 149 us -> 0.09 us  [the longest x3 0.02 us: spread_columns(): lax.all_gather(mine.reshape(-1, mine.shape[-1]), 'fsdp', axis=0, tiled=True)]
    dot_general x14 -> x12, matrix products: 236 us -> 102 us  [weight_grad(): jnp.einsum('tc,td->cd', left, right, preferred_element_type=jnp.float32)]
    all_to_all x28 -> x3, starting transfers between devices: 112 us -> 11.2 us  [collect_columns(): return lax.all_to_all(part, 'seq', split_axis=0, concat_axis=0, tiled=True)]
    unnamed x2 -> x0, blocking collectives: 82.6 us -> none
    all_to_all x28 -> x3, waiting for transfers between devices: 88.2 us -> 19.2 us  [collect_columns(): return lax.all_to_all(part, 'seq', split_axis=0, concat_axis=0, tiled=True)]
    convert_element_type x34 -> x7, local copies, waits for them, and re-layouts: 72.5 us -> 8.19 us  [the longest x2 4.54 us: on_device(): hidden = gather_tokens(to_gathered((normed * gain_ffn).astype(bf16)))]
  transfers between devices with their start and end apart: 47 -> 68, of which waited for: 22 -> 38; matrix products, arithmetic and copies ran while one was open for 35% -> 52% of each run, Pallas kernels for 0% -> 0%
where the time goes in v1:
time: 2750 us; the launch traced here: 2720 us
  local copies, waits for them, and re-layouts  889 us (32%)
  matrix products  841 us (31%)
  waiting for transfers between devices  406 us (15%)
  other arithmetic  395 us (14%)
  starting transfers between devices  75.1 us (3%)
  loops' own time  54.4 us (2%)
  blocking collectives  42.7 us (2%)
    dynamic_update_slice x64, local copies, waits for them, and re-layouts, ssd_scan(): lax.scan(jax.checkpoint(block_step), start_carry, seq_items)  381 us
    ppermute x24, waiting for transfers between devices, scatter_tokens(): arrived.append(lax.ppermute(part, 'seq', peers(count, flip)))  201 us
    ppermute x24, waiting for transfers between devices, gather_tokens(): part = rows if flip == 0 else lax.ppermute(rows, 'seq', peers(count, flip))  182 us
    dot_general x30, matrix products, matmul_back(): jnp.einsum('td,cd->tc', left, right, preferred_element_type=jnp.float32)  138 us
    dot_general x30, matrix products, matmul_rows(): jnp.einsum('tc,cd->td', left, right, preferred_element_type=jnp.float32)  123 us
    dot_general x48, matrix products, block_step(): y_inner = jnp.einsum('tsh,shp->thp', mixing, x_block, precision=PRECISE)  119 us
    dot_general x12, matrix products, weight_grad(): jnp.einsum('tc,td->cd', left, right, preferred_element_type=jnp.float32)  102 us
    dot_general x16, matrix products, one_block(): jnp.einsum('qhe,khe->hqk', q_block, k_rot, precision=PRECISE)  101 us
  transfers between devices with their start and end apart: 68, of which 38 were waited for; matrix products, arithmetic and copies ran while one was open for 52% of the time, Pallas kernels for 0%

profile of v1, /device:TPU:0, one launch (start us, length us, event | category | flops | bytes accessed | tf_op | source)
XLA Modules:
  0.0 2721.4 jit_solution(2150682788921743391)
XLA Ops:
  14.4 16.0 all_to_all.30
  32.0 11.9 all_to_all.31
  48.5 14.7 all_to_all.32
  95.9 21.0 collective-permute-done.13
  121.4 17.0 collective-permute-done
  144.4 12.2 collective-permute-done.1
  196.0 11.4 multiply_convert_fusion.1
  254.1 209.1 %while.156 = (s32[]{:T(128)}, f32[12,64,256]{2,1,0:T(8,128)S(1)}, s32[]{:T(128)}, f32[8,128,12,64]{1,0,3,2:T(8,128)}, f32[8,12,64,256]{3,2,1,0:T(8,128)}, /*inde...) while((s32[]{:T(128)}, f32[12,64,256]{2,1,0:T(8,128)S(1)}, ...), condition=%wide.region_3.5_spmd.clone, body=%wide.region_1.4_spmd.clone.sunk | while | flops 807818240 | bytes 7522307 | solution.py:111
  263.5 11.0 dynamic_update_slice.383
  289.7 11.0 dynamic_update_slice.383
  315.8 11.0 dynamic_update_slice.383
  486.0 20.3 while.154
  528.8 13.8 collective-permute-done.3
  543.7 11.6 collective-permute-done.4
  596.2 13.9 collective-permute-done.26
  618.2 11.4 collective-permute-done.6
  650.1 14.6 fusion.540
  664.8 13.4 multiply_convert_fusion.4
  706.0 11.1 collective-permute-done.28
  749.8 243.0 %while.157 = (s32[]{:T(128)}, f32[12,64,256]{2,1,0:T(8,128)}, s32[]{:T(128)}, f32[8,128,12,64]{1,0,3,2:T(8,128)}, f32[8,12,64,256]{3,2,1,0:T(8,128)}, /*index=5*...) while((s32[]{:T(128)}, f32[12,64,256]{2,1,0:T(8,128)}, ...), condition=%wide.region_12.14_spmd.clone, body=%wide.region_10.13_spmd.clone.sunk | while | flops 807818240 | bytes 7522307 | solution.py:111
  1036.6 349.9 %while.158 = (s32[]{:T(128)}, f32[12,64,256]{2,1,0:T(8,128)}, f32[8,128,12,64]{1,0,3,2:T(8,128)}, f32[8,128,12]{2,1,0:T(8,128)}, f32[8,128,12]{2,1,0:T(8,128)}, ...) while((s32[]{:T(128)}, f32[12,64,256]{2,1,0:T(8,128)}, ...), condition=%wide.region_30.32_spmd.clone, body=%wide.region_20.31_spmd.clone.sunk | while | flops 1969253888 | bytes 19669596 | solution.py:111
  1408.0 76.0 %while.159 = (s32[]{:T(128)}, f32[1024,2,128]{2,0,1:T(8,128)}, f32[1024,2,128]{2,0,1:T(8,128)}, f32[1024,2,128]{0,2,1:T(8,128)}, s32[2]{0:T(128)S(1)}, /*index=5...) while((s32[]{:T(128)}, f32[1024,2,128]{2,0,1:T(8,128)}, ...), condition=%wide.region_35.37_spmd.clone, body=%wide.region_31.36_spmd.clone.sunk | while | flops 8077839872 | bytes 125376976 | solution.py:136
  1491.8 22.0 while.155
  1526.7 17.7 collective-permute-done.15
  1546.1 14.9 collective-permute-done.16
  1594.9 17.0 collective-permute-done.38
  1619.9 14.4 collective-permute-done.18
  1655.5 14.8 fusion.541
  1670.4 11.9 multiply_convert_fusion.2
  1714.6 15.7 collective-permute-done.40
  1766.4 12.3 collective-permute-done.42
  1778.9 20.4 collective-permute-done.43
  1807.0 76.1 %while.161 = (s32[]{:T(128)}, f32[1024,2,128]{2,0,1:T(8,128)}, f32[1024,2,128]{2,0,1:T(8,128)}, f32[1024,2,128]{0,2,1:T(8,128)}, s32[2]{0:T(128)S(1)}, /*index=5...) while((s32[]{:T(128)}, f32[1024,2,128]{2,0,1:T(8,128)}, ...), condition=%wide.region_56.58_spmd.clone, body=%wide.region_52.57_spmd.clone.sunk | while | flops 8077839872 | bytes 125376976 | solution.py:136
  1899.9 13.2 add_convert_fusion.2
  1915.1 15.0 multiply_reduce_fusion.17
  1960.3 349.8 %while.160 = (s32[]{:T(128)}, f32[12,64,256]{2,1,0:T(8,128)}, f32[8,128,12,64]{1,0,3,2:T(8,128)}, f32[8,128,12]{2,1,0:T(8,128)}, f32[8,128,12]{2,1,0:T(8,128)}, ...) while((s32[]{:T(128)}, f32[12,64,256]{2,1,0:T(8,128)}, ...), condition=%wide.region_51.53_spmd.clone, body=%wide.region_41.52_spmd.clone.sunk | while | flops 1969253888 | bytes 19669596 | solution.py:111
  1988.6 11.0 dynamic_update_slice.398
  2032.5 11.0 dynamic_update_slice.398
  2329.7 13.2 multiply_reduce_fusion.13
  2343.1 11.8 multiply_multiply_fusion.6
  2358.9 16.4 fusion.243
  2385.2 12.5 add_convert_fusion.1
  2415.2 13.0 collective-permute-done.10
  2433.3 20.9 collective-permute-done.9
  2475.0 12.1 fusion.252
  2487.1 16.1 add_convert_fusion
  2588.3 14.3 collective-permute-done.45
  2602.6 21.4 collective-permute-done.46
  (2303 shorter events, 2080.6 us)
Async XLA Ops:
  7.2 161.8 %all-gather.7.cloned.1.call-start = ((), (), s32[]{:S(2)}) async-start(), calls=%async_computation.12 | async-start | bytes 6488064 | tf_op jit(solution)/shard_map/all_gather | solution.py:257
  30.4 183.2 %all-gather.9.cloned.1.call-start = ((), (), s32[]{:S(2)}) async-start(), calls=%async_computation.13 | async-start | bytes 5898240 | tf_op jit(solution)/shard_map/all_gather | solution.py:257
  44.0 463.1 %all-gather.13.cloned.1.call-start = ((), (), s32[]{:S(2)}) async-start(), calls=%async_computation.15 | async-start | bytes 1179648 | tf_op jit(solution)/shard_map/all_gather | solution.py:370
  44.7 465.8 %all-gather.11.cloned.1.call-start = ((), (), s32[]{:S(2)}) async-start(), calls=%async_computation.14 | async-start | bytes 3538944 | tf_op jit(solution)/shard_map/all_gather | solution.py:369
  45.3 604.9 %all-gather.15.cloned.1.call-start = ((), (), s32[]{:S(2)}) async-start(), calls=%async_computation.16 | async-start | bytes 9437184 | tf_op jit(solution)/shard_map/all_gather | solution.py:257
  63.3 601.5 %all-gather.17.cloned.1.call-start = ((), (), s32[]{:S(2)}) async-start(), calls=%async_computation.17 | async-start | bytes 4718592 | tf_op jit(solution)/shard_map/all_gather | solution.py:372
  68.0 48.9 %collective-permute-start.13 = (bf16[256,2048]{0,1:T(8,128)(2,1)}, bf16[256,2048]{0,1:T(8,128)(2,1)}, u32[]{:S(2)}, u32[]{:S(2)}) collective-permute-start(bf16[256,2048]{0,1:T(8,128)(2,1)} %bitcast.36), channel_id=1, source_target_pairs={{0,16},{8,24},{16,0},{24,8},{1,17},{9,25},{17,1},{25,9},{2,18},{10... | collective-permute-start | bytes 3145736 | tf_op jit(solution)/shard_map/ppermute | solution.py:227
  68.6 50.6 %collective-permute-start.14 = (bf16[256,2048]{0,1:T(8,128)(2,1)}, bf16[256,2048]{0,1:T(8,128)(2,1)}, u32[]{:S(2)}, u32[]{:S(2)}) collective-permute-start(bf16[256,2048]{0,1:T(8,128)(2,1)} %bitcast.36), channel_id=1, source_target_pairs={{0,24},{8,16},{16,8},{24,0},{1,25},{9,17},{17,9},{25,1},{2,26},{10... | collective-permute-start | bytes 3145736 | tf_op jit(solution)/shard_map/ppermute | solution.py:227
  72.2 66.3 %collective-permute-start = (bf16[256,2048]{0,1:T(8,128)(2,1)}, bf16[256,2048]{0,1:T(8,128)(2,1)}, u32[]{:S(2)}, u32[]{:S(2)}) collective-permute-start(bf16[256,2048]{0,1:T(8,128)(2,1)} %bitcast.3), channel_id=1, source_target_pairs={{0,8},{8,0},{16,24},{24,16},{1,9},{9,1},{17,25},{25,17},{2,10},{10... | collective-permute-start | bytes 3145736 | tf_op jit(solution)/shard_map/ppermute | solution.py:227
  73.2 83.4 %collective-permute-start.1 = (bf16[256,2048]{0,1:T(8,128)(2,1)}, bf16[256,2048]{0,1:T(8,128)(2,1)}, u32[]{:S(2)}, u32[]{:S(2)}) collective-permute-start(bf16[256,2048]{0,1:T(8,128)(2,1)} %bitcast.3), channel_id=1, source_target_pairs={{0,16},{8,24},{16,0},{24,8},{1,17},{9,25},{17,1},{25,9},{2,18},{10... | collective-permute-start | bytes 3145736 | tf_op jit(solution)/shard_map/ppermute | solution.py:227
  73.7 2593.4 %reduce-scatter.7.cloned.1.call-start = ((), (), s32[]{:S(2)}) async-start(), calls=%async_computation.18 | async-start | bytes 5898240 | tf_op jit(solution)/shard_map/reduce_scatter | solution.py:263
  93.5 69.8 %collective-permute-start.2 = (bf16[256,2048]{0,1:T(8,128)(2,1)}, bf16[256,2048]{0,1:T(8,128)(2,1)}, u32[]{:S(2)}, u32[]{:S(2)}) collective-permute-start(bf16[256,2048]{0,1:T(8,128)(2,1)} %bitcast.3), channel_id=1, source_target_pairs={{0,24},{8,16},{16,8},{24,0},{1,25},{9,17},{17,9},{25,1},{2,26},{10... | collective-permute-start | bytes 3145736 | tf_op jit(solution)/shard_map/ppermute | solution.py:227
  522.2 40.5 %collective-permute-start.5 = (bf16[256,2048]{1,0:T(8,128)(2,1)}, bf16[256,2048]{1,0:T(8,128)(2,1)}, u32[]{:S(2)}, u32[]{:S(2)}) collective-permute-start(bf16[256,2048]{1,0:T(8,128)(2,1)} %fusion.271), channel_id=1, source_target_pairs={{0,8},{8,0},{16,24},{24,16},{1,9},{9,1},{17,25},{25,17},{2,10},{10... | collective-permute-start | bytes 3145736 | tf_op jit(solution)/shard_map/ppermute | solution.py:238
  525.3 59.9 %collective-permute-start.24 = (bf16[256,2048]{1,0:T(8,128)(2,1)}, bf16[256,2048]{1,0:T(8,128)(2,1)}, u32[]{:S(2)}, u32[]{:S(2)}) collective-permute-start(bf16[256,2048]{1,0:T(8,128)(2,1)} %get-tuple-element.2975), channel_id=1, source_target_pairs={{0,8},{8,0},{16,24},{24,16},{1,9},{9,1},{17,25},{25,17},{2,10},{10... | collective-permute-start | bytes 3145736 | tf_op jit(solution)/shard_map/ppermute | solution.py:227
  525.7 68.2 %collective-permute-start.25 = (bf16[256,2048]{1,0:T(8,128)(2,1)}, bf16[256,2048]{1,0:T(8,128)(2,1)}, u32[]{:S(2)}, u32[]{:S(2)}) collective-permute-start(bf16[256,2048]{1,0:T(8,128)(2,1)} %get-tuple-element.2975), channel_id=1, source_target_pairs={{0,16},{8,24},{16,0},{24,8},{1,17},{9,25},{17,1},{25,9},{2,18},{10... | collective-permute-start | bytes 3145736 | tf_op jit(solution)/shard_map/ppermute | solution.py:227
  542.6 67.5 %collective-permute-start.26 = (bf16[256,2048]{1,0:T(8,128)(2,1)}, bf16[256,2048]{1,0:T(8,128)(2,1)}, u32[]{:S(2)}, u32[]{:S(2)}) collective-permute-start(bf16[256,2048]{1,0:T(8,128)(2,1)} %get-tuple-element.2975), channel_id=1, source_target_pairs={{0,24},{8,16},{16,8},{24,0},{1,25},{9,17},{17,9},{25,1},{2,26},{10... | collective-permute-start | bytes 3145736 | tf_op jit(solution)/shard_map/ppermute | solution.py:227
  574.0 55.6 %collective-permute-start.6 = (bf16[256,2048]{0,1:T(8,128)(2,1)}, bf16[256,2048]{0,1:T(8,128)(2,1)}, u32[]{:S(2)}, u32[]{:S(2)}) collective-permute-start(bf16[256,2048]{0,1:T(8,128)(2,1)} %bitcast.28), channel_id=1, source_target_pairs={{0,8},{8,0},{16,24},{24,16},{1,9},{9,1},{17,25},{25,17},{2,10},{10... | collective-permute-start | bytes 3145736 | tf_op jit(solution)/shard_map/ppermute | solution.py:227
  576.5 55.3 %collective-permute-start.7 = (bf16[256,2048]{0,1:T(8,128)(2,1)}, bf16[256,2048]{0,1:T(8,128)(2,1)}, u32[]{:S(2)}, u32[]{:S(2)}) collective-permute-start(bf16[256,2048]{0,1:T(8,128)(2,1)} %bitcast.28), channel_id=1, source_target_pairs={{0,16},{8,24},{16,0},{24,8},{1,17},{9,25},{17,1},{25,9},{2,18},{10... | collective-permute-start | bytes 3145736 | tf_op jit(solution)/shard_map/ppermute | solution.py:227
  585.2 56.8 %collective-permute-start.8 = (bf16[256,2048]{0,1:T(8,128)(2,1)}, bf16[256,2048]{0,1:T(8,128)(2,1)}, u32[]{:S(2)}, u32[]{:S(2)}) collective-permute-start(bf16[256,2048]{0,1:T(8,128)(2,1)} %bitcast.28), channel_id=1, source_target_pairs={{0,24},{8,16},{16,8},{24,0},{1,25},{9,17},{17,9},{25,1},{2,26},{10... | collective-permute-start | bytes 3145736 | tf_op jit(solution)/shard_map/ppermute | solution.py:227
  740.3 272.8 %collective-permute-start.30 = (bf16[256,2048]{1,0:T(8,128)(2,1)}, bf16[256,2048]{1,0:T(8,128)(2,1)}, u32[]{:S(2)}, u32[]{:S(2)}) collective-permute-start(bf16[256,2048]{1,0:T(8,128)(2,1)} %get-tuple-element.2886), channel_id=1, source_target_pairs={{0,8},{8,0},{16,24},{24,16},{1,9},{9,1},{17,25},{25,17},{2,10},{10... | collective-permute-start | bytes 3145736 | tf_op jit(solution)/shard_map/ppermute | solution.py:227
  741.2 273.4 %collective-permute-start.31 = (bf16[256,2048]{1,0:T(8,128)(2,1)}, bf16[256,2048]{1,0:T(8,128)(2,1)}, u32[]{:S(2)}, u32[]{:S(2)}) collective-permute-start(bf16[256,2048]{1,0:T(8,128)(2,1)} %get-tuple-element.2886), channel_id=1, source_target_pairs={{0,16},{8,24},{16,0},{24,8},{1,17},{9,25},{17,1},{25,9},{2,18},{10... | collective-permute-start | bytes 3145736 | tf_op jit(solution)/shard_map/ppermute | solution.py:227
  742.6 273.4 %collective-permute-start.32 = (bf16[256,2048]{1,0:T(8,128)(2,1)}, bf16[256,2048]{1,0:T(8,128)(2,1)}, u32[]{:S(2)}, u32[]{:S(2)}) collective-permute-start(bf16[256,2048]{1,0:T(8,128)(2,1)} %get-tuple-element.2886), channel_id=1, source_target_pairs={{0,24},{8,16},{16,8},{24,0},{1,25},{9,17},{17,9},{25,1},{2,26},{10... | collective-permute-start | bytes 3145736 | tf_op jit(solution)/shard_map/ppermute | solution.py:227
  1520.6 40.4 %collective-permute-start.16 = (bf16[256,2048]{1,0:T(8,128)(2,1)S(1)}, bf16[256,2048]{1,0:T(8,128)(2,1)S(1)}, u32[]{:S(2)}, u32[]{:S(2)}) collective-permute-start(bf16[256,2048]{1,0:T(8,128)(2,1)S(1)} %fusion.273), channel_id=1, source_target_pairs={{0,16},{8,24},{16,0},{24,8},{1,17},{9,25},{17,1},{25,9},{2,18},{10... | collective-permute-start | bytes 3145736 | tf_op jit(solution)/shard_map/ppermute | solution.py:238
  1522.7 44.0 %collective-permute-start.17 = (bf16[256,2048]{1,0:T(8,128)(2,1)S(1)}, bf16[256,2048]{1,0:T(8,128)(2,1)S(1)}, u32[]{:S(2)}, u32[]{:S(2)}) collective-permute-start(bf16[256,2048]{1,0:T(8,128)(2,1)S(1)} %fusion.274), channel_id=1, source_target_pairs={{0,8},{8,0},{16,24},{24,16},{1,9},{9,1},{17,25},{25,17},{2,10},{10... | collective-permute-start | bytes 3145736 | tf_op jit(solution)/shard_map/ppermute | solution.py:238
  1523.9 65.4 %collective-permute-start.36 = (bf16[256,2048]{1,0:T(8,128)(2,1)}, bf16[256,2048]{1,0:T(8,128)(2,1)}, u32[]{:S(2)}, u32[]{:S(2)}) collective-permute-start(bf16[256,2048]{1,0:T(8,128)(2,1)} %get-tuple-element.2976), channel_id=1, source_target_pairs={{0,8},{8,0},{16,24},{24,16},{1,9},{9,1},{17,25},{25,17},{2,10},{10... | collective-permute-start | bytes 3145736 | tf_op jit(solution)/shard_map/ppermute | solution.py:227
  1524.8 67.8 %collective-permute-start.37 = (bf16[256,2048]{1,0:T(8,128)(2,1)}, bf16[256,2048]{1,0:T(8,128)(2,1)}, u32[]{:S(2)}, u32[]{:S(2)}) collective-permute-start(bf16[256,2048]{1,0:T(8,128)(2,1)} %get-tuple-element.2976), channel_id=1, source_target_pairs={{0,16},{8,24},{16,0},{24,8},{1,17},{9,25},{17,1},{25,9},{2,18},{10... | collective-permute-start | bytes 3145736 | tf_op jit(solution)/shard_map/ppermute | solution.py:227
  1544.4 67.6 %collective-permute-start.38 = (bf16[256,2048]{1,0:T(8,128)(2,1)}, bf16[256,2048]{1,0:T(8,128)(2,1)}, u32[]{:S(2)}, u32[]{:S(2)}) collective-permute-start(bf16[256,2048]{1,0:T(8,128)(2,1)} %get-tuple-element.2976), channel_id=1, source_target_pairs={{0,24},{8,16},{16,8},{24,0},{1,25},{9,17},{17,9},{25,1},{2,26},{10... | collective-permute-start | bytes 3145736 | tf_op jit(solution)/shard_map/ppermute | solution.py:227
  1574.7 59.6 %collective-permute-start.18 = (bf16[256,2048]{0,1:T(8,128)(2,1)}, bf16[256,2048]{0,1:T(8,128)(2,1)}, u32[]{:S(2)}, u32[]{:S(2)}) collective-permute-start(bf16[256,2048]{0,1:T(8,128)(2,1)} %bitcast.46), channel_id=1, source_target_pairs={{0,8},{8,0},{16,24},{24,16},{1,9},{9,1},{17,25},{25,17},{2,10},{10... | collective-permute-start | bytes 3145736 | tf_op jit(solution)/shard_map/ppermute | solution.py:227
  1575.6 61.0 %collective-permute-start.19 = (bf16[256,2048]{0,1:T(8,128)(2,1)}, bf16[256,2048]{0,1:T(8,128)(2,1)}, u32[]{:S(2)}, u32[]{:S(2)}) collective-permute-start(bf16[256,2048]{0,1:T(8,128)(2,1)} %bitcast.46), channel_id=1, source_target_pairs={{0,16},{8,24},{16,0},{24,8},{1,17},{9,25},{17,1},{25,9},{2,18},{10... | collective-permute-start | bytes 3145736 | tf_op jit(solution)/shard_map/ppermute | solution.py:227
  1591.7 59.3 %collective-permute-start.20 = (bf16[256,2048]{0,1:T(8,128)(2,1)}, bf16[256,2048]{0,1:T(8,128)(2,1)}, u32[]{:S(2)}, u32[]{:S(2)}) collective-permute-start(bf16[256,2048]{0,1:T(8,128)(2,1)} %bitcast.46), channel_id=1, source_target_pairs={{0,24},{8,16},{16,8},{24,0},{1,25},{9,17},{17,9},{25,1},{2,26},{10... | collective-permute-start | bytes 3145736 | tf_op jit(solution)/shard_map/ppermute | solution.py:227
  1692.2 38.1 %collective-permute-start.40 = (bf16[256,2048]{1,0:T(8,128)(2,1)}, bf16[256,2048]{1,0:T(8,128)(2,1)}, u32[]{:S(2)}, u32[]{:S(2)}) collective-permute-start(bf16[256,2048]{1,0:T(8,128)(2,1)} %convolution_convert_fusion.9), channel_id=1, source_target_pairs={{0,16},{8,24},{16,0},{24,8},{1,17},{9,25},{17,1},{25,9},{2,18},{10... | collective-permute-start | bytes 3145736 | tf_op jit(solution)/shard_map/ppermute | solution.py:238
  1752.9 46.3 %collective-permute-start.43 = (bf16[256,2048]{1,0:T(8,128)(2,1)S(1)}, bf16[256,2048]{1,0:T(8,128)(2,1)S(1)}, u32[]{:S(2)}, u32[]{:S(2)}) collective-permute-start(bf16[256,2048]{1,0:T(8,128)(2,1)S(1)} %get-tuple-element.2888), channel_id=1, source_target_pairs={{0,16},{8,24},{16,0},{24,8},{1,17},{9,25},{17,1},{25,9},{2,18},{10... | collective-permute-start | bytes 3145736 | tf_op jit(solution)/shard_map/ppermute | solution.py:227
  1754.2 46.9 %collective-permute-start.44 = (bf16[256,2048]{1,0:T(8,128)(2,1)S(1)}, bf16[256,2048]{1,0:T(8,128)(2,1)S(1)}, u32[]{:S(2)}, u32[]{:S(2)}) collective-permute-start(bf16[256,2048]{1,0:T(8,128)(2,1)S(1)} %get-tuple-element.2888), channel_id=1, source_target_pairs={{0,24},{8,16},{16,8},{24,0},{1,25},{9,17},{17,9},{25,1},{2,26},{10... | collective-permute-start | bytes 3145736 | tf_op jit(solution)/shard_map/ppermute | solution.py:227
  1913.2 760.3 %reduce-scatter.13.cloned.1.call-start = ((), (), s32[]{:S(2)}) async-start(), calls=%async_computation.21 | async-start | bytes 1179648 | tf_op jit(solution)/shard_map/reduce_scatter | solution.py:269
  1934.7 740.4 %reduce-scatter.17.cloned.1.call-start = ((), (), s32[]{:S(2)}) async-start(), calls=%async_computation.23 | async-start | bytes 4718592 | tf_op jit(solution)/shard_map/reduce_scatter | solution.py:269
  1950.3 727.0 %reduce-scatter.11.cloned.1.call-start = ((), (), s32[]{:S(2)}) async-start(), calls=%async_computation.20 | async-start | bytes 3538944 | tf_op jit(solution)/shard_map/reduce_scatter | solution.py:269
  2329.6 349.9 %reduce-scatter.9.cloned.1.call-start = ((), (), s32[]{:S(2)}) async-start(), calls=%async_computation.19 | async-start | bytes 6488064 | tf_op jit(solution)/shard_map/reduce_scatter | solution.py:263
  2397.8 297.7 %reduce-scatter.15.cloned.1.call-start = ((), (), s32[]{:S(2)}) async-start(), calls=%async_computation.22 | async-start | bytes 9437184 | tf_op jit(solution)/shard_map/reduce_scatter | solution.py:263
  2411.9 42.3 %collective-permute-start.9 = (bf16[256,2048]{1,0:T(8,128)(2,1)}, bf16[256,2048]{1,0:T(8,128)(2,1)}, u32[]{:S(2)}, u32[]{:S(2)}) collective-permute-start(bf16[256,2048]{1,0:T(8,128)(2,1)} %convolution_convert_fusion.7), channel_id=1, source_target_pairs={{0,24},{8,16},{16,8},{24,0},{1,25},{9,17},{17,9},{25,1},{2,26},{10... | collective-permute-start | bytes 3145736 | tf_op jit(solution)/shard_map/ppermute | solution.py:238
  2467.0 37.0 %collective-permute-start.21 = (bf16[256,2048]{1,0:T(8,128)(2,1)}, bf16[256,2048]{1,0:T(8,128)(2,1)}, u32[]{:S(2)}, u32[]{:S(2)}) collective-permute-start(bf16[256,2048]{1,0:T(8,128)(2,1)} %convolution_convert_fusion.4), channel_id=1, source_target_pairs={{0,24},{8,16},{16,8},{24,0},{1,25},{9,17},{17,9},{25,1},{2,26},{10... | collective-permute-start | bytes 3145736 | tf_op jit(solution)/shard_map/ppermute | solution.py:238
  2470.8 42.8 %collective-permute-start.22 = (bf16[256,2048]{1,0:T(8,128)(2,1)}, bf16[256,2048]{1,0:T(8,128)(2,1)}, u32[]{:S(2)}, u32[]{:S(2)}) collective-permute-start(bf16[256,2048]{1,0:T(8,128)(2,1)} %convolution_convert_fusion.3), channel_id=1, source_target_pairs={{0,16},{8,24},{16,0},{24,8},{1,17},{9,25},{17,1},{25,9},{2,18},{10... | collective-permute-start | bytes 3145736 | tf_op jit(solution)/shard_map/ppermute | solution.py:238
  2473.6 40.0 %collective-permute-start.23 = (bf16[256,2048]{1,0:T(8,128)(2,1)}, bf16[256,2048]{1,0:T(8,128)(2,1)}, u32[]{:S(2)}, u32[]{:S(2)}) collective-permute-start(bf16[256,2048]{1,0:T(8,128)(2,1)} %convolution_convert_fusion.2), channel_id=1, source_target_pairs={{0,8},{8,0},{16,24},{24,16},{1,9},{9,1},{17,25},{25,17},{2,10},{10... | collective-permute-start | bytes 3145736 | tf_op jit(solution)/shard_map/ppermute | solution.py:238
  2530.4 38.7 %collective-permute-start.33 = (bf16[256,2048]{1,0:T(8,128)(2,1)}, bf16[256,2048]{1,0:T(8,128)(2,1)S(1)}, u32[]{:S(2)}, u32[]{:S(2)}) collective-permute-start(bf16[256,2048]{1,0:T(8,128)(2,1)} %fusion.263), channel_id=1, source_target_pairs={{0,24},{8,16},{16,8},{24,0},{1,25},{9,17},{17,9},{25,1},{2,26},{10... | collective-permute-start | bytes 3145736 | tf_op jit(solution)/shard_map/ppermute | solution.py:238
  2535.9 44.3 %collective-permute-start.34 = (bf16[256,2048]{1,0:T(8,128)(2,1)}, bf16[256,2048]{1,0:T(8,128)(2,1)}, u32[]{:S(2)}, u32[]{:S(2)}) collective-permute-start(bf16[256,2048]{1,0:T(8,128)(2,1)} %fusion.264), channel_id=1, source_target_pairs={{0,16},{8,24},{16,0},{24,8},{1,17},{9,25},{17,1},{25,9},{2,18},{10... | collective-permute-start | bytes 3145736 | tf_op jit(solution)/shard_map/ppermute | solution.py:238
  2541.2 39.0 %collective-permute-start.35 = (bf16[256,2048]{1,0:T(8,128)(2,1)}, bf16[256,2048]{1,0:T(8,128)(2,1)}, u32[]{:S(2)}, u32[]{:S(2)}) collective-permute-start(bf16[256,2048]{1,0:T(8,128)(2,1)} %fusion.265), channel_id=1, source_target_pairs={{0,8},{8,0},{16,24},{24,16},{1,9},{9,1},{17,25},{25,17},{2,10},{10... | collective-permute-start | bytes 3145736 | tf_op jit(solution)/shard_map/ppermute | solution.py:238
  2547.7 54.9 %collective-permute-start.45 = (bf16[256,2048]{1,0:T(8,128)(2,1)}, bf16[256,2048]{1,0:T(8,128)(2,1)}, u32[]{:S(2)}, u32[]{:S(2)}) collective-permute-start(bf16[256,2048]{1,0:T(8,128)(2,1)} %fusion.266), channel_id=1, source_target_pairs={{0,24},{8,16},{16,8},{24,0},{1,25},{9,17},{17,9},{25,1},{2,26},{10... | collective-permute-start | bytes 3145736 | tf_op jit(solution)/shard_map/ppermute | solution.py:238
  2553.4 70.6 %collective-permute-start.46 = (bf16[256,2048]{1,0:T(8,128)(2,1)}, bf16[256,2048]{1,0:T(8,128)(2,1)}, u32[]{:S(2)}, u32[]{:S(2)}) collective-permute-start(bf16[256,2048]{1,0:T(8,128)(2,1)} %fusion.267), channel_id=1, source_target_pairs={{0,16},{8,24},{16,0},{24,8},{1,17},{9,25},{17,1},{25,9},{2,18},{10... | collective-permute-start | bytes 3145736 | tf_op jit(solution)/shard_map/ppermute | solution.py:238
  2569.1 55.0 %collective-permute-start.47 = (bf16[256,2048]{1,0:T(8,128)(2,1)}, bf16[256,2048]{1,0:T(8,128)(2,1)}, u32[]{:S(2)}, u32[]{:S(2)}) collective-permute-start(bf16[256,2048]{1,0:T(8,128)(2,1)} %fusion.268), channel_id=1, source_target_pairs={{0,8},{8,0},{16,24},{24,16},{1,9},{9,1},{17,25},{25,17},{2,10},{10... | collective-permute-start | bytes 3145736 | tf_op jit(solution)/shard_map/ppermute | solution.py:238
  (362 other events, 5198.5 us)
Sparse Core Ops, SparseCore 0:
  30.5 59.9 all-gather.6
  92.2 54.7 all-gather.8
  148.5 20.8 all-gather.12
  170.9 37.8 all-gather.10
  210.3 80.9 all-gather.14
  292.7 45.6 all-gather.16
  1913.3 60.6 reduce-scatter.6
  1976.3 30.5 reduce-scatter.12
  2009.2 48.4 reduce-scatter.16
  2329.7 41.0 reduce-scatter.10
  2397.9 65.4 reduce-scatter.8
  2503.4 90.2 reduce-scatter.14

commit v2 on v1

--- a/solution.py
+++ b/solution.py
@@ -1,6 +1,10 @@
+import functools
+
 import jax
 import jax.numpy as jnp
 from jax import lax
+from jax.experimental import pallas as pl
+from jax.experimental.pallas import tpu as pltpu
 from jax.sharding import PartitionSpec as P
 
 SSM_HEADS = 48
@@ -12,9 +16,10 @@
 HEAD_DIM = 128
 MICRO = 2
 SPAN = 128
-ATT_BLOCK = 512
 SSM_INNER = 3072
 CONV_CH = 3584
+ATT_ROWS = 256
+VMEM_BYTES = 48 * 1024 * 1024
 
 
 PRECISE = lax.Precision.HIGHEST
@@ -22,184 +27,470 @@
 ROPE_BASE = 10000.0
 
 
-def round_plain(value):
-    return lax.optimization_barrier(value.astype(jnp.bfloat16)).astype(jnp.float32)
-
-
-def round_keep(value):
-    return (round_plain(value), None)
-
-
-def round_pass(kept, grad):
-    return (grad,)
-
-
-def make_rounder():
-    rounder = jax.custom_vjp(round_plain)
-    rounder.defvjp(round_keep, round_pass)
-    return rounder
-
-
-def rotate(head_rows, positions):
-    half_width = head_rows.shape[-1] // 2
-    frequency = ROPE_BASE ** (-jnp.arange(half_width).astype(jnp.float32) / half_width)
-    angles = positions.astype(jnp.float32)[:, None] * frequency[None, :]
-    cosine = jnp.cos(angles)[:, None, :]
-    sine_part = jnp.sin(angles)[:, None, :]
-    lead_half = head_rows[..., :half_width]
-    tail_half = head_rows[..., half_width:]
-    return jnp.concatenate(
-        [lead_half * cosine - tail_half * sine_part, tail_half * cosine + lead_half * sine_part],
-        axis=-1,
+def lanes_iota(shape):
+    return lax.broadcasted_iota(jnp.int32, shape, 1)
+
+
+def rows_iota(shape):
+    return lax.broadcasted_iota(jnp.int32, shape, 0)
+
+
+def dot_last(left, right):
+    return lax.dot_general(left, right, (((1,), (1,)), ((), ())), preferred_element_type=jnp.float32)
+
+
+def dot_first(left, right):
+    return lax.dot_general(left, right, (((0,), (0,)), ((), ())), preferred_element_type=jnp.float32)
+
+
+def dot_plain(left, right):
+    return jnp.dot(left, right, preferred_element_type=jnp.float32)
+
+
+def head_steps(block, head_ref, heads):
+    pre = block.astype(jnp.float32) + head_ref[0:1, :]
+    live = lanes_iota(pre.shape) < heads
+    pre = jnp.where(live, pre, 0.0)
+    step = jnp.maximum(pre, 0.0) + jnp.log1p(jnp.exp(-jnp.abs(pre)))
+    step = jnp.where(live, step, 0.0)
+    rate = -jnp.exp(head_ref[1:2, :])
+    decay = rate * step
+    lower = (rows_iota((SPAN, SPAN)) >= lanes_iota((SPAN, SPAN))).astype(jnp.float32)
+    total = jnp.dot(lower, decay, precision=PRECISE, preferred_element_type=jnp.float32)
+    return step, rate, decay, total, pre
+
+
+def convolve(ubuf, aux_ref, conv_ref, lanes):
+    acc = conv_ref[CONV : CONV + 1, lanes] + conv_ref[CONV - 1 : CONV, lanes] * ubuf[8 : 8 + SPAN, lanes]
+    for offset in range(1, CONV):
+        shifted = ubuf[8 - offset : 8 - offset + SPAN, lanes]
+        weight = conv_ref[CONV - 1 - offset : CONV - offset, lanes]
+        acc = acc + weight * shifted * aux_ref[:, 2 + offset : 3 + offset]
+    return acc
+
+
+def pair_of(values, first_head, low_lanes):
+    one = jnp.broadcast_to(values[:, first_head : first_head + 1], (SPAN, 128))
+    two = jnp.broadcast_to(values[:, first_head + 1 : first_head + 2], (SPAN, 128))
+    return one, two, jnp.where(low_lanes, one, two)
+
+
+def ssd_forward_kernel(
+    heads, first_ref, aux_ref, seg_ref, conv_ref, head_ref, skip_ref, y_ref, start_ref, ubuf, taps, state
+):
+    f32, bf16 = jnp.float32, jnp.bfloat16
+    inner = heads * SSM_DIM
+    width = inner + 2 * STATE
+
+    @pl.when(pl.program_id(0) == 0)
+    def _():
+        ubuf[SPAN : SPAN + 8, :] = jnp.zeros((8, width), f32)
+        state[...] = jnp.zeros((STATE, inner), f32)
+
+    ubuf[0:8, :] = ubuf[SPAN : SPAN + 8, :]
+    ubuf[8 : 8 + SPAN, :] = first_ref[:, :width].astype(f32)
+    for lane in range(0, width, 128):
+        lanes = slice(lane, lane + 128)
+        pre = convolve(ubuf, aux_ref, conv_ref, lanes)
+        taps[:, lanes] = (pre * jax.nn.sigmoid(pre)).astype(bf16)
+    step, rate, decay, total, unused = head_steps(first_ref[:, width : width + 128], head_ref, heads)
+    total_rows = total.T
+    low_lanes = lanes_iota((SPAN, 128)) < SSM_DIM
+    same = (aux_ref[:, 0:1] == seg_ref[0]) & (rows_iota((SPAN, SPAN)) >= lanes_iota((SPAN, SPAN)))
+    b_rows = taps[:, inner : inner + STATE]
+    c_rows = taps[:, inner + STATE :]
+    b_cols = b_rows.astype(f32).T.astype(bf16)
+    scores = dot_last(c_rows, b_rows)
+    carry_keep = aux_ref[:, 1:2]
+    end_keep = aux_ref[:, 2:3]
+    for pair in range(heads // 2):
+        lanes = slice(pair * 128, pair * 128 + 128)
+        sum_one, sum_two, sums = pair_of(total, 2 * pair, low_lanes)
+        steps = pair_of(step, 2 * pair, low_lanes)[2]
+        row_one = total_rows[2 * pair : 2 * pair + 1, :]
+        row_two = total_rows[2 * pair + 1 : 2 * pair + 2, :]
+        mix_one = (jnp.exp(jnp.where(same, sum_one - row_one, -1e30)) * scores).astype(bf16)
+        mix_two = (jnp.exp(jnp.where(same, sum_two - row_two, -1e30)) * scores).astype(bf16)
+        x = taps[:, lanes].astype(f32)
+        stepped = (x * steps).astype(bf16)
+        none = jnp.zeros_like(stepped)
+        split = jnp.concatenate(
+            [jnp.where(low_lanes, stepped, none), jnp.where(low_lanes, none, stepped)], axis=0
+        )
+        held = state[:, lanes]
+        held_low = held.astype(bf16)
+        start_ref[0, :, lanes] = held_low
+        y = dot_plain(jnp.concatenate([mix_one, mix_two], axis=1), split)
+        y = y + jnp.exp(sums) * carry_keep * dot_plain(c_rows, held_low)
+        y_ref[:, lanes] = (y + skip_ref[0:1, lanes] * x).astype(bf16)
+        last = sums[SPAN - 1 : SPAN, :]
+        weighted = (jnp.exp(last - sums) * end_keep * stepped.astype(f32)).astype(bf16)
+        kept = jnp.exp(last) * aux_ref[SPAN - 1 : SPAN, 1:2]
+        state[:, lanes] = held * kept + dot_plain(b_cols, weighted)
+
+
+def ssd_backward_kernel(
+    heads,
+    first_ref,
+    before_ref,
+    aux_ref,
+    seg_ref,
+    conv_ref,
+    head_ref,
+    skip_ref,
+    start_ref,
+    dy_ref,
+    grad_ref,
+    conv_grad_ref,
+    head_grad_ref,
+    skip_grad_ref,
+    ubuf,
+    taps,
+    slope,
+    gbuf,
+    dstate,
+):
+    f32, bf16 = jnp.float32, jnp.bfloat16
+    inner = heads * SSM_DIM
+    width = inner + 2 * STATE
+
+    @pl.when(pl.program_id(0) == 0)
+    def _():
+        gbuf[0:8, :] = jnp.zeros((8, width), f32)
+        dstate[...] = jnp.zeros((STATE, inner), f32)
+        conv_grad_ref[...] = jnp.zeros(conv_grad_ref.shape, f32)
+        head_grad_ref[...] = jnp.zeros(head_grad_ref.shape, f32)
+        skip_grad_ref[...] = jnp.zeros(skip_grad_ref.shape, f32)
+
+    ubuf[0:8, :] = before_ref[8:16, :width].astype(f32)
+    ubuf[8 : 8 + SPAN, :] = first_ref[:, :width].astype(f32)
+    gbuf[SPAN : SPAN + 8, :] = gbuf[0:8, :]
+    for lane in range(0, width, 128):
+        lanes = slice(lane, lane + 128)
+        pre = convolve(ubuf, aux_ref, conv_ref, lanes)
+        sig = jax.nn.sigmoid(pre)
+        taps[:, lanes] = (pre * sig).astype(bf16)
+        slope[:, lanes] = sig * (1.0 + pre * (1.0 - sig))
+    step, rate, decay, total, pre_step = head_steps(first_ref[:, width : width + 128], head_ref, heads)
+    total_rows = total.T
+    square = (SPAN, SPAN)
+    low_lanes = lanes_iota((SPAN, 128)) < SSM_DIM
+    low_row = lanes_iota((1, 128)) < SSM_DIM
+    same = (aux_ref[:, 0:1] == seg_ref[0]) & (rows_iota(square) >= lanes_iota(square))
+    b_rows = taps[:, inner : inner + STATE]
+    c_rows = taps[:, inner + STATE :]
+    c_cols = c_rows.astype(f32).T.astype(bf16)
+    scores = dot_last(c_rows, b_rows)
+    carry_keep = aux_ref[:, 1:2]
+    end_keep = aux_ref[:, 2:3]
+    head_lane = lanes_iota((SPAN, 128))
+    is_last = rows_iota((SPAN, 1)) == SPAN - 1
+    grad_scores = jnp.zeros(square, f32)
+    grad_b = jnp.zeros((SPAN, STATE), f32)
+    grad_c = jnp.zeros((SPAN, STATE), f32)
+    grad_total = jnp.zeros((SPAN, 128), f32)
+    grad_step = jnp.zeros((SPAN, 128), f32)
+    for pair in range(heads // 2):
+        lanes = slice(pair * 128, pair * 128 + 128)
+        sum_one, sum_two, sums = pair_of(total, 2 * pair, low_lanes)
+        steps = pair_of(step, 2 * pair, low_lanes)[2]
+        row_one = total_rows[2 * pair : 2 * pair + 1, :]
+        row_two = total_rows[2 * pair + 1 : 2 * pair + 2, :]
+        decay_one = jnp.exp(jnp.where(same, sum_one - row_one, -1e30))
+        decay_two = jnp.exp(jnp.where(same, sum_two - row_two, -1e30))
+        mix_one = (decay_one * scores).astype(bf16)
+        mix_two = (decay_two * scores).astype(bf16)
+        x = taps[:, lanes].astype(f32)
+        stepped = (x * steps).astype(bf16)
+        none = jnp.zeros_like(stepped)
+        x_one = jnp.where(low_lanes, stepped, none)
+        x_two = jnp.where(low_lanes, none, stepped)
+        dy_low = dy_ref[:, lanes]
+        dy = dy_low.astype(f32)
+        dy_one = jnp.where(low_lanes, dy_low, none)
+        dy_two = jnp.where(low_lanes, none, dy_low)
+        grad_scores = grad_scores + dot_last(dy_one, stepped) * decay_one + dot_last(dy_two, stepped) * decay_two
+        y = dot_plain(
+            jnp.concatenate([mix_one, mix_two], axis=1), jnp.concatenate([x_one, x_two], axis=0)
+        )
+        grad_in = dot_first(
+            jnp.concatenate([mix_one, mix_two], axis=0), jnp.concatenate([dy_one, dy_two], axis=0)
+        )
+        held = start_ref[0, :, lanes]
+        dheld = dstate[:, lanes]
+        dheld_low = dheld.astype(bf16)
+        grown = jnp.exp(sums) * carry_keep
+        y = y + grown * dot_plain(c_rows, held)
+        grown_dy = (grown * dy).astype(bf16)
+        last = sums[SPAN - 1 : SPAN, :]
+        fade = jnp.exp(last - sums) * end_keep
+        stepped_wide = stepped.astype(f32)
+        weighted = (fade * stepped_wide).astype(bf16)
+        from_end = dot_plain(b_rows, dheld_low)
+        grad_in = grad_in + fade * from_end
+        grad_c = grad_c + dot_last(grown_dy, held)
+        grad_b = grad_b + dot_last(weighted, dheld_low)
+        kept = jnp.exp(last) * aux_ref[SPAN - 1 : SPAN, 1:2]
+        ends = jnp.sum(fade * stepped_wide * from_end, axis=0, keepdims=True) + kept * jnp.sum(
+            dheld * held.astype(f32), axis=0, keepdims=True
+        )
+        dstate[:, lanes] = dheld * kept + dot_plain(c_cols, grown_dy)
+        gaps = dy * y - stepped_wide * grad_in
+        by_step = x * grad_in
+        for half in range(2):
+            keep = low_lanes if half == 0 else ~low_lanes
+            keep_row = low_row if half == 0 else ~low_row
+            end_sum = jnp.sum(jnp.where(keep_row, ends, 0.0), axis=1, keepdims=True)
+            gap_sum = jnp.sum(jnp.where(keep, gaps, 0.0), axis=1, keepdims=True)
+            gap_sum = gap_sum + jnp.where(is_last, end_sum, 0.0)
+            step_sum = jnp.sum(jnp.where(keep, by_step, 0.0), axis=1, keepdims=True)
+            here = head_lane == 2 * pair + half
+            grad_total = jnp.where(here, gap_sum, grad_total)
+            grad_step = jnp.where(here, step_sum, grad_step)
+        skip = skip_ref[0:1, lanes]
+        skip_grad_ref[0:1, lanes] += jnp.sum(dy * x, axis=0, keepdims=True)
+        gbuf[0:SPAN, lanes] = (steps * grad_in + skip * dy) * slope[:, lanes]
+    low_scores = grad_scores.astype(bf16)
+    grad_c = grad_c + dot_plain(low_scores, b_rows)
+    grad_b = grad_b + dot_first(low_scores, c_rows)
+    gbuf[0:SPAN, inner : inner + STATE] = grad_b * slope[:, inner : inner + STATE]
+    gbuf[0:SPAN, inner + STATE : width] = grad_c * slope[:, inner + STATE : width]
+
+    upper = (rows_iota(square) <= lanes_iota(square)).astype(f32)
+    grad_decay = jnp.dot(upper, grad_total, precision=PRECISE, preferred_element_type=f32)
+    grad_pre = (grad_step + rate * grad_decay) * jax.nn.sigmoid(pre_step)
+    grad_pre = jnp.where(head_lane < heads, grad_pre, 0.0)
+    grad_ref[:, width : width + 128] = grad_pre.astype(bf16)
+    head_grad_ref[0:1, :] += jnp.sum(grad_decay * decay, axis=0, keepdims=True)
+    head_grad_ref[1:2, :] += jnp.sum(grad_pre, axis=0, keepdims=True)
+
+    for lane in range(0, width, 128):
+        lanes = slice(lane, lane + 128)
+        grad = gbuf[0:SPAN, lanes]
+        conv_grad_ref[CONV : CONV + 1, lanes] += jnp.sum(grad, axis=0, keepdims=True)
+        conv_grad_ref[CONV - 1 : CONV, lanes] += jnp.sum(grad * ubuf[8 : 8 + SPAN, lanes], axis=0, keepdims=True)
+        acc = conv_ref[CONV - 1 : CONV, lanes] * grad
+        for offset in range(1, CONV):
+            at = CONV - 1 - offset
+            shifted = ubuf[8 - offset : 8 - offset + SPAN, lanes] * aux_ref[:, 2 + offset : 3 + offset]
+            conv_grad_ref[at : at + 1, lanes] += jnp.sum(grad * shifted, axis=0, keepdims=True)
+            later = gbuf[offset : offset + SPAN, lanes] * aux_ref[:, 5 + offset : 6 + offset]
+            acc = acc + conv_ref[at : at + 1, lanes] * later
+        grad_ref[:, lanes] = acc.astype(bf16)
+
+
+def token_aux(segment):
+    length = segment.shape[0]
+    ends = segment.reshape(-1, SPAN)[:, -1]
+    end_of = jnp.repeat(ends, SPAN)
+    before = jnp.repeat(jnp.concatenate([jnp.full((1,), -1, segment.dtype), ends[:-1]]), SPAN)
+    columns = [segment, segment == before, segment == end_of]
+    for offset in range(1, CONV):
+        columns.append(jnp.pad(segment, (offset, 0), constant_values=-1)[:length] == segment)
+    for offset in range(1, CONV):
+        columns.append(jnp.pad(segment, (0, offset), constant_values=-1)[offset:] == segment)
+    columns = [column.astype(jnp.float32) for column in columns]
+    return jnp.stack(columns + [jnp.zeros((length,), jnp.float32)] * (16 - len(columns)), axis=1)
+
+
+def ssd_specs(heads, wide, order):
+    inner = heads * SSM_DIM
+    width = inner + 2 * STATE
+    return [
+        pl.BlockSpec((SPAN, wide), lambda i: (order(i), 0)),
+        pl.BlockSpec((SPAN, 16), lambda i: (order(i), 0)),
+        pl.BlockSpec((1, 1, SPAN), lambda i: (order(i), 0, 0)),
+        pl.BlockSpec((8, width), lambda i: (0, 0)),
+        pl.BlockSpec((8, 128), lambda i: (0, 0)),
+        pl.BlockSpec((8, inner), lambda i: (0, 0)),
+    ]
+
+
+def ssd_forward(first, aux, seg_rows, conv, head, skip, heads):
+    length, wide = first.shape
+    inner = heads * SSM_DIM
+    width = inner + 2 * STATE
+    blocks = length // SPAN
+    return pl.pallas_call(
+        functools.partial(ssd_forward_kernel, heads),
+        grid=(blocks,),
+        in_specs=ssd_specs(heads, wide, lambda i: i),
+        out_specs=[
+            pl.BlockSpec((SPAN, inner), lambda i: (i, 0)),
+            pl.BlockSpec((1, STATE, inner), lambda i: (i, 0, 0)),
+        ],
+        out_shape=[
+            jax.ShapeDtypeStruct((length, inner), jnp.bfloat16),
+            jax.ShapeDtypeStruct((blocks, STATE, inner), jnp.bfloat16),
+        ],
+        scratch_shapes=[
+            pltpu.VMEM((SPAN + 8, width), jnp.float32),
+            pltpu.VMEM((SPAN, width), jnp.bfloat16),
+            pltpu.VMEM((STATE, inner), jnp.float32),
+        ],
+        compiler_params=pltpu.CompilerParams(
+            dimension_semantics=("arbitrary",), vmem_limit_bytes=VMEM_BYTES
+        ),
+        cost_estimate=pl.CostEstimate(
+            flops=60_000_000_000 * heads // 12, bytes_accessed=12_000_000, transcendentals=4_000_000
+        ),
+        name="ssd_forward",
+    )(first, aux, seg_rows, conv, head, skip)
+
+
+def ssd_backward(first, aux, seg_rows, conv, head, skip, starts, dy, heads):
+    length, wide = first.shape
+    inner = heads * SSM_DIM
+    width = inner + 2 * STATE
+    blocks = length // SPAN
+    specs = ssd_specs(heads, wide, lambda i: blocks - 1 - i)
+    per_block = SPAN // 16
+    specs.insert(
+        1, pl.BlockSpec((16, wide), lambda i: (jnp.maximum((blocks - 1 - i) * per_block - 1, 0), 0))
     )
-
-
-def causal_conv(channels, segment, conv_weight, conv_bias):
-    length = channels.shape[0]
-    summed = jnp.broadcast_to(conv_bias[None, :], channels.shape)
-    for offset in range(CONV):
-        shifted = jnp.pad(channels, ((offset, 0), (0, 0)))[:length]
-        earlier = jnp.pad(segment, (offset, 0), constant_values=-1)[:length]
-        keep_mask = (earlier == segment).astype(jnp.float32)
-        summed = summed + conv_weight[CONV - 1 - offset][None, :] * shifted * keep_mask[:, None]
-    return jax.nn.silu(summed)
-
-
-def ssd_scan(x_heads, log_decay, step_size, b_rows, c_rows, segment):
-    length, head_count, head_width = x_heads.shape
-    block_count = length // SPAN
-    seq_items = (
-        x_heads.reshape(block_count, SPAN, head_count, head_width),
-        log_decay.reshape(block_count, SPAN, head_count),
-        step_size.reshape(block_count, SPAN, head_count),
-        b_rows.reshape(block_count, SPAN, STATE),
-        c_rows.reshape(block_count, SPAN, STATE),
-        segment.reshape(block_count, SPAN),
-    )
-    lower_mask = jnp.tril(jnp.ones((SPAN, SPAN), dtype=bool))
-
-    def block_step(block_carry, block_items):
-        ssm_state, last_segment = block_carry
-        x_block, decay_block, step_block, b_block, c_block, seg_block = block_items
-        cumulative = jnp.cumsum(decay_block, axis=0)
-        same_doc = ((seg_block[:, None] == seg_block[None, :]) & lower_mask)[:, :, None]
-        decay_gap = cumulative[:, None, :] - cumulative[None, :, :]
-        inner_weight = jnp.where(same_doc, jnp.exp(jnp.where(same_doc, decay_gap, 0.0)), 0.0)
-        block_scores = jnp.dot(c_block, b_block.T, precision=PRECISE)
-        mixing = inner_weight * block_scores[:, :, None] * step_block[None, :, :]
-        y_inner = jnp.einsum("tsh,shp->thp", mixing, x_block, precision=PRECISE)
-        carry_keep = (seg_block == last_segment).astype(jnp.float32)
-        state_weight = jnp.exp(cumulative) * carry_keep[:, None]
-        from_state = (
-            jnp.einsum("tn,hpn->thp", c_block, ssm_state, precision=PRECISE)
-            * state_weight[:, :, None]
-        )
-        end_keep = (seg_block == seg_block[-1]).astype(jnp.float32)
-        input_weight = (
-            jnp.exp(cumulative[-1][None, :] - cumulative) * step_block * end_keep[:, None]
-        )
-        state_keep = jnp.exp(cumulative[-1]) * (seg_block[-1] == last_segment).astype(jnp.float32)
-        new_state = ssm_state * state_keep[:, None, None] + jnp.einsum(
-            "sh,shp,sn->hpn", input_weight, x_block, b_block, precision=PRECISE
-        )
-        return ((new_state, seg_block[-1]), y_inner + from_state)
-
-    start_carry = (
-        jnp.zeros((head_count, head_width, STATE), jnp.float32),
-        jnp.array(-1, jnp.int32),
-    )
-    unused, y_blocks = lax.scan(jax.checkpoint(block_step), start_carry, seq_items)
-    return y_blocks.reshape(length, head_count, head_width)
-
-
-def attend(q_rot, k_rot, value_heads, segment):
-    length, head_count, head_width = q_rot.shape
-    block_count = length // ATT_BLOCK
-    positions = jnp.arange(length, dtype=jnp.int32)
-    rounder = make_rounder()
-
-    def one_block(block_index):
-        first_row = block_index * ATT_BLOCK
-        q_block = lax.dynamic_slice_in_dim(q_rot, first_row, ATT_BLOCK, 0)
-        seg_query = lax.dynamic_slice_in_dim(segment, first_row, ATT_BLOCK, 0)
-        pos_query = first_row + jnp.arange(ATT_BLOCK, dtype=jnp.int32)
-        scores = jnp.einsum("qhe,khe->hqk", q_block, k_rot, precision=PRECISE) * head_width ** (
-            -0.5
-        )
-        allowed = (pos_query[:, None] >= positions[None, :]) & (
-            seg_query[:, None] == segment[None, :]
-        )
-        scores = jnp.where(allowed[None, :, :], scores, -1e30)
-        attn_probs = rounder(jax.nn.softmax(scores, axis=-1))
-        return jnp.einsum("hqk,khe->qhe", attn_probs, value_heads, precision=PRECISE)
-
-    blocks = lax.map(jax.checkpoint(one_block), jnp.arange(block_count, dtype=jnp.int32))
-    return blocks.reshape(length, head_count, head_width)
-
-
-def mixer_heads(
-    x_part,
-    dt_part,
-    query_rows,
-    key_rep,
-    value_rep,
-    bc_part,
-    segment,
-    conv_weight,
-    conv_bias,
-    log_rate,
-    step_bias,
-    skip_gain,
+    specs += [
+        pl.BlockSpec((1, STATE, inner), lambda i: (blocks - 1 - i, 0, 0)),
+        pl.BlockSpec((SPAN, inner), lambda i: (blocks - 1 - i, 0)),
+    ]
+    return pl.pallas_call(
+        functools.partial(ssd_backward_kernel, heads),
+        grid=(blocks,),
+        in_specs=specs,
+        out_specs=[
+            pl.BlockSpec((SPAN, wide), lambda i: (blocks - 1 - i, 0)),
+            pl.BlockSpec((8, width), lambda i: (0, 0)),
+            pl.BlockSpec((8, 128), lambda i: (0, 0)),
+            pl.BlockSpec((8, inner), lambda i: (0, 0)),
+        ],
+        out_shape=[
+            jax.ShapeDtypeStruct((length, wide), jnp.bfloat16),
+            jax.ShapeDtypeStruct((8, width), jnp.float32),
+            jax.ShapeDtypeStruct((8, 128), jnp.float32),
+            jax.ShapeDtypeStruct((8, inner), jnp.float32),
+        ],
+        scratch_shapes=[
+            pltpu.VMEM((SPAN + 8, width), jnp.float32),
+            pltpu.VMEM((SPAN, width), jnp.bfloat16),
+            pltpu.VMEM((SPAN, width), jnp.float32),
+            pltpu.VMEM((SPAN + 8, width), jnp.float32),
+            pltpu.VMEM((STATE, inner), jnp.float32),
+        ],
+        compiler_params=pltpu.CompilerParams(
+            dimension_semantics=("arbitrary",), vmem_limit_bytes=VMEM_BYTES
+        ),
+        cost_estimate=pl.CostEstimate(
+            flops=120_000_000_000 * heads // 12, bytes_accessed=16_000_000, transcendentals=5_000_000
+        ),
+        name="ssd_backward",
+    )(first, first, aux, seg_rows, conv, head, skip, starts, dy)
+
+
+def rotary_tables(length):
+    half = HEAD_DIM // 2
+    frequency = ROPE_BASE ** (-jnp.arange(half).astype(jnp.float32) / half)
+    angles = jnp.arange(length, dtype=jnp.int32).astype(jnp.float32)[:, None] * frequency[None, :]
+    cosine, sine = jnp.cos(angles), jnp.sin(angles)
+    return jnp.concatenate([cosine, cosine], axis=1), jnp.concatenate([-sine, sine], axis=1)
+
+
+def turn(rows, cosine, sine):
+    wide = rows.astype(jnp.float32)
+    return (wide * cosine + pltpu.roll(wide, HEAD_DIM // 2, 1) * sine).astype(jnp.bfloat16)
+
+
+def turn_back(grads, cosine, sine):
+    return (grads * cosine + pltpu.roll(grads * sine, HEAD_DIM // 2, 1)).astype(jnp.bfloat16)
+
+
+def block_scores(q_block, k_part, first_row, seg_col, seg_row):
+    scores = dot_last(q_block, k_part) * HEAD_DIM ** (-0.5)
+    shape = scores.shape
+    allowed = (rows_iota(shape) + first_row >= lanes_iota(shape)) & (seg_col == seg_row)
+    return jnp.where(allowed, scores, -1e30)
+
+
+def attend_forward_kernel(query_heads, block, qkv_ref, cos_ref, sin_ref, aux_ref, seg_ref, out_ref, lse_ref, k_rot):
+    length = qkv_ref.shape[0]
+    q_width = query_heads * HEAD_DIM
+    k_rot[...] = turn(qkv_ref[:, q_width : q_width + HEAD_DIM], cos_ref[...], sin_ref[...])
+    for start in range(0, length, block):
+        rows = slice(start, start + block)
+        end = start + block
+        for head in range(query_heads):
+            lanes = slice(head * HEAD_DIM, (head + 1) * HEAD_DIM)
+            q_block = turn(qkv_ref[rows, lanes], cos_ref[rows, :], sin_ref[rows, :])
+            scores = block_scores(q_block, k_rot[:end, :], start, aux_ref[rows, 0:1], seg_ref[:, :end])
+            top = jnp.max(scores, axis=1, keepdims=True)
+            raised = jnp.exp(scores - top)
+            total = jnp.sum(raised, axis=1, keepdims=True)
+            probs = (raised * (1.0 / total)).astype(jnp.bfloat16)
+            value = qkv_ref[:end, q_width + HEAD_DIM :]
+            out_ref[rows, lanes] = dot_plain(probs, value).astype(jnp.bfloat16)
+            lse_ref[rows, head : head + 1] = top + jnp.log(total)
+
+
+def attend_backward_kernel(
+    query_heads, block, qkv_ref, cos_ref, sin_ref, aux_ref, seg_ref, lse_ref, grad_ref, out_ref, k_rot, dk, dv
 ):
-    rounder = make_rounder()
-    length = x_part.shape[0]
-    inner_width = x_part.shape[1]
-    head_count = dt_part.shape[1]
-    conv_out = rounder(
-        causal_conv(jnp.concatenate([x_part, bc_part], axis=1), segment, conv_weight, conv_bias)
-    )
-    x_heads = conv_out[:, :inner_width].reshape(length, head_count, inner_width // head_count)
-    b_rows = conv_out[:, inner_width : inner_width + STATE]
-    c_rows = conv_out[:, inner_width + STATE :]
-    step_size = jax.nn.softplus(dt_part + step_bias[None, :])
-    log_decay = -jnp.exp(log_rate)[None, :] * step_size
-    y_heads = (
-        ssd_scan(x_heads, log_decay, step_size, b_rows, c_rows, segment)
-        + skip_gain[None, :, None] * x_heads
-    )
-    y_rows = rounder(y_heads.reshape(length, inner_width))
-    positions = jnp.arange(length, dtype=jnp.int32)
-    query_heads = query_rows.shape[1] // HEAD_DIM
-    q_rot = rounder(rotate(query_rows.reshape(length, query_heads, HEAD_DIM), positions))
-    k_rot = rounder(rotate(key_rep.reshape(length, query_heads, HEAD_DIM), positions))
-    attended = attend(q_rot, k_rot, value_rep.reshape(length, query_heads, HEAD_DIM), segment)
-    attended = rounder(attended.reshape(length, query_heads * HEAD_DIM))
-    return (y_rows, attended)
-
-
-def norm_forward(token_rows, gain_vec):
-    inv_scale = lax.rsqrt(jnp.mean(token_rows * token_rows, axis=-1, keepdims=True) + EPSILON)
-    return (token_rows * inv_scale * gain_vec, inv_scale)
-
-
-def norm_backward(token_rows, inv_scale, gain_vec, grad_rows):
-    normed = token_rows * inv_scale
-    gain_grad = jnp.sum(normed * grad_rows, axis=0)
-    weighted = grad_rows * gain_vec
-    row_grad = inv_scale * (weighted - normed * jnp.mean(weighted * normed, axis=-1, keepdims=True))
-    return (row_grad, gain_grad)
-
-
-def repeat_heads(kv_rows, groups):
-    length = kv_rows.shape[0]
-    shaped = kv_rows.reshape(length, -1, 1, HEAD_DIM)
-    return jnp.broadcast_to(shaped, (length, shaped.shape[1], groups, HEAD_DIM)).reshape(length, -1)
-
-
-def fold_heads(rep_rows, groups):
-    length = rep_rows.shape[0]
-    summed = jnp.sum(rep_rows.astype(jnp.float32).reshape(length, -1, groups, HEAD_DIM), axis=2)
-    return summed.reshape(length, -1).astype(jnp.bfloat16)
+    f32, bf16 = jnp.float32, jnp.bfloat16
+    length = qkv_ref.shape[0]
+    q_width = query_heads * HEAD_DIM
+    k_rot[...] = turn(qkv_ref[:, q_width : q_width + HEAD_DIM], cos_ref[...], sin_ref[...])
+    dk[...] = jnp.zeros(dk.shape, f32)
+    dv[...] = jnp.zeros(dv.shape, f32)
+    for start in range(0, length, block):
+        rows = slice(start, start + block)
+        end = start + block
+        for head in range(query_heads):
+            lanes = slice(head * HEAD_DIM, (head + 1) * HEAD_DIM)
+            cosine, sine = cos_ref[rows, :], sin_ref[rows, :]
+            q_block = turn(qkv_ref[rows, lanes], cosine, sine)
+            scores = block_scores(q_block, k_rot[:end, :], start, aux_ref[rows, 0:1], seg_ref[:, :end])
+            probs = jnp.exp(scores - lse_ref[rows, head : head + 1])
+            grad = grad_ref[rows, lanes]
+            grad_probs = dot_last(grad, qkv_ref[:end, q_width + HEAD_DIM :])
+            mean = jnp.sum(grad_probs * probs, axis=1, keepdims=True)
+            grad_scores = (probs * (grad_probs - mean) * HEAD_DIM ** (-0.5)).astype(bf16)
+            out_ref[rows, lanes] = turn_back(dot_plain(grad_scores, k_rot[:end, :]), cosine, sine)
+            dk[:end, :] += dot_first(grad_scores, q_block)
+            dv[:end, :] += dot_first(probs.astype(bf16), grad)
+    out_ref[:, q_width : q_width + HEAD_DIM] = turn_back(dk[...], cos_ref[...], sin_ref[...])
+    out_ref[:, q_width + HEAD_DIM :] = dv[...].astype(bf16)
+
+
+def attend_forward(qkv, tables, aux, seg_row, query_heads):
+    length = qkv.shape[0]
+    return pl.pallas_call(
+        functools.partial(attend_forward_kernel, query_heads, min(ATT_ROWS, length)),
+        out_shape=[
+            jax.ShapeDtypeStruct((length, query_heads * HEAD_DIM), jnp.bfloat16),
+            jax.ShapeDtypeStruct((length, 8), jnp.float32),
+        ],
+        scratch_shapes=[pltpu.VMEM((length, HEAD_DIM), jnp.bfloat16)],
+        compiler_params=pltpu.CompilerParams(vmem_limit_bytes=VMEM_BYTES),
+        cost_estimate=pl.CostEstimate(
+            flops=8_000_000_000 * query_heads, bytes_accessed=4_000_000, transcendentals=1_000_000
+        ),
+        name="attend_forward",
+    )(qkv, tables[0], tables[1], aux, seg_row)
+
+
+def attend_backward(qkv, tables, aux, seg_row, lse, grad, query_heads):
+    length = qkv.shape[0]
+    return pl.pallas_call(
+        functools.partial(attend_backward_kernel, query_heads, min(ATT_ROWS, length)),
+        out_shape=jax.ShapeDtypeStruct(qkv.shape, jnp.bfloat16),
+        scratch_shapes=[
+            pltpu.VMEM((length, HEAD_DIM), jnp.bfloat16),
+            pltpu.VMEM((length, HEAD_DIM), jnp.float32),
+            pltpu.VMEM((length, HEAD_DIM), jnp.float32),
+        ],
+        compiler_params=pltpu.CompilerParams(vmem_limit_bytes=VMEM_BYTES),
+        cost_estimate=pl.CostEstimate(
+            flops=20_000_000_000 * query_heads, bytes_accessed=6_000_000, transcendentals=1_000_000
+        ),
+        name="attend_backward",
+    )(qkv, tables[0], tables[1], aux, seg_row, lse, grad)
 
 
 def matmul_rows(left, right):
@@ -383,48 +674,35 @@
         [lax.dynamic_slice_in_dim(conv_all, inner_start, inner, 1), conv_all[:, SSM_INNER:]], axis=1
     )
 
+    conv_table = jnp.pad(conv_local, ((0, 8 - CONV - 1), (0, 0)))
+    head_table = jnp.pad(jnp.stack([bias_local, rate_local]), ((0, 6), (0, 128 - heads)))
+    skip_table = jnp.broadcast_to(jnp.repeat(skip_local, SSM_DIM)[None], (8, inner))
+    tables = rotary_tables(segments.shape[2])
+    z_w, qkv_w = second_w[:, :inner], second_w[:, inner:]
+
     micro = range(MICRO)
     token_rows = [inputs[m, 0].astype(f32) for m in micro]
     rows_all = [gather_tokens(to_gathered(inputs[m, 0])) for m in micro]
     cot_all = [gather_tokens(cotangent[m, 0]) for m in micro]
     hidden_all, normed_all = [], []
-    mixer_out, pullbacks, gate_zs, middles, dts = [], [], [], [], []
+    mixer_out, kept, gate_zs, middles = [], [], [], []
     for m in micro:
         segment = segments[m, 0]
+        aux = token_aux(segment)
+        seg_float = segment.astype(f32)
+        seg_blocks, seg_row = seg_float.reshape(-1, 1, SPAN), seg_float[None]
         wide = rows_all[m].astype(f32)
         normed = wide * inv_rms(wide)
         hidden = (normed * gain_in).astype(bf16)
         hidden_all.append(hidden)
         first = matmul_rows(hidden, first_w).astype(bf16)
-        second = matmul_rows(hidden, second_w)
-        gate_z = second[:, :inner]
-        attn_rows = second[:, inner:].astype(bf16).astype(f32)
-
-        def local_mixer(x_part, dt_part, query, key, value, bc_part, weight, bias, rate, step_bias, skip):
-            key_rep = jnp.tile(key, (1, query_heads))
-            value_rep = jnp.tile(value, (1, query_heads))
-            return mixer_heads(
-                x_part, dt_part, query, key_rep, value_rep, bc_part, segment, weight, bias, rate, step_bias, skip
-            )
-
-        (y_rows, attended), pullback = jax.vjp(
-            local_mixer,
-            first[:, :inner].astype(f32),
-            first[:, inner + 2 * STATE : inner + 2 * STATE + heads].astype(f32),
-            attn_rows[:, :q_width],
-            attn_rows[:, q_width : q_width + HEAD_DIM],
-            attn_rows[:, q_width + HEAD_DIM :],
-            first[:, inner : inner + 2 * STATE].astype(f32),
-            conv_local[:CONV],
-            conv_local[CONV],
-            rate_local,
-            bias_local,
-            skip_local,
-        )
+        gate_z = matmul_rows(hidden, z_w)
+        qkv = matmul_rows(hidden, qkv_w).astype(bf16)
+        y_rows, starts = ssd_forward(first, aux, seg_blocks, conv_table, head_table, skip_table, heads)
+        attended, lse = attend_forward(qkv, tables, aux, seg_row, query_heads)
         gate_zs.append(gate_z)
-        pullbacks.append(pullback)
-        gated = (y_rows * jax.nn.silu(gate_z)).astype(bf16)
-        attended = attended.astype(bf16)
+        kept.append((first, aux, seg_blocks, seg_row, starts, qkv, lse))
+        gated = (y_rows.astype(f32) * jax.nn.silu(gate_z)).astype(bf16)
         mixer_out.append((y_rows, gated, attended))
 
         def mixed_rows(block):
@@ -477,22 +755,22 @@
         gate_z = gate_zs[m]
         sig = jax.nn.sigmoid(gate_z)
         grad_y = (grad_gated * gate_z * sig).astype(bf16)
-        grad_z = (grad_gated * y_rows * sig * (1.0 + gate_z * (1.0 - sig))).astype(bf16)
-        (g_x, g_dt, g_query, g_key, g_value, g_bc, g_w, g_b, g_rate, g_bias, g_skip) = pullbacks[m](
-            (grad_y.astype(f32), grad_attended.astype(f32))
+        y_wide = y_rows.astype(f32)
+        grad_z = (grad_gated * y_wide * sig * (1.0 + gate_z * (1.0 - sig))).astype(bf16)
+        first, aux, seg_blocks, seg_row, starts, qkv, lse = kept[m]
+        grad_qkv = attend_backward(qkv, tables, aux, seg_row, lse, grad_attended, query_heads)
+        first_grad, g_conv, g_head, g_skip = ssd_backward(
+            first, aux, seg_blocks, conv_table, head_table, skip_table, starts, grad_y, heads
         )
-        conv_grad = conv_grad + jnp.concatenate([g_w, g_b[None]], axis=0)
-        rate_sum, bias_sum, skip_sum = rate_sum + g_rate, bias_sum + g_bias, skip_sum + g_skip
-        first_grad = jnp.concatenate([g_x, g_bc, g_dt], axis=1).astype(bf16)
-        first_grad = jnp.pad(first_grad, ((0, 0), (0, first_w.shape[1] - first_grad.shape[1])))
-        second_grad = jnp.concatenate(
-            [grad_z, g_query.astype(bf16), g_key.astype(bf16), g_value.astype(bf16)], axis=1
-        )
+        conv_grad = conv_grad + g_conv[: CONV + 1]
+        rate_sum, bias_sum = rate_sum + g_head[0, :heads], bias_sum + g_head[1, :heads]
+        skip_sum = skip_sum + jnp.sum(g_skip[0].reshape(heads, SSM_DIM), axis=1)
 
         def in_rows(block):
             one = lax.dynamic_slice_in_dim(first_grad, block * tokens, tokens, 0)
-            two = lax.dynamic_slice_in_dim(second_grad, block * tokens, tokens, 0)
-            return matmul_back(one, first_w) + matmul_back(two, second_w)
+            two = lax.dynamic_slice_in_dim(grad_z, block * tokens, tokens, 0)
+            three = lax.dynamic_slice_in_dim(grad_qkv, block * tokens, tokens, 0)
+            return matmul_back(one, first_w) + matmul_back(two, z_w) + matmul_back(three, qkv_w)
 
         grad_hidden = from_gathered(scatter_tokens(in_rows))
         gain_row = from_gathered(gain_in)
@@ -505,15 +783,17 @@
         mixer_grads.append(
             (
                 weight_grad(hidden_all[m], first_grad),
-                weight_grad(hidden_all[m], second_grad),
+                weight_grad(hidden_all[m], grad_z),
+                weight_grad(hidden_all[m], grad_qkv),
                 weight_grad(gated, grad_mixed),
                 weight_grad(attended, grad_mixed),
             )
         )
-    first_sum, second_sum, ssm_out_sum, attn_out_sum = (a + b for a, b in zip(*mixer_grads))
+    first_sum, z_sum, qkv_sum, ssm_out_sum, attn_out_sum = (a + b for a, b in zip(*mixer_grads))
     ssm_out_grad = collect_rows(ssm_out_sum)
     attn_out_grad = collect_rows(attn_out_sum)
-    second_back = collect_columns(second_sum).astype(f32)
+    z_back = collect_columns(z_sum).astype(f32)
+    qkv_back = collect_columns(qkv_sum).astype(f32)
     first_back = collect_columns(first_sum).astype(f32)
 
     def own_columns(block):
@@ -521,7 +801,7 @@
 
     ssm_in_grad = jnp.concatenate(
         [
-            own_columns(second_back[:, :, :inner]),
+            own_columns(z_back),
             own_columns(first_back[:, :, :inner]),
             jnp.sum(first_back[:, :, inner : inner + 2 * STATE], axis=0),
             own_columns(first_back[:, :, inner + 2 * STATE : inner + 2 * STATE + heads]),
@@ -536,9 +816,9 @@
 
     attn_in_grad = jnp.concatenate(
         [
-            own_columns(second_back[:, :, inner : inner + q_width]),
-            kv_columns(second_back[:, :, inner + q_width : inner + q_width + HEAD_DIM]),
-            kv_columns(second_back[:, :, inner + q_width + HEAD_DIM :]),
+            own_columns(qkv_back[:, :, :q_width]),
+            kv_columns(qkv_back[:, :, q_width : q_width + HEAD_DIM]),
+            kv_columns(qkv_back[:, :, q_width + HEAD_DIM :]),
         ],
         axis=1,
     )

time: 2750 us -> 1230 us (0.45)
  local copies, waits for them, and re-layouts: 889 us -> 167 us
  matrix products: 841 us -> 387 us
  other arithmetic: 395 us -> 47.3 us
  Pallas kernels: 0 us -> 158 us
  waiting for transfers between devices: 406 us -> 328 us
  loops' own time: 54.4 us -> 0 us
    dot_general x252 -> x0, matrix products: 478 us -> none  [the longest x48 119 us: block_step(): y_inner = jnp.einsum('tsh,shp->thp', mixing, x_block, precision=PRECISE)]
    dynamic_update_slice x64 -> x1, local copies, waits for them, and re-layouts: 381 us -> 0.01 us  [on_device(): lax.dynamic_update_slice_in_dim(conv_whole, conv_grad[:, inner:], SSM_INN...]
    pallas_call x0 -> x8, Pallas kernels: none -> 158 us  [the longest x2 105 us: ssd_backward(): pl.pallas_call(functools.partial(ssd_backward_kernel, heads), grid=(block...]
    ppermute x24, waiting for transfers between devices: 201 us -> 94.2 us  [scatter_tokens(): arrived.append(lax.ppermute(part, 'seq', peers(count, flip)))]
    another operation x83 -> x3, other arithmetic: 85.9 us -> 0.16 us  [the longest x2 0.15 us: token_aux(): jnp.stack(columns + [jnp.zeros((length,), jnp.float32)] * (16 - len(colum...]
    squeeze x128 -> x0, local copies, waits for them, and re-layouts: 80.7 us -> none  [the longest x112 80.5 us: ssd_scan(): lax.scan(jax.checkpoint(block_step), start_carry, seq_items)]
    convert_element_type x69 -> x5, other arithmetic: 76.1 us -> 0.1 us  [the longest x1 0.05 us: on_device(): qkv_back = collect_columns(qkv_sum).astype(f32)]
    dynamic_slice x57 -> x0, local copies, waits for them, and re-layouts: 66.4 us -> none  [the longest x32 55.9 us: ssd_scan(): lax.scan(jax.checkpoint(block_step), start_carry, seq_items)]
  transfers between devices with their start and end apart: 68 -> 70, of which waited for: 38 -> 29; matrix products, arithmetic and copies ran while one was open for 52% -> 43% of each run, Pallas kernels for 0% -> 12%
where the time goes in v2:
time: 1230 us; the launch traced here: 1220 us
  matrix products  387 us (31%)
  waiting for transfers between devices  328 us (27%)
  local copies, waits for them, and re-layouts  167 us (14%)
  Pallas kernels  158 us (13%)
  starting transfers between devices  76 us (6%)
  other arithmetic  47.3 us (4%)
  blocking collectives  42.7 us (3%)
  between operations  17 us (1%)
    ppermute x24, waiting for transfers between devices, gather_tokens(): part = rows if flip == 0 else lax.ppermute(rows, 'seq', peers(count, flip))  205 us
    dot_general x32, matrix products, matmul_rows(): jnp.einsum('tc,cd->td', left, right, preferred_element_type=jnp.float32)  141 us
    dot_general x38, matrix products, matmul_back(): jnp.einsum('td,cd->tc', left, right, preferred_element_type=jnp.float32)  139 us
    dot_general x14, matrix products, weight_grad(): jnp.einsum('tc,td->cd', left, right, preferred_element_type=jnp.float32)  107 us
    pallas_call x2, Pallas kernels, ssd_backward(): pl.pallas_call(functools.partial(ssd_backward_kernel, heads), grid=(block...  105 us
    ppermute x24, waiting for transfers between devices, scatter_tokens(): arrived.append(lax.ppermute(part, 'seq', peers(count, flip)))  94.2 us
    all_to_all x3, blocking collectives, spread_columns(): lax.all_to_all(stacked, 'seq', split_axis=0, concat_axis=0, tiled=True)  42.7 us
    dynamic_update_slice x30, local copies, waits for them, and re-layouts, gather_tokens(): lax.dynamic_update_slice_in_dim(whole, part, (index ^ flip) * tokens, 0)  39.1 us
  transfers between devices with their start and end apart: 70, of which 29 were waited for; matrix products, arithmetic and copies ran while one was open for 43% of the time, Pallas kernels for 12%

profile of v2, /device:TPU:0, one launch (start us, length us, event | category | flops | bytes accessed | tf_op | source)
XLA Modules:
  0.0 1222.7 jit_solution(7854273956632501919)
XLA Ops:
  14.3 15.9 %all_to_all.35 = bf16[4,64,1408]{2,1,0:T(8,128)(2,1)} all-to-all(bf16[4,64,1408]{2,1,0:T(8,128)(2,1)S(1)} %copy.508), channel_id=1, replica_groups=mesh['seq'=4,'fsdp'=8] {'seq'}, dimensions={0} | all-to-all | bytes 1441792 | tf_op jit(solution)/shard_map/all_to_all | solution.py:547
  31.8 11.9 all_to_all.36
  47.2 14.9 %all_to_all.37 = bf16[4,64,2048]{2,1,0:T(8,128)(2,1)} all-to-all(bf16[4,64,2048]{2,1,0:T(8,128)(2,1)S(1)} %copy.531), channel_id=1, replica_groups=mesh['seq'=4,'fsdp'=8] {'seq'}, dimensions={0} | all-to-all | bytes 2097152 | tf_op jit(solution)/shard_map/all_to_all | solution.py:547
  101.7 14.0 %collective-permute-done.13 = bf16[256,2048]{0,1:T(8,128)(2,1)} collective-permute-done((bf16[256,2048]{0,1:T(8,128)(2,1)}, bf16[256,2048]{0,1:T(8,128)(2,1)}, u32[]{:S(2)}, u32[]{:S(2)}) %collective-permute-start.13) | collective-permute-done | bytes 1048608 | tf_op jit(solution)/shard_map/ppermute | solution.py:518
  121.6 15.7 %collective-permute-done = bf16[256,2048]{0,1:T(8,128)(2,1)} collective-permute-done((bf16[256,2048]{0,1:T(8,128)(2,1)}, bf16[256,2048]{0,1:T(8,128)(2,1)}, u32[]{:S(2)}, u32[]{:S(2)}) %collective-permute-start) | collective-permute-done | bytes 1048608 | tf_op jit(solution)/shard_map/ppermute | solution.py:518
  140.5 20.2 %collective-permute-done.1 = bf16[256,2048]{0,1:T(8,128)(2,1)} collective-permute-done((bf16[256,2048]{0,1:T(8,128)(2,1)}, bf16[256,2048]{0,1:T(8,128)(2,1)}, u32[]{:S(2)}, u32[]{:S(2)}) %collective-permute-start.1) | collective-permute-done | bytes 1048608 | tf_op jit(solution)/shard_map/ppermute | solution.py:518
  185.6 20.0 %collective-permute-done.25 = bf16[256,2048]{1,0:T(8,128)(2,1)} collective-permute-done((bf16[256,2048]{1,0:T(8,128)(2,1)}, bf16[256,2048]{1,0:T(8,128)(2,1)}, u32[]{:S(2)}, u32[]{:S(2)}) %collective-permute-start.25) | collective-permute-done | bytes 1048608 | tf_op jit(solution)/shard_map/ppermute | solution.py:518
  210.3 17.0 %collective-permute-done.36 = bf16[256,2048]{1,0:T(8,128)(2,1)} collective-permute-done((bf16[256,2048]{1,0:T(8,128)(2,1)}, bf16[256,2048]{1,0:T(8,128)(2,1)}, u32[]{:S(2)}, u32[]{:S(2)}) %collective-permute-start.36) | collective-permute-done | bytes 1048608 | tf_op jit(solution)/shard_map/ppermute | solution.py:518
  229.7 15.7 %collective-permute-done.37 = bf16[256,2048]{1,0:T(8,128)(2,1)} collective-permute-done((bf16[256,2048]{1,0:T(8,128)(2,1)}, bf16[256,2048]{1,0:T(8,128)(2,1)}, u32[]{:S(2)}, u32[]{:S(2)}) %collective-permute-start.37) | collective-permute-done | bytes 1048608 | tf_op jit(solution)/shard_map/ppermute | solution.py:518
  263.6 9.3 convolution_convert_fusion.1.first_ref.before_ref
  273.0 15.1 %ssd_forward.2 = (bf16[1024,768]{1,0:T(8,128)(2,1)S(1)}, bf16[8,256,768]{2,1,0:T(8,128)(2,1)}) custom-call(bf16[1024,1408]{1,0:T(8,128)(2,1)S(1)} %convolution_convert_fusion.1.first_ref.before_ref, f32[1024,16]{1,0:T(8,128)S(1)} %copy.513.aux_ref, f32[8,1,128]{2,1,0:T(1,128)S(1)} %get-tuple-element.208.seg_ref, f32[8,1280]{1,0:T(8,128)S(1)} %select_maximum_fusion.conv_ref, ...), custom_call_target="tpu_custom_call" | custom-call | flops 60000002048 | bytes 12000000 | tf_op jit(solution)/shard_map/ssd_forward/pallas_call | solution.py:314
  289.3 8.2 fusion.7
  323.5 10.8 convolution_convert_fusion.first_ref.before_ref
  334.3 14.5 %ssd_forward.3 = (bf16[1024,768]{1,0:T(8,128)(2,1)S(1)}, bf16[8,256,768]{2,1,0:T(8,128)(2,1)}) custom-call(bf16[1024,1408]{1,0:T(8,128)(2,1)S(1)} %convolution_convert_fusion.first_ref.before_ref, f32[1024,16]{1,0:T(8,128)S(1)} %copy.540.aux_ref, f32[8,1,128]{2,1,0:T(1,128)S(1)} %get-tuple-element.212.seg_ref, f32[8,1280]{1,0:T(8,128)S(1)} %select_maximum_fusion.conv_ref, ...), custom_call_target="tpu_custom_call" | custom-call | flops 60000002048 | bytes 12000000 | tf_op jit(solution)/shard_map/ssd_forward/pallas_call | solution.py:314
  348.8 8.1 fusion.11
  388.3 20.0 %collective-permute-done.6 = bf16[256,2048]{0,1:T(8,128)(2,1)} collective-permute-done((bf16[256,2048]{0,1:T(8,128)(2,1)}, bf16[256,2048]{0,1:T(8,128)(2,1)}, u32[]{:S(2)}, u32[]{:S(2)}) %collective-permute-start.6) | collective-permute-done | bytes 1048608 | tf_op jit(solution)/shard_map/ppermute | solution.py:518
  410.7 34.6 %collective-permute-done.7 = bf16[256,2048]{0,1:T(8,128)(2,1)} collective-permute-done((bf16[256,2048]{0,1:T(8,128)(2,1)}, bf16[256,2048]{0,1:T(8,128)(2,1)}, u32[]{:S(2)}, u32[]{:S(2)}) %collective-permute-start.7) | collective-permute-done | bytes 1048608 | tf_op jit(solution)/shard_map/ppermute | solution.py:518
  454.3 14.8 %fusion.294 = f32[1024,2048]{1,0:T(8,128)} fusion(bf16[1024,2048]{1,0:T(8,128)(2,1)} %constant_dynamic-update-slice_fusion.26, bf16[2048,2048]{1,0:T(8,128)(2,1)} %all-gather.15.cloned.1.call-done), kind=kOutput, calls=%fused_computation.490 | convolution fusion | flops 8589934592 | bytes 20971520 | tf_op jit(solution)/shard_map/tc,cd->td/dot_general | solution.py:497
  469.2 13.4 %multiply_convert_fusion.2 = (bf16[1024,1024]{1,0:T(8,128)(2,1)S(1)}, bf16[1024,1024]{1,0:T(8,128)(2,1)S(1)}, bf16[1024,1024]{1,0:T(8,128)(2,1)}) fusion(f32[1024,2048]{1,0:T(8,128)} %fusion.294, bf16[1024,2048]{1,0:T(8,128)(2,1)} %constant_dynamic-update-slice_fusion.14, bf16[1024,2048]{1,0:T(8,128)(2,1)} %all-gather.17.cloned.1.call-done), kind=kOutput, calls=%fused_computation.37 | convolution fusion | flops 4311744512 | bytes 23068672 | tf_op jit(solution)/shard_map/td,cd->tc/dot_general | solution.py:501
  499.8 15.9 %collective-permute-done.28 = bf16[256,2048]{1,0:T(8,128)(2,1)S(1)} collective-permute-done((bf16[256,2048]{1,0:T(8,128)(2,1)S(1)}, bf16[256,2048]{1,0:T(8,128)(2,1)S(1)}, u32[]{:S(2)}, u32[]{:S(2)}) %collective-permute-start.28) | collective-permute-done | bytes 1048608 | tf_op jit(solution)/shard_map/ppermute | solution.py:529
  551.3 14.2 %collective-permute-done.18 = bf16[256,2048]{0,1:T(8,128)(2,1)} collective-permute-done((bf16[256,2048]{0,1:T(8,128)(2,1)}, bf16[256,2048]{0,1:T(8,128)(2,1)}, u32[]{:S(2)}, u32[]{:S(2)}) %collective-permute-start.18) | collective-permute-done | bytes 1048608 | tf_op jit(solution)/shard_map/ppermute | solution.py:518
  568.5 13.9 %collective-permute-done.19 = bf16[256,2048]{0,1:T(8,128)(2,1)} collective-permute-done((bf16[256,2048]{0,1:T(8,128)(2,1)}, bf16[256,2048]{0,1:T(8,128)(2,1)}, u32[]{:S(2)}, u32[]{:S(2)}) %collective-permute-start.19) | collective-permute-done | bytes 1048608 | tf_op jit(solution)/shard_map/ppermute | solution.py:518
  588.5 14.5 %fusion.295 = f32[1024,2048]{1,0:T(8,128)} fusion(bf16[1024,2048]{1,0:T(8,128)(2,1)} %constant_dynamic-update-slice_fusion.18, bf16[2048,2048]{1,0:T(8,128)(2,1)} %all-gather.15.cloned.1.call-done), kind=kOutput, calls=%fused_computation.491 | convolution fusion | flops 8589934592 | bytes 20971520 | tf_op jit(solution)/shard_map/tc,cd->td/dot_general | solution.py:497
  603.0 11.5 multiply_convert_fusion
  641.2 6.5 attend_backward.2
  650.5 5.5 convert_add_fusion.3
  675.3 9.1 fusion.10
  686.4 11.1 collective-permute-done.43
  702.0 6.8 attend_backward.3
  719.8 53.1 %ssd_backward.2 = (bf16[1024,1408]{1,0:T(8,128)(2,1)S(1)}, f32[8,1280]{1,0:T(8,128)S(1)}, f32[8,128]{1,0:T(8,128)S(1)}, f32[8,768]{1,0:T(8,128)S(1)}) custom-call(bf16[1024,1408]{1,0:T(8,128)(2,1)} %copy-done.37, bf16[1024,1408]{1,0:T(8,128)(2,1)} %copy-done.37, f32[1024,16]{1,0:T(8,128)S(1)} %copy-done.13, f32[8,1,128]{2,1,0:T(1,128)S(1)} %copy-done.21, ...), custom_call_target="tpu_custom_call" | custom-call | flops 120000004096 | bytes 16000000 | tf_op jit(solution)/shard_map/ssd_backward/pallas_call | solution.py:355
  772.9 9.8 fusion.282
  788.8 9.5 fusion.14
  798.3 6.5 fusion.276
  804.8 5.7 add_convert_fusion.4
  812.0 52.3 %ssd_backward.3 = (bf16[1024,1408]{1,0:T(8,128)(2,1)S(1)}, f32[8,1280]{1,0:T(8,128)S(1)}, f32[8,128]{1,0:T(8,128)S(1)}, f32[8,768]{1,0:T(8,128)S(1)}) custom-call(bf16[1024,1408]{1,0:T(8,128)(2,1)} %copy-done.36, bf16[1024,1408]{1,0:T(8,128)(2,1)} %copy-done.36, f32[1024,16]{1,0:T(8,128)S(1)} %copy.540.aux_ref, f32[8,1,128]{2,1,0:T(1,128)S(1)} %copy-done.19, ...), custom_call_target="tpu_custom_call" | custom-call | flops 120000004096 | bytes 16000000 | tf_op jit(solution)/shard_map/ssd_backward/pallas_call | solution.py:355
  865.9 13.4 %add_convert_fusion.1 = bf16[2048,1408]{1,0:T(8,128)(2,1)} fusion(f32[2048,1408]{1,0:T(8,128)} %fusion.282, bf16[1024,1408]{1,0:T(8,128)(2,1)S(1)} %get-tuple-element.40, bf16[1024,2048]{1,0:T(8,128)(2,1)} %constant_dynamic-update-slice_fusion.22, f32[1024]{0:T(1024)S(1)} %copy-done.135, f32[2048]{0:T(1024)S(1)} %copy-done.120), kind=kOutput, calls=%fused_computation.1 | convolution fusion | flops 5919735808 | bytes 24391680 | tf_op jit(solution)/shard_map/tc,td->cd/dot_general | solution.py:505
  880.8 5.5 fusion.296
  886.3 7.4 add_convert_fusion.3
  905.1 6.4 fusion.298
  911.5 8.4 add_convert_fusion.2
  928.0 20.7 %collective-permute-done.9 = bf16[256,2048]{1,0:T(8,128)(2,1)} collective-permute-done((bf16[256,2048]{1,0:T(8,128)(2,1)}, bf16[256,2048]{1,0:T(8,128)(2,1)}, u32[]{:S(2)}, u32[]{:S(2)}) %collective-permute-start.9) | collective-permute-done | bytes 1048608 | tf_op jit(solution)/shard_map/ppermute | solution.py:529
  948.7 6.2 fusion.46
  967.8 12.3 %fusion.6 = f32[2048,2048]{1,0:T(8,128)} fusion(bf16[1024,2048]{1,0:T(8,128)(2,1)S(1)} %copy-done.102, bf16[1024,1024]{1,0:T(8,128)(2,1)S(1)} %copy-done.145, bf16[1024,1024]{1,0:T(8,128)(2,1)S(1)} %copy-done.148), kind=kOutput, calls=%fused_computation.33 | convolution fusion | flops 8598323200 | bytes 25165824 | tf_op jit(solution)/shard_map/tc,td->cd/dot_general | solution.py:505
  980.1 16.1 %add_convert_fusion = bf16[2048,2048]{1,0:T(8,128)(2,1)} fusion(f32[2048,2048]{1,0:T(8,128)} %fusion.6, bf16[1024,2048]{1,0:T(8,128)(2,1)S(1)} %copy-done.100, bf16[1024,1024]{1,0:T(8,128)(2,1)} %copy-done.142, bf16[1024,1024]{1,0:T(8,128)(2,1)} %copy-done.143), kind=kOutput, calls=%fused_computation | convolution fusion | flops 8606711808 | bytes 33554432 | tf_op jit(solution)/shard_map/tc,td->cd/dot_general | solution.py:505
  1027.4 24.3 %collective-permute-done.34 = bf16[256,2048]{1,0:T(8,128)(2,1)} collective-permute-done((bf16[256,2048]{1,0:T(8,128)(2,1)}, bf16[256,2048]{1,0:T(8,128)(2,1)}, u32[]{:S(2)}, u32[]{:S(2)}) %collective-permute-start.34) | collective-permute-done | bytes 1048608 | tf_op jit(solution)/shard_map/ppermute | solution.py:529
  1106.8 21.0 %collective-permute-done.46 = bf16[256,2048]{1,0:T(8,128)(2,1)} collective-permute-done((bf16[256,2048]{1,0:T(8,128)(2,1)}, bf16[256,2048]{1,0:T(8,128)(2,1)}, u32[]{:S(2)}, u32[]{:S(2)}) %collective-permute-start.46) | collective-permute-done | bytes 1048608 | tf_op jit(solution)/shard_map/ppermute | solution.py:529
  1183.0 5.8 all-to-all-done.3
  1205.3 8.1 all-to-all-done.6
  (786 shorter events, 510.2 us)
Async XLA Ops:
  7.2 241.6 %all-gather.7.cloned.1.call-start = ((), (), s32[]{:S(2)}) async-start(), calls=%async_computation.14 | async-start | bytes 6488064 | tf_op jit(solution)/shard_map/all_gather | solution.py:548
  30.2 223.4 %all-gather.9.cloned.1.call-start = ((), (), s32[]{:S(2)}) async-start(), calls=%async_computation.15 | async-start | bytes 5898240 | tf_op jit(solution)/shard_map/all_gather | solution.py:548
  43.8 253.7 %all-gather.13.cloned.1.call-start = ((), (), s32[]{:S(2)}) async-start(), calls=%async_computation.17 | async-start | bytes 1179648 | tf_op jit(solution)/shard_map/all_gather | solution.py:661
  44.5 256.0 %all-gather.11.cloned.1.call-start = ((), (), s32[]{:S(2)}) async-start(), calls=%async_computation.16 | async-start | bytes 3538944 | tf_op jit(solution)/shard_map/all_gather | solution.py:660
  45.1 409.2 %all-gather.15.cloned.1.call-start = ((), (), s32[]{:S(2)}) async-start(), calls=%async_computation.18 | async-start | bytes 9437184 | tf_op jit(solution)/shard_map/all_gather | solution.py:548
  62.1 407.1 %all-gather.17.cloned.1.call-start = ((), (), s32[]{:S(2)}) async-start(), calls=%async_computation.19 | async-start | bytes 4718592 | tf_op jit(solution)/shard_map/all_gather | solution.py:663
  66.0 31.2 %collective-permute-start.12 = (bf16[256,2048]{0,1:T(8,128)(2,1)}, bf16[256,2048]{0,1:T(8,128)(2,1)}, u32[]{:S(2)}, u32[]{:S(2)}) collective-permute-start(bf16[256,2048]{0,1:T(8,128)(2,1)} %bitcast.46), channel_id=1, source_target_pairs={{0,8},{8,0},{16,24},{24,16},{1,9},{9,1},{17,25},{25,17},{2,10},{10... | collective-permute-start | bytes 3145736 | tf_op jit(solution)/shard_map/ppermute | solution.py:518
  66.9 48.9 %collective-permute-start.13 = (bf16[256,2048]{0,1:T(8,128)(2,1)}, bf16[256,2048]{0,1:T(8,128)(2,1)}, u32[]{:S(2)}, u32[]{:S(2)}) collective-permute-start(bf16[256,2048]{0,1:T(8,128)(2,1)} %bitcast.46), channel_id=1, source_target_pairs={{0,16},{8,24},{16,0},{24,8},{1,17},{9,25},{17,1},{25,9},{2,18},{10... | collective-permute-start | bytes 3145736 | tf_op jit(solution)/shard_map/ppermute | solution.py:518
  67.4 50.9 %collective-permute-start.14 = (bf16[256,2048]{0,1:T(8,128)(2,1)}, bf16[256,2048]{0,1:T(8,128)(2,1)}, u32[]{:S(2)}, u32[]{:S(2)}) collective-permute-start(bf16[256,2048]{0,1:T(8,128)(2,1)} %bitcast.46), channel_id=1, source_target_pairs={{0,24},{8,16},{16,8},{24,0},{1,25},{9,17},{17,9},{25,1},{2,26},{10... | collective-permute-start | bytes 3145736 | tf_op jit(solution)/shard_map/ppermute | solution.py:518
  71.2 66.2 %collective-permute-start = (bf16[256,2048]{0,1:T(8,128)(2,1)}, bf16[256,2048]{0,1:T(8,128)(2,1)}, u32[]{:S(2)}, u32[]{:S(2)}) collective-permute-start(bf16[256,2048]{0,1:T(8,128)(2,1)} %bitcast.3), channel_id=1, source_target_pairs={{0,8},{8,0},{16,24},{24,16},{1,9},{9,1},{17,25},{25,17},{2,10},{10... | collective-permute-start | bytes 3145736 | tf_op jit(solution)/shard_map/ppermute | solution.py:518
  72.1 88.6 %collective-permute-start.1 = (bf16[256,2048]{0,1:T(8,128)(2,1)}, bf16[256,2048]{0,1:T(8,128)(2,1)}, u32[]{:S(2)}, u32[]{:S(2)}) collective-permute-start(bf16[256,2048]{0,1:T(8,128)(2,1)} %bitcast.3), channel_id=1, source_target_pairs={{0,16},{8,24},{16,0},{24,8},{1,17},{9,25},{17,1},{25,9},{2,18},{10... | collective-permute-start | bytes 3145736 | tf_op jit(solution)/shard_map/ppermute | solution.py:518
  72.7 1097.9 %reduce-scatter.12.cloned.1.call-start = ((), (), s32[]{:S(2)}) async-start(), calls=%async_computation.22 | async-start | bytes 2359296 | tf_op jit(solution)/shard_map/reduce_scatter | solution.py:554
  97.1 72.7 %collective-permute-start.2 = (bf16[256,2048]{0,1:T(8,128)(2,1)}, bf16[256,2048]{0,1:T(8,128)(2,1)}, u32[]{:S(2)}, u32[]{:S(2)}) collective-permute-start(bf16[256,2048]{0,1:T(8,128)(2,1)} %bitcast.3), channel_id=1, source_target_pairs={{0,24},{8,16},{16,8},{24,0},{1,25},{9,17},{17,9},{25,1},{2,26},{10... | collective-permute-start | bytes 3145736 | tf_op jit(solution)/shard_map/ppermute | solution.py:518
  115.8 66.6 %collective-permute-start.24 = (bf16[256,2048]{1,0:T(8,128)(2,1)}, bf16[256,2048]{1,0:T(8,128)(2,1)}, u32[]{:S(2)}, u32[]{:S(2)}) collective-permute-start(bf16[256,2048]{1,0:T(8,128)(2,1)} %get-tuple-element.188), channel_id=1, source_target_pairs={{0,8},{8,0},{16,24},{24,16},{1,9},{9,1},{17,25},{25,17},{2,10},{10... | collective-permute-start | bytes 3145736 | tf_op jit(solution)/shard_map/ppermute | solution.py:518
  118.4 87.3 %collective-permute-start.25 = (bf16[256,2048]{1,0:T(8,128)(2,1)}, bf16[256,2048]{1,0:T(8,128)(2,1)}, u32[]{:S(2)}, u32[]{:S(2)}) collective-permute-start(bf16[256,2048]{1,0:T(8,128)(2,1)} %get-tuple-element.188), channel_id=1, source_target_pairs={{0,16},{8,24},{16,0},{24,8},{1,17},{9,25},{17,1},{25,9},{2,18},{10... | collective-permute-start | bytes 3145736 | tf_op jit(solution)/shard_map/ppermute | solution.py:518
  137.4 70.6 %collective-permute-start.26 = (bf16[256,2048]{1,0:T(8,128)(2,1)}, bf16[256,2048]{1,0:T(8,128)(2,1)}, u32[]{:S(2)}, u32[]{:S(2)}) collective-permute-start(bf16[256,2048]{1,0:T(8,128)(2,1)} %get-tuple-element.188), channel_id=1, source_target_pairs={{0,24},{8,16},{16,8},{24,0},{1,25},{9,17},{17,9},{25,1},{2,26},{10... | collective-permute-start | bytes 3145736 | tf_op jit(solution)/shard_map/ppermute | solution.py:518
  160.7 66.6 %collective-permute-start.36 = (bf16[256,2048]{1,0:T(8,128)(2,1)}, bf16[256,2048]{1,0:T(8,128)(2,1)}, u32[]{:S(2)}, u32[]{:S(2)}) collective-permute-start(bf16[256,2048]{1,0:T(8,128)(2,1)} %get-tuple-element.189), channel_id=1, source_target_pairs={{0,8},{8,0},{16,24},{24,16},{1,9},{9,1},{17,25},{25,17},{2,10},{10... | collective-permute-start | bytes 3145736 | tf_op jit(solution)/shard_map/ppermute | solution.py:518
  169.8 75.5 %collective-permute-start.37 = (bf16[256,2048]{1,0:T(8,128)(2,1)}, bf16[256,2048]{1,0:T(8,128)(2,1)}, u32[]{:S(2)}, u32[]{:S(2)}) collective-permute-start(bf16[256,2048]{1,0:T(8,128)(2,1)} %get-tuple-element.189), channel_id=1, source_target_pairs={{0,16},{8,24},{16,0},{24,8},{1,17},{9,25},{17,1},{25,9},{2,18},{10... | collective-permute-start | bytes 3145736 | tf_op jit(solution)/shard_map/ppermute | solution.py:518
  182.4 65.3 %collective-permute-start.38 = (bf16[256,2048]{1,0:T(8,128)(2,1)}, bf16[256,2048]{1,0:T(8,128)(2,1)S(1)}, u32[]{:S(2)}, u32[]{:S(2)}) collective-permute-start(bf16[256,2048]{1,0:T(8,128)(2,1)} %get-tuple-element.189), channel_id=1, source_target_pairs={{0,24},{8,16},{16,8},{24,0},{1,25},{9,17},{17,9},{25,1},{2,26},{10... | collective-permute-start | bytes 3145736 | tf_op jit(solution)/shard_map/ppermute | solution.py:518
  305.3 57.7 %collective-permute-start.5 = (bf16[256,2048]{1,0:T(8,128)(2,1)}, bf16[256,2048]{1,0:T(8,128)(2,1)}, u32[]{:S(2)}, u32[]{:S(2)}) collective-permute-start(bf16[256,2048]{1,0:T(8,128)(2,1)} %fusion.17), channel_id=1, source_target_pairs={{0,8},{8,0},{16,24},{24,16},{1,9},{9,1},{17,25},{25,17},{2,10},{10... | collective-permute-start | bytes 3145736 | tf_op jit(solution)/shard_map/ppermute | solution.py:529
  309.2 53.8 %collective-permute-start.4 = (bf16[256,2048]{1,0:T(8,128)(2,1)}, bf16[256,2048]{1,0:T(8,128)(2,1)}, u32[]{:S(2)}, u32[]{:S(2)}) collective-permute-start(bf16[256,2048]{1,0:T(8,128)(2,1)} %fusion.16), channel_id=1, source_target_pairs={{0,16},{8,24},{16,0},{24,8},{1,17},{9,25},{17,1},{25,9},{2,18},{10... | collective-permute-start | bytes 3145736 | tf_op jit(solution)/shard_map/ppermute | solution.py:529
  312.3 50.7 %collective-permute-start.3 = (bf16[256,2048]{1,0:T(8,128)(2,1)}, bf16[256,2048]{1,0:T(8,128)(2,1)}, u32[]{:S(2)}, u32[]{:S(2)}) collective-permute-start(bf16[256,2048]{1,0:T(8,128)(2,1)} %fusion.15), channel_id=1, source_target_pairs={{0,24},{8,16},{16,8},{24,0},{1,25},{9,17},{17,9},{25,1},{2,26},{10... | collective-permute-start | bytes 3145736 | tf_op jit(solution)/shard_map/ppermute | solution.py:529
  359.4 131.6 %collective-permute-start.17 = (bf16[256,2048]{1,0:T(8,128)(2,1)}, bf16[256,2048]{1,0:T(8,128)(2,1)}, u32[]{:S(2)}, u32[]{:S(2)}) collective-permute-start(bf16[256,2048]{1,0:T(8,128)(2,1)} %fusion.20), channel_id=1, source_target_pairs={{0,8},{8,0},{16,24},{24,16},{1,9},{9,1},{17,25},{25,17},{2,10},{10... | collective-permute-start | bytes 3145736 | tf_op jit(solution)/shard_map/ppermute | solution.py:529
  373.1 35.1 %collective-permute-start.6 = (bf16[256,2048]{0,1:T(8,128)(2,1)}, bf16[256,2048]{0,1:T(8,128)(2,1)}, u32[]{:S(2)}, u32[]{:S(2)}) collective-permute-start(bf16[256,2048]{0,1:T(8,128)(2,1)} %bitcast.38), channel_id=1, source_target_pairs={{0,8},{8,0},{16,24},{24,16},{1,9},{9,1},{17,25},{25,17},{2,10},{10... | collective-permute-start | bytes 3145736 | tf_op jit(solution)/shard_map/ppermute | solution.py:518
  374.0 71.4 %collective-permute-start.7 = (bf16[256,2048]{0,1:T(8,128)(2,1)}, bf16[256,2048]{0,1:T(8,128)(2,1)}, u32[]{:S(2)}, u32[]{:S(2)}) collective-permute-start(bf16[256,2048]{0,1:T(8,128)(2,1)} %bitcast.38), channel_id=1, source_target_pairs={{0,16},{8,24},{16,0},{24,8},{1,17},{9,25},{17,1},{25,9},{2,18},{10... | collective-permute-start | bytes 3145736 | tf_op jit(solution)/shard_map/ppermute | solution.py:518
  375.1 72.4 %collective-permute-start.8 = (bf16[256,2048]{0,1:T(8,128)(2,1)}, bf16[256,2048]{0,1:T(8,128)(2,1)}, u32[]{:S(2)}, u32[]{:S(2)}) collective-permute-start(bf16[256,2048]{0,1:T(8,128)(2,1)} %bitcast.38), channel_id=1, source_target_pairs={{0,24},{8,16},{16,8},{24,0},{1,25},{9,17},{17,9},{25,1},{2,26},{10... | collective-permute-start | bytes 3145736 | tf_op jit(solution)/shard_map/ppermute | solution.py:518
  381.2 112.6 %collective-permute-start.16 = (bf16[256,2048]{1,0:T(8,128)(2,1)}, bf16[256,2048]{1,0:T(8,128)(2,1)}, u32[]{:S(2)}, u32[]{:S(2)}) collective-permute-start(bf16[256,2048]{1,0:T(8,128)(2,1)} %fusion.19), channel_id=1, source_target_pairs={{0,16},{8,24},{16,0},{24,8},{1,17},{9,25},{17,1},{25,9},{2,18},{10... | collective-permute-start | bytes 3145736 | tf_op jit(solution)/shard_map/ppermute | solution.py:529
  408.2 85.6 %collective-permute-start.15 = (bf16[256,2048]{1,0:T(8,128)(2,1)}, bf16[256,2048]{1,0:T(8,128)(2,1)}, u32[]{:S(2)}, u32[]{:S(2)}) collective-permute-start(bf16[256,2048]{1,0:T(8,128)(2,1)} %fusion.18), channel_id=1, source_target_pairs={{0,24},{8,16},{16,8},{24,0},{1,25},{9,17},{17,9},{25,1},{2,26},{10... | collective-permute-start | bytes 3145736 | tf_op jit(solution)/shard_map/ppermute | solution.py:529
  539.1 43.3 %collective-permute-start.19 = (bf16[256,2048]{0,1:T(8,128)(2,1)}, bf16[256,2048]{0,1:T(8,128)(2,1)}, u32[]{:S(2)}, u32[]{:S(2)}) collective-permute-start(bf16[256,2048]{0,1:T(8,128)(2,1)} %bitcast.64), channel_id=1, source_target_pairs={{0,16},{8,24},{16,0},{24,8},{1,17},{9,25},{17,1},{25,9},{2,18},{10... | collective-permute-start | bytes 3145736 | tf_op jit(solution)/shard_map/ppermute | solution.py:518
  541.1 44.8 %collective-permute-start.20 = (bf16[256,2048]{0,1:T(8,128)(2,1)}, bf16[256,2048]{0,1:T(8,128)(2,1)}, u32[]{:S(2)}, u32[]{:S(2)}) collective-permute-start(bf16[256,2048]{0,1:T(8,128)(2,1)} %bitcast.64), channel_id=1, source_target_pairs={{0,24},{8,16},{16,8},{24,0},{1,25},{9,17},{17,9},{25,1},{2,26},{10... | collective-permute-start | bytes 3145736 | tf_op jit(solution)/shard_map/ppermute | solution.py:518
  548.6 80.9 %collective-permute-start.30 = (bf16[256,2048]{1,0:T(8,128)(2,1)}, bf16[256,2048]{1,0:T(8,128)(2,1)}, u32[]{:S(2)}, u32[]{:S(2)}) collective-permute-start(bf16[256,2048]{1,0:T(8,128)(2,1)} %get-tuple-element.173), channel_id=1, source_target_pairs={{0,8},{8,0},{16,24},{24,16},{1,9},{9,1},{17,25},{25,17},{2,10},{10... | collective-permute-start | bytes 3145736 | tf_op jit(solution)/shard_map/ppermute | solution.py:518
  548.7 84.1 %collective-permute-start.31 = (bf16[256,2048]{1,0:T(8,128)(2,1)}, bf16[256,2048]{1,0:T(8,128)(2,1)}, u32[]{:S(2)}, u32[]{:S(2)}) collective-permute-start(bf16[256,2048]{1,0:T(8,128)(2,1)} %get-tuple-element.173), channel_id=1, source_target_pairs={{0,16},{8,24},{16,0},{24,8},{1,17},{9,25},{17,1},{25,9},{2,18},{10... | collective-permute-start | bytes 3145736 | tf_op jit(solution)/shard_map/ppermute | solution.py:518
  565.5 69.6 %collective-permute-start.32 = (bf16[256,2048]{1,0:T(8,128)(2,1)}, bf16[256,2048]{1,0:T(8,128)(2,1)}, u32[]{:S(2)}, u32[]{:S(2)}) collective-permute-start(bf16[256,2048]{1,0:T(8,128)(2,1)} %get-tuple-element.173), channel_id=1, source_target_pairs={{0,24},{8,16},{16,8},{24,0},{1,25},{9,17},{17,9},{25,1},{2,26},{10... | collective-permute-start | bytes 3145736 | tf_op jit(solution)/shard_map/ppermute | solution.py:518
  619.2 28.6 %collective-permute-start.41 = (bf16[256,2048]{1,0:T(8,128)(2,1)}, bf16[256,2048]{1,0:T(8,128)(2,1)S(1)}, u32[]{:S(2)}, u32[]{:S(2)}) collective-permute-start(bf16[256,2048]{1,0:T(8,128)(2,1)} %convolution_convert_fusion.8), channel_id=1, source_target_pairs={{0,8},{8,0},{16,24},{24,16},{1,9},{9,1},{17,25},{25,17},{2,10},{10... | collective-permute-start | bytes 3145736 | tf_op jit(solution)/shard_map/ppermute | solution.py:529
  718.3 456.2 %reduce-scatter.16.cloned.1.call-start = ((), (), s32[]{:S(2)}) async-start(), calls=%async_computation.24 | async-start | bytes 1179648 | tf_op jit(solution)/shard_map/reduce_scatter | solution.py:560
  788.6 390.8 %reduce-scatter.8.cloned.1.call-start = ((), (), s32[]{:S(2)}) async-start(), calls=%async_computation.20 | async-start | bytes 3538944 | tf_op jit(solution)/shard_map/reduce_scatter | solution.py:554
  810.6 378.2 %reduce-scatter.10.cloned.1.call-start = ((), (), s32[]{:S(2)}) async-start(), calls=%async_computation.21 | async-start | bytes 6488064 | tf_op jit(solution)/shard_map/reduce_scatter | solution.py:554
  879.4 313.0 %reduce-scatter.14.cloned.1.call-start = ((), (), s32[]{:S(2)}) async-start(), calls=%async_computation.23 | async-start | bytes 3538944 | tf_op jit(solution)/shard_map/reduce_scatter | solution.py:560
  893.7 300.7 %reduce-scatter.20.cloned.1.call-start = ((), (), s32[]{:S(2)}) async-start(), calls=%async_computation.26 | async-start | bytes 4718592 | tf_op jit(solution)/shard_map/reduce_scatter | solution.py:560
  919.9 280.5 %reduce-scatter.18.cloned.1.call-start = ((), (), s32[]{:S(2)}) async-start(), calls=%async_computation.25 | async-start | bytes 9437184 | tf_op jit(solution)/shard_map/reduce_scatter | solution.py:554
  957.1 107.9 %collective-permute-start.23 = (bf16[256,2048]{1,0:T(8,128)(2,1)}, bf16[256,2048]{1,0:T(8,128)(2,1)}, u32[]{:S(2)}, u32[]{:S(2)}) collective-permute-start(bf16[256,2048]{1,0:T(8,128)(2,1)} %convolution_convert_fusion.2), channel_id=1, source_target_pairs={{0,8},{8,0},{16,24},{24,16},{1,9},{9,1},{17,25},{25,17},{2,10},{10... | collective-permute-start | bytes 3145736 | tf_op jit(solution)/shard_map/ppermute | solution.py:529
  959.4 105.6 %collective-permute-start.22 = (bf16[256,2048]{1,0:T(8,128)(2,1)}, bf16[256,2048]{1,0:T(8,128)(2,1)}, u32[]{:S(2)}, u32[]{:S(2)}) collective-permute-start(bf16[256,2048]{1,0:T(8,128)(2,1)} %convolution_convert_fusion.3), channel_id=1, source_target_pairs={{0,16},{8,24},{16,0},{24,8},{1,17},{9,25},{17,1},{25,9},{2,18},{10... | collective-permute-start | bytes 3145736 | tf_op jit(solution)/shard_map/ppermute | solution.py:529
  966.2 52.5 %collective-permute-start.35 = (bf16[256,2048]{1,0:T(8,128)(2,1)}, bf16[256,2048]{1,0:T(8,128)(2,1)}, u32[]{:S(2)}, u32[]{:S(2)}) collective-permute-start(bf16[256,2048]{1,0:T(8,128)(2,1)} %fusion.23), channel_id=1, source_target_pairs={{0,8},{8,0},{16,24},{24,16},{1,9},{9,1},{17,25},{25,17},{2,10},{10... | collective-permute-start | bytes 3145736 | tf_op jit(solution)/shard_map/ppermute | solution.py:529
  1007.8 44.0 %collective-permute-start.34 = (bf16[256,2048]{1,0:T(8,128)(2,1)}, bf16[256,2048]{1,0:T(8,128)(2,1)}, u32[]{:S(2)}, u32[]{:S(2)}) collective-permute-start(bf16[256,2048]{1,0:T(8,128)(2,1)} %fusion.22), channel_id=1, source_target_pairs={{0,16},{8,24},{16,0},{24,8},{1,17},{9,25},{17,1},{25,9},{2,18},{10... | collective-permute-start | bytes 3145736 | tf_op jit(solution)/shard_map/ppermute | solution.py:529
  1014.2 37.6 %collective-permute-start.33 = (bf16[256,2048]{1,0:T(8,128)(2,1)}, bf16[256,2048]{1,0:T(8,128)(2,1)}, u32[]{:S(2)}, u32[]{:S(2)}) collective-permute-start(bf16[256,2048]{1,0:T(8,128)(2,1)} %fusion.21), channel_id=1, source_target_pairs={{0,24},{8,16},{16,8},{24,0},{1,25},{9,17},{17,9},{25,1},{2,26},{10... | collective-permute-start | bytes 3145736 | tf_op jit(solution)/shard_map/ppermute | solution.py:529
  1018.7 46.4 %collective-permute-start.21 = (bf16[256,2048]{1,0:T(8,128)(2,1)}, bf16[256,2048]{1,0:T(8,128)(2,1)}, u32[]{:S(2)}, u32[]{:S(2)}) collective-permute-start(bf16[256,2048]{1,0:T(8,128)(2,1)} %convolution_convert_fusion.4), channel_id=1, source_target_pairs={{0,24},{8,16},{16,8},{24,0},{1,25},{9,17},{17,9},{25,1},{2,26},{10... | collective-permute-start | bytes 3145736 | tf_op jit(solution)/shard_map/ppermute | solution.py:529
  1086.3 41.6 %collective-permute-start.46 = (bf16[256,2048]{1,0:T(8,128)(2,1)}, bf16[256,2048]{1,0:T(8,128)(2,1)}, u32[]{:S(2)}, u32[]{:S(2)}) collective-permute-start(bf16[256,2048]{1,0:T(8,128)(2,1)} %fusion.25), channel_id=1, source_target_pairs={{0,16},{8,24},{16,0},{24,8},{1,17},{9,25},{17,1},{25,9},{2,18},{10... | collective-permute-start | bytes 3145736 | tf_op jit(solution)/shard_map/ppermute | solution.py:529
  1091.4 36.4 %collective-permute-start.45 = (bf16[256,2048]{1,0:T(8,128)(2,1)}, bf16[256,2048]{1,0:T(8,128)(2,1)}, u32[]{:S(2)}, u32[]{:S(2)}) collective-permute-start(bf16[256,2048]{1,0:T(8,128)(2,1)} %fusion.24), channel_id=1, source_target_pairs={{0,24},{8,16},{16,8},{24,0},{1,25},{9,17},{17,9},{25,1},{2,26},{10... | collective-permute-start | bytes 3145736 | tf_op jit(solution)/shard_map/ppermute | solution.py:529
  (190 other events, 4799.0 us)
Sparse Core Ops, SparseCore 0:
  30.3 59.9 all-gather.6
  92.0 54.6 all-gather.8
  148.4 20.6 all-gather.12
  170.5 38.0 all-gather.10
  210.0 80.9 all-gather.14
  292.4 45.6 all-gather.16
  718.4 36.4 reduce-scatter.11
  788.7 33.0 reduce-scatter.15
  824.1 38.6 reduce-scatter.7
  879.5 65.5 reduce-scatter.9
  947.4 38.6 reduce-scatter.13
  988.3 49.1 reduce-scatter.19
  1039.7 87.7 reduce-scatter.17

commit v3 on v2

v3 whole, which is shorter than its diff:
```python
import functools

import jax
import jax.numpy as jnp
from jax import lax
from jax.experimental import pallas as pl
from jax.experimental.pallas import tpu as pltpu
from jax.sharding import PartitionSpec as P

SSM_HEADS = 48
SSM_DIM = 64
STATE = 256
CONV = 4
Q_HEADS = 8
KV_HEADS = 2
HEAD_DIM = 128
MICRO = 2
SPAN = 128
SSM_INNER = 3072
CONV_CH = 3584
ATT_ROWS = 256
VMEM_BYTES = 48 * 1024 * 1024


PRECISE = lax.Precision.HIGHEST
EPSILON = 1e-05
ROPE_BASE = 10000.0


def lanes_iota(shape):
    return lax.broadcasted_iota(jnp.int32, shape, 1)


def rows_iota(shape):
    return lax.broadcasted_iota(jnp.int32, shape, 0)


def dot_last(left, right):
    return lax.dot_general(left, right, (((1,), (1,)), ((), ())), preferred_element_type=jnp.float32)


def dot_first(left, right):
    return lax.dot_general(left, right, (((0,), (0,)), ((), ())), preferred_element_type=jnp.float32)


def dot_plain(left, right):
    return jnp.dot(left, right, preferred_element_type=jnp.float32)


def head_steps(block, head_ref, heads):
    pre = block.astype(jnp.float32) + head_ref[0:1, :]
    live = lanes_iota(pre.shape) < heads
    pre = jnp.where(live, pre, 0.0)
    step = jnp.maximum(pre, 0.0) + jnp.log1p(jnp.exp(-jnp.abs(pre)))
    step = jnp.where(live, step, 0.0)
    rate = -jnp.exp(head_ref[1:2, :])
    decay = rate * step
    lower = (rows_iota((SPAN, SPAN)) >= lanes_iota((SPAN, SPAN))).astype(jnp.float32)
    total = jnp.dot(lower, decay, precision=PRECISE, preferred_element_type=jnp.float32)
    return step, rate, decay, total, pre


def convolve(ubuf, aux_ref, conv_ref, lanes):
    acc = conv_ref[CONV : CONV + 1, lanes] + conv_ref[CONV - 1 : CONV, lanes] * ubuf[8 : 8 + SPAN, lanes]
    for offset in range(1, CONV):
        shifted = ubuf[8 - offset : 8 - offset + SPAN, lanes]
        weight = conv_ref[CONV - 1 - offset : CONV - offset, lanes]
        acc = acc + weight * shifted * aux_ref[:, 2 + offset : 3 + offset]
    return acc


def pair_of(values, first_head, low_lanes):
    one = jnp.broadcast_to(values[:, first_head : first_head + 1], (SPAN, 128))
    two = jnp.broadcast_to(values[:, first_head + 1 : first_head + 2], (SPAN, 128))
    return one, two, jnp.where(low_lanes, one, two)


def ssd_forward_kernel(
    heads,
    order_ref,
    first_ref,
    aux_ref,
    seg_ref,
    conv_ref,
    head_ref,
    skip_ref,
    y_ref,
    start_ref,
    ubuf,
    taps,
    state,
):
    f32, bf16 = jnp.float32, jnp.bfloat16
    inner = heads * SSM_DIM
    width = inner + 2 * STATE

    @pl.when(pl.program_id(0) == 0)
    def _():
        ubuf[SPAN : SPAN + 8, :] = jnp.zeros((8, width), f32)
        state[...] = jnp.zeros((STATE, inner), f32)

    ubuf[0:8, :] = ubuf[SPAN : SPAN + 8, :]
    ubuf[8 : 8 + SPAN, :] = first_ref[:, :width].astype(f32)
    for lane in range(0, width, 128):
        lanes = slice(lane, lane + 128)
        pre = convolve(ubuf, aux_ref, conv_ref, lanes)
        taps[:, lanes] = (pre * jax.nn.sigmoid(pre)).astype(bf16)
    step, rate, decay, total, unused = head_steps(first_ref[:, width:], head_ref, heads)
    total_rows = total.T
    low_lanes = lanes_iota((SPAN, 128)) < SSM_DIM
    same = (aux_ref[:, 0:1] == seg_ref[0]) & (rows_iota((SPAN, SPAN)) >= lanes_iota((SPAN, SPAN)))
    b_rows = taps[:, inner : inner + STATE]
    c_rows = taps[:, inner + STATE :]
    b_cols = b_rows.astype(f32).T.astype(bf16)
    scores = dot_last(c_rows, b_rows)
    carry_keep = aux_ref[:, 1:2]
    end_keep = aux_ref[:, 2:3]
    for pair in range(heads // 2):
        lanes = slice(pair * 128, pair * 128 + 128)
        sum_one, sum_two, sums = pair_of(total, 2 * pair, low_lanes)
        steps = pair_of(step, 2 * pair, low_lanes)[2]
        row_one = total_rows[2 * pair : 2 * pair + 1, :]
        row_two = total_rows[2 * pair + 1 : 2 * pair + 2, :]
        mix_one = (jnp.exp(jnp.where(same, sum_one - row_one, -1e30)) * scores).astype(bf16)
        mix_two = (jnp.exp(jnp.where(same, sum_two - row_two, -1e30)) * scores).astype(bf16)
        x = taps[:, lanes].astype(f32)
        stepped = (x * steps).astype(bf16)
        none = jnp.zeros_like(stepped)
        split = jnp.concatenate(
            [jnp.where(low_lanes, stepped, none), jnp.where(low_lanes, none, stepped)], axis=0
        )
        held = state[:, lanes]
        held_low = held.astype(bf16)
        start_ref[0, :, lanes] = held_low
        y = dot_plain(jnp.concatenate([mix_one, mix_two], axis=1), split)
        y = y + jnp.exp(sums) * carry_keep * dot_plain(c_rows, held_low)
        y_ref[:, lanes] = (y + skip_ref[0:1, lanes] * x).astype(bf16)
        last = sums[SPAN - 1 : SPAN, :]
        weighted = (jnp.exp(last - sums) * end_keep * stepped.astype(f32)).astype(bf16)
        kept = jnp.exp(last) * aux_ref[SPAN - 1 : SPAN, 1:2]
        state[:, lanes] = held * kept + dot_plain(b_cols, weighted)


def ssd_backward_kernel(
    heads,
    order_ref,
    first_ref,
    before_ref,
    aux_ref,
    seg_ref,
    conv_ref,
    head_ref,
    skip_ref,
    start_ref,
    dy_ref,
    grad_ref,
    conv_grad_ref,
    head_grad_ref,
    skip_grad_ref,
    ubuf,
    taps,
    slope,
    gbuf,
    dstate,
):
    f32, bf16 = jnp.float32, jnp.bfloat16
    inner = heads * SSM_DIM
    width = inner + 2 * STATE

    @pl.when(pl.program_id(0) == 0)
    def _():
        gbuf[0:8, :] = jnp.zeros((8, width), f32)
        dstate[...] = jnp.zeros((STATE, inner), f32)
        conv_grad_ref[...] = jnp.zeros(conv_grad_ref.shape, f32)
        head_grad_ref[...] = jnp.zeros(head_grad_ref.shape, f32)
        skip_grad_ref[...] = jnp.zeros(skip_grad_ref.shape, f32)

    ubuf[0:8, :] = before_ref[8:16, :width].astype(f32)
    ubuf[8 : 8 + SPAN, :] = first_ref[:, :width].astype(f32)
    gbuf[SPAN : SPAN + 8, :] = gbuf[0:8, :]
    for lane in range(0, width, 128):
        lanes = slice(lane, lane + 128)
        pre = convolve(ubuf, aux_ref, conv_ref, lanes)
        sig = jax.nn.sigmoid(pre)
        taps[:, lanes] = (pre * sig).astype(bf16)
        slope[:, lanes] = sig * (1.0 + pre * (1.0 - sig))
    step, rate, decay, total, pre_step = head_steps(first_ref[:, width:], head_ref, heads)
    total_rows = total.T
    square = (SPAN, SPAN)
    low_lanes = lanes_iota((SPAN, 128)) < SSM_DIM
    low_row = lanes_iota((1, 128)) < SSM_DIM
    same = (aux_ref[:, 0:1] == seg_ref[0]) & (rows_iota(square) >= lanes_iota(square))
    b_rows = taps[:, inner : inner + STATE]
    c_rows = taps[:, inner + STATE :]
    c_cols = c_rows.astype(f32).T.astype(bf16)
    scores = dot_last(c_rows, b_rows)
    carry_keep = aux_ref[:, 1:2]
    end_keep = aux_ref[:, 2:3]
    head_lane = lanes_iota((SPAN, 128))
    is_last = rows_iota((SPAN, 1)) == SPAN - 1
    grad_scores = jnp.zeros(square, f32)
    grad_b = jnp.zeros((SPAN, STATE), f32)
    grad_c = jnp.zeros((SPAN, STATE), f32)
    grad_total = jnp.zeros((SPAN, 128), f32)
    grad_step = jnp.zeros((SPAN, 128), f32)
    for pair in range(heads // 2):
        lanes = slice(pair * 128, pair * 128 + 128)
        sum_one, sum_two, sums = pair_of(total, 2 * pair, low_lanes)
        steps = pair_of(step, 2 * pair, low_lanes)[2]
        row_one = total_rows[2 * pair : 2 * pair + 1, :]
        row_two = total_rows[2 * pair + 1 : 2 * pair + 2, :]
        decay_one = jnp.exp(jnp.where(same, sum_one - row_one, -1e30))
        decay_two = jnp.exp(jnp.where(same, sum_two - row_two, -1e30))
        mix_one = (decay_one * scores).astype(bf16)
        mix_two = (decay_two * scores).astype(bf16)
        x = taps[:, lanes].astype(f32)
        stepped = (x * steps).astype(bf16)
        none = jnp.zeros_like(stepped)
        x_one = jnp.where(low_lanes, stepped, none)
        x_two = jnp.where(low_lanes, none, stepped)
        dy_low = dy_ref[:, lanes]
        dy = dy_low.astype(f32)
        dy_one = jnp.where(low_lanes, dy_low, none)
        dy_two = jnp.where(low_lanes, none, dy_low)
        grad_scores = grad_scores + dot_last(dy_one, stepped) * decay_one + dot_last(dy_two, stepped) * decay_two
        y = dot_plain(
            jnp.concatenate([mix_one, mix_two], axis=1), jnp.concatenate([x_one, x_two], axis=0)
        )
        grad_in = dot_first(
            jnp.concatenate([mix_one, mix_two], axis=0), jnp.concatenate([dy_one, dy_two], axis=0)
        )
        held = start_ref[0, :, lanes]
        dheld = dstate[:, lanes]
        dheld_low = dheld.astype(bf16)
        grown = jnp.exp(sums) * carry_keep
        y = y + grown * dot_plain(c_rows, held)
        grown_dy = (grown * dy).astype(bf16)
        last = sums[SPAN - 1 : SPAN, :]
        fade = jnp.exp(last - sums) * end_keep
        stepped_wide = stepped.astype(f32)
        weighted = (fade * stepped_wide).astype(bf16)
        from_end = dot_plain(b_rows, dheld_low)
        grad_in = grad_in + fade * from_end
        grad_c = grad_c + dot_last(grown_dy, held)
        grad_b = grad_b + dot_last(weighted, dheld_low)
        kept = jnp.exp(last) * aux_ref[SPAN - 1 : SPAN, 1:2]
        ends = jnp.sum(fade * stepped_wide * from_end, axis=0, keepdims=True) + kept * jnp.sum(
            dheld * held.astype(f32), axis=0, keepdims=True
        )
        dstate[:, lanes] = dheld * kept + dot_plain(c_cols, grown_dy)
        gaps = dy * y - stepped_wide * grad_in
        by_step = x * grad_in
        for half in range(2):
            keep = low_lanes if half == 0 else ~low_lanes
            keep_row = low_row if half == 0 else ~low_row
            end_sum = jnp.sum(jnp.where(keep_row, ends, 0.0), axis=1, keepdims=True)
            gap_sum = jnp.sum(jnp.where(keep, gaps, 0.0), axis=1, keepdims=True)
            gap_sum = gap_sum + jnp.where(is_last, end_sum, 0.0)
            step_sum = jnp.sum(jnp.where(keep, by_step, 0.0), axis=1, keepdims=True)
            here = head_lane == 2 * pair + half
            grad_total = jnp.where(here, gap_sum, grad_total)
            grad_step = jnp.where(here, step_sum, grad_step)
        skip = skip_ref[0:1, lanes]
        skip_grad_ref[0:1, lanes] += jnp.sum(dy * x, axis=0, keepdims=True)
        gbuf[0:SPAN, lanes] = (steps * grad_in + skip * dy) * slope[:, lanes]
    low_scores = grad_scores.astype(bf16)
    grad_c = grad_c + dot_plain(low_scores, b_rows)
    grad_b = grad_b + dot_first(low_scores, c_rows)
    gbuf[0:SPAN, inner : inner + STATE] = grad_b * slope[:, inner : inner + STATE]
    gbuf[0:SPAN, inner + STATE : width] = grad_c * slope[:, inner + STATE : width]

    upper = (rows_iota(square) <= lanes_iota(square)).astype(f32)
    grad_decay = jnp.dot(upper, grad_total, precision=PRECISE, preferred_element_type=f32)
    grad_pre = (grad_step + rate * grad_decay) * jax.nn.sigmoid(pre_step)
    grad_pre = jnp.where(head_lane < heads, grad_pre, 0.0)
    grad_ref[:, width:] = grad_pre.astype(bf16)
    head_grad_ref[0:1, :] += jnp.sum(grad_decay * decay, axis=0, keepdims=True)
    head_grad_ref[1:2, :] += jnp.sum(grad_pre, axis=0, keepdims=True)

    for lane in range(0, width, 128):
        lanes = slice(lane, lane + 128)
        grad = gbuf[0:SPAN, lanes]
        conv_grad_ref[CONV : CONV + 1, lanes] += jnp.sum(grad, axis=0, keepdims=True)
        conv_grad_ref[CONV - 1 : CONV, lanes] += jnp.sum(grad * ubuf[8 : 8 + SPAN, lanes], axis=0, keepdims=True)
        acc = conv_ref[CONV - 1 : CONV, lanes] * grad
        for offset in range(1, CONV):
            at = CONV - 1 - offset
            shifted = ubuf[8 - offset : 8 - offset + SPAN, lanes] * aux_ref[:, 2 + offset : 3 + offset]
            conv_grad_ref[at : at + 1, lanes] += jnp.sum(grad * shifted, axis=0, keepdims=True)
            later = gbuf[offset : offset + SPAN, lanes] * aux_ref[:, 5 + offset : 6 + offset]
            acc = acc + conv_ref[at : at + 1, lanes] * later
        grad_ref[:, lanes] = acc.astype(bf16)


def token_aux(segment):
    length = segment.shape[0]
    ends = segment.reshape(-1, SPAN)[:, -1]
    end_of = jnp.repeat(ends, SPAN)
    before = jnp.repeat(jnp.concatenate([jnp.full((1,), -1, segment.dtype), ends[:-1]]), SPAN)
    columns = [segment, segment == before, segment == end_of]
    for offset in range(1, CONV):
        columns.append(jnp.pad(segment, (offset, 0), constant_values=-1)[:length] == segment)
    for offset in range(1, CONV):
        columns.append(jnp.pad(segment, (0, offset), constant_values=-1)[offset:] == segment)
    columns = [column.astype(jnp.float32) for column in columns]
    return jnp.stack(columns + [jnp.zeros((length,), jnp.float32)] * (16 - len(columns)), axis=1)


def ssd_specs(heads, at):
    inner = heads * SSM_DIM
    width = inner + 2 * STATE
    return [
        pl.BlockSpec((SPAN, width + 128), lambda i, order: (order[at(i)], 0)),
        pl.BlockSpec((SPAN, 16), lambda i, order: (at(i), 0)),
        pl.BlockSpec((1, 1, SPAN), lambda i, order: (at(i), 0, 0)),
        pl.BlockSpec((8, width), lambda i, order: (0, 0)),
        pl.BlockSpec((8, 128), lambda i, order: (0, 0)),
        pl.BlockSpec((8, inner), lambda i, order: (0, 0)),
    ]


def ssd_forward(order, first, aux, seg_rows, conv, head, skip, heads):
    length = first.shape[0]
    inner = heads * SSM_DIM
    width = inner + 2 * STATE
    blocks = length // SPAN
    return pl.pallas_call(
        functools.partial(ssd_forward_kernel, heads),
        grid_spec=pltpu.PrefetchScalarGridSpec(
            num_scalar_prefetch=1,
            grid=(blocks,),
            in_specs=ssd_specs(heads, lambda i: i),
            out_specs=[
                pl.BlockSpec((SPAN, inner), lambda i, order: (order[i], 0)),
                pl.BlockSpec((1, STATE, inner), lambda i, order: (i, 0, 0)),
            ],
            scratch_shapes=[
                pltpu.VMEM((SPAN + 8, width), jnp.float32),
                pltpu.VMEM((SPAN, width), jnp.bfloat16),
                pltpu.VMEM((STATE, inner), jnp.float32),
            ],
        ),
        out_shape=[
            jax.ShapeDtypeStruct((length, inner), jnp.bfloat16),
            jax.ShapeDtypeStruct((blocks, STATE, inner), jnp.bfloat16),
        ],
        compiler_params=pltpu.CompilerParams(
            dimension_semantics=("arbitrary",), vmem_limit_bytes=VMEM_BYTES
        ),
        cost_estimate=pl.CostEstimate(
            flops=8_000_000_000 * heads // 12, bytes_accessed=12_000_000, transcendentals=4_000_000
        ),
        name="ssd_forward",
    )(order, first, aux, seg_rows, conv, head, skip)


def ssd_backward(order, first, aux, seg_rows, conv, head, skip, starts, dy, heads):
    length = first.shape[0]
    inner = heads * SSM_DIM
    width = inner + 2 * STATE
    blocks = length // SPAN
    per_block = SPAN // 16

    def at(i):
        return blocks - 1 - i

    specs = ssd_specs(heads, at)
    specs.insert(
        1,
        pl.BlockSpec(
            (16, width + 128), lambda i, order: (order[jnp.maximum(at(i) - 1, 0)] * per_block + per_block - 1, 0)
        ),
    )
    specs += [
        pl.BlockSpec((1, STATE, inner), lambda i, order: (at(i), 0, 0)),
        pl.BlockSpec((SPAN, inner), lambda i, order: (order[at(i)], 0)),
    ]
    return pl.pallas_call(
        functools.partial(ssd_backward_kernel, heads),
        grid_spec=pltpu.PrefetchScalarGridSpec(
            num_scalar_prefetch=1,
            grid=(blocks,),
            in_specs=specs,
            out_specs=[
                pl.BlockSpec((SPAN, width + 128), lambda i, order: (order[at(i)], 0)),
                pl.BlockSpec((8, width), lambda i, order: (0, 0)),
                pl.BlockSpec((8, 128), lambda i, order: (0, 0)),
                pl.BlockSpec((8, inner), lambda i, order: (0, 0)),
            ],
            scratch_shapes=[
                pltpu.VMEM((SPAN + 8, width), jnp.float32),
                pltpu.VMEM((SPAN, width), jnp.bfloat16),
                pltpu.VMEM((SPAN, width), jnp.float32),
                pltpu.VMEM((SPAN + 8, width), jnp.float32),
                pltpu.VMEM((STATE, inner), jnp.float32),
            ],
        ),
        out_shape=[
            jax.ShapeDtypeStruct((length, width + 128), jnp.bfloat16),
            jax.ShapeDtypeStruct((8, width), jnp.float32),
            jax.ShapeDtypeStruct((8, 128), jnp.float32),
            jax.ShapeDtypeStruct((8, inner), jnp.float32),
        ],
        compiler_params=pltpu.CompilerParams(
            dimension_semantics=("arbitrary",), vmem_limit_bytes=VMEM_BYTES
        ),
        cost_estimate=pl.CostEstimate(
            flops=30_000_000_000 * heads // 12, bytes_accessed=16_000_000, transcendentals=5_000_000
        ),
        name="ssd_backward",
    )(order, first, first, aux, seg_rows, conv, head, skip, starts, dy)


def rotary_tables(length):
    half = HEAD_DIM // 2
    frequency = ROPE_BASE ** (-jnp.arange(half).astype(jnp.float32) / half)
    angles = jnp.arange(length, dtype=jnp.int32).astype(jnp.float32)[:, None] * frequency[None, :]
    cosine, sine = jnp.cos(angles), jnp.sin(angles)
    return jnp.concatenate([cosine, cosine], axis=1), jnp.concatenate([-sine, sine], axis=1)


def turn(rows, cosine, sine):
    wide = rows.astype(jnp.float32)
    return (wide * cosine + pltpu.roll(wide, HEAD_DIM // 2, 1) * sine).astype(jnp.bfloat16)


def turn_back(grads, cosine, sine):
    return (grads * cosine + pltpu.roll(grads * sine, HEAD_DIM // 2, 1)).astype(jnp.bfloat16)


def block_scores(q_block, k_part, first_row, seg_col, seg_row):
    scores = dot_last(q_block, k_part) * HEAD_DIM ** (-0.5)
    shape = scores.shape
    allowed = (rows_iota(shape) + first_row >= lanes_iota(shape)) & (seg_col == seg_row)
    return jnp.where(allowed, scores, -1e30)


def place_of(order_ref, block):
    return pl.ds(pl.multiple_of(order_ref[block] * SPAN, SPAN), SPAN)


def load_keys(order_ref, qkv_ref, q_width, cos_ref, sin_ref, k_rot, value):
    for block in range(qkv_ref.shape[0] // SPAN):
        there, here = place_of(order_ref, block), slice(block * SPAN, (block + 1) * SPAN)
        k_rot[here, :] = turn(qkv_ref[there, q_width : q_width + HEAD_DIM], cos_ref[here, :], sin_ref[here, :])
        value[here, :] = qkv_ref[there, q_width + HEAD_DIM : q_width + 2 * HEAD_DIM]


def load_rows(order_ref, ref, start, count, lanes):
    blocks = range(start // SPAN, (start + count) // SPAN)
    return jnp.concatenate([ref[place_of(order_ref, block), lanes] for block in blocks], axis=0)


def store_rows(order_ref, ref, start, lanes, values):
    for part in range(values.shape[0] // SPAN):
        ref[place_of(order_ref, start // SPAN + part), lanes] = values[part * SPAN : (part + 1) * SPAN, :]


def attend_forward_kernel(
    query_heads, block, order_ref, qkv_ref, cos_ref, sin_ref, aux_ref, seg_ref, out_ref, lse_ref, k_rot, value
):
    length = qkv_ref.shape[0]
    load_keys(order_ref, qkv_ref, query_heads * HEAD_DIM, cos_ref, sin_ref, k_rot, value)
    for start in range(0, length, block):
        rows = slice(start, start + block)
        end = start + block
        for head in range(query_heads):
            lanes = slice(head * HEAD_DIM, (head + 1) * HEAD_DIM)
            q_rows = load_rows(order_ref, qkv_ref, start, block, lanes)
            q_block = turn(q_rows, cos_ref[rows, :], sin_ref[rows, :])
            scores = block_scores(q_block, k_rot[:end, :], start, aux_ref[rows, 0:1], seg_ref[:, :end])
            top = jnp.max(scores, axis=1, keepdims=True)
            raised = jnp.exp(scores - top)
            total = jnp.sum(raised, axis=1, keepdims=True)
            probs = (raised * (1.0 / total)).astype(jnp.bfloat16)
            store_rows(order_ref, out_ref, start, lanes, dot_plain(probs, value[:end, :]).astype(jnp.bfloat16))
            lse_ref[rows, head : head + 1] = top + jnp.log(total)


def attend_backward_kernel(
    query_heads,
    block,
    order_ref,
    qkv_ref,
    cos_ref,
    sin_ref,
    aux_ref,
    seg_ref,
    lse_ref,
    grad_ref,
    out_ref,
    k_rot,
    value,
    dk,
    dv,
):
    f32, bf16 = jnp.float32, jnp.bfloat16
    length = qkv_ref.shape[0]
    q_width = query_heads * HEAD_DIM
    load_keys(order_ref, qkv_ref, q_width, cos_ref, sin_ref, k_rot, value)
    dk[...] = jnp.zeros(dk.shape, f32)
    dv[...] = jnp.zeros(dv.shape, f32)
    for start in range(0, length, block):
        rows = slice(start, start + block)
        end = start + block
        for head in range(query_heads):
            lanes = slice(head * HEAD_DIM, (head + 1) * HEAD_DIM)
            cosine, sine = cos_ref[rows, :], sin_ref[rows, :]
            q_block = turn(load_rows(order_ref, qkv_ref, start, block, lanes), cosine, sine)
            scores = block_scores(q_block, k_rot[:end, :], start, aux_ref[rows, 0:1], seg_ref[:, :end])
            probs = jnp.exp(scores - lse_ref[rows, head : head + 1])
            grad = load_rows(order_ref, grad_ref, start, block, lanes)
            grad_probs = dot_last(grad, value[:end, :])
            mean = jnp.sum(grad_probs * probs, axis=1, keepdims=True)
            grad_scores = (probs * (grad_probs - mean) * HEAD_DIM ** (-0.5)).astype(bf16)
            grad_query = turn_back(dot_plain(grad_scores, k_rot[:end, :]), cosine, sine)
            store_rows(order_ref, out_ref, start, lanes, grad_query)
            dk[:end, :] += dot_first(grad_scores, q_block)
            dv[:end, :] += dot_first(probs.astype(bf16), grad)
    k_lanes = slice(q_width, q_width + HEAD_DIM)
    v_lanes = slice(q_width + HEAD_DIM, q_width + 2 * HEAD_DIM)
    store_rows(order_ref, out_ref, 0, k_lanes, turn_back(dk[...], cos_ref[...], sin_ref[...]))
    store_rows(order_ref, out_ref, 0, v_lanes, dv[...].astype(bf16))


def attend_specs(arrays):
    return [pl.BlockSpec(memory_space=pltpu.SMEM)] + [pl.BlockSpec(memory_space=pltpu.VMEM)] * arrays


def attend_forward(order, early, tables, aux, seg_row, query_heads):
    length = early.shape[0]
    return pl.pallas_call(
        functools.partial(attend_forward_kernel, query_heads, min(ATT_ROWS, length)),
        in_specs=attend_specs(5),
        out_shape=[
            jax.ShapeDtypeStruct((length, query_heads * HEAD_DIM), jnp.bfloat16),
            jax.ShapeDtypeStruct((length, 8), jnp.float32),
        ],
        scratch_shapes=[pltpu.VMEM((length, HEAD_DIM), jnp.bfloat16), pltpu.VMEM((length, HEAD_DIM), jnp.bfloat16)],
        compiler_params=pltpu.CompilerParams(vmem_limit_bytes=VMEM_BYTES),
        cost_estimate=pl.CostEstimate(
            flops=2_000_000_000 * query_heads, bytes_accessed=4_000_000, transcendentals=1_000_000
        ),
        name="attend_forward",
    )(order, early, tables[0], tables[1], aux, seg_row)


def attend_backward(order, early, tables, aux, seg_row, lse, grad, query_heads):
    length = early.shape[0]
    return pl.pallas_call(
        functools.partial(attend_backward_kernel, query_heads, min(ATT_ROWS, length)),
        in_specs=attend_specs(7),
        out_shape=jax.ShapeDtypeStruct((length, (query_heads + 2) * HEAD_DIM), jnp.bfloat16),
        scratch_shapes=[
            pltpu.VMEM((length, HEAD_DIM), jnp.bfloat16),
            pltpu.VMEM((length, HEAD_DIM), jnp.bfloat16),
            pltpu.VMEM((length, HEAD_DIM), jnp.float32),
            pltpu.VMEM((length, HEAD_DIM), jnp.float32),
        ],
        compiler_params=pltpu.CompilerParams(vmem_limit_bytes=VMEM_BYTES),
        cost_estimate=pl.CostEstimate(
            flops=4_000_000_000 * query_heads, bytes_accessed=6_000_000, transcendentals=1_000_000
        ),
        name="attend_backward",
    )(order, early, tables[0], tables[1], aux, seg_row, lse, grad)


def after_kernel(*refs):
    pass


def after(value, *others):
    return pl.pallas_call(
        after_kernel,
        in_specs=[pl.BlockSpec(memory_space=pl.ANY)] * (1 + len(others)),
        out_specs=pl.BlockSpec(memory_space=pl.ANY),
        out_shape=jax.ShapeDtypeStruct(value.shape, value.dtype),
        input_output_aliases={0: 0},
        name="after",
    )(value, *others)


def move_blocks(tiles, width, here, there):
    per = 128 // width
    lane = lanes_iota(tiles[0].shape)
    moved = []
    for tile in range(len(tiles)):
        out = None
        for part in range(per):
            source = there(tile * per + part)
            piece = tiles[source // per]
            shift = ((part - source % per) * width) % 128
            if shift:
                piece = pltpu.roll(piece, shift, 1)
            out = piece if out is None else jnp.where(lane >= part * width, piece, out)
        moved.append(out)
    return moved


def to_gathered_tiles(tiles, width, seq, fsdp):
    return move_blocks(tiles, width, None, lambda b: (b % seq) * fsdp + b // seq)


def from_gathered_tiles(tiles, width, seq, fsdp):
    return move_blocks(tiles, width, None, lambda b: (b % fsdp) * seq + b // fsdp)


def tiles_of(array):
    return [array[:, lane : lane + 128] for lane in range(0, array.shape[1], 128)]


def add_arrived(split, own, arrived):
    total = own[...]
    if split:
        first = pl.program_id(0) == 0
        one, one_late, two, two_late = (ref[...].astype(jnp.float32) for ref in arrived)
        return total + jnp.where(first, one + one_late, two + two_late)
    for ref in arrived:
        total = total + ref[...].astype(jnp.float32)
    return total


def row_sum(tiles):
    total = tiles[0]
    for tile in tiles[1:]:
        total = total + tile
    return jnp.sum(total, axis=1, keepdims=True)


def store_block(blocks, value):
    for block, out in enumerate(blocks):

        @pl.when(pl.program_id(0) == block)
        def _(out=out):
            out[...] = value


def middle_kernel(split, places, count, own, rows, gain, *refs):
    arrived, outs = refs[:count], refs[count:]
    blocks, middle_ref = outs[: places[3]], outs[places[3]]
    middle = rows[...].astype(jnp.float32) + add_arrived(split, own, arrived)
    middle_ref[...] = middle
    mean = jnp.sum(middle * middle, axis=1, keepdims=True) / middle.shape[1]
    hidden = middle * lax.rsqrt(mean + EPSILON) * gain[0:1, :]
    moved = jnp.concatenate(to_gathered_tiles(tiles_of(hidden), *places[:3]), axis=1).astype(jnp.bfloat16)
    store_block(blocks, moved)


def norm_back_kernel(split, places, count, skip, in_blocks, own, rows, passed, gain, *refs):
    arrived, outs = refs[:count], refs[count + skip :]
    grads = add_arrived(split, own, arrived)
    grads = jnp.concatenate(from_gathered_tiles(tiles_of(grads), *places[:3]), axis=1)
    wide = rows[...].astype(jnp.float32)
    width = wide.shape[1]
    scale = lax.rsqrt(jnp.sum(wide * wide, axis=1, keepdims=True) / width + EPSILON)
    normed = wide * scale
    weighted = grads * gain[0:1, :]
    mean = jnp.sum(weighted * normed, axis=1, keepdims=True) / width
    total = passed[...].astype(jnp.float32) + scale * (weighted - normed * mean)
    if in_blocks:
        store_block(outs[: places[3]], total.astype(jnp.bfloat16))
        outs[-2][...] = total
    else:
        outs[0][...] = total.astype(jnp.bfloat16)
    gain_grad = outs[-1]

    @pl.when(pl.program_id(0) == 0)
    def _():
        gain_grad[...] = jnp.zeros(gain_grad.shape, jnp.float32)

    gain_grad[0:1, :] += jnp.sum(normed * grads, axis=0, keepdims=True)


def rows_call(kernel, tokens, width, split, inputs, gain, arrived, outs, deps, name):
    block = pl.BlockSpec((SPAN, width), lambda i: (i, 0))
    whole = pl.BlockSpec((8, width), lambda i: (0, 0))
    fixed = pl.BlockSpec((SPAN, width), lambda i: (0, 0))
    out_specs = [whole if shape[0] == 8 else fixed if shape[0] == SPAN else block for shape, dtype in outs]
    return pl.pallas_call(
        kernel,
        grid=(tokens // SPAN,),
        in_specs=[block] * len(inputs)
        + [whole]
        + [fixed if split else block] * len(arrived)
        + [pl.BlockSpec(memory_space=pl.ANY)] * len(deps),
        out_specs=out_specs,
        out_shape=[jax.ShapeDtypeStruct(shape, dtype) for shape, dtype in outs],
        compiler_params=pltpu.CompilerParams(
            dimension_semantics=("arbitrary",), vmem_limit_bytes=VMEM_BYTES
        ),
        cost_estimate=pl.CostEstimate(flops=40 * tokens * width, bytes_accessed=20 * tokens * width, transcendentals=0),
        name=name,
    )(*inputs, gain, *arrived, *deps)


def norm_pieces_kernel(gain, *refs):
    pieces, out = refs[:-1], refs[-1]
    for block, piece in enumerate(pieces):

        @pl.when(pl.program_id(0) == block)
        def _(piece=piece):
            wide = piece[...].astype(jnp.float32)
            mean = jnp.sum(wide * wide, axis=1, keepdims=True) / wide.shape[1]
            out[...] = (wide * lax.rsqrt(mean + EPSILON) * gain[0:1, :]).astype(jnp.bfloat16)


def norm_pieces(pieces, gain):
    width = pieces[0].shape[1]
    length = len(pieces) * SPAN
    return pl.pallas_call(
        norm_pieces_kernel,
        grid=(len(pieces),),
        in_specs=[pl.BlockSpec((8, width), lambda i: (0, 0))]
        + [pl.BlockSpec((SPAN, width), lambda i: (0, 0)) for piece in pieces],
        out_specs=pl.BlockSpec((SPAN, width), lambda i: (i, 0)),
        out_shape=jax.ShapeDtypeStruct((length, width), jnp.bfloat16),
        compiler_params=pltpu.CompilerParams(
            dimension_semantics=("arbitrary",), vmem_limit_bytes=VMEM_BYTES
        ),
        cost_estimate=pl.CostEstimate(flops=6 * length * width, bytes_accessed=4 * length * width, transcendentals=0),
        name="norm_pieces",
    )(gain, *pieces)


def assemble_kernel(count, *refs):
    pieces, out, held, sems = refs[:count], refs[-3], refs[-2], refs[-1]
    places = [pl.ds(block * SPAN, SPAN) for block in range(count)]
    loads = [pltpu.make_async_copy(pieces[b], held.at[places[b]], sems.at[0, b]) for b in range(count)]
    stores = [pltpu.make_async_copy(held.at[places[b]], out.at[places[b]], sems.at[1, b]) for b in range(count)]
    for load in loads:
        load.start()
    for load, store in zip(loads, stores):
        load.wait()
        store.start()
    for store in stores:
        store.wait()


def assemble(pieces, *deps):
    width = pieces[0].shape[1]
    length = len(pieces) * SPAN
    return pl.pallas_call(
        functools.partial(assemble_kernel, len(pieces)),
        in_specs=[pl.BlockSpec(memory_space=pl.ANY)] * (len(pieces) + len(deps)),
        out_specs=pl.BlockSpec(memory_space=pl.ANY),
        out_shape=jax.ShapeDtypeStruct((length, width), pieces[0].dtype),
        scratch_shapes=[
            pltpu.VMEM((length, width), pieces[0].dtype),
            pltpu.SemaphoreType.DMA((2, len(pieces))),
        ],
        compiler_params=pltpu.CompilerParams(vmem_limit_bytes=VMEM_BYTES),
        cost_estimate=pl.CostEstimate(flops=0, bytes_accessed=4 * length * width, transcendentals=0),
        name="assemble",
    )(*pieces, *deps)


def gathered_blocks_kernel(places, rows, *outs):
    for block, out in enumerate(outs):

        @pl.when(pl.program_id(0) == block)
        def _(out=out):
            moved = to_gathered_tiles(tiles_of(rows[...].astype(jnp.float32)), *places)
            out[...] = jnp.concatenate(moved, axis=1).astype(out.dtype)


def gathered_blocks(rows, places):
    tokens, width = rows.shape
    blocks = tokens // SPAN
    return pl.pallas_call(
        functools.partial(gathered_blocks_kernel, places),
        grid=(blocks,),
        in_specs=[pl.BlockSpec((SPAN, width), lambda i: (i, 0))],
        out_specs=[pl.BlockSpec((SPAN, width), lambda i: (0, 0))] * blocks,
        out_shape=[jax.ShapeDtypeStruct((SPAN, width), rows.dtype)] * blocks,
        compiler_params=pltpu.CompilerParams(
            dimension_semantics=("arbitrary",), vmem_limit_bytes=VMEM_BYTES
        ),
        cost_estimate=pl.CostEstimate(flops=4 * tokens * width, bytes_accessed=4 * tokens * width, transcendentals=0),
        name="gathered_blocks",
    )(rows)


def matmul_rows(left, right):
    return jnp.einsum("tc,cd->td", left, right, preferred_element_type=jnp.float32)


def matmul_back(left, right):
    return jnp.einsum("td,cd->tc", left, right, preferred_element_type=jnp.float32)


def weight_grad(left, right):
    return jnp.einsum("tc,td->cd", left, right, preferred_element_type=jnp.float32)


def peers(count, flip):
    return [(i, i ^ flip) for i in range(count)]


def swap(value, flip):
    return lax.ppermute(value, "seq", peers(lax.axis_size("seq"), flip))


def balanced(tokens):
    return lax.axis_size("seq") == 4 and tokens == 2 * SPAN


def block_places(tokens):
    index = lax.axis_index("seq")
    halves = tokens // SPAN
    blocks = jnp.arange(lax.axis_size("seq") * halves, dtype=jnp.int32)
    place = (blocks // halves) ^ index
    place = place * halves + blocks % halves
    if balanced(tokens):
        place = jnp.array([0, 1, 2, 7, 6, 4, 3, 5], jnp.int32)[place]
    return place


def fetch_tokens(halves):
    if balanced(len(halves) * SPAN):
        a, b = halves
        one_a, two_b = swap(a, 1), swap(b, 2)
        three_a, three_b = swap(one_a, 2), swap(two_b, 1)
        one_b, two_a = swap(b, 1), swap(a, 2)
        return [a, b, one_a, three_a, two_b, three_b, two_a, one_b]
    return list(halves) + [swap(half, flip) for flip in range(1, lax.axis_size("seq")) for half in halves]


def scatter_tokens(product, tokens, hold=()):
    f32, bf16 = jnp.float32, jnp.bfloat16

    def held(part):
        return after(part, *hold) if hold else part

    if balanced(tokens):
        to_one = product(tokens, 2 * tokens).astype(bf16)
        from_one = swap(held(to_one), 1)
        to_two = product(2 * tokens, 3 * tokens).astype(bf16)
        from_two = swap(held(to_two), 2)
        second = product(3 * tokens, 4 * tokens, to_one, to_two)
        own = product(0, tokens, to_one, to_two)
        two_a = (second[:SPAN] + from_one[SPAN:].astype(f32)).astype(bf16)
        one_b = (second[SPAN:] + from_two[SPAN:].astype(f32)).astype(bf16)
        return own, (from_one, swap(two_a, 2), from_two, swap(one_b, 1)), (to_one, to_two, second, own)
    sent = [
        product(flip * tokens, (flip + 1) * tokens).astype(bf16) for flip in range(1, lax.axis_size("seq"))
    ]
    own = product(0, tokens, *sent)
    return own, tuple(swap(held(part), flip + 1) for flip, part in enumerate(sent)), (*sent, own)


def cut_rows(whole, start, end, deps):
    part = whole[start:end]
    return after(part, *deps) if deps else part


def add_small(vector):
    for axis in ("fsdp", "seq"):
        count = lax.axis_size(axis)
        flip = 1
        while flip < count:
            vector = vector + lax.ppermute(vector, axis, peers(count, flip))
            flip *= 2
    return vector


def trade(stacked):
    return lax.all_to_all(stacked, "seq", split_axis=0, concat_axis=0, tiled=True)


def gather_weights(rows):
    return lax.all_gather(rows.reshape(-1, rows.shape[-1]), "fsdp", axis=0, tiled=True)


def spread_sums(grad):
    return lax.psum_scatter(grad, "fsdp", scatter_dimension=0, tiled=True)


def to_gathered(rows):
    seq, fsdp = lax.axis_size("seq"), lax.axis_size("fsdp")
    shape = rows.shape
    split = rows.reshape(shape[:-1] + (seq, fsdp, -1))
    return jnp.swapaxes(split, -3, -2).reshape(shape)


def from_gathered(rows):
    seq, fsdp = lax.axis_size("seq"), lax.axis_size("fsdp")
    shape = rows.shape
    split = rows.reshape(shape[:-1] + (fsdp, seq, -1))
    return jnp.swapaxes(split, -3, -2).reshape(shape)


def on_device(
    inputs,
    cotangent,
    segments,
    norm_in,
    ssm_in,
    attn_in,
    conv_w,
    conv_b,
    a_log,
    dt_bias,
    d_skip,
    ssm_out,
    attn_out,
    norm_ffn,
    w_gate,
    w_up,
    w_down,
):
    f32, bf16 = jnp.float32, jnp.bfloat16
    seq = lax.axis_size("seq")
    fsdp = lax.axis_size("fsdp")
    index = lax.axis_index("seq")
    rows = ssm_in.shape[0]
    tokens = inputs.shape[2]
    length = segments.shape[2]
    heads = SSM_HEADS // seq
    inner = heads * SSM_DIM
    query_heads = Q_HEADS // seq
    q_width = query_heads * HEAD_DIM
    qkv_width = q_width + 2 * HEAD_DIM
    groups = Q_HEADS // KV_HEADS
    kv_of = [(s * query_heads) // groups for s in range(seq)]
    head_start = index * heads
    inner_start = index * inner
    z_end, x_end, bc_end = SSM_INNER, 2 * SSM_INNER, 2 * SSM_INNER + 2 * STATE
    q_end = Q_HEADS * HEAD_DIM
    kv_end = q_end + KV_HEADS * HEAD_DIM

    def by_seq(block):
        return jnp.swapaxes(block.reshape(rows, seq, -1), 0, 1)

    def for_all(block):
        return jnp.broadcast_to(block[None], (seq,) + block.shape)

    def by_kv(block):
        return jnp.stack([block[:, h * HEAD_DIM : (h + 1) * HEAD_DIM] for h in kv_of])

    channels = conv_b.shape[0]
    conv_pack = jnp.concatenate([conv_w, conv_b[None]], axis=0).reshape(-1)
    conv_cols = -(-conv_pack.shape[0] // rows)
    conv_pack = jnp.pad(conv_pack, (0, conv_cols * rows - conv_pack.shape[0])).reshape(rows, conv_cols)
    misc = jnp.concatenate([norm_in[:, None], norm_ffn[:, None], conv_pack], axis=1)
    misc = jnp.pad(misc, ((0, 0), (0, 128 - misc.shape[1])))
    early_send = jnp.concatenate(
        [by_seq(attn_in[:, :q_end]), by_kv(attn_in[:, q_end:kv_end]), by_kv(attn_in[:, kv_end:]), for_all(misc)],
        axis=2,
    )
    halves = tokens // SPAN
    places = (rows, seq, fsdp, halves)
    mine = gathered_blocks(inputs[0, 0], places[:3])
    dt_block = jnp.pad(by_seq(ssm_in[:, bc_end:]), ((0, 0), (0, 0), (0, 128 - heads)))
    first_send = jnp.concatenate(
        [by_seq(ssm_in[:, z_end:x_end]), for_all(ssm_in[:, x_end:bc_end]), dt_block], axis=2
    )
    start_mine = trade(after(jnp.concatenate([early_send, first_send], axis=2), *mine))
    early_mine, first_mine = start_mine[:, :, : early_send.shape[2]], start_mine[:, :, early_send.shape[2] :]
    pieces = [fetch_tokens([after(half, start_mine) for half in mine])]
    out_send = jnp.concatenate([ssm_out, attn_out], axis=0)
    later_send = jnp.concatenate([by_seq(ssm_in[:, :z_end]), by_seq(w_gate), by_seq(w_up)], axis=2)
    early_w = gather_weights(early_mine)
    first_w = gather_weights(first_mine)
    out_rows = ssm_out.shape[0]
    units = w_down.shape[0] * fsdp
    small = early_w[:, qkv_width:]

    def gain_rows(gain):
        return jnp.broadcast_to(gain.astype(f32)[None], (8, gain.shape[0]))

    gain_in_gathered = gain_rows(small[:, 0])
    gain_in = gain_rows(from_gathered(small[:, 0]))
    gain_ffn = gain_rows(from_gathered(small[:, 1]))
    conv_all = small[:, 2 : 2 + conv_cols].reshape(fsdp, seq, -1)[:, :, : (CONV + 1) * channels]
    conv_all = conv_all.reshape(fsdp, seq, CONV + 1, channels).transpose(2, 1, 0, 3)
    conv_all = conv_all.reshape(CONV + 1, CONV_CH).astype(f32)
    conv_local = jnp.concatenate(
        [lax.dynamic_slice_in_dim(conv_all, inner_start, inner, 1), conv_all[:, SSM_INNER:]], axis=1
    )
    conv_table = jnp.pad(conv_local, ((0, 8 - CONV - 1), (0, 0)))
    rate_local = lax.dynamic_slice_in_dim(a_log.astype(f32), head_start, heads)
    bias_local = lax.dynamic_slice_in_dim(dt_bias.astype(f32), head_start, heads)
    skip_local = lax.dynamic_slice_in_dim(d_skip.astype(f32), head_start, heads)
    head_table = jnp.pad(jnp.stack([bias_local, rate_local]), ((0, 6), (0, 128 - heads)))
    skip_table = jnp.broadcast_to(jnp.repeat(skip_local, SSM_DIM)[None], (8, inner))
    tables = rotary_tables(length)
    order = block_places(tokens)

    micro = range(MICRO)
    auxes = [token_aux(segments[m, 0]) for m in micro]
    seg_blocks = [segments[m, 0].astype(f32).reshape(-1, 1, SPAN) for m in micro]
    seg_rows = [segments[m, 0].astype(f32)[None] for m in micro]
    split = balanced(tokens)
    width = inputs.shape[3]
    head_tables = (conv_table, head_table, skip_table)

    hiddens, earlies, attendeds, lses, firsts, ys, all_starts = [], [], [], [], [], [], []
    for m in range(1, MICRO):
        mine = gathered_blocks(inputs[m, 0], places[:3])
        pieces.append(fetch_tokens([after(half, *pieces[m - 1][-2:]) for half in mine]))
    cot_alls = []
    for m in micro:
        if m > 0:
            pieces[m][0] = after(pieces[m][0], ys[m - 1])
        hidden = norm_pieces(pieces[m], gain_in_gathered)
        early = matmul_rows(hidden, early_w).astype(bf16)
        attended, lse = attend_forward(order, early, tables, auxes[m], seg_rows[m], query_heads)
        earlies.append(early)
        attendeds.append(attended)
        lses.append(lse)
        if m == 0:
            later_mine = trade(after(later_send, attended))
            z_mine, ffn_mine = later_mine[:, :, :inner], later_mine[:, :, inner:]
            z_w = gather_weights(z_mine)
            out_send = after(out_send, z_mine)
            out_w = gather_weights(out_send)
            gate_up_w = gather_weights(after(ffn_mine, out_send))
        hidden = after(hidden, attended, *([later_mine] if m == 0 else cot_pieces))
        hiddens.append(hidden)
        first = matmul_rows(hidden, first_w).astype(bf16)
        behind = [first, *pieces[MICRO - 1][-2:]] if m == 0 else [first, *cot_pieces]
        blocks = [after(cotangent[m, 0, half * SPAN : (half + 1) * SPAN], *behind) for half in range(halves)]
        cot_pieces = fetch_tokens(blocks)
        cot_alls.append(assemble(cot_pieces))
        y_rows, starts = ssd_forward(order, first, auxes[m], seg_blocks[m], *head_tables, heads)
        firsts.append(first)
        ys.append(y_rows)
        all_starts.append(starts)
    down_w = gather_weights(after(w_down, ys[0]))
    out_w = out_w.reshape(fsdp, -1, out_w.shape[1])
    out_w = jnp.concatenate(
        [out_w[:, :out_rows].reshape(inner, -1), out_w[:, out_rows:].reshape(q_width, -1)], axis=0
    )
    side_w = jnp.concatenate([early_w[:, :qkv_width], z_w], axis=1)
    gate_zs, out_ins, mixeds = [], [], []

    def mixer_out(m, deps, hold=()):
        hiddens[m] = after(hiddens[m], *deps)
        gate_z = matmul_rows(hiddens[m], z_w)
        gated = (ys[m].astype(f32) * jax.nn.silu(gate_z)).astype(bf16)
        gate_zs.append(gate_z)
        out_in = jnp.concatenate([gated, attendeds[m]], axis=1)
        out_ins.append(out_in)

        def mixed_rows(start, end, *late):
            return matmul_rows(cut_rows(out_in, start, end, late), out_w)

        mixeds.append(scatter_tokens(mixed_rows, tokens, hold))

    middles, ffn_hiddens, activateds, grad_gus, grad_hiddens = [], [], [], [], []
    grad_middles, lows, gain_ffn_grads, grads_mixed = [], [], [], []

    def middle_forward(m, hold):
        own, arrived, sent = mixeds[m]
        *blocks, middle = rows_call(
            functools.partial(middle_kernel, split, places, len(arrived)),
            tokens,
            width,
            split,
            [own, inputs[m, 0]],
            gain_ffn,
            arrived,
            [((SPAN, width), bf16)] * halves + [((tokens, width), f32)],
            [],
            "middle",
        )
        middles.append(middle)
        if hold:
            blocks = [after(block, *hold) for block in blocks]
        ffn_hiddens.append(assemble(fetch_tokens(blocks)))

    def feed_forward(m, deps):
        ffn_hidden = after(ffn_hiddens[m], *deps)
        ffn_hiddens[m] = ffn_hidden
        gate_up = matmul_rows(ffn_hidden, gate_up_w)
        gate_pre, up_pre = gate_up[:, :units], gate_up[:, units:]
        sig = jax.nn.sigmoid(gate_pre)
        activateds.append((gate_pre * sig * up_pre).astype(bf16))
        grad_act = matmul_back(cot_alls[m], down_w)
        grad_up = grad_act * gate_pre * sig
        grad_gate = grad_act * up_pre * sig * (1.0 + gate_pre * (1.0 - sig))
        grad_gu = jnp.concatenate([grad_gate, grad_up], axis=1).astype(bf16)
        grad_gus.append(grad_gu)

        def hidden_rows(start, end, *late):
            return matmul_back(cut_rows(grad_gu, start, end, late), gate_up_w)

        grad_hiddens.append(scatter_tokens(hidden_rows, tokens))

    def middle_back(m, deps):
        own, arrived, sent = grad_hiddens[m]
        *blocks, wide, gain_grad = rows_call(
            functools.partial(norm_back_kernel, split, places, len(arrived), len(deps), True),
            tokens,
            width,
            split,
            [own, middles[m], cotangent[m, 0]],
            gain_ffn,
            arrived,
            [((SPAN, width), bf16)] * halves + [((tokens, width), f32), ((8, width), f32)],
            deps,
            "middle_back",
        )
        grad_middles.append(wide)
        lows.append(blocks[0])
        gain_ffn_grads.append(gain_grad[0])
        grads_mixed.append(assemble(fetch_tokens(blocks)))

    grad_ys, grad_sides, outs, back, in_backs, outputs = [], [], [], [], [], []

    def heads_back(m, deps):
        grad_mixed = after(grads_mixed[m], *deps)
        grads_mixed[m] = grad_mixed
        grad_gated = matmul_back(grad_mixed, out_w[:inner])
        grad_attended = matmul_back(grad_mixed, out_w[inner:]).astype(bf16)
        gate_z = gate_zs[m]
        sig = jax.nn.sigmoid(gate_z)
        y_wide = ys[m].astype(f32)
        grad_ys.append((grad_gated * gate_z * sig).astype(bf16))
        grad_z = (grad_gated * y_wide * sig * (1.0 + gate_z * (1.0 - sig))).astype(bf16)
        grad_qkv = attend_backward(
            order, earlies[m], tables, auxes[m], seg_rows[m], lses[m], grad_attended, query_heads
        )
        grad_sides.append(jnp.concatenate([grad_qkv, grad_z], axis=1))

    def output_rows(m, deps, hold=()):
        activateds[m] = after(activateds[m], *deps)

        def down_rows(start, end, *late):
            return matmul_rows(cut_rows(activateds[m], start, end, late), down_w)

        outs.append(scatter_tokens(down_rows, tokens, hold))

    def scan_back(m, deps):
        grad_y = after(grad_ys[m], *deps)
        back.append(
            ssd_backward(order, firsts[m], auxes[m], seg_blocks[m], *head_tables, all_starts[m], grad_y, heads)
        )

    def hidden_back(m, deps, hold=(), later=()):
        grad_first = after(back[m][0], *deps)

        def in_rows(start, end, *late):
            one = cut_rows(grad_first, start, end, late + tuple(later if late else ()))
            return matmul_back(one, first_w) + matmul_back(grad_sides[m][start:end], side_w)

        in_backs.append(scatter_tokens(in_rows, tokens, hold))

    def finish_input(m):
        own, arrived, sent = in_backs[m]
        low, gain_grad = rows_call(
            functools.partial(norm_back_kernel, split, places, len(arrived), 0, False),
            tokens,
            width,
            split,
            [own, inputs[m, 0], grad_middles[m]],
            gain_in,
            arrived,
            [((tokens, width), bf16), ((8, width), f32)],
            [],
            "input_back",
        )
        return low, gain_grad[0]

    def finish_output(m):
        own, arrived, sent = outs[m]
        if split:
            arrived = [
                jnp.concatenate([arrived[0][:SPAN], arrived[2][:SPAN]]),
                jnp.concatenate([arrived[1], arrived[3]]),
            ]
        return (middles[m] + own + sum(part.astype(f32) for part in arrived)).astype(bf16)

    def both(lefts, rights):
        return (weight_grad(lefts[0], rights[0]) + weight_grad(lefts[1], rights[1])).astype(bf16)

    def back_to_rows(part):
        return trade(part.reshape(seq, rows, -1)).astype(f32)

    def first_arrived(scattered):
        return scattered[1][::2]

    mixer_out(0, [ys[1], *cot_pieces[2:5]])
    middle_forward(0, ())
    mixer_out(1, mixeds[0][2], [ffn_hiddens[0]])
    feed_forward(0, mixeds[1][2])
    ffn_hiddens[0] = after(ffn_hiddens[0], *grad_hiddens[0][2])
    gate_up_sum = weight_grad(ffn_hiddens[0], grad_gus[0])
    activateds[0] = after(activateds[0], gate_up_sum)
    down_sum = weight_grad(activateds[0], cot_alls[0])
    middle_back(0, [gate_up_sum])
    middle_forward(1, [grads_mixed[0]])
    heads_back(0, [down_sum])
    output_rows(0, grad_sides, [ffn_hiddens[1]])
    feed_forward(1, outs[0][2])
    ffn_hiddens[1] = after(ffn_hiddens[1], *grad_hiddens[1][2])
    gate_up_sum = (gate_up_sum + weight_grad(ffn_hiddens[1], grad_gus[1])).astype(bf16)
    activateds[1] = after(activateds[1], gate_up_sum)
    down_sum = (down_sum + weight_grad(activateds[1], cot_alls[1])).astype(bf16)
    gate_up_part = spread_sums(gate_up_sum)
    down_part = spread_sums(down_sum)
    scan_back(0, [down_sum, *first_arrived(grad_hiddens[1])])
    outputs.append(finish_output(0))
    middle_back(1, [back[0][0], outputs[0]])
    hidden_back(0, [lows[1]], [grads_mixed[1]])
    output_rows(1, in_backs[0][2], [grads_mixed[1]])
    heads_back(1, [*outs[1][2], gate_up_part])
    gate_up_back = back_to_rows(gate_up_part)
    out_ins[0] = after(out_ins[0], grad_sides[1], gate_up_back)
    out_sum = both(out_ins, grads_mixed)
    out_sum = jnp.concatenate(
        [out_sum[:inner].reshape(fsdp, -1, width), out_sum[inner:].reshape(fsdp, -1, width)], axis=1
    ).reshape(inner + q_width, width)
    out_part = spread_sums(out_sum)
    hiddens[0] = after(hiddens[0], out_sum, down_part, *first_arrived(in_backs[0]))
    side_sum = both(hiddens, grad_sides)
    side_part = spread_sums(side_sum)
    input_grads, gain_in_grads = [], []
    low, gain_grad = finish_input(0)
    input_grads.append(low)
    gain_in_grads.append(gain_grad)
    scan_back(1, [side_sum, low, *first_arrived(outs[1])])
    outputs.append(finish_output(1))
    hiddens[0] = after(hiddens[0], outputs[1], out_part)
    first_sum = both(hiddens, [b[0] for b in back])
    first_part = spread_sums(first_sum)
    side_back = back_to_rows(side_part)
    hidden_back(1, [first_sum], (), [side_back])
    low, gain_grad = finish_input(1)
    input_grads.append(low)
    gain_in_grads.append(gain_grad)

    gain_in_grad = gain_in_grads[0] + gain_in_grads[1]
    gain_ffn_grad = gain_ffn_grads[0] + gain_ffn_grads[1]
    conv_grad = (back[0][1] + back[1][1])[: CONV + 1]
    head_grad = back[0][2] + back[1][2]
    rate_sum, bias_sum = head_grad[0, :heads], head_grad[1, :heads]
    skip_sum = jnp.sum((back[0][3] + back[1][3])[0].reshape(heads, SSM_DIM), axis=1)

    def own_columns(block):
        return jnp.swapaxes(block, 0, 1).reshape(rows, -1)

    def kv_columns(block):
        return jnp.concatenate(
            [sum(block[s] for s in range(seq) if kv_of[s] == h) for h in range(KV_HEADS)], axis=1
        )

    gate_grad = own_columns(gate_up_back[:, :, :units])
    up_grad = own_columns(gate_up_back[:, :, units:])
    first_back = back_to_rows(first_part)
    ssm_in_grad = jnp.concatenate(
        [
            own_columns(side_back[:, :, qkv_width:]),
            own_columns(first_back[:, :, :inner]),
            jnp.sum(first_back[:, :, inner : inner + 2 * STATE], axis=0),
            own_columns(first_back[:, :, inner + 2 * STATE : inner + 2 * STATE + heads]),
        ],
        axis=1,
    )
    attn_in_grad = jnp.concatenate(
        [
            own_columns(side_back[:, :, :q_width]),
            kv_columns(side_back[:, :, q_width : q_width + HEAD_DIM]),
            kv_columns(side_back[:, :, q_width + HEAD_DIM : qkv_width]),
        ],
        axis=1,
    )
    out_part = out_part.astype(f32)

    conv_whole = jnp.zeros((CONV + 1, CONV_CH), f32)
    conv_whole = lax.dynamic_update_slice_in_dim(conv_whole, conv_grad[:, :inner], inner_start, 1)
    conv_whole = lax.dynamic_update_slice_in_dim(conv_whole, conv_grad[:, inner:], SSM_INNER, 1)
    head_sums = lax.dynamic_update_slice_in_dim(
        jnp.zeros((3, SSM_HEADS), f32), jnp.stack([rate_sum, bias_sum, skip_sum]), head_start, 1
    )
    pieces = [conv_whole.reshape(-1), head_sums.reshape(-1), gain_in_grad, gain_ffn_grad]
    ends = [0]
    for piece in pieces:
        ends.append(ends[-1] + piece.shape[0])
    total = add_small(jnp.concatenate(pieces))
    conv_total, head_total, gain_in_total, gain_ffn_total = (
        total[a:b] for a, b in zip(ends[:-1], ends[1:])
    )
    place = index * fsdp + lax.axis_index("fsdp")
    conv_total = lax.dynamic_slice_in_dim(conv_total.reshape(CONV + 1, CONV_CH), place * channels, channels, 1)
    head_total = head_total.reshape(3, SSM_HEADS)
    return (
        jnp.stack(outputs)[:, None],
        jnp.stack(input_grads)[:, None],
        lax.dynamic_slice_in_dim(gain_in_total, place * rows, rows),
        ssm_in_grad,
        attn_in_grad,
        conv_total[:CONV],
        conv_total[CONV],
        head_total[0],
        head_total[1],
        head_total[2],
        out_part[:out_rows],
        out_part[out_rows:],
        lax.dynamic_slice_in_dim(gain_ffn_total, place * rows, rows),
        gate_grad,
        up_grad,
        down_part.astype(f32),
    )


def solution(mesh):
    return jax.shard_map(
        on_device,
        mesh=mesh,
        in_specs=(
            P(None, "fsdp", "seq", None),
            P(None, "fsdp", "seq", None),
            P(None, "fsdp", None),
            P(("seq", "fsdp")),
            P(("seq", "fsdp"), None),
            P(("seq", "fsdp"), None),
            P(None, ("seq", "fsdp")),
            P(("seq", "fsdp")),
            P(),
            P(),
            P(),
            P(("seq", "fsdp"), None),
            P(("seq", "fsdp"), None),
            P(("seq", "fsdp")),
            P(("seq", "fsdp"), None),
            P(("seq", "fsdp"), None),
            P(("seq", "fsdp"), None),
        ),
        out_specs=(
            P(None, "fsdp", "seq", None),
            P(None, "fsdp", "seq", None),
            P(("seq", "fsdp")),
            P(("seq", "fsdp"), None),
            P(("seq", "fsdp"), None),
            P(None, ("seq", "fsdp")),
            P(("seq", "fsdp")),
            P(),
            P(),
            P(),
            P(("seq", "fsdp"), None),
            P(("seq", "fsdp"), None),
            P(("seq", "fsdp")),
            P(("seq", "fsdp"), None),
            P(("seq", "fsdp"), None),
            P(("seq", "fsdp"), None),
        ),
        check_vma=False,
    )
```

time: 1230 us -> 1150 us (0.935)
  waiting for transfers between devices: 328 us -> 174 us
  Pallas kernels: 158 us -> 220 us
  local copies, waits for them, and re-layouts: 167 us -> 125 us
  starting transfers between devices: 76 us -> 105 us
    ppermute x48 -> x80, waiting for transfers between devices: 299 us -> 142 us  [swap(): return lax.ppermute(value, 'seq', peers(lax.axis_size('seq'), flip))]
    pallas_call x4 -> x81, Pallas kernels: 135 us -> 196 us  [the longest x2 106 us: ssd_backward(): pl.pallas_call(functools.partial(ssd_backward_kernel, heads), grid_spec=p...]
    unnamed x343 -> x449, local copies, waits for them, and re-layouts: 22.6 us -> 62.4 us
    dynamic_update_slice x30 -> x0, local copies, waits for them, and re-layouts: 39.1 us -> none  [gather_tokens(): lax.dynamic_update_slice_in_dim(whole, part, (index ^ flip) * tokens, 0)]
    ppermute x48 -> x80, starting transfers between devices: 54.1 us -> 87.4 us  [swap(): return lax.ppermute(value, 'seq', peers(lax.axis_size('seq'), flip))]
    slice x7 -> x25, local copies, waits for them, and re-layouts: 5.6 us -> 32.5 us  [the longest x4 8.23 us: cut_rows(): part = whole[start:end]]
    ppermute x12 -> x0, local copies, waits for them, and re-layouts: 21.9 us -> none  [gather_tokens(): part = rows if flip == 0 else lax.ppermute(rows, 'seq', peers(count, flip))]
    reshape x13 -> x4, local copies, waits for them, and re-layouts: 25.4 us -> 3.83 us  [the longest x1 1.87 us: gather_weights(): rows.reshape(-1, rows.shape[-1])]
  transfers between devices with their start and end apart: 70 -> 99, of which waited for: 29 -> 42; matrix products, arithmetic and copies ran while one was open for 43% -> 39% of each run, Pallas kernels for 12% -> 19%
where the time goes in v3:
time: 1150 us; the launch traced here: 1140 us
  matrix products  399 us (35%)
  Pallas kernels  220 us (19%)
  waiting for transfers between devices  174 us (15%)
  local copies, waits for them, and re-layouts  125 us (11%)
  starting transfers between devices  105 us (9%)
  other arithmetic  58.5 us (5%)
  blocking collectives  39.5 us (3%)
  between operations  17.1 us (1%)
    dot_general x30, matrix products, matmul_back(): jnp.einsum('td,cd->tc', left, right, preferred_element_type=jnp.float32)  155 us
    ppermute x80, waiting for transfers between devices, swap(): return lax.ppermute(value, 'seq', peers(lax.axis_size('seq'), flip))  142 us
    dot_general x24, matrix products, matmul_rows(): jnp.einsum('tc,cd->td', left, right, preferred_element_type=jnp.float32)  140 us
    pallas_call x2, Pallas kernels, ssd_backward(): pl.pallas_call(functools.partial(ssd_backward_kernel, heads), grid_spec=p...  106 us
    dot_general x10, matrix products, weight_grad(): jnp.einsum('tc,td->cd', left, right, preferred_element_type=jnp.float32)  104 us
    ppermute x80, starting transfers between devices, swap(): return lax.ppermute(value, 'seq', peers(lax.axis_size('seq'), flip))  87.4 us
    unnamed x449, local copies, waits for them, and re-layouts  62.4 us
    all_to_all x2, blocking collectives, trade(): lax.all_to_all(stacked, 'seq', split_axis=0, concat_axis=0, tiled=True)  39.5 us
  transfers between devices with their start and end apart: 99, of which 42 were waited for; matrix products, arithmetic and copies ran while one was open for 39% of the time, Pallas kernels for 19%

profile of v3, /device:TPU:0, one launch (start us, length us, event | category | flops | bytes accessed | tf_op | source)
XLA Modules:
  0.0 1139.1 jit_solution(15477804037672311435)
XLA Ops:
  21.2 19.4 %all_to_all.25.refs_1_ = bf16[4,64,2048]{2,1,0:T(8,128)(2,1)S(1)} all-to-all(bf16[4,64,2048]{2,1,0:T(8,128)(2,1)} %after.61), channel_id=1, replica_groups=mesh['seq'=4,'fsdp'=8] {'seq'}, dimensions={0} | all-to-all | bytes 2097152 | tf_op jit(solution)/shard_map/all_to_all | solution.py:867
  60.0 6.7 collective-permute-done.refs_2_
  70.0 8.1 all-gather.7.cloned.1.call-done
  78.9 8.4 collective-permute-done.1.refs_3_
  87.4 6.8 norm_pieces.2.refs_0_
  106.0 20.1 %all_to_all.26.refs_2_ = bf16[4,64,2816]{2,1,0:T(8,128)(2,1)S(1)} all-to-all(bf16[4,64,2816]{2,1,0:T(8,128)(2,1)} %after.64), channel_id=1, replica_groups=mesh['seq'=4,'fsdp'=8] {'seq'}, dimensions={0} | all-to-all | bytes 2883584 | tf_op jit(solution)/shard_map/all_to_all | solution.py:867
  141.7 6.8 collective-permute-done.6.refs_2_
  154.6 11.3 convolution_convert_fusion.1.first_ref.refs_1_.before_ref
  172.7 15.0 %ssd_forward.2 = (bf16[1024,768]{1,0:T(8,128)(2,1)S(1)}, bf16[8,256,768]{2,1,0:T(8,128)(2,1)}) custom-call(s32[8]{0:T(128)S(1)} %gather_fusion, bf16[1024,1408]{1,0:T(8,128)(2,1)S(1)} %copy-done.6, f32[1024,16]{1,0:T(8,128)S(1)} %copy-done.99, f32[8,1,128]{2,1,0:T(1,128)S(1)} %get-tuple-element.224.seg_ref, f32[8,1280]{1,0:T(8,128)S(1)} %select_maximum_fusion.conv_ref, ...), custom_call_target="tpu_custom_call" | custom-call | flops 8000000000 | bytes 12000000 | tf_op jit(solution)/shard_map/ssd_forward/pallas_call | solution.py:327
  194.1 6.6 norm_pieces.3.refs_0_
  217.3 11.4 convolution_convert_fusion.first_ref.refs_1_.before_ref
  230.7 7.3 collective-permute-done.18.refs_2_
  240.8 15.1 %ssd_forward.3 = (bf16[1024,768]{1,0:T(8,128)(2,1)S(1)}, bf16[8,256,768]{2,1,0:T(8,128)(2,1)}) custom-call(s32[8]{0:T(128)S(1)} %gather_fusion, bf16[1024,1408]{1,0:T(8,128)(2,1)S(1)} %copy-done.9, f32[1024,16]{1,0:T(8,128)S(1)} %copy-done.95, f32[8,1,128]{2,1,0:T(1,128)S(1)} %get-tuple-element.221.seg_ref, f32[8,1280]{1,0:T(8,128)S(1)} %select_maximum_fusion.conv_ref, ...), custom_call_target="tpu_custom_call" | custom-call | flops 8000000000 | bytes 12000000 | tf_op jit(solution)/shard_map/ssd_forward/pallas_call | solution.py:327
  258.1 9.5 fusion.1
  302.3 8.5 fusion.5
  362.6 13.8 %collective-permute-done.41.refs_0_ = bf16[256,2048]{1,0:T(8,128)(2,1)S(1)} collective-permute-done((bf16[256,2048]{1,0:T(8,128)(2,1)}, bf16[256,2048]{1,0:T(8,128)(2,1)S(1)}, u32[]{:S(2)}, u32[]{:S(2)}) %collective-permute-start.41) | collective-permute-done | bytes 1048608 | tf_op jit(solution)/shard_map/ppermute | solution.py:800
  380.8 14.9 %fusion.155 = f32[1024,2048]{1,0:T(8,128)} fusion(bf16[1024,2048]{1,0:T(8,128)(2,1)} %after.81.refs_0_, bf16[2048,2048]{1,0:T(8,128)(2,1)} %all-gather.15.cloned.1.call-done), kind=kOutput, calls=%fused_computation.359 | convolution fusion | flops 8589934592 | bytes 20971520 | tf_op jit(solution)/shard_map/tc,cd->td/dot_general | solution.py:784
  395.8 13.4 %multiply_convert_fusion.3 = (bf16[1024,1024]{1,0:T(8,128)(2,1)S(1)}, bf16[1024,1024]{1,0:T(8,128)(2,1)S(1)}, bf16[1024,1024]{1,0:T(8,128)(2,1)}) fusion(f32[1024,2048]{1,0:T(8,128)} %fusion.155, bf16[1024,2048]{1,0:T(8,128)(2,1)} %assemble.7, bf16[1024,2048]{1,0:T(8,128)(2,1)} %all-gather.17.cloned.1.call-done), kind=kOutput, calls=%fused_computation.52 | convolution fusion | flops 4311744512 | bytes 23068672 | tf_op jit(solution)/shard_map/td,cd->tc/dot_general | solution.py:788
  419.4 7.4 fusion.157.refs_4_.own
  426.8 7.7 fusion.156.refs_3_
  439.0 13.9 %fusion.refs_1_.refs_4_ = f32[2048,2048]{1,0:T(8,128)} fusion(bf16[1024,2048]{1,0:T(8,128)(2,1)S(1)} %copy-done.129, bf16[1024,1024]{1,0:T(8,128)(2,1)} %copy-done.161, bf16[1024,1024]{1,0:T(8,128)(2,1)} %copy-done.162), kind=kOutput, calls=%fused_computation.45 | convolution fusion | flops 8598323200 | bytes 25165824 | tf_op jit(solution)/shard_map/tc,td->cd/dot_general | solution.py:792
  471.3 10.7 fusion.158.refs_1_
  482.4 9.0 collective-permute-done.36.refs_3_
  503.8 7.3 multiply_convert_fusion.7
  511.2 6.8 attend_backward.2
  572.6 6.2 add_convert_fusion.6
  578.8 14.7 %fusion.160 = f32[1024,2048]{1,0:T(8,128)} fusion(bf16[1024,2048]{1,0:T(8,128)(2,1)} %after.98.refs_0_, bf16[2048,2048]{1,0:T(8,128)(2,1)} %all-gather.15.cloned.1.call-done), kind=kOutput, calls=%fused_computation.364 | convolution fusion | flops 8589934592 | bytes 20971520 | tf_op jit(solution)/shard_map/tc,cd->td/dot_general | solution.py:784
  593.5 9.8 multiply_convert_fusion
  604.7 8.7 convolution_convert_fusion.11.refs_1_
  618.0 7.2 fusion.161.refs_3_
  625.2 7.0 fusion.162.refs_4_.own
  632.3 16.7 %add_convert_fusion.refs_1_ = bf16[2048,2048]{1,0:T(8,128)(2,1)} fusion(f32[2048,2048]{1,0:T(8,128)} %fusion.refs_1_.refs_4_, bf16[1024,2048]{1,0:T(8,128)(2,1)} %after.101, bf16[1024,1024]{1,0:T(8,128)(2,1)} %copy-done.163, bf16[1024,1024]{1,0:T(8,128)(2,1)} %copy-done.164), kind=kOutput, calls=%fused_computation.1 | convolution fusion | flops 8606711808 | bytes 33554432 | tf_op jit(solution)/shard_map/tc,td->cd/dot_general | solution.py:792
  667.6 12.0 %add_convert_fusion.4.refs_1_ = bf16[1024,2048]{1,0:T(8,128)(2,1)} fusion(f32[1024,2048]{1,0:T(8,128)} %fusion.158.refs_1_, bf16[1024,1024]{1,0:T(8,128)(2,1)} %after.102.refs_0_, bf16[1024,2048]{1,0:T(8,128)(2,1)} %assemble.10), kind=kOutput, calls=%fused_computation.5 | convolution fusion | flops 4299161600 | bytes 18874368 | tf_op jit(solution)/shard_map/tc,td->cd/dot_general | solution.py:792
  689.4 53.2 %ssd_backward.2 = (bf16[1024,1408]{1,0:T(8,128)(2,1)S(1)}, f32[8,1280]{1,0:T(8,128)S(1)}, f32[8,128]{1,0:T(8,128)S(1)}, f32[8,768]{1,0:T(8,128)S(1)}) custom-call(s32[8]{0:T(128)S(1)} %copy-done.115, bf16[1024,1408]{1,0:T(8,128)(2,1)} %convolution_convert_fusion.1.first_ref.refs_1_.before_ref, ...), custom_call_target="tpu_custom_call" | custom-call | flops 30000001024 | bytes 16000000 | tf_op jit(solution)/shard_map/ssd_backward/pallas_call | solution.py:378
  758.7 6.5 fusion.9.refs_1_.refs_0_
  814.0 11.6 %collective-permute-done.69.refs_4_ = bf16[256,2048]{1,0:T(8,128)(2,1)S(1)} collective-permute-done((bf16[256,2048]{1,0:T(8,128)(2,1)}, bf16[256,2048]{1,0:T(8,128)(2,1)S(1)}, u32[]{:S(2)}, u32[]{:S(2)}) %collective-permute-start.69) | collective-permute-done | bytes 1048608 | tf_op jit(solution)/shard_map/ppermute | solution.py:800
  854.2 6.8 attend_backward.3
  861.1 8.2 fusion.8
  872.4 7.1 fusion.13
  881.1 9.8 add_convert_fusion.3
  897.3 17.2 %collective-permute-done.72.refs_0_.refs_3_ = bf16[256,2048]{1,0:T(8,128)(2,1)S(1)} collective-permute-done((bf16[256,2048]{1,0:T(8,128)(2,1)}, bf16[256,2048]{1,0:T(8,128)(2,1)S(1)}, u32[]{:S(2)}, u32[]{:S(2)}) %collective-permute-start.72) | collective-permute-done | bytes 1048608 | tf_op jit(solution)/shard_map/ppermute | solution.py:800
  915.8 8.9 fusion.143
  924.7 7.9 add_convert_fusion.2.refs_1_
  938.8 7.7 collective-permute-done.73.refs_1_
  955.2 52.7 %ssd_backward.3 = (bf16[1024,1408]{1,0:T(8,128)(2,1)S(1)}, f32[8,1280]{1,0:T(8,128)S(1)}, f32[8,128]{1,0:T(8,128)S(1)}, f32[8,768]{1,0:T(8,128)S(1)}) custom-call(s32[8]{0:T(128)S(1)} %copy-done.115, bf16[1024,1408]{1,0:T(8,128)(2,1)} %convolution_convert_fusion.first_ref.refs_1_.before_ref, ...), custom_call_target="tpu_custom_call" | custom-call | flops 30000001024 | bytes 16000000 | tf_op jit(solution)/shard_map/ssd_backward/pallas_call | solution.py:378
  1011.4 8.7 fusion.166
  1020.1 8.8 add_convert_fusion.1.refs_1_
  1060.4 9.8 all-to-all-done.3
  (938 shorter events, 548.9 us)
Async XLA Ops:
  7.2 70.9 %all-gather.7.cloned.1.call-start = ((), (), s32[]{:S(2)}) async-start(), calls=%async_computation.10 | async-start | bytes 2949120 | tf_op jit(solution)/shard_map/all_gather | solution.py:871
  43.3 111.3 %all-gather.9.cloned.1.call-start = ((), (), s32[]{:S(2)}) async-start(), calls=%async_computation.11 | async-start | bytes 6488064 | tf_op jit(solution)/shard_map/all_gather | solution.py:871
  44.3 213.8 %all-gather.11.cloned.1.call-start = ((), (), s32[]{:S(2)}) async-start(), calls=%async_computation.12 | async-start | bytes 3538944 | tf_op jit(solution)/shard_map/all_gather | solution.py:871
  57.3 21.6 %collective-permute-start.4 = (bf16[128,2048]{1,0:T(8,128)(2,1)S(1)}, bf16[128,2048]{1,0:T(8,128)(2,1)}, u32[]{:S(2)}, u32[]{:S(2)}) collective-permute-start(bf16[128,2048]{1,0:T(8,128)(2,1)S(1)} %copy-done.48), channel_id=1, source_target_pairs={{0,16},{8,24},{16,0},{24,8},{1,17},{9,25},{17,1},{25,9},{2,18},{10... | collective-permute-start | bytes 1572872 | tf_op jit(solution)/shard_map/ppermute | solution.py:800
  58.8 20.1 %collective-permute-start.5 = (bf16[128,2048]{1,0:T(8,128)(2,1)S(1)}, bf16[128,2048]{1,0:T(8,128)(2,1)}, u32[]{:S(2)}, u32[]{:S(2)}) collective-permute-start(bf16[128,2048]{1,0:T(8,128)(2,1)S(1)} %copy-done.46), channel_id=1, source_target_pairs={{0,8},{8,0},{16,24},{24,16},{1,9},{9,1},{17,25},{25,17},{2,10},{10... | collective-permute-start | bytes 1572872 | tf_op jit(solution)/shard_map/ppermute | solution.py:800
  66.7 20.7 %collective-permute-start.1 = (bf16[128,2048]{1,0:T(8,128)(2,1)}, bf16[128,2048]{1,0:T(8,128)(2,1)}, u32[]{:S(2)}, u32[]{:S(2)}) collective-permute-start(bf16[128,2048]{1,0:T(8,128)(2,1)} %collective-permute-done.refs_2_), channel_id=1, source_target_pairs={{0,16},{8,24},{16,0},{24,8},{1,17},{9,25},{17,1},{25,9},{2,18},{10... | collective-permute-start | bytes 1572872 | tf_op jit(solution)/shard_map/ppermute | solution.py:800
  127.4 140.2 %all-gather.13.cloned.1.call-start = ((), (), s32[]{:S(2)}) async-start(), calls=%async_computation.13 | async-start | bytes 4718592 | tf_op jit(solution)/shard_map/all_gather | solution.py:871
  128.3 252.5 %all-gather.15.cloned.1.call-start = ((), (), s32[]{:S(2)}) async-start(), calls=%async_computation.14 | async-start | bytes 9437184 | tf_op jit(solution)/shard_map/all_gather | solution.py:871
  130.7 265.0 %all-gather.17.cloned.1.call-start = ((), (), s32[]{:S(2)}) async-start(), calls=%async_computation.15 | async-start | bytes 4718592 | tf_op jit(solution)/shard_map/all_gather | solution.py:871
  139.1 26.7 %collective-permute-start.10 = (bf16[128,2048]{1,0:T(8,128)(2,1)S(1)}, bf16[128,2048]{1,0:T(8,128)(2,1)S(1)}, u32[]{:S(2)}, u32[]{:S(2)}) collective-permute-start(bf16[128,2048]{1,0:T(8,128)(2,1)S(1)} %copy-done.43), channel_id=1, source_target_pairs={{0,16},{8,24},{16,0},{24,8},{1,17},{9,25},{17,1},{25,9},{2,18},{10... | collective-permute-start | bytes 1572872 | tf_op jit(solution)/shard_map/ppermute | solution.py:800
  140.6 25.3 %collective-permute-start.11 = (bf16[128,2048]{1,0:T(8,128)(2,1)S(1)}, bf16[128,2048]{1,0:T(8,128)(2,1)S(1)}, u32[]{:S(2)}, u32[]{:S(2)}) collective-permute-start(bf16[128,2048]{1,0:T(8,128)(2,1)S(1)} %copy-done.72), channel_id=1, source_target_pairs={{0,8},{8,0},{16,24},{24,16},{1,9},{9,1},{17,25},{25,17},{2,10},{10... | collective-permute-start | bytes 1572872 | tf_op jit(solution)/shard_map/ppermute | solution.py:800
  148.5 40.3 %collective-permute-start.7 = (bf16[128,2048]{1,0:T(8,128)(2,1)}, bf16[128,2048]{1,0:T(8,128)(2,1)}, u32[]{:S(2)}, u32[]{:S(2)}) collective-permute-start(bf16[128,2048]{1,0:T(8,128)(2,1)} %collective-permute-done.6.refs_2_), channel_id=1, source_target_pairs={{0,16},{8,24},{16,0},{24,8},{1,17},{9,25},{17,1},{25,9},{2,18},{10... | collective-permute-start | bytes 1572872 | tf_op jit(solution)/shard_map/ppermute | solution.py:800
  149.4 40.5 %collective-permute-start.9 = (bf16[128,2048]{1,0:T(8,128)(2,1)}, bf16[128,2048]{1,0:T(8,128)(2,1)}, u32[]{:S(2)}, u32[]{:S(2)}) collective-permute-start(bf16[128,2048]{1,0:T(8,128)(2,1)} %collective-permute-done.8.refs_4_), channel_id=1, source_target_pairs={{0,8},{8,0},{16,24},{24,16},{1,9},{9,1},{17,25},{25,17},{2,10},{10... | collective-permute-start | bytes 1572872 | tf_op jit(solution)/shard_map/ppermute | solution.py:800
  166.8 33.9 %collective-permute-start.12 = (bf16[128,2048]{1,0:T(8,128)(2,1)}, bf16[128,2048]{1,0:T(8,128)(2,1)S(1)}, u32[]{:S(2)}, u32[]{:S(2)}) collective-permute-start(bf16[128,2048]{1,0:T(8,128)(2,1)} %after.69.refs_2_.refs_0_), channel_id=1, source_target_pairs={{0,8},{8,0},{16,24},{24,16},{1,9},{9,1},{17,25},{25,17},{2,10},{10... | collective-permute-start | bytes 1572872 | tf_op jit(solution)/shard_map/ppermute | solution.py:800
  167.8 47.6 %collective-permute-start.16 = (bf16[128,2048]{1,0:T(8,128)(2,1)}, bf16[128,2048]{1,0:T(8,128)(2,1)S(1)}, u32[]{:S(2)}, u32[]{:S(2)}) collective-permute-start(bf16[128,2048]{1,0:T(8,128)(2,1)} %after.69.refs_2_.refs_0_), channel_id=1, source_target_pairs={{0,16},{8,24},{16,0},{24,8},{1,17},{9,25},{17,1},{25,9},{2,18},{10... | collective-permute-start | bytes 1572872 | tf_op jit(solution)/shard_map/ppermute | solution.py:800
  168.9 32.8 %collective-permute-start.14 = (bf16[128,2048]{1,0:T(8,128)(2,1)}, bf16[128,2048]{1,0:T(8,128)(2,1)S(1)}, u32[]{:S(2)}, u32[]{:S(2)}) collective-permute-start(bf16[128,2048]{1,0:T(8,128)(2,1)} %after.70.refs_3_.refs_1_), channel_id=1, source_target_pairs={{0,16},{8,24},{16,0},{24,8},{1,17},{9,25},{17,1},{25,9},{2,18},{10... | collective-permute-start | bytes 1572872 | tf_op jit(solution)/shard_map/ppermute | solution.py:800
  188.8 26.5 %collective-permute-start.17 = (bf16[128,2048]{1,0:T(8,128)(2,1)S(1)}, bf16[128,2048]{1,0:T(8,128)(2,1)S(1)}, u32[]{:S(2)}, u32[]{:S(2)}) collective-permute-start(bf16[128,2048]{1,0:T(8,128)(2,1)S(1)} %copy-done), channel_id=1, source_target_pairs={{0,8},{8,0},{16,24},{24,16},{1,9},{9,1},{17,25},{25,17},{2,10},{10... | collective-permute-start | bytes 1572872 | tf_op jit(solution)/shard_map/ppermute | solution.py:800
  229.6 27.5 %collective-permute-start.20 = (bf16[128,2048]{1,0:T(8,128)(2,1)}, bf16[128,2048]{1,0:T(8,128)(2,1)S(1)}, u32[]{:S(2)}, u32[]{:S(2)}) collective-permute-start(bf16[128,2048]{1,0:T(8,128)(2,1)} %after.73.refs_1_), channel_id=1, source_target_pairs={{0,16},{8,24},{16,0},{24,8},{1,17},{9,25},{17,1},{25,9},{2,18},{10... | collective-permute-start | bytes 1572872 | tf_op jit(solution)/shard_map/ppermute | solution.py:800
  276.3 20.6 %collective-permute-start.21 = (bf16[256,2048]{1,0:T(8,128)(2,1)}, bf16[256,2048]{1,0:T(8,128)(2,1)S(1)}, u32[]{:S(2)}, u32[]{:S(2)}) collective-permute-start(bf16[256,2048]{1,0:T(8,128)(2,1)} %convolution_convert_fusion.9.refs_1_), channel_id=1, source_target_pairs={{0,8},{8,0},{16,24},{24,16},{1,9},{9,1},{17,25},{25,17},{2,10},{10... | collective-permute-start | bytes 3145736 | tf_op jit(solution)/shard_map/ppermute | solution.py:800
  277.5 20.7 %collective-permute-start.23 = (bf16[256,2048]{1,0:T(8,128)(2,1)}, bf16[256,2048]{1,0:T(8,128)(2,1)}, u32[]{:S(2)}, u32[]{:S(2)}) collective-permute-start(bf16[256,2048]{1,0:T(8,128)(2,1)} %convolution_convert_fusion.8.refs_2_), channel_id=1, source_target_pairs={{0,16},{8,24},{16,0},{24,8},{1,17},{9,25},{17,1},{25,9},{2,18},{10... | collective-permute-start | bytes 3145736 | tf_op jit(solution)/shard_map/ppermute | solution.py:800
  280.1 565.6 %reduce-scatter.6.cloned.1.call-start = ((), (), s32[]{:S(2)}) async-start(), calls=%async_computation.16 | async-start | bytes 9437184 | tf_op jit(solution)/shard_map/reduce_scatter | solution.py:875
  355.7 20.7 %collective-permute-start.41 = (bf16[256,2048]{1,0:T(8,128)(2,1)}, bf16[256,2048]{1,0:T(8,128)(2,1)S(1)}, u32[]{:S(2)}, u32[]{:S(2)}) collective-permute-start(bf16[256,2048]{1,0:T(8,128)(2,1)} %after.91), channel_id=1, source_target_pairs={{0,8},{8,0},{16,24},{24,16},{1,9},{9,1},{17,25},{25,17},{2,10},{10... | collective-permute-start | bytes 3145736 | tf_op jit(solution)/shard_map/ppermute | solution.py:800
  378.7 81.8 %collective-permute-start.42 = (bf16[128,2048]{1,0:T(8,128)(2,1)}, bf16[128,2048]{1,0:T(8,128)(2,1)}, u32[]{:S(2)}, u32[]{:S(2)}) collective-permute-start(bf16[128,2048]{1,0:T(8,128)(2,1)} %get-tuple-element.197), channel_id=1, source_target_pairs={{0,16},{8,24},{16,0},{24,8},{1,17},{9,25},{17,1},{25,9},{2,18},{10... | collective-permute-start | bytes 1572872 | tf_op jit(solution)/shard_map/ppermute | solution.py:800
  379.8 80.7 %collective-permute-start.44 = (bf16[128,2048]{1,0:T(8,128)(2,1)}, bf16[128,2048]{1,0:T(8,128)(2,1)}, u32[]{:S(2)}, u32[]{:S(2)}) collective-permute-start(bf16[128,2048]{1,0:T(8,128)(2,1)} %get-tuple-element.196), channel_id=1, source_target_pairs={{0,8},{8,0},{16,24},{24,16},{1,9},{9,1},{17,25},{25,17},{2,10},{10... | collective-permute-start | bytes 1572872 | tf_op jit(solution)/shard_map/ppermute | solution.py:800
  414.1 20.3 %collective-permute-start.31 = (bf16[256,2048]{1,0:T(8,128)(2,1)}, bf16[256,2048]{1,0:T(8,128)(2,1)}, u32[]{:S(2)}, u32[]{:S(2)}) collective-permute-start(bf16[256,2048]{1,0:T(8,128)(2,1)} %convolution_convert_fusion.13.refs_1_), channel_id=1, source_target_pairs={{0,8},{8,0},{16,24},{24,16},{1,9},{9,1},{17,25},{25,17},{2,10},{10... | collective-permute-start | bytes 3145736 | tf_op jit(solution)/shard_map/ppermute | solution.py:800
  469.0 22.3 %collective-permute-start.36 = (bf16[128,2048]{1,0:T(8,128)(2,1)S(1)}, bf16[128,2048]{1,0:T(8,128)(2,1)S(1)}, u32[]{:S(2)}, u32[]{:S(2)}) collective-permute-start(bf16[128,2048]{1,0:T(8,128)(2,1)S(1)} %collective-permute-done.35.refs_2_), channel_id=1, source_target_pairs={{0,16},{8,24},{16,0},{24,8},{1,17},{9,25},{17,1},{25,9},{2,18},{10... | collective-permute-start | bytes 1572872 | tf_op jit(solution)/shard_map/ppermute | solution.py:800
  470.9 20.4 %collective-permute-start.38 = (bf16[128,2048]{1,0:T(8,128)(2,1)S(1)}, bf16[128,2048]{1,0:T(8,128)(2,1)S(1)}, u32[]{:S(2)}, u32[]{:S(2)}) collective-permute-start(bf16[128,2048]{1,0:T(8,128)(2,1)S(1)} %collective-permute-done.37.refs_4_), channel_id=1, source_target_pairs={{0,8},{8,0},{16,24},{24,16},{1,9},{9,1},{17,25},{25,17},{2,10},{10... | collective-permute-start | bytes 1572872 | tf_op jit(solution)/shard_map/ppermute | solution.py:800
  494.5 26.3 %collective-permute-start.45 = (bf16[128,2048]{1,0:T(8,128)(2,1)}, bf16[128,2048]{1,0:T(8,128)(2,1)S(1)}, u32[]{:S(2)}, u32[]{:S(2)}) collective-permute-start(bf16[128,2048]{1,0:T(8,128)(2,1)} %after.93.refs_0_), channel_id=1, source_target_pairs={{0,8},{8,0},{16,24},{24,16},{1,9},{9,1},{17,25},{25,17},{2,10},{10... | collective-permute-start | bytes 1572872 | tf_op jit(solution)/shard_map/ppermute | solution.py:800
  495.7 35.8 %collective-permute-start.49 = (bf16[128,2048]{1,0:T(8,128)(2,1)}, bf16[128,2048]{1,0:T(8,128)(2,1)S(1)}, u32[]{:S(2)}, u32[]{:S(2)}) collective-permute-start(bf16[128,2048]{1,0:T(8,128)(2,1)} %after.93.refs_0_), channel_id=1, source_target_pairs={{0,16},{8,24},{16,0},{24,8},{1,17},{9,25},{17,1},{25,9},{2,18},{10... | collective-permute-start | bytes 1572872 | tf_op jit(solution)/shard_map/ppermute | solution.py:800
  497.2 24.5 %collective-permute-start.47 = (bf16[128,2048]{1,0:T(8,128)(2,1)}, bf16[128,2048]{1,0:T(8,128)(2,1)S(1)}, u32[]{:S(2)}, u32[]{:S(2)}) collective-permute-start(bf16[128,2048]{1,0:T(8,128)(2,1)} %after.94.refs_1_), channel_id=1, source_target_pairs={{0,16},{8,24},{16,0},{24,8},{1,17},{9,25},{17,1},{25,9},{2,18},{10... | collective-permute-start | bytes 1572872 | tf_op jit(solution)/shard_map/ppermute | solution.py:800
  497.7 33.8 %collective-permute-start.50 = (bf16[128,2048]{1,0:T(8,128)(2,1)}, bf16[128,2048]{1,0:T(8,128)(2,1)S(1)}, u32[]{:S(2)}, u32[]{:S(2)}) collective-permute-start(bf16[128,2048]{1,0:T(8,128)(2,1)} %after.94.refs_1_), channel_id=1, source_target_pairs={{0,8},{8,0},{16,24},{24,16},{1,9},{9,1},{17,25},{25,17},{2,10},{10... | collective-permute-start | bytes 1572872 | tf_op jit(solution)/shard_map/ppermute | solution.py:800
  543.6 23.4 %collective-permute-start.55 = (bf16[128,2048]{1,0:T(8,128)(2,1)S(1)}, bf16[128,2048]{1,0:T(8,128)(2,1)}, u32[]{:S(2)}, u32[]{:S(2)}) collective-permute-start(bf16[128,2048]{1,0:T(8,128)(2,1)S(1)} %copy-done.59), channel_id=1, source_target_pairs={{0,8},{8,0},{16,24},{24,16},{1,9},{9,1},{17,25},{25,17},{2,10},{10... | collective-permute-start | bytes 1572872 | tf_op jit(solution)/shard_map/ppermute | solution.py:800
  649.0 265.6 %reduce-scatter.8.cloned.1.call-start = ((), (), s32[]{:S(2)}) async-start(), calls=%async_computation.17 | async-start | bytes 4718592 | tf_op jit(solution)/shard_map/reduce_scatter | solution.py:875
  684.3 60.0 %collective-permute-start.60 = (bf16[128,2048]{1,0:T(8,128)(2,1)}, bf16[128,2048]{1,0:T(8,128)(2,1)}, u32[]{:S(2)}, u32[]{:S(2)}) collective-permute-start(bf16[128,2048]{1,0:T(8,128)(2,1)} %get-tuple-element.189), channel_id=1, source_target_pairs={{0,16},{8,24},{16,0},{24,8},{1,17},{9,25},{17,1},{25,9},{2,18},{10... | collective-permute-start | bytes 1572872 | tf_op jit(solution)/shard_map/ppermute | solution.py:800
  685.8 58.5 %collective-permute-start.61 = (bf16[128,2048]{1,0:T(8,128)(2,1)}, bf16[128,2048]{1,0:T(8,128)(2,1)}, u32[]{:S(2)}, u32[]{:S(2)}) collective-permute-start(bf16[128,2048]{1,0:T(8,128)(2,1)} %get-tuple-element.188), channel_id=1, source_target_pairs={{0,8},{8,0},{16,24},{24,16},{1,9},{9,1},{17,25},{25,17},{2,10},{10... | collective-permute-start | bytes 1572872 | tf_op jit(solution)/shard_map/ppermute | solution.py:800
  752.0 34.7 %collective-permute-start.62 = (bf16[128,2048]{1,0:T(8,128)(2,1)S(1)}, bf16[128,2048]{1,0:T(8,128)(2,1)S(1)}, u32[]{:S(2)}, u32[]{:S(2)}) collective-permute-start(bf16[128,2048]{1,0:T(8,128)(2,1)S(1)} %get-tuple-element.73.refs_1_.refs_0_), channel_id=1, source_target_pairs={{0,8},{8,0},{16,24},{24,16},{1,9},{9,1},{17,25},{25,17},{2,10},{10... | collective-permute-start | bytes 1572872 | tf_op jit(solution)/shard_map/ppermute | solution.py:800
  753.7 43.3 %collective-permute-start.66 = (bf16[128,2048]{1,0:T(8,128)(2,1)S(1)}, bf16[128,2048]{1,0:T(8,128)(2,1)S(1)}, u32[]{:S(2)}, u32[]{:S(2)}) collective-permute-start(bf16[128,2048]{1,0:T(8,128)(2,1)S(1)} %get-tuple-element.73.refs_1_.refs_0_), channel_id=1, source_target_pairs={{0,16},{8,24},{16,0},{24,8},{1,17},{9,25},{17,1},{25,9},{2,18},{10... | collective-permute-start | bytes 1572872 | tf_op jit(solution)/shard_map/ppermute | solution.py:800
  754.2 33.3 %collective-permute-start.64 = (bf16[128,2048]{1,0:T(8,128)(2,1)S(1)}, bf16[128,2048]{1,0:T(8,128)(2,1)}, u32[]{:S(2)}, u32[]{:S(2)}) collective-permute-start(bf16[128,2048]{1,0:T(8,128)(2,1)S(1)} %get-tuple-element.74.refs_1_), channel_id=1, source_target_pairs={{0,16},{8,24},{16,0},{24,8},{1,17},{9,25},{17,1},{25,9},{2,18},{10... | collective-permute-start | bytes 1572872 | tf_op jit(solution)/shard_map/ppermute | solution.py:800
  755.7 41.3 %collective-permute-start.67 = (bf16[128,2048]{1,0:T(8,128)(2,1)S(1)}, bf16[128,2048]{1,0:T(8,128)(2,1)}, u32[]{:S(2)}, u32[]{:S(2)}) collective-permute-start(bf16[128,2048]{1,0:T(8,128)(2,1)S(1)} %get-tuple-element.74.refs_1_), channel_id=1, source_target_pairs={{0,8},{8,0},{16,24},{24,16},{1,9},{9,1},{17,25},{25,17},{2,10},{10... | collective-permute-start | bytes 1572872 | tf_op jit(solution)/shard_map/ppermute | solution.py:800
  804.9 20.7 %collective-permute-start.69 = (bf16[256,2048]{1,0:T(8,128)(2,1)}, bf16[256,2048]{1,0:T(8,128)(2,1)S(1)}, u32[]{:S(2)}, u32[]{:S(2)}) collective-permute-start(bf16[256,2048]{1,0:T(8,128)(2,1)} %after.110), channel_id=1, source_target_pairs={{0,16},{8,24},{16,0},{24,8},{1,17},{9,25},{17,1},{25,9},{2,18},{10... | collective-permute-start | bytes 3145736 | tf_op jit(solution)/shard_map/ppermute | solution.py:800
  806.2 20.6 %collective-permute-start.68 = (bf16[256,2048]{1,0:T(8,128)(2,1)}, bf16[256,2048]{1,0:T(8,128)(2,1)S(1)}, u32[]{:S(2)}, u32[]{:S(2)}) collective-permute-start(bf16[256,2048]{1,0:T(8,128)(2,1)} %after.109), channel_id=1, source_target_pairs={{0,8},{8,0},{16,24},{24,16},{1,9},{9,1},{17,25},{25,17},{2,10},{10... | collective-permute-start | bytes 3145736 | tf_op jit(solution)/shard_map/ppermute | solution.py:800
  845.7 33.8 %all-to-all-start.2 = ((bf16[4,64,2048]{2,1,0:T(8,128)(2,1)}), bf16[4,64,2048]{2,1,0:T(8,128)(2,1)S(1)}, u32[]{:S(2)}, u32[]{:S(2)}) async-start(bf16[4,64,2048]{2,1,0:T(8,128)(2,1)} %bitcast.284), calls=%async_computation.3 | async-start | bytes 2097152 | tf_op jit(solution)/shard_map/all_to_all | solution.py:867
  849.2 160.4 %reduce-scatter.10.cloned.1.call-start = ((), (), s32[]{:S(2)}) async-start(), calls=%async_computation.18 | async-start | bytes 4718592 | tf_op jit(solution)/shard_map/reduce_scatter | solution.py:875
  893.8 160.9 %reduce-scatter.12.cloned.1.call-start = ((), (), s32[]{:S(2)}) async-start(), calls=%async_computation.19 | async-start | bytes 5898240 | tf_op jit(solution)/shard_map/reduce_scatter | solution.py:875
  893.8 20.7 %collective-permute-start.72 = (bf16[256,2048]{1,0:T(8,128)(2,1)}, bf16[256,2048]{1,0:T(8,128)(2,1)S(1)}, u32[]{:S(2)}, u32[]{:S(2)}) collective-permute-start(bf16[256,2048]{1,0:T(8,128)(2,1)} %after.112), channel_id=1, source_target_pairs={{0,8},{8,0},{16,24},{24,16},{1,9},{9,1},{17,25},{25,17},{2,10},{10... | collective-permute-start | bytes 3145736 | tf_op jit(solution)/shard_map/ppermute | solution.py:800
  932.7 186.5 %reduce-scatter.14.cloned.1.call-start = ((), (), s32[]{:S(2)}) async-start(), calls=%async_computation.20 | async-start | bytes 6488064 | tf_op jit(solution)/shard_map/reduce_scatter | solution.py:875
  1046.3 33.1 %collective-permute-start.76 = (bf16[256,2048]{1,0:T(8,128)(2,1)}, bf16[256,2048]{1,0:T(8,128)(2,1)}, u32[]{:S(2)}, u32[]{:S(2)}) collective-permute-start(bf16[256,2048]{1,0:T(8,128)(2,1)} %fusion.11.refs_1_), channel_id=1, source_target_pairs={{0,8},{8,0},{16,24},{24,16},{1,9},{9,1},{17,25},{25,17},{2,10},{10... | collective-permute-start | bytes 3145736 | tf_op jit(solution)/shard_map/ppermute | solution.py:800
  1051.6 27.8 %collective-permute-start.78 = (bf16[256,2048]{1,0:T(8,128)(2,1)}, bf16[256,2048]{1,0:T(8,128)(2,1)}, u32[]{:S(2)}, u32[]{:S(2)}) collective-permute-start(bf16[256,2048]{1,0:T(8,128)(2,1)} %fusion.12.refs_2_), channel_id=1, source_target_pairs={{0,16},{8,24},{16,0},{24,8},{1,17},{9,25},{17,1},{25,9},{2,18},{10... | collective-permute-start | bytes 3145736 | tf_op jit(solution)/shard_map/ppermute | solution.py:800
  (269 other events, 3140.5 us)
Sparse Core Ops, SparseCore 0:
  43.4 34.6 all-gather.6
  80.3 58.9 all-gather.8
  141.6 36.9 all-gather.10
  180.6 46.0 all-gather.12
  228.1 80.7 all-gather.14
  310.3 45.6 all-gather.16
  649.1 90.0 reduce-scatter.5
  741.5 48.3 reduce-scatter.7
  893.9 50.9 reduce-scatter.9
  947.1 58.0 reduce-scatter.11
  1029.1 64.8 reduce-scatter.13

commit v4 on v3

--- a/solution.py
+++ b/solution.py
@@ -27,6 +27,10 @@
 ROPE_BASE = 10000.0
 
 
+def work(us):
+    return pl.CostEstimate(flops=int(us * 1150000000), bytes_accessed=0, transcendentals=0)
+
+
 def lanes_iota(shape):
     return lax.broadcasted_iota(jnp.int32, shape, 1)
 
@@ -60,12 +64,16 @@
     return step, rate, decay, total, pre
 
 
-def convolve(ubuf, aux_ref, conv_ref, lanes):
+def over_lanes(column):
+    return jnp.broadcast_to(column, (column.shape[0], 128))
+
+
+def convolve(ubuf, near, conv_ref, lanes):
     acc = conv_ref[CONV : CONV + 1, lanes] + conv_ref[CONV - 1 : CONV, lanes] * ubuf[8 : 8 + SPAN, lanes]
     for offset in range(1, CONV):
         shifted = ubuf[8 - offset : 8 - offset + SPAN, lanes]
         weight = conv_ref[CONV - 1 - offset : CONV - offset, lanes]
-        acc = acc + weight * shifted * aux_ref[:, 2 + offset : 3 + offset]
+        acc = acc + weight * (shifted * near[offset])
     return acc
 
 
@@ -101,9 +109,10 @@
 
     ubuf[0:8, :] = ubuf[SPAN : SPAN + 8, :]
     ubuf[8 : 8 + SPAN, :] = first_ref[:, :width].astype(f32)
+    near = [None] + [over_lanes(aux_ref[:, 2 + offset : 3 + offset]) for offset in range(1, CONV)]
     for lane in range(0, width, 128):
         lanes = slice(lane, lane + 128)
-        pre = convolve(ubuf, aux_ref, conv_ref, lanes)
+        pre = convolve(ubuf, near, conv_ref, lanes)
         taps[:, lanes] = (pre * jax.nn.sigmoid(pre)).astype(bf16)
     step, rate, decay, total, unused = head_steps(first_ref[:, width:], head_ref, heads)
     total_rows = total.T
@@ -113,8 +122,7 @@
     c_rows = taps[:, inner + STATE :]
     b_cols = b_rows.astype(f32).T.astype(bf16)
     scores = dot_last(c_rows, b_rows)
-    carry_keep = aux_ref[:, 1:2]
-    end_keep = aux_ref[:, 2:3]
+    carry_keep, end_keep = over_lanes(aux_ref[:, 1:2]), over_lanes(aux_ref[:, 2:3])
     for pair in range(heads // 2):
         lanes = slice(pair * 128, pair * 128 + 128)
         sum_one, sum_two, sums = pair_of(total, 2 * pair, low_lanes)
@@ -139,6 +147,11 @@
         weighted = (jnp.exp(last - sums) * end_keep * stepped.astype(f32)).astype(bf16)
         kept = jnp.exp(last) * aux_ref[SPAN - 1 : SPAN, 1:2]
         state[:, lanes] = held * kept + dot_plain(b_cols, weighted)
+
+
+def halves_of(values):
+    high = values.astype(jnp.bfloat16)
+    return [high, (values - high.astype(jnp.float32)).astype(jnp.bfloat16)]
 
 
 def ssd_backward_kernel(
@@ -178,9 +191,10 @@
     ubuf[0:8, :] = before_ref[8:16, :width].astype(f32)
     ubuf[8 : 8 + SPAN, :] = first_ref[:, :width].astype(f32)
     gbuf[SPAN : SPAN + 8, :] = gbuf[0:8, :]
+    near = [None] + [over_lanes(aux_ref[:, 2 + offset : 3 + offset]) for offset in range(1, CONV)]
     for lane in range(0, width, 128):
         lanes = slice(lane, lane + 128)
-        pre = convolve(ubuf, aux_ref, conv_ref, lanes)
+        pre = convolve(ubuf, near, conv_ref, lanes)
         sig = jax.nn.sigmoid(pre)
         taps[:, lanes] = (pre * sig).astype(bf16)
         slope[:, lanes] = sig * (1.0 + pre * (1.0 - sig))
@@ -189,13 +203,13 @@
     square = (SPAN, SPAN)
     low_lanes = lanes_iota((SPAN, 128)) < SSM_DIM
     low_row = lanes_iota((1, 128)) < SSM_DIM
+    head_row = lanes_iota((1, 128))
     same = (aux_ref[:, 0:1] == seg_ref[0]) & (rows_iota(square) >= lanes_iota(square))
     b_rows = taps[:, inner : inner + STATE]
     c_rows = taps[:, inner + STATE :]
     c_cols = c_rows.astype(f32).T.astype(bf16)
     scores = dot_last(c_rows, b_rows)
-    carry_keep = aux_ref[:, 1:2]
-    end_keep = aux_ref[:, 2:3]
+    carry_keep, end_keep = over_lanes(aux_ref[:, 1:2]), over_lanes(aux_ref[:, 2:3])
     head_lane = lanes_iota((SPAN, 128))
     is_last = rows_iota((SPAN, 1)) == SPAN - 1
     grad_scores = jnp.zeros(square, f32)
@@ -250,16 +264,13 @@
         dstate[:, lanes] = dheld * kept + dot_plain(c_cols, grown_dy)
         gaps = dy * y - stepped_wide * grad_in
         by_step = x * grad_in
-        for half in range(2):
-            keep = low_lanes if half == 0 else ~low_lanes
-            keep_row = low_row if half == 0 else ~low_row
-            end_sum = jnp.sum(jnp.where(keep_row, ends, 0.0), axis=1, keepdims=True)
-            gap_sum = jnp.sum(jnp.where(keep, gaps, 0.0), axis=1, keepdims=True)
-            gap_sum = gap_sum + jnp.where(is_last, end_sum, 0.0)
-            step_sum = jnp.sum(jnp.where(keep, by_step, 0.0), axis=1, keepdims=True)
-            here = head_lane == 2 * pair + half
-            grad_total = jnp.where(here, gap_sum, grad_total)
-            grad_step = jnp.where(here, step_sum, grad_step)
+        ends_one = jnp.sum(jnp.where(low_row, ends, 0.0), axis=1, keepdims=True)
+        ends_two = jnp.sum(jnp.where(low_row, 0.0, ends), axis=1, keepdims=True)
+        ends_here = jnp.where(head_row == 2 * pair, ends_one, jnp.where(head_row == 2 * pair + 1, ends_two, 0.0))
+        of_head = (lanes_iota(square) == 2 * pair + rows_iota(square) // SSM_DIM).astype(bf16)
+        by_head = dot_plain(jnp.concatenate(halves_of(gaps) + halves_of(by_step), axis=0), of_head)
+        grad_total = grad_total + by_head[:SPAN] + by_head[SPAN : 2 * SPAN] + jnp.where(is_last, ends_here, 0.0)
+        grad_step = grad_step + by_head[2 * SPAN : 3 * SPAN] + by_head[3 * SPAN :]
         skip = skip_ref[0:1, lanes]
         skip_grad_ref[0:1, lanes] += jnp.sum(dy * x, axis=0, keepdims=True)
         gbuf[0:SPAN, lanes] = (steps * grad_in + skip * dy) * slope[:, lanes]
@@ -277,6 +288,7 @@
     head_grad_ref[0:1, :] += jnp.sum(grad_decay * decay, axis=0, keepdims=True)
     head_grad_ref[1:2, :] += jnp.sum(grad_pre, axis=0, keepdims=True)
 
+    ahead = [None] + [over_lanes(aux_ref[:, 5 + offset : 6 + offset]) for offset in range(1, CONV)]
     for lane in range(0, width, 128):
         lanes = slice(lane, lane + 128)
         grad = gbuf[0:SPAN, lanes]
@@ -285,9 +297,9 @@
         acc = conv_ref[CONV - 1 : CONV, lanes] * grad
         for offset in range(1, CONV):
             at = CONV - 1 - offset
-            shifted = ubuf[8 - offset : 8 - offset + SPAN, lanes] * aux_ref[:, 2 + offset : 3 + offset]
+            shifted = ubuf[8 - offset : 8 - offset + SPAN, lanes] * near[offset]
             conv_grad_ref[at : at + 1, lanes] += jnp.sum(grad * shifted, axis=0, keepdims=True)
-            later = gbuf[offset : offset + SPAN, lanes] * aux_ref[:, 5 + offset : 6 + offset]
+            later = gbuf[offset : offset + SPAN, lanes] * ahead[offset]
             acc = acc + conv_ref[at : at + 1, lanes] * later
         grad_ref[:, lanes] = acc.astype(bf16)
 
@@ -347,9 +359,7 @@
         compiler_params=pltpu.CompilerParams(
             dimension_semantics=("arbitrary",), vmem_limit_bytes=VMEM_BYTES
         ),
-        cost_estimate=pl.CostEstimate(
-            flops=8_000_000_000 * heads // 12, bytes_accessed=12_000_000, transcendentals=4_000_000
-        ),
+        cost_estimate=work(15),
         name="ssd_forward",
     )(order, first, aux, seg_rows, conv, head, skip)
 
@@ -404,9 +414,7 @@
         compiler_params=pltpu.CompilerParams(
             dimension_semantics=("arbitrary",), vmem_limit_bytes=VMEM_BYTES
         ),
-        cost_estimate=pl.CostEstimate(
-            flops=30_000_000_000 * heads // 12, bytes_accessed=16_000_000, transcendentals=5_000_000
-        ),
+        cost_estimate=work(53),
         name="ssd_backward",
     )(order, first, first, aux, seg_rows, conv, head, skip, starts, dy)
 
@@ -538,9 +546,7 @@
         ],
         scratch_shapes=[pltpu.VMEM((length, HEAD_DIM), jnp.bfloat16), pltpu.VMEM((length, HEAD_DIM), jnp.bfloat16)],
         compiler_params=pltpu.CompilerParams(vmem_limit_bytes=VMEM_BYTES),
-        cost_estimate=pl.CostEstimate(
-            flops=2_000_000_000 * query_heads, bytes_accessed=4_000_000, transcendentals=1_000_000
-        ),
+        cost_estimate=work(5),
         name="attend_forward",
     )(order, early, tables[0], tables[1], aux, seg_row)
 
@@ -558,9 +564,7 @@
             pltpu.VMEM((length, HEAD_DIM), jnp.float32),
         ],
         compiler_params=pltpu.CompilerParams(vmem_limit_bytes=VMEM_BYTES),
-        cost_estimate=pl.CostEstimate(
-            flops=4_000_000_000 * query_heads, bytes_accessed=6_000_000, transcendentals=1_000_000
-        ),
+        cost_estimate=work(7),
         name="attend_backward",
     )(order, early, tables[0], tables[1], aux, seg_row, lse, grad)
 
@@ -609,12 +613,8 @@
     return [array[:, lane : lane + 128] for lane in range(0, array.shape[1], 128)]
 
 
-def add_arrived(split, own, arrived):
+def add_arrived(own, arrived):
     total = own[...]
-    if split:
-        first = pl.program_id(0) == 0
-        one, one_late, two, two_late = (ref[...].astype(jnp.float32) for ref in arrived)
-        return total + jnp.where(first, one + one_late, two + two_late)
     for ref in arrived:
         total = total + ref[...].astype(jnp.float32)
     return total
@@ -627,29 +627,20 @@
     return jnp.sum(total, axis=1, keepdims=True)
 
 
-def store_block(blocks, value):
-    for block, out in enumerate(blocks):
-
-        @pl.when(pl.program_id(0) == block)
-        def _(out=out):
-            out[...] = value
-
-
-def middle_kernel(split, places, count, own, rows, gain, *refs):
-    arrived, outs = refs[:count], refs[count:]
-    blocks, middle_ref = outs[: places[3]], outs[places[3]]
-    middle = rows[...].astype(jnp.float32) + add_arrived(split, own, arrived)
+def middle_kernel(places, count, skip, own, rows, gain, *refs):
+    arrived, (hidden_ref, middle_ref) = refs[:count], refs[count + skip :]
+    middle = rows[...].astype(jnp.float32) + add_arrived(own, arrived)
     middle_ref[...] = middle
     mean = jnp.sum(middle * middle, axis=1, keepdims=True) / middle.shape[1]
     hidden = middle * lax.rsqrt(mean + EPSILON) * gain[0:1, :]
-    moved = jnp.concatenate(to_gathered_tiles(tiles_of(hidden), *places[:3]), axis=1).astype(jnp.bfloat16)
-    store_block(blocks, moved)
-
-
-def norm_back_kernel(split, places, count, skip, in_blocks, own, rows, passed, gain, *refs):
+    moved = to_gathered_tiles(tiles_of(hidden), *places)
+    hidden_ref[...] = jnp.concatenate(moved, axis=1).astype(jnp.bfloat16)
+
+
+def norm_back_kernel(places, count, skip, keep_wide, own, rows, passed, gain, *refs):
     arrived, outs = refs[:count], refs[count + skip :]
-    grads = add_arrived(split, own, arrived)
-    grads = jnp.concatenate(from_gathered_tiles(tiles_of(grads), *places[:3]), axis=1)
+    grads = add_arrived(own, arrived)
+    grads = jnp.concatenate(from_gathered_tiles(tiles_of(grads), *places), axis=1)
     wide = rows[...].astype(jnp.float32)
     width = wide.shape[1]
     scale = lax.rsqrt(jnp.sum(wide * wide, axis=1, keepdims=True) / width + EPSILON)
@@ -657,11 +648,9 @@
     weighted = grads * gain[0:1, :]
     mean = jnp.sum(weighted * normed, axis=1, keepdims=True) / width
     total = passed[...].astype(jnp.float32) + scale * (weighted - normed * mean)
-    if in_blocks:
-        store_block(outs[: places[3]], total.astype(jnp.bfloat16))
-        outs[-2][...] = total
-    else:
-        outs[0][...] = total.astype(jnp.bfloat16)
+    outs[0][...] = total.astype(jnp.bfloat16)
+    if keep_wide:
+        outs[1][...] = total
     gain_grad = outs[-1]
 
     @pl.when(pl.program_id(0) == 0)
@@ -671,24 +660,27 @@
     gain_grad[0:1, :] += jnp.sum(normed * grads, axis=0, keepdims=True)
 
 
-def rows_call(kernel, tokens, width, split, inputs, gain, arrived, outs, deps, name):
+def add_rows_kernel(count, own, rows, gain, *refs):
+    refs[-1][...] = (rows[...] + add_arrived(own, refs[:count])).astype(refs[-1].dtype)
+
+
+def rows_call(kernel, tokens, width, inputs, gain, arrived, outs, deps, name):
     block = pl.BlockSpec((SPAN, width), lambda i: (i, 0))
     whole = pl.BlockSpec((8, width), lambda i: (0, 0))
-    fixed = pl.BlockSpec((SPAN, width), lambda i: (0, 0))
-    out_specs = [whole if shape[0] == 8 else fixed if shape[0] == SPAN else block for shape, dtype in outs]
+    out_specs = [whole if shape[0] == 8 else block for shape, dtype in outs]
     return pl.pallas_call(
         kernel,
         grid=(tokens // SPAN,),
         in_specs=[block] * len(inputs)
         + [whole]
-        + [fixed if split else block] * len(arrived)
+        + [block] * len(arrived)
         + [pl.BlockSpec(memory_space=pl.ANY)] * len(deps),
         out_specs=out_specs,
         out_shape=[jax.ShapeDtypeStruct(shape, dtype) for shape, dtype in outs],
         compiler_params=pltpu.CompilerParams(
             dimension_semantics=("arbitrary",), vmem_limit_bytes=VMEM_BYTES
         ),
-        cost_estimate=pl.CostEstimate(flops=40 * tokens * width, bytes_accessed=20 * tokens * width, transcendentals=0),
+        cost_estimate=work(5),
         name=name,
     )(*inputs, gain, *arrived, *deps)
 
@@ -704,29 +696,34 @@
             out[...] = (wide * lax.rsqrt(mean + EPSILON) * gain[0:1, :]).astype(jnp.bfloat16)
 
 
-def norm_pieces(pieces, gain):
+def norm_pieces(pieces, spots, gain):
     width = pieces[0].shape[1]
-    length = len(pieces) * SPAN
+    length = len(spots) * SPAN
     return pl.pallas_call(
         norm_pieces_kernel,
-        grid=(len(pieces),),
+        grid=(len(spots),),
         in_specs=[pl.BlockSpec((8, width), lambda i: (0, 0))]
-        + [pl.BlockSpec((SPAN, width), lambda i: (0, 0)) for piece in pieces],
+        + [pl.BlockSpec((SPAN, width), functools.partial(lambda half, i: (half, 0), half)) for piece, half in spots],
         out_specs=pl.BlockSpec((SPAN, width), lambda i: (i, 0)),
         out_shape=jax.ShapeDtypeStruct((length, width), jnp.bfloat16),
         compiler_params=pltpu.CompilerParams(
             dimension_semantics=("arbitrary",), vmem_limit_bytes=VMEM_BYTES
         ),
-        cost_estimate=pl.CostEstimate(flops=6 * length * width, bytes_accessed=4 * length * width, transcendentals=0),
+        cost_estimate=work(5),
         name="norm_pieces",
-    )(gain, *pieces)
-
-
-def assemble_kernel(count, *refs):
+    )(gain, *[pieces[piece] for piece, half in spots])
+
+
+def assemble_kernel(count, spots, *refs):
     pieces, out, held, sems = refs[:count], refs[-3], refs[-2], refs[-1]
-    places = [pl.ds(block * SPAN, SPAN) for block in range(count)]
-    loads = [pltpu.make_async_copy(pieces[b], held.at[places[b]], sems.at[0, b]) for b in range(count)]
-    stores = [pltpu.make_async_copy(held.at[places[b]], out.at[places[b]], sems.at[1, b]) for b in range(count)]
+    places = [pl.ds(block * SPAN, SPAN) for block in range(len(spots))]
+    loads = [
+        pltpu.make_async_copy(pieces[piece].at[places[half]], held.at[places[b]], sems.at[0, b])
+        for b, (piece, half) in enumerate(spots)
+    ]
+    stores = [
+        pltpu.make_async_copy(held.at[places[b]], out.at[places[b]], sems.at[1, b]) for b in range(len(spots))
+    ]
     for load in loads:
         load.start()
     for load, store in zip(loads, stores):
@@ -736,47 +733,197 @@
         store.wait()
 
 
-def assemble(pieces, *deps):
+def assemble(pieces, spots):
     width = pieces[0].shape[1]
-    length = len(pieces) * SPAN
+    length = len(spots) * SPAN
     return pl.pallas_call(
-        functools.partial(assemble_kernel, len(pieces)),
-        in_specs=[pl.BlockSpec(memory_space=pl.ANY)] * (len(pieces) + len(deps)),
+        functools.partial(assemble_kernel, len(pieces), spots),
+        in_specs=[pl.BlockSpec(memory_space=pl.ANY)] * len(pieces),
         out_specs=pl.BlockSpec(memory_space=pl.ANY),
         out_shape=jax.ShapeDtypeStruct((length, width), pieces[0].dtype),
         scratch_shapes=[
             pltpu.VMEM((length, width), pieces[0].dtype),
-            pltpu.SemaphoreType.DMA((2, len(pieces))),
+            pltpu.SemaphoreType.DMA((2, len(spots))),
         ],
         compiler_params=pltpu.CompilerParams(vmem_limit_bytes=VMEM_BYTES),
-        cost_estimate=pl.CostEstimate(flops=0, bytes_accessed=4 * length * width, transcendentals=0),
+        cost_estimate=work(3),
         name="assemble",
-    )(*pieces, *deps)
-
-
-def gathered_blocks_kernel(places, rows, *outs):
-    for block, out in enumerate(outs):
-
-        @pl.when(pl.program_id(0) == block)
-        def _(out=out):
-            moved = to_gathered_tiles(tiles_of(rows[...].astype(jnp.float32)), *places)
-            out[...] = jnp.concatenate(moved, axis=1).astype(out.dtype)
-
-
-def gathered_blocks(rows, places):
+    )(*pieces)
+
+
+def start_rows_kernel(places, halves, rows, cot, out):
+    @pl.when(pl.program_id(0) < halves)
+    def _():
+        moved = to_gathered_tiles(tiles_of(rows[...].astype(jnp.float32)), *places)
+        out[...] = jnp.concatenate(moved, axis=1).astype(out.dtype)
+
+    @pl.when(pl.program_id(0) >= halves)
+    def _():
+        out[...] = cot[...]
+
+
+def start_rows(rows, cot, places):
     tokens, width = rows.shape
-    blocks = tokens // SPAN
+    halves = tokens // SPAN
+
     return pl.pallas_call(
-        functools.partial(gathered_blocks_kernel, places),
-        grid=(blocks,),
-        in_specs=[pl.BlockSpec((SPAN, width), lambda i: (i, 0))],
-        out_specs=[pl.BlockSpec((SPAN, width), lambda i: (0, 0))] * blocks,
-        out_shape=[jax.ShapeDtypeStruct((SPAN, width), rows.dtype)] * blocks,
+        functools.partial(start_rows_kernel, places, halves),
+        grid=(2 * halves,),
+        in_specs=[
+            pl.BlockSpec((SPAN, width), lambda i: (jnp.minimum(i, halves - 1), 0)),
+            pl.BlockSpec((SPAN, width), lambda i: (jnp.maximum(i - halves, 0), 0)),
+        ],
+        out_specs=pl.BlockSpec((SPAN, width), lambda i: (i, 0)),
+        out_shape=jax.ShapeDtypeStruct((2 * tokens, width), rows.dtype),
         compiler_params=pltpu.CompilerParams(
             dimension_semantics=("arbitrary",), vmem_limit_bytes=VMEM_BYTES
         ),
-        cost_estimate=pl.CostEstimate(flops=4 * tokens * width, bytes_accessed=4 * tokens * width, transcendentals=0),
-        name="gathered_blocks",
+        cost_estimate=work(2),
+        name="start_rows",
+    )(rows, cot)
+
+
+def product_kernel(back, pairs, skip, sets, *refs):
+    lefts, rights, outs = refs[:pairs], refs[pairs : 2 * pairs], refs[2 * pairs + skip :]
+    blocks = lefts[0].shape[0] // SPAN
+    where = {block: (out, place) for out, held in enumerate(sets) for place, block in enumerate(held)}
+    for block in range(0, blocks, 2):
+        total = None
+        for left, right in zip(lefts, rights):
+            rows = left[block * SPAN : (block + 2) * SPAN, :]
+            part = dot_last(rows, right[...]) if back else dot_plain(rows, right[...])
+            total = part if total is None else total + part
+        for half in range(2):
+            out, place = where[block + half]
+            part = total[half * SPAN : (half + 1) * SPAN, :]
+            outs[out][place * SPAN : (place + 1) * SPAN, :] = part.astype(outs[out].dtype)
+
+
+def product_rows(lefts, rights, back, sets, dtypes, deps=()):
+    length = lefts[0].shape[0]
+    width = rights[0].shape[0 if back else 1]
+    slab = 512
+    specs = [pl.BlockSpec(left.shape, lambda n: (0, 0)) for left in lefts]
+    for right in rights:
+        if back:
+            specs.append(pl.BlockSpec((slab, right.shape[1]), lambda n: (n, 0)))
+        else:
+            specs.append(pl.BlockSpec((right.shape[0], slab), lambda n: (0, n)))
+    return pl.pallas_call(
+        functools.partial(product_kernel, back, len(lefts), len(deps), sets),
+        grid=(width // slab,),
+        in_specs=specs + [pl.BlockSpec(memory_space=pl.ANY)] * len(deps),
+        out_specs=[pl.BlockSpec((len(held) * SPAN, slab), lambda n: (0, n)) for held in sets],
+        out_shape=[
+            jax.ShapeDtypeStruct((len(held) * SPAN, width), dtype) for held, dtype in zip(sets, dtypes)
+        ],
+        compiler_params=pltpu.CompilerParams(
+            dimension_semantics=("arbitrary",), vmem_limit_bytes=VMEM_BYTES
+        ),
+        cost_estimate=work(sum(2 * length * left.shape[1] * width for left in lefts) / 0.66e9),
+        name="product_rows",
+    )(*lefts, *rights, *deps)
+
+
+def feed_kernel(units, slab, hidden, cot, gate_w, up_w, down_w, act_ref, grad_ref):
+    here = pl.multiple_of(pl.program_id(0) * slab, slab)
+    for row in range(0, hidden.shape[0], 256):
+        rows = slice(row, row + 256)
+        gate_pre = dot_plain(hidden[rows, :], gate_w[...])
+        up_pre = dot_plain(hidden[rows, :], up_w[...])
+        grad_act = dot_last(cot[rows, :], down_w[...])
+        sig = jax.nn.sigmoid(gate_pre)
+        silu = gate_pre * sig
+        act_ref[rows, :] = (silu * up_pre).astype(jnp.bfloat16)
+        grad_gate = grad_act * up_pre * sig * (1.0 + gate_pre * (1.0 - sig))
+        grad_ref[rows, pl.ds(here, slab)] = grad_gate.astype(jnp.bfloat16)
+        grad_ref[rows, pl.ds(units + here, slab)] = (grad_act * silu).astype(jnp.bfloat16)
+
+
+def feed_products(hidden, cot, gate_up_w, down_w):
+    length, width = hidden.shape
+    units = down_w.shape[0]
+    slab = min(256, units)
+    steps = units // slab
+    whole = pl.BlockSpec((length, width), lambda n: (0, 0))
+    return pl.pallas_call(
+        functools.partial(feed_kernel, units, slab),
+        grid=(steps,),
+        in_specs=[
+            whole,
+            whole,
+            pl.BlockSpec((width, slab), lambda n: (0, n)),
+            pl.BlockSpec((width, slab), lambda n: (0, steps + n)),
+            pl.BlockSpec((slab, width), lambda n: (n, 0)),
+        ],
+        out_specs=[
+            pl.BlockSpec((length, slab), lambda n: (0, n)),
+            pl.BlockSpec((length, 2 * units), lambda n: (0, 0)),
+        ],
+        out_shape=[
+            jax.ShapeDtypeStruct((length, units), jnp.bfloat16),
+            jax.ShapeDtypeStruct((length, 2 * units), jnp.bfloat16),
+        ],
+        compiler_params=pltpu.CompilerParams(
+            dimension_semantics=("arbitrary",), vmem_limit_bytes=VMEM_BYTES
+        ),
+        cost_estimate=work(6 * length * width * units / 0.6e9),
+        name="feed_products",
+    )(hidden, cot, gate_up_w, gate_up_w, down_w)
+
+
+def sums_kernel(pairs, before, skip, *refs):
+    out = refs[-1]
+    total = refs[2 * pairs][...] if before else None
+    for left, right in zip(refs[:pairs], refs[pairs : 2 * pairs]):
+        part = dot_first(left[...], right[...])
+        total = part if total is None else total + part
+    out[...] = total.astype(out.dtype)
+
+
+def weight_sums(lefts, rights, dtype, before=None, deps=()):
+    length, rows = lefts[0].shape
+    columns = rights[0].shape[1]
+    wide = columns if columns <= 1408 else 1024
+    tall = next(t for t in (1024, 768, 512, 384, 256, 128) if rows % t == 0 and t * wide <= 1024 * 1024)
+    block = pl.BlockSpec((tall, wide), lambda i, j: (i, j))
+    extra = [] if before is None else [before]
+    return pl.pallas_call(
+        functools.partial(sums_kernel, len(lefts), len(extra), len(deps)),
+        grid=(rows // tall, columns // wide),
+        in_specs=[pl.BlockSpec((length, tall), lambda i, j: (0, i)) for left in lefts]
+        + [pl.BlockSpec((length, wide), lambda i, j: (0, j)) for right in rights]
+        + [block] * len(extra)
+        + [pl.BlockSpec(memory_space=pl.ANY)] * len(deps),
+        out_specs=block,
+        out_shape=jax.ShapeDtypeStruct((rows, columns), dtype),
+        compiler_params=pltpu.CompilerParams(
+            dimension_semantics=("arbitrary", "arbitrary"), vmem_limit_bytes=VMEM_BYTES
+        ),
+        cost_estimate=work(sum(2 * length * rows * columns for left in lefts) / 0.66e9),
+        name="weight_sums",
+    )(*lefts, *rights, *extra, *deps)
+
+
+def gathered_rows_kernel(places, rows, out):
+    moved = to_gathered_tiles(tiles_of(rows[...].astype(jnp.float32)), *places)
+    out[...] = jnp.concatenate(moved, axis=1).astype(out.dtype)
+
+
+def gathered_rows(rows, places):
+    tokens, width = rows.shape
+    block = pl.BlockSpec((SPAN, width), lambda i: (i, 0))
+    return pl.pallas_call(
+        functools.partial(gathered_rows_kernel, places),
+        grid=(tokens // SPAN,),
+        in_specs=[block],
+        out_specs=block,
+        out_shape=jax.ShapeDtypeStruct((tokens, width), rows.dtype),
+        compiler_params=pltpu.CompilerParams(
+            dimension_semantics=("arbitrary",), vmem_limit_bytes=VMEM_BYTES
+        ),
+        cost_estimate=work(1.5),
+        name="gathered_rows",
     )(rows)
 
 
@@ -800,57 +947,28 @@
     return lax.ppermute(value, "seq", peers(lax.axis_size("seq"), flip))
 
 
-def balanced(tokens):
-    return lax.axis_size("seq") == 4 and tokens == 2 * SPAN
+def block_order(tokens):
+    return [(flip, half) for flip in range(lax.axis_size("seq")) for half in range(tokens // SPAN)]
 
 
 def block_places(tokens):
-    index = lax.axis_index("seq")
     halves = tokens // SPAN
     blocks = jnp.arange(lax.axis_size("seq") * halves, dtype=jnp.int32)
-    place = (blocks // halves) ^ index
-    place = place * halves + blocks % halves
-    if balanced(tokens):
-        place = jnp.array([0, 1, 2, 7, 6, 4, 3, 5], jnp.int32)[place]
-    return place
-
-
-def fetch_tokens(halves):
-    if balanced(len(halves) * SPAN):
-        a, b = halves
-        one_a, two_b = swap(a, 1), swap(b, 2)
-        three_a, three_b = swap(one_a, 2), swap(two_b, 1)
-        one_b, two_a = swap(b, 1), swap(a, 2)
-        return [a, b, one_a, three_a, two_b, three_b, two_a, one_b]
-    return list(halves) + [swap(half, flip) for flip in range(1, lax.axis_size("seq")) for half in halves]
-
-
-def scatter_tokens(product, tokens, hold=()):
+    return ((blocks // halves) ^ lax.axis_index("seq")) * halves + blocks % halves
+
+
+def fetch_tokens(rows):
+    return [rows] + [swap(rows, flip) for flip in range(1, lax.axis_size("seq"))]
+
+
+def scatter_tokens(lefts, rights, back, tokens, hold=(), deps=()):
     f32, bf16 = jnp.float32, jnp.bfloat16
-
-    def held(part):
-        return after(part, *hold) if hold else part
-
-    if balanced(tokens):
-        to_one = product(tokens, 2 * tokens).astype(bf16)
-        from_one = swap(held(to_one), 1)
-        to_two = product(2 * tokens, 3 * tokens).astype(bf16)
-        from_two = swap(held(to_two), 2)
-        second = product(3 * tokens, 4 * tokens, to_one, to_two)
-        own = product(0, tokens, to_one, to_two)
-        two_a = (second[:SPAN] + from_one[SPAN:].astype(f32)).astype(bf16)
-        one_b = (second[SPAN:] + from_two[SPAN:].astype(f32)).astype(bf16)
-        return own, (from_one, swap(two_a, 2), from_two, swap(one_b, 1)), (to_one, to_two, second, own)
-    sent = [
-        product(flip * tokens, (flip + 1) * tokens).astype(bf16) for flip in range(1, lax.axis_size("seq"))
-    ]
-    own = product(0, tokens, *sent)
-    return own, tuple(swap(held(part), flip + 1) for flip, part in enumerate(sent)), (*sent, own)
-
-
-def cut_rows(whole, start, end, deps):
-    part = whole[start:end]
-    return after(part, *deps) if deps else part
+    halves = tokens // SPAN
+    count = lax.axis_size("seq")
+    sets = tuple(tuple(range(flip * halves, (flip + 1) * halves)) for flip in range(count))
+    own, *parts = product_rows(lefts, rights, back, sets, (f32,) + (bf16,) * (count - 1), deps)
+    arrived = [swap(after(part, *hold) if hold else part, flip + 1) for flip, part in enumerate(parts)]
+    return own, tuple(arrived), tuple(parts)
 
 
 def add_small(vector):
@@ -948,17 +1066,18 @@
         axis=2,
     )
     halves = tokens // SPAN
-    places = (rows, seq, fsdp, halves)
-    mine = gathered_blocks(inputs[0, 0], places[:3])
+    places = (rows, seq, fsdp)
+    spots = block_order(tokens)
+    mine = gathered_rows(inputs[0, 0], places)
     dt_block = jnp.pad(by_seq(ssm_in[:, bc_end:]), ((0, 0), (0, 0), (0, 128 - heads)))
     first_send = jnp.concatenate(
         [by_seq(ssm_in[:, z_end:x_end]), for_all(ssm_in[:, x_end:bc_end]), dt_block], axis=2
     )
-    start_mine = trade(after(jnp.concatenate([early_send, first_send], axis=2), *mine))
+    start_mine = trade(jnp.concatenate([early_send, first_send], axis=2))
     early_mine, first_mine = start_mine[:, :, : early_send.shape[2]], start_mine[:, :, early_send.shape[2] :]
-    pieces = [fetch_tokens([after(half, start_mine) for half in mine])]
+    later_send = jnp.concatenate([by_seq(ssm_in[:, :z_end]), by_seq(w_gate), by_seq(w_up)], axis=2)
+    pieces = [fetch_tokens(after(mine, start_mine))]
     out_send = jnp.concatenate([ssm_out, attn_out], axis=0)
-    later_send = jnp.concatenate([by_seq(ssm_in[:, :z_end]), by_seq(w_gate), by_seq(w_up)], axis=2)
     early_w = gather_weights(early_mine)
     first_w = gather_weights(first_mine)
     out_rows = ssm_out.shape[0]
@@ -990,129 +1109,116 @@
     auxes = [token_aux(segments[m, 0]) for m in micro]
     seg_blocks = [segments[m, 0].astype(f32).reshape(-1, 1, SPAN) for m in micro]
     seg_rows = [segments[m, 0].astype(f32)[None] for m in micro]
-    split = balanced(tokens)
     width = inputs.shape[3]
     head_tables = (conv_table, head_table, skip_table)
 
     hiddens, earlies, attendeds, lses, firsts, ys, all_starts = [], [], [], [], [], [], []
-    for m in range(1, MICRO):
-        mine = gathered_blocks(inputs[m, 0], places[:3])
-        pieces.append(fetch_tokens([after(half, *pieces[m - 1][-2:]) for half in mine]))
-    cot_alls = []
-    for m in micro:
-        if m > 0:
-            pieces[m][0] = after(pieces[m][0], ys[m - 1])
-        hidden = norm_pieces(pieces[m], gain_in_gathered)
+    gate_zs, gateds, mixeds, cot_alls = [], [], [], []
+    def mixer_start(m, deps=()):
+        if deps:
+            pieces[m][0] = after(pieces[m][0], *deps)
+        hidden = norm_pieces(pieces[m], spots, gain_in_gathered)
         early = matmul_rows(hidden, early_w).astype(bf16)
         attended, lse = attend_forward(order, early, tables, auxes[m], seg_rows[m], query_heads)
+        hiddens.append(hidden)
         earlies.append(early)
         attendeds.append(attended)
         lses.append(lse)
-        if m == 0:
-            later_mine = trade(after(later_send, attended))
-            z_mine, ffn_mine = later_mine[:, :, :inner], later_mine[:, :, inner:]
-            z_w = gather_weights(z_mine)
-            out_send = after(out_send, z_mine)
-            out_w = gather_weights(out_send)
-            gate_up_w = gather_weights(after(ffn_mine, out_send))
-        hidden = after(hidden, attended, *([later_mine] if m == 0 else cot_pieces))
-        hiddens.append(hidden)
-        first = matmul_rows(hidden, first_w).astype(bf16)
-        behind = [first, *pieces[MICRO - 1][-2:]] if m == 0 else [first, *cot_pieces]
-        blocks = [after(cotangent[m, 0, half * SPAN : (half + 1) * SPAN], *behind) for half in range(halves)]
-        cot_pieces = fetch_tokens(blocks)
-        cot_alls.append(assemble(cot_pieces))
+
+    def mixer_scan(m, deps):
+        hiddens[m] = after(hiddens[m], *deps)
+        first = matmul_rows(hiddens[m], first_w).astype(bf16)
         y_rows, starts = ssd_forward(order, first, auxes[m], seg_blocks[m], *head_tables, heads)
         firsts.append(first)
         ys.append(y_rows)
         all_starts.append(starts)
-    down_w = gather_weights(after(w_down, ys[0]))
-    out_w = out_w.reshape(fsdp, -1, out_w.shape[1])
-    out_w = jnp.concatenate(
-        [out_w[:, :out_rows].reshape(inner, -1), out_w[:, out_rows:].reshape(q_width, -1)], axis=0
-    )
-    side_w = jnp.concatenate([early_w[:, :qkv_width], z_w], axis=1)
-    gate_zs, out_ins, mixeds = [], [], []
-
-    def mixer_out(m, deps, hold=()):
+
+    def mixer_gate(m, deps):
         hiddens[m] = after(hiddens[m], *deps)
         gate_z = matmul_rows(hiddens[m], z_w)
-        gated = (ys[m].astype(f32) * jax.nn.silu(gate_z)).astype(bf16)
         gate_zs.append(gate_z)
-        out_in = jnp.concatenate([gated, attendeds[m]], axis=1)
-        out_ins.append(out_in)
-
-        def mixed_rows(start, end, *late):
-            return matmul_rows(cut_rows(out_in, start, end, late), out_w)
-
-        mixeds.append(scatter_tokens(mixed_rows, tokens, hold))
+        gateds.append((ys[m].astype(f32) * jax.nn.silu(gate_z)).astype(bf16))
+
+    def mixer_out(m, deps, hold=()):
+        mixeds.append(
+            scatter_tokens([gateds[m], attendeds[m]], [ssm_out_w, attn_out_w], False, tokens, hold, deps)
+        )
+
+    def fetch_cotangent(m, deps):
+        cot_alls.append(assemble(fetch_tokens(after(cotangent[m, 0], *deps)), spots))
+
+    mixer_start(0)
+    later_mine = trade(after(later_send, attendeds[0]))
+    pieces.append(fetch_tokens(after(start_rows(inputs[1, 0], cotangent[0, 0], places), later_mine)))
+    z_mine, ffn_mine = later_mine[:, :, :inner], later_mine[:, :, inner:]
+    z_w = gather_weights(z_mine)
+    out_send = after(out_send, z_mine)
+    out_w = gather_weights(out_send)
+    gate_up_w = gather_weights(after(ffn_mine, out_send))
+    mixer_scan(0, [attendeds[0], later_mine])
+    down_w = gather_weights(after(w_down, firsts[0]))
+    out_w = out_w.reshape(fsdp, -1, out_w.shape[1])
+    ssm_out_w, attn_out_w = out_w[:, :out_rows].reshape(inner, -1), out_w[:, out_rows:].reshape(q_width, -1)
+    side_w = jnp.concatenate([early_w[:, :qkv_width], z_w], axis=1)
+    mixer_gate(0, [ys[0]])
+    mixer_out(0, [gateds[0]])
+    mixer_start(1, [mixeds[0][0]])
+    cot_alls.append(assemble(pieces[1], [(flip, half + halves) for flip, half in spots]))
+    mixer_scan(1, [attendeds[1]])
 
     middles, ffn_hiddens, activateds, grad_gus, grad_hiddens = [], [], [], [], []
     grad_middles, lows, gain_ffn_grads, grads_mixed = [], [], [], []
 
-    def middle_forward(m, hold):
-        own, arrived, sent = mixeds[m]
-        *blocks, middle = rows_call(
-            functools.partial(middle_kernel, split, places, len(arrived)),
+    def middle_forward(m, deps, hold=()):
+        own, arrived, parts = mixeds[m]
+        hidden, middle = rows_call(
+            functools.partial(middle_kernel, places, len(arrived), len(deps)),
             tokens,
             width,
-            split,
             [own, inputs[m, 0]],
             gain_ffn,
             arrived,
-            [((SPAN, width), bf16)] * halves + [((tokens, width), f32)],
-            [],
+            [((tokens, width), bf16), ((tokens, width), f32)],
+            deps,
             "middle",
         )
         middles.append(middle)
         if hold:
-            blocks = [after(block, *hold) for block in blocks]
-        ffn_hiddens.append(assemble(fetch_tokens(blocks)))
-
-    def feed_forward(m, deps):
-        ffn_hidden = after(ffn_hiddens[m], *deps)
-        ffn_hiddens[m] = ffn_hidden
-        gate_up = matmul_rows(ffn_hidden, gate_up_w)
-        gate_pre, up_pre = gate_up[:, :units], gate_up[:, units:]
-        sig = jax.nn.sigmoid(gate_pre)
-        activateds.append((gate_pre * sig * up_pre).astype(bf16))
-        grad_act = matmul_back(cot_alls[m], down_w)
-        grad_up = grad_act * gate_pre * sig
-        grad_gate = grad_act * up_pre * sig * (1.0 + gate_pre * (1.0 - sig))
-        grad_gu = jnp.concatenate([grad_gate, grad_up], axis=1).astype(bf16)
+            hidden = after(hidden, *hold)
+        ffn_hiddens.append(assemble(fetch_tokens(hidden), spots))
+
+    def feed_forward(m, deps, late=()):
+        ffn_hiddens[m] = after(ffn_hiddens[m], *deps)
+        activated, grad_gu = feed_products(ffn_hiddens[m], cot_alls[m], gate_up_w, down_w)
+        activateds.append(activated)
         grad_gus.append(grad_gu)
-
-        def hidden_rows(start, end, *late):
-            return matmul_back(cut_rows(grad_gu, start, end, late), gate_up_w)
-
-        grad_hiddens.append(scatter_tokens(hidden_rows, tokens))
+        grad_hiddens.append(scatter_tokens([grad_gu], [gate_up_w], True, tokens, (), late))
 
     def middle_back(m, deps):
-        own, arrived, sent = grad_hiddens[m]
-        *blocks, wide, gain_grad = rows_call(
-            functools.partial(norm_back_kernel, split, places, len(arrived), len(deps), True),
+        own, arrived, parts = grad_hiddens[m]
+        low, wide, gain_grad = rows_call(
+            functools.partial(norm_back_kernel, places, len(arrived), len(deps), True),
             tokens,
             width,
-            split,
             [own, middles[m], cotangent[m, 0]],
             gain_ffn,
             arrived,
-            [((SPAN, width), bf16)] * halves + [((tokens, width), f32), ((8, width), f32)],
+            [((tokens, width), bf16), ((tokens, width), f32), ((8, width), f32)],
             deps,
             "middle_back",
         )
         grad_middles.append(wide)
-        lows.append(blocks[0])
+        lows.append(low)
         gain_ffn_grads.append(gain_grad[0])
-        grads_mixed.append(assemble(fetch_tokens(blocks)))
+        grads_mixed.append(assemble(fetch_tokens(low), spots))
 
     grad_ys, grad_sides, outs, back, in_backs, outputs = [], [], [], [], [], []
 
     def heads_back(m, deps):
         grad_mixed = after(grads_mixed[m], *deps)
         grads_mixed[m] = grad_mixed
-        grad_gated = matmul_back(grad_mixed, out_w[:inner])
-        grad_attended = matmul_back(grad_mixed, out_w[inner:]).astype(bf16)
+        grad_gated = matmul_back(grad_mixed, ssm_out_w)
+        grad_attended = matmul_back(grad_mixed, attn_out_w).astype(bf16)
         gate_z = gate_zs[m]
         sig = jax.nn.sigmoid(gate_z)
         y_wide = ys[m].astype(f32)
@@ -1124,12 +1230,7 @@
         grad_sides.append(jnp.concatenate([grad_qkv, grad_z], axis=1))
 
     def output_rows(m, deps, hold=()):
-        activateds[m] = after(activateds[m], *deps)
-
-        def down_rows(start, end, *late):
-            return matmul_rows(cut_rows(activateds[m], start, end, late), down_w)
-
-        outs.append(scatter_tokens(down_rows, tokens, hold))
+        outs.append(scatter_tokens([activateds[m]], [down_w], False, tokens, hold, deps))
 
     def scan_back(m, deps):
         grad_y = after(grad_ys[m], *deps)
@@ -1137,39 +1238,39 @@
             ssd_backward(order, firsts[m], auxes[m], seg_blocks[m], *head_tables, all_starts[m], grad_y, heads)
         )
 
-    def hidden_back(m, deps, hold=(), later=()):
-        grad_first = after(back[m][0], *deps)
-
-        def in_rows(start, end, *late):
-            one = cut_rows(grad_first, start, end, late + tuple(later if late else ()))
-            return matmul_back(one, first_w) + matmul_back(grad_sides[m][start:end], side_w)
-
-        in_backs.append(scatter_tokens(in_rows, tokens, hold))
-
-    def finish_input(m):
-        own, arrived, sent = in_backs[m]
+    def hidden_back(m, deps, hold=()):
+        in_backs.append(
+            scatter_tokens([back[m][0], grad_sides[m]], [first_w, side_w], True, tokens, hold, deps)
+        )
+
+    def finish_input(m, deps=()):
+        own, arrived, parts = in_backs[m]
         low, gain_grad = rows_call(
-            functools.partial(norm_back_kernel, split, places, len(arrived), 0, False),
+            functools.partial(norm_back_kernel, places, len(arrived), len(deps), False),
             tokens,
             width,
-            split,
             [own, inputs[m, 0], grad_middles[m]],
             gain_in,
             arrived,
             [((tokens, width), bf16), ((8, width), f32)],
-            [],
+            deps,
             "input_back",
         )
         return low, gain_grad[0]
 
-    def finish_output(m):
-        own, arrived, sent = outs[m]
-        if split:
-            arrived = [
-                jnp.concatenate([arrived[0][:SPAN], arrived[2][:SPAN]]),
-                jnp.concatenate([arrived[1], arrived[3]]),
-            ]
-        return (middles[m] + own + sum(part.astype(f32) for part in arrived)).astype(bf16)
+    def finish_output(m, deps=()):
+        own, arrived, parts = outs[m]
+        return rows_call(
+            functools.partial(add_rows_kernel, len(arrived)),
+            tokens,
+            width,
+            [own, middles[m]],
+            gain_ffn,
+            arrived,
+            [((tokens, width), bf16)],
+            deps,
+            "output_rows",
+        )[0]
 
     def both(lefts, rights):
         return (weight_grad(lefts[0], rights[0]) + weight_grad(lefts[1], rights[1])).astype(bf16)
@@ -1177,65 +1278,76 @@
     def back_to_rows(part):
         return trade(part.reshape(seq, rows, -1)).astype(f32)
 
-    def first_arrived(scattered):
-        return scattered[1][::2]
-
-    mixer_out(0, [ys[1], *cot_pieces[2:5]])
-    middle_forward(0, ())
-    mixer_out(1, mixeds[0][2], [ffn_hiddens[0]])
-    feed_forward(0, mixeds[1][2])
-    ffn_hiddens[0] = after(ffn_hiddens[0], *grad_hiddens[0][2])
-    gate_up_sum = weight_grad(ffn_hiddens[0], grad_gus[0])
-    activateds[0] = after(activateds[0], gate_up_sum)
-    down_sum = weight_grad(activateds[0], cot_alls[0])
-    middle_back(0, [gate_up_sum])
-    middle_forward(1, [grads_mixed[0]])
-    heads_back(0, [down_sum])
-    output_rows(0, grad_sides, [ffn_hiddens[1]])
-    feed_forward(1, outs[0][2])
-    ffn_hiddens[1] = after(ffn_hiddens[1], *grad_hiddens[1][2])
-    gate_up_sum = (gate_up_sum + weight_grad(ffn_hiddens[1], grad_gus[1])).astype(bf16)
-    activateds[1] = after(activateds[1], gate_up_sum)
-    down_sum = (down_sum + weight_grad(activateds[1], cot_alls[1])).astype(bf16)
+    middle_forward(0, [ys[1]])
+    mixer_gate(1, [middles[0]])
+    mixer_out(1, [gateds[1]])
+    mixeds[1] = (
+        mixeds[1][0],
+        tuple(swap(after(part, ffn_hiddens[0]), flip + 1) for flip, part in enumerate(mixeds[1][2])),
+        (),
+    )
+    feed_forward(0, ())
+    gate_up_sum = weight_sums(ffn_hiddens[:1], grad_gus[:1], f32, None, [grad_hiddens[0][0], *mixeds[1][1]])
+    down_sum = weight_sums(activateds[:1], cot_alls[:1], f32, None, [gate_up_sum])
+    middle_back(0, [down_sum])
+    middle_forward(1, (), [grads_mixed[0]])
+    fetch_cotangent(1, [grads_mixed[0]])
+    heads_back(0, ())
+    output_rows(0, grad_sides, [ffn_hiddens[1], cot_alls[1]])
+    scan_back(0, [outs[0][0]])
+    hidden_back(0, ())
+    feed_forward(1, [in_backs[0][0]])
+    outputs.append(finish_output(0, [grad_hiddens[1][0]]))
+    gate_up_sum = weight_sums(ffn_hiddens[1:], grad_gus[1:], bf16, gate_up_sum, [outputs[0]])
     gate_up_part = spread_sums(gate_up_sum)
+    middle_back(1, [gate_up_sum])
+
+    def send_late(scattered):
+        late = [swap(after(part, grads_mixed[1]), flip + 1) for flip, part in enumerate(scattered[2])]
+        return scattered[0], tuple(late), ()
+
+    down_sum = weight_sums(activateds[1:], cot_alls[1:], bf16, down_sum, [lows[1]])
     down_part = spread_sums(down_sum)
-    scan_back(0, [down_sum, *first_arrived(grad_hiddens[1])])
-    outputs.append(finish_output(0))
-    middle_back(1, [back[0][0], outputs[0]])
-    hidden_back(0, [lows[1]], [grads_mixed[1]])
-    output_rows(1, in_backs[0][2], [grads_mixed[1]])
-    heads_back(1, [*outs[1][2], gate_up_part])
-    gate_up_back = back_to_rows(gate_up_part)
-    out_ins[0] = after(out_ins[0], grad_sides[1], gate_up_back)
-    out_sum = both(out_ins, grads_mixed)
+    in_backs[0] = send_late(in_backs[0])
+    output_rows(1, [down_sum], [grads_mixed[1]])
+    ssm_out_sum = weight_sums(gateds, grads_mixed, bf16, None, [outs[1][0]])
+    attn_out_sum = weight_sums(attendeds, grads_mixed, bf16, None, [ssm_out_sum])
     out_sum = jnp.concatenate(
-        [out_sum[:inner].reshape(fsdp, -1, width), out_sum[inner:].reshape(fsdp, -1, width)], axis=1
+        [ssm_out_sum.reshape(fsdp, -1, width), attn_out_sum.reshape(fsdp, -1, width)], axis=1
     ).reshape(inner + q_width, width)
     out_part = spread_sums(out_sum)
-    hiddens[0] = after(hiddens[0], out_sum, down_part, *first_arrived(in_backs[0]))
-    side_sum = both(hiddens, grad_sides)
+    heads_back(1, [out_sum, gate_up_part])
+    outputs.append(finish_output(1, [grad_sides[1]]))
+    side_sum = weight_sums(hiddens, grad_sides, bf16, None, [outputs[1]])
     side_part = spread_sums(side_sum)
-    input_grads, gain_in_grads = [], []
-    low, gain_grad = finish_input(0)
-    input_grads.append(low)
-    gain_in_grads.append(gain_grad)
-    scan_back(1, [side_sum, low, *first_arrived(outs[1])])
-    outputs.append(finish_output(1))
-    hiddens[0] = after(hiddens[0], outputs[1], out_part)
-    first_sum = both(hiddens, [b[0] for b in back])
+    gate_up_back = back_to_rows(gate_up_part)
+    side_back = back_to_rows(side_part)
+    scan_back(1, [side_sum, down_part])
+    low, gain_grad = finish_input(0, [back[1][0]])
+    input_grads, gain_in_grads = [low], [gain_grad]
+    first_sum = weight_sums(hiddens, [b[0] for b in back], bf16, None, [low, gate_up_back, out_part])
     first_part = spread_sums(first_sum)
-    side_back = back_to_rows(side_part)
-    hidden_back(1, [first_sum], (), [side_back])
-    low, gain_grad = finish_input(1)
-    input_grads.append(low)
-    gain_in_grads.append(gain_grad)
-
-    gain_in_grad = gain_in_grads[0] + gain_in_grads[1]
-    gain_ffn_grad = gain_ffn_grads[0] + gain_ffn_grads[1]
+    hidden_back(1, [first_sum])
+    first_back = back_to_rows(first_part)
     conv_grad = (back[0][1] + back[1][1])[: CONV + 1]
     head_grad = back[0][2] + back[1][2]
-    rate_sum, bias_sum = head_grad[0, :heads], head_grad[1, :heads]
     skip_sum = jnp.sum((back[0][3] + back[1][3])[0].reshape(heads, SSM_DIM), axis=1)
+    conv_whole = jnp.zeros((CONV + 1, CONV_CH), f32)
+    conv_whole = lax.dynamic_update_slice_in_dim(conv_whole, conv_grad[:, :inner], inner_start, 1)
+    conv_whole = lax.dynamic_update_slice_in_dim(conv_whole, conv_grad[:, inner:], SSM_INNER, 1)
+    head_sums = lax.dynamic_update_slice_in_dim(
+        jnp.zeros((3, SSM_HEADS), f32), jnp.stack([head_grad[0, :heads], head_grad[1, :heads], skip_sum]), head_start, 1
+    )
+    small_sums = [conv_whole.reshape(-1), head_sums.reshape(-1), gain_ffn_grads[0] + gain_ffn_grads[1]]
+    ends = [0]
+    for piece in small_sums:
+        ends.append(ends[-1] + piece.shape[0])
+    total = add_small(after(jnp.concatenate(small_sums), in_backs[1][0]))
+    low, gain_grad = finish_input(1, [total])
+    input_grads.append(low)
+    gain_in_total = add_small(gain_in_grads[0] + gain_grad)
+
+    out_part = after(out_part, first_back).astype(f32)
 
     def own_columns(block):
         return jnp.swapaxes(block, 0, 1).reshape(rows, -1)
@@ -1247,7 +1359,6 @@
 
     gate_grad = own_columns(gate_up_back[:, :, :units])
     up_grad = own_columns(gate_up_back[:, :, units:])
-    first_back = back_to_rows(first_part)
     ssm_in_grad = jnp.concatenate(
         [
             own_columns(side_back[:, :, qkv_width:]),
@@ -1265,22 +1376,8 @@
         ],
         axis=1,
     )
-    out_part = out_part.astype(f32)
-
-    conv_whole = jnp.zeros((CONV + 1, CONV_CH), f32)
-    conv_whole = lax.dynamic_update_slice_in_dim(conv_whole, conv_grad[:, :inner], inner_start, 1)
-    conv_whole = lax.dynamic_update_slice_in_dim(conv_whole, conv_grad[:, inner:], SSM_INNER, 1)
-    head_sums = lax.dynamic_update_slice_in_dim(
-        jnp.zeros((3, SSM_HEADS), f32), jnp.stack([rate_sum, bias_sum, skip_sum]), head_start, 1
-    )
-    pieces = [conv_whole.reshape(-1), head_sums.reshape(-1), gain_in_grad, gain_ffn_grad]
-    ends = [0]
-    for piece in pieces:
-        ends.append(ends[-1] + piece.shape[0])
-    total = add_small(jnp.concatenate(pieces))
-    conv_total, head_total, gain_in_total, gain_ffn_total = (
-        total[a:b] for a, b in zip(ends[:-1], ends[1:])
-    )
+
+    conv_total, head_total, gain_ffn_total = (total[a:b] for a, b in zip(ends[:-1], ends[1:]))
     place = index * fsdp + lax.axis_index("fsdp")
     conv_total = lax.dynamic_slice_in_dim(conv_total.reshape(CONV + 1, CONV_CH), place * channels, channels, 1)
     head_total = head_total.reshape(3, SSM_HEADS)
@@ -1300,7 +1397,7 @@
         lax.dynamic_slice_in_dim(gain_ffn_total, place * rows, rows),
         gate_grad,
         up_grad,
-        down_part.astype(f32),
+        after(down_part, first_back).astype(f32),
     )
 
 

time: 1150 us -> 1080 us (0.939)
  matrix products: 399 us -> 74.1 us
  Pallas kernels: 220 us -> 404 us
  waiting for transfers between devices: 174 us -> 327 us
  local copies, waits for them, and re-layouts: 125 us -> 94.7 us
  other arithmetic: 58.5 us -> 30.9 us
  starting transfers between devices: 105 us -> 77.7 us
    pallas_call x10 -> x28, Pallas kernels: 31.9 us -> 265 us  [the longest x8 98.3 us: weight_sums(): pl.pallas_call(functools.partial(sums_kernel, len(lefts), len(extra), len...]
    dot_general x30 -> x4, matrix products: 155 us -> 22.9 us  [matmul_back(): jnp.einsum('td,cd->tc', left, right, preferred_element_type=jnp.float32)]
    dot_general x10 -> x0, matrix products: 104 us -> none  [weight_grad(): jnp.einsum('tc,td->cd', left, right, preferred_element_type=jnp.float32)]
    ppermute x80 -> x45, waiting for transfers between devices: 142 us -> 239 us  [swap(): return lax.ppermute(value, 'seq', peers(lax.axis_size('seq'), flip))]
    dot_general x24 -> x6, matrix products: 140 us -> 51.2 us  [matmul_rows(): jnp.einsum('tc,cd->td', left, right, preferred_element_type=jnp.float32)]
    pallas_call x2, Pallas kernels: 106 us -> 56.1 us  [ssd_backward(): pl.pallas_call(functools.partial(ssd_backward_kernel, heads), grid_spec=p...]
    all_gather x6, waiting for transfers between devices: 8.16 us -> 44.6 us  [gather_weights(): lax.all_gather(rows.reshape(-1, rows.shape[-1]), 'fsdp', axis=0, tiled=True)]
    ppermute x80 -> x45, starting transfers between devices: 87.4 us -> 52.9 us  [swap(): return lax.ppermute(value, 'seq', peers(lax.axis_size('seq'), flip))]
  transfers between devices with their start and end apart: 99 -> 69, of which waited for: 42 -> 30; matrix products, arithmetic and copies ran while one was open for 39% -> 12% of each run, Pallas kernels for 19% -> 35%
where the time goes in v4:
time: 1080 us; the launch traced here: 1060 us
  Pallas kernels  404 us (37%)
  waiting for transfers between devices  327 us (30%)
  local copies, waits for them, and re-layouts  94.7 us (9%)
  starting transfers between devices  77.7 us (7%)
  matrix products  74.1 us (7%)
  blocking collectives  39.1 us (4%)
  other arithmetic  30.9 us (3%)
  between operations  16.2 us (2%)
    ppermute x45, waiting for transfers between devices, swap(): return lax.ppermute(value, 'seq', peers(lax.axis_size('seq'), flip))  239 us
    pallas_call x8, Pallas kernels, weight_sums(): pl.pallas_call(functools.partial(sums_kernel, len(lefts), len(extra), len...  98.3 us
    pallas_call x8, Pallas kernels, product_rows(): pl.pallas_call(functools.partial(product_kernel, back, len(lefts), len(de...  90.6 us
    unnamed x298, local copies, waits for them, and re-layouts  58.6 us
    pallas_call x2, Pallas kernels, ssd_backward(): pl.pallas_call(functools.partial(ssd_backward_kernel, heads), grid_spec=p...  56.1 us
    ppermute x45, starting transfers between devices, swap(): return lax.ppermute(value, 'seq', peers(lax.axis_size('seq'), flip))  52.9 us
    dot_general x6, matrix products, matmul_rows(): jnp.einsum('tc,cd->td', left, right, preferred_element_type=jnp.float32)  51.2 us
    all_gather x6, waiting for transfers between devices, gather_weights(): lax.all_gather(rows.reshape(-1, rows.shape[-1]), 'fsdp', axis=0, tiled=True)  44.6 us
  transfers between devices with their start and end apart: 69, of which 30 were waited for; matrix products, arithmetic and copies ran while one was open for 12% of the time, Pallas kernels for 35%

profile of v4, /device:TPU:0, one launch (start us, length us, event | category | flops | bytes accessed | tf_op | source)
XLA Modules:
  0.0 1064.1 jit_solution(10336995305656795770)
XLA Ops:
  12.2 19.1 %all_to_all.25.refs_1_ = bf16[4,64,2048]{2,1,0:T(8,128)(2,1)S(1)} all-to-all(bf16[4,64,2048]{2,1,0:T(8,128)(2,1)S(1)} %pad_dynamic-update-slice_fusion), channel_id=1, replica_groups=mesh['seq'=4,'fsdp'=8] {'seq'}, dimensions={0} | all-to-all | bytes 2097152 | tf_op jit(solution)/shard_map/all_to_all | solution.py:985
  50.9 15.0 %all-gather.7.cloned.1.call-done = bf16[2048,640]{1,0:T(8,128)(2,1)} async-done(((bf16[256,640]{1,0:T(8,128)(2,1)}), bf16[2048,640]{1,0:T(8,128)(2,1)}) %all-gather.7.cloned.1.call-update) | async-done | bytes 2621456 | tf_op jit(solution)/shard_map/all_gather | solution.py:989
  69.3 20.7 %collective-permute-done.1.refs_4_.refs_5_ = bf16[256,2048]{1,0:T(8,128)(2,1)} collective-permute-done((bf16[256,2048]{1,0:T(8,128)(2,1)}, bf16[256,2048]{1,0:T(8,128)(2,1)}, u32[]{:S(2)}, u32[]{:S(2)}) %collective-permute-start.1) | collective-permute-done | bytes 1048608 | tf_op jit(solution)/shard_map/ppermute | solution.py:947
  109.1 20.0 %all_to_all.26.refs_2_.refs_1_ = bf16[4,64,2816]{2,1,0:T(8,128)(2,1)S(1)} all-to-all(bf16[4,64,2816]{2,1,0:T(8,128)(2,1)} %after.35), channel_id=1, replica_groups=mesh['seq'=4,'fsdp'=8] {'seq'}, dimensions={0} | all-to-all | bytes 2883584 | tf_op jit(solution)/shard_map/all_to_all | solution.py:985
  132.3 11.3 %convolution_convert_fusion.1.first_ref.refs_1_.before_ref = bf16[1024,1408]{1,0:T(8,128)(2,1)} fusion(bf16[1024,2048]{1,0:T(8,128)(2,1)} %after.36.refs_0_, bf16[2048,1408]{1,0:T(8,128)(2,1)} %all-gather.9.cloned.1.call-done.refs_2_), kind=kOutput, calls=%fused_computation.7 | convolution fusion | flops 5907021824 | bytes 12845056 | tf_op jit(solution)/shard_map/tc,cd->td/dot_general | solution.py:931
  162.5 13.5 %ssd_forward.2 = (bf16[1024,768]{1,0:T(8,128)(2,1)S(1)}, bf16[8,256,768]{2,1,0:T(8,128)(2,1)}) custom-call(s32[8]{0:T(128)S(1)} %copy-done.90, bf16[1024,1408]{1,0:T(8,128)(2,1)S(1)} %copy-done.9, f32[1024,16]{1,0:T(8,128)S(1)} %copy-done.78, f32[8,1,128]{2,1,0:T(1,128)S(1)} %get-tuple-element.236.seg_ref, f32[8,1280]{1,0:T(8,128)S(1)} %select_maximum_fusion.conv_ref, ...), custom_call_target="tpu_custom_call" | custom-call | flops 17250000896 | tf_op jit(solution)/shard_map/ssd_forward/pallas_call | solution.py:339
  178.6 9.0 fusion
  187.7 29.6 %all-gather.13.cloned.1.call-done = bf16[1024,2048]{1,0:T(8,128)(2,1)} async-done(((bf16[128,2048]{1,0:T(8,128)(2,1)}), bf16[1024,2048]{1,0:T(8,128)(2,1)}) %all-gather.13.cloned.1.call-update) | async-done | bytes 4194320 | tf_op jit(solution)/shard_map/all_gather | solution.py:989
  222.7 7.9 product_rows.8
  233.5 14.2 %collective-permute-done.7.refs_4_.refs_5_.refs_2_ = bf16[512,2048]{1,0:T(8,128)(2,1)} collective-permute-done((bf16[512,2048]{1,0:T(8,128)(2,1)}, bf16[512,2048]{1,0:T(8,128)(2,1)}, u32[]{:S(2)}, u32[]{:S(2)}) %collective-permute-start.7) | collective-permute-done | bytes 2097184 | tf_op jit(solution)/shard_map/ppermute | solution.py:947
  276.3 10.2 convolution_convert_fusion.first_ref.before_ref
  286.5 13.5 %ssd_forward.3 = (bf16[1024,768]{1,0:T(8,128)(2,1)S(1)}, bf16[8,256,768]{2,1,0:T(8,128)(2,1)}) custom-call(s32[8]{0:T(128)S(1)} %copy-done.91, bf16[1024,1408]{1,0:T(8,128)(2,1)S(1)} %convolution_convert_fusion.first_ref.before_ref, f32[1024,16]{1,0:T(8,128)S(1)} %copy-done.74, f32[8,1,128]{2,1,0:T(1,128)S(1)} %get-tuple-element.233.seg_ref, ...), custom_call_target="tpu_custom_call" | custom-call | flops 17250000896 | tf_op jit(solution)/shard_map/ssd_forward/pallas_call | solution.py:339
  301.2 16.2 %collective-permute-done.4.refs_1_ = bf16[256,2048]{1,0:T(8,128)(2,1)S(1)} collective-permute-done((bf16[256,2048]{1,0:T(8,128)(2,1)}, bf16[256,2048]{1,0:T(8,128)(2,1)S(1)}, u32[]{:S(2)}, u32[]{:S(2)}) %collective-permute-start.4) | collective-permute-done | bytes 1048608 | tf_op jit(solution)/shard_map/ppermute | solution.py:947
  324.6 9.4 fusion.4
  334.0 7.5 product_rows.10
  347.2 21.3 %collective-permute-done.10.refs_2_ = bf16[256,2048]{1,0:T(8,128)(2,1)} collective-permute-done((bf16[256,2048]{1,0:T(8,128)(2,1)S(1)}, bf16[256,2048]{1,0:T(8,128)(2,1)}, u32[]{:S(2)}, u32[]{:S(2)}) %collective-permute-start.10) | collective-permute-done | bytes 1048608 | tf_op jit(solution)/shard_map/ppermute | solution.py:947
  375.7 21.4 %feed_products.2 = (bf16[1024,1024]{1,0:T(8,128)(2,1)S(1)}, bf16[1024,2048]{1,0:T(8,128)(2,1)}) custom-call(bf16[1024,2048]{1,0:T(8,128)(2,1)} %after.42.hidden.refs_0_, bf16[1024,2048]{1,0:T(8,128)(2,1)} %assemble.7.cot.refs_1_, bf16[2048,2048]{1,0:T(8,128)(2,1)} %all-gather.15.cloned.1.call-done.gate_w.up_w.refs_1_, ...), custom_call_target="tpu_custom_call" | custom-call | flops 24696061952 | tf_op jit(solution)/shard_map/feed_products/pallas_call | solution.py:849
  397.1 14.0 %product_rows.9 = (f32[256,2048]{1,0:T(8,128)S(1)}, bf16[256,2048]{1,0:T(8,128)(2,1)}, bf16[256,2048]{1,0:T(8,128)(2,1)S(1)}, bf16[256,2048]{1,0:T(8,128)(2,1)S(1)}) custom-call(bf16[1024,2048]{1,0:T(8,128)(2,1)} %get-tuple-element.93.refs_0_.refs_1_, bf16[2048,2048]{1,0:T(8,128)(2,1)} %all-gather.15.cloned.1.call-done.gate_w.up_w.refs_1_), custom_call_target="tpu_custom_call" | custom-call | flops 14967310336 | tf_op jit(solution)/shard_map/product_rows/pallas_call | solution.py:812
  421.4 16.1 %weight_sums.8.refs_2_ = f32[2048,2048]{1,0:T(8,128)} custom-call(bf16[1024,2048]{1,0:T(8,128)(2,1)} %after.42.hidden.refs_0_, bf16[1024,2048]{1,0:T(8,128)(2,1)} %get-tuple-element.93.refs_0_.refs_1_, f32[256,2048]{1,0:T(8,128)S(1)} %get-tuple-element.94.refs_2_.own, bf16[256,2048]{1,0:T(8,128)(2,1)} %collective-permute-done.15.refs_3_.refs_0_, ...), custom_call_target="tpu_custom_call" | custom-call | flops 14967310336 | tf_op jit(solution)/shard_map/weight_sums/pallas_call | solution.py:891
  437.5 8.7 weight_sums.9.refs_3_.refs_2_
  446.2 15.8 %collective-permute-done.13.refs_1_ = bf16[256,2048]{1,0:T(8,128)(2,1)S(1)} collective-permute-done((bf16[256,2048]{1,0:T(8,128)(2,1)S(1)}, bf16[256,2048]{1,0:T(8,128)(2,1)S(1)}, u32[]{:S(2)}, u32[]{:S(2)}) %collective-permute-start.13) | collective-permute-done | bytes 1048608 | tf_op jit(solution)/shard_map/ppermute | solution.py:947
  477.5 16.1 %collective-permute-done.18.refs_1_ = bf16[256,2048]{1,0:T(8,128)(2,1)S(1)} collective-permute-done((bf16[256,2048]{1,0:T(8,128)(2,1)S(1)}, bf16[256,2048]{1,0:T(8,128)(2,1)S(1)}, u32[]{:S(2)}, u32[]{:S(2)}) %collective-permute-start.18) | collective-permute-done | bytes 1048608 | tf_op jit(solution)/shard_map/ppermute | solution.py:947
  493.6 22.6 %collective-permute-done.19.refs_2_ = bf16[256,2048]{1,0:T(8,128)(2,1)S(1)} collective-permute-done((bf16[256,2048]{1,0:T(8,128)(2,1)S(1)}, bf16[256,2048]{1,0:T(8,128)(2,1)S(1)}, u32[]{:S(2)}, u32[]{:S(2)}) %collective-permute-start.19) | collective-permute-done | bytes 1048608 | tf_op jit(solution)/shard_map/ppermute | solution.py:947
  529.5 7.4 fusion.3
  545.6 7.3 product_rows.11
  558.5 27.9 %ssd_backward.2 = (bf16[1024,1408]{1,0:T(8,128)(2,1)S(1)}, f32[8,1280]{1,0:T(8,128)S(1)}, f32[8,128]{1,0:T(8,128)S(1)}, f32[8,768]{1,0:T(8,128)S(1)}) custom-call(s32[8]{0:T(128)S(1)} %copy-done.91, bf16[1024,1408]{1,0:T(8,128)(2,1)} %convolution_convert_fusion.1.first_ref.refs_1_.before_ref, ...), custom_call_target="tpu_custom_call" | custom-call | flops 60949999616 | tf_op jit(solution)/shard_map/ssd_backward/pallas_call | solution.py:388
  589.3 16.8 %product_rows.12 = (f32[256,2048]{1,0:T(8,128)S(1)}, bf16[256,2048]{1,0:T(8,128)(2,1)S(1)}, bf16[256,2048]{1,0:T(8,128)(2,1)S(1)}, bf16[256,2048]{1,0:T(8,128)(2,1)S(1)}) custom-call(bf16[1024,1408]{1,0:T(8,128)(2,1)} %copy-done.112, bf16[1024,1280]{1,0:T(8,128)(2,1)} %pad_maximum_fusion.2.refs_2_.refs_1_, ...), custom_call_target="tpu_custom_call" | custom-call | flops 19644594176 | tf_op jit(solution)/shard_map/product_rows/pallas_call | solution.py:812
  620.3 21.4 %feed_products.3 = (bf16[1024,1024]{1,0:T(8,128)(2,1)S(1)}, bf16[1024,2048]{1,0:T(8,128)(2,1)}) custom-call(bf16[1024,2048]{1,0:T(8,128)(2,1)} %after.56.hidden.refs_0_, bf16[1024,2048]{1,0:T(8,128)(2,1)} %assemble.10.refs_2_.cot.refs_1_, bf16[2048,2048]{1,0:T(8,128)(2,1)} %all-gather.15.cloned.1.call-done.gate_w.up_w.refs_1_, ...), custom_call_target="tpu_custom_call" | custom-call | flops 24696061952 | tf_op jit(solution)/shard_map/feed_products/pallas_call | solution.py:849
  643.1 12.6 %product_rows.13 = (f32[256,2048]{1,0:T(8,128)S(1)}, bf16[256,2048]{1,0:T(8,128)(2,1)S(1)}, bf16[256,2048]{1,0:T(8,128)(2,1)S(1)}, bf16[256,2048]{1,0:T(8,128)(2,1)S(1)}) custom-call(bf16[1024,2048]{1,0:T(8,128)(2,1)} %get-tuple-element.112.refs_0_.refs_1_, bf16[2048,2048]{1,0:T(8,128)(2,1)} %all-gather.15.cloned.1.call-done.gate_w.up_w.refs_1_), custom_call_target="tpu_custom_call" | custom-call | flops 14967310336 | tf_op jit(solution)/shard_map/product_rows/pallas_call | solution.py:812
  666.5 15.5 %weight_sums.10.refs_3_ = bf16[2048,2048]{1,0:T(8,128)(2,1)} custom-call(bf16[1024,2048]{1,0:T(8,128)(2,1)S(1)} %copy-done, bf16[1024,2048]{1,0:T(8,128)(2,1)} %get-tuple-element.112.refs_0_.refs_1_, f32[2048,2048]{1,0:T(8,128)} %weight_sums.8.refs_2_, bf16[256,2048]{1,0:T(8,128)(2,1)S(1)} %output_rows.2.refs_3_), custom_call_target="tpu_custom_call" | custom-call | flops 14967310336 | tf_op jit(solution)/shard_map/weight_sums/pallas_call | solution.py:891
  687.1 22.4 %collective-permute-done.30.refs_0_ = bf16[256,2048]{1,0:T(8,128)(2,1)S(1)} collective-permute-done((bf16[256,2048]{1,0:T(8,128)(2,1)}, bf16[256,2048]{1,0:T(8,128)(2,1)S(1)}, u32[]{:S(2)}, u32[]{:S(2)}) %collective-permute-start.30) | collective-permute-done | bytes 1048608 | tf_op jit(solution)/shard_map/ppermute | solution.py:947
  709.5 18.0 %collective-permute-done.31.refs_1_ = bf16[256,2048]{1,0:T(8,128)(2,1)S(1)} collective-permute-done((bf16[256,2048]{1,0:T(8,128)(2,1)S(1)}, bf16[256,2048]{1,0:T(8,128)(2,1)S(1)}, u32[]{:S(2)}, u32[]{:S(2)}) %collective-permute-start.31) | collective-permute-done | bytes 1048608 | tf_op jit(solution)/shard_map/ppermute | solution.py:947
  732.3 9.1 weight_sums.11.refs_2_
  745.0 7.3 product_rows.14
  754.2 13.3 %collective-permute-done.33.refs_1_ = bf16[256,2048]{1,0:T(8,128)(2,1)S(1)} collective-permute-done((bf16[256,2048]{1,0:T(8,128)(2,1)S(1)}, bf16[256,2048]{1,0:T(8,128)(2,1)S(1)}, u32[]{:S(2)}, u32[]{:S(2)}) %collective-permute-start.33) | collective-permute-done | bytes 1048608 | tf_op jit(solution)/shard_map/ppermute | solution.py:947
  767.6 17.0 %collective-permute-done.34.refs_2_ = bf16[256,2048]{1,0:T(8,128)(2,1)S(1)} collective-permute-done((bf16[256,2048]{1,0:T(8,128)(2,1)S(1)}, bf16[256,2048]{1,0:T(8,128)(2,1)S(1)}, u32[]{:S(2)}, u32[]{:S(2)}) %collective-permute-start.34) | collective-permute-done | bytes 1048608 | tf_op jit(solution)/shard_map/ppermute | solution.py:947
  787.1 10.4 weight_sums.12.refs_4_
  816.9 7.5 multiply_convert_fusion
  833.4 15.1 %collective-permute-done.37.refs_1_ = bf16[256,2048]{1,0:T(8,128)(2,1)S(1)} collective-permute-done((bf16[256,2048]{1,0:T(8,128)(2,1)}, bf16[256,2048]{1,0:T(8,128)(2,1)S(1)}, u32[]{:S(2)}, u32[]{:S(2)}) %collective-permute-start.37) | collective-permute-done | bytes 1048608 | tf_op jit(solution)/shard_map/ppermute | solution.py:947
  851.4 15.2 %weight_sums.14.refs_1_ = bf16[2048,1280]{1,0:T(8,128)(2,1)} custom-call(bf16[1024,2048]{1,0:T(8,128)(2,1)} %after.37.refs_0_, bf16[1024,2048]{1,0:T(8,128)(2,1)} %after.45.refs_1_, bf16[1024,1280]{1,0:T(8,128)(2,1)S(1)} %copy-done.10, bf16[1024,1280]{1,0:T(8,128)(2,1)} %pad_maximum_fusion.3.refs_3_.refs_1_, bf16[256,2048]{1,0:T(8,128)(2,1)S(1)} %output_rows.3.refs_4_), custom_call_target="tpu_custom_call" | custom-call | flops 18709137408 | tf_op jit(solution)/shard_map/weight_sums/pallas_call | solution.py:891
  879.1 28.2 %ssd_backward.3 = (bf16[1024,1408]{1,0:T(8,128)(2,1)S(1)}, f32[8,1280]{1,0:T(8,128)S(1)}, f32[8,128]{1,0:T(8,128)S(1)}, f32[8,768]{1,0:T(8,128)S(1)}) custom-call(s32[8]{0:T(128)S(1)} %copy-done.92, bf16[1024,1408]{1,0:T(8,128)(2,1)} %copy-done.107, bf16[1024,1408]{1,0:T(8,128)(2,1)} %copy-done.107, f32[1024,16]{1,0:T(8,128)S(1)} %copy-done.76, ...), custom_call_target="tpu_custom_call" | custom-call | flops 60949999616 | tf_op jit(solution)/shard_map/ssd_backward/pallas_call | solution.py:388
  908.9 10.4 collective-permute-done.40.refs_1_
  926.4 18.4 %weight_sums.15.refs_4_ = bf16[2048,1408]{1,0:T(8,128)(2,1)} custom-call(bf16[1024,2048]{1,0:T(8,128)(2,1)} %after.37.refs_0_, bf16[1024,2048]{1,0:T(8,128)(2,1)} %after.45.refs_1_, bf16[1024,1408]{1,0:T(8,128)(2,1)} %copy-done.112, bf16[1024,1408]{1,0:T(8,128)(2,1)} %copy-done.97, bf16[256,2048]{1,0:T(8,128)(2,1)S(1)} %get-tuple-element.131.refs_4_, ...), custom_call_target="tpu_custom_call" | custom-call | flops 20580050944 | tf_op jit(solution)/shard_map/weight_sums/pallas_call | solution.py:891
  944.9 17.2 %product_rows.15 = (f32[256,2048]{1,0:T(8,128)S(1)}, bf16[256,2048]{1,0:T(8,128)(2,1)}, bf16[256,2048]{1,0:T(8,128)(2,1)}, bf16[256,2048]{1,0:T(8,128)(2,1)}) custom-call(bf16[1024,1408]{1,0:T(8,128)(2,1)} %copy-done.97, bf16[1024,1280]{1,0:T(8,128)(2,1)} %pad_maximum_fusion.3.refs_3_.refs_1_, bf16[2048,1408]{1,0:T(8,128)(2,1)} %all-gather.9.cloned.1.call-done.refs_2_, ...), custom_call_target="tpu_custom_call" | custom-call | flops 19644594176 | tf_op jit(solution)/shard_map/product_rows/pallas_call | solution.py:812
  971.7 7.0 collective-permute-done.46
  980.5 8.8 collective-permute-done.47
  989.5 12.4 %collective-permute-done.48 = f32[20112]{0:T(1024)S(1)} collective-permute-done((f32[20112]{0:T(1024)S(1)}, f32[20112]{0:T(1024)S(1)}, u32[]{:S(2)}, u32[]{:S(2)}) %collective-permute-start.48) | collective-permute-done | bytes 80480 | tf_op jit(solution)/shard_map/ppermute | solution.py:979
  1040.1 7.6 all-to-all-done.4
  (638 shorter events, 340.3 us)
Async XLA Ops:
  7.3 58.7 %all-gather.7.cloned.1.call-start = ((), (), s32[]{:S(2)}) async-start(), calls=%async_computation.10 | async-start | bytes 2949120 | tf_op jit(solution)/shard_map/all_gather | solution.py:989
  32.2 100.1 %all-gather.9.cloned.1.call-start = ((), (), s32[]{:S(2)}) async-start(), calls=%async_computation.11 | async-start | bytes 6488064 | tf_op jit(solution)/shard_map/all_gather | solution.py:989
  33.2 144.0 %all-gather.11.cloned.1.call-start = ((), (), s32[]{:S(2)}) async-start(), calls=%async_computation.12 | async-start | bytes 3538944 | tf_op jit(solution)/shard_map/all_gather | solution.py:989
  43.8 46.2 %collective-permute-start.1 = (bf16[256,2048]{1,0:T(8,128)(2,1)}, bf16[256,2048]{1,0:T(8,128)(2,1)}, u32[]{:S(2)}, u32[]{:S(2)}) collective-permute-start(bf16[256,2048]{1,0:T(8,128)(2,1)} %after.34.refs_0_.refs_1_), channel_id=1, source_target_pairs={{0,16},{8,24},{16,0},{24,8},{1,17},{9,25},{17,1},{25,9},{2,18},{10... | collective-permute-start | bytes 3145736 | tf_op jit(solution)/shard_map/ppermute | solution.py:947
  44.4 45.7 %collective-permute-start.2 = (bf16[256,2048]{1,0:T(8,128)(2,1)}, bf16[256,2048]{1,0:T(8,128)(2,1)}, u32[]{:S(2)}, u32[]{:S(2)}) collective-permute-start(bf16[256,2048]{1,0:T(8,128)(2,1)} %after.34.refs_0_.refs_1_), channel_id=1, source_target_pairs={{0,24},{8,16},{16,8},{24,0},{1,25},{9,17},{17,9},{25,1},{2,26},{10... | collective-permute-start | bytes 3145736 | tf_op jit(solution)/shard_map/ppermute | solution.py:947
  131.0 86.2 %all-gather.13.cloned.1.call-start = ((), (), s32[]{:S(2)}) async-start(), calls=%async_computation.13 | async-start | bytes 4718592 | tf_op jit(solution)/shard_map/all_gather | solution.py:989
  132.0 243.7 %all-gather.17.cloned.1.call-start = ((), (), s32[]{:S(2)}) async-start(), calls=%async_computation.15 | async-start | bytes 4718592 | tf_op jit(solution)/shard_map/all_gather | solution.py:989
  143.6 232.1 %all-gather.15.cloned.1.call-start = ((), (), s32[]{:S(2)}) async-start(), calls=%async_computation.14 | async-start | bytes 9437184 | tf_op jit(solution)/shard_map/all_gather | solution.py:989
  146.0 664.6 %reduce-scatter.6.cloned.1.call-start = ((), (), s32[]{:S(2)}) async-start(), calls=%async_computation.16 | async-start | bytes 9437184 | tf_op jit(solution)/shard_map/reduce_scatter | solution.py:993
  157.6 76.0 %collective-permute-start.8 = (bf16[512,2048]{1,0:T(8,128)(2,1)}, bf16[512,2048]{1,0:T(8,128)(2,1)}, u32[]{:S(2)}, u32[]{:S(2)}) collective-permute-start(bf16[512,2048]{1,0:T(8,128)(2,1)} %after.39.refs_0_), channel_id=1, source_target_pairs={{0,24},{8,16},{16,8},{24,0},{1,25},{9,17},{17,9},{25,1},{2,26},{10... | collective-permute-start | bytes 6291464 | tf_op jit(solution)/shard_map/ppermute | solution.py:947
  158.4 89.4 %collective-permute-start.7 = (bf16[512,2048]{1,0:T(8,128)(2,1)}, bf16[512,2048]{1,0:T(8,128)(2,1)}, u32[]{:S(2)}, u32[]{:S(2)}) collective-permute-start(bf16[512,2048]{1,0:T(8,128)(2,1)} %after.39.refs_0_), channel_id=1, source_target_pairs={{0,16},{8,24},{16,0},{24,8},{1,17},{9,25},{17,1},{25,9},{2,18},{10... | collective-permute-start | bytes 6291464 | tf_op jit(solution)/shard_map/ppermute | solution.py:947
  160.1 87.7 %collective-permute-start.6 = (bf16[512,2048]{1,0:T(8,128)(2,1)}, bf16[512,2048]{1,0:T(8,128)(2,1)}, u32[]{:S(2)}, u32[]{:S(2)}) collective-permute-start(bf16[512,2048]{1,0:T(8,128)(2,1)} %after.39.refs_0_), channel_id=1, source_target_pairs={{0,8},{8,0},{16,24},{24,16},{1,9},{9,1},{17,25},{25,17},{2,10},{10... | collective-permute-start | bytes 6291464 | tf_op jit(solution)/shard_map/ppermute | solution.py:947
  269.9 47.5 %collective-permute-start.4 = (bf16[256,2048]{1,0:T(8,128)(2,1)}, bf16[256,2048]{1,0:T(8,128)(2,1)S(1)}, u32[]{:S(2)}, u32[]{:S(2)}) collective-permute-start(bf16[256,2048]{1,0:T(8,128)(2,1)} %copy-done.86), channel_id=1, source_target_pairs={{0,16},{8,24},{16,0},{24,8},{1,17},{9,25},{17,1},{25,9},{2,18},{10... | collective-permute-start | bytes 3145736 | tf_op jit(solution)/shard_map/ppermute | solution.py:947
  271.0 46.5 %collective-permute-start.5 = (bf16[256,2048]{1,0:T(8,128)(2,1)}, bf16[256,2048]{1,0:T(8,128)(2,1)S(1)}, u32[]{:S(2)}, u32[]{:S(2)}) collective-permute-start(bf16[256,2048]{1,0:T(8,128)(2,1)} %copy-done.83), channel_id=1, source_target_pairs={{0,24},{8,16},{16,8},{24,0},{1,25},{9,17},{17,9},{25,1},{2,26},{10... | collective-permute-start | bytes 3145736 | tf_op jit(solution)/shard_map/ppermute | solution.py:947
  321.9 46.6 %collective-permute-start.10 = (bf16[256,2048]{1,0:T(8,128)(2,1)S(1)}, bf16[256,2048]{1,0:T(8,128)(2,1)}, u32[]{:S(2)}, u32[]{:S(2)}) collective-permute-start(bf16[256,2048]{1,0:T(8,128)(2,1)S(1)} %get-tuple-element.90.refs_0_), channel_id=1, source_target_pairs={{0,16},{8,24},{16,0},{24,8},{1,17},{9,25},{17,1},{25,9},{2,18},{10... | collective-permute-start | bytes 3145736 | tf_op jit(solution)/shard_map/ppermute | solution.py:947
  323.1 45.4 %collective-permute-start.11 = (bf16[256,2048]{1,0:T(8,128)(2,1)S(1)}, bf16[256,2048]{1,0:T(8,128)(2,1)}, u32[]{:S(2)}, u32[]{:S(2)}) collective-permute-start(bf16[256,2048]{1,0:T(8,128)(2,1)S(1)} %get-tuple-element.90.refs_0_), channel_id=1, source_target_pairs={{0,24},{8,16},{16,8},{24,0},{1,25},{9,17},{17,9},{25,1},{2,26},{10... | collective-permute-start | bytes 3145736 | tf_op jit(solution)/shard_map/ppermute | solution.py:947
  372.0 41.1 %collective-permute-start.15 = (bf16[256,2048]{1,0:T(8,128)(2,1)}, bf16[256,2048]{1,0:T(8,128)(2,1)}, u32[]{:S(2)}, u32[]{:S(2)}) collective-permute-start(bf16[256,2048]{1,0:T(8,128)(2,1)} %after.46), channel_id=1, source_target_pairs={{0,8},{8,0},{16,24},{24,16},{1,9},{9,1},{17,25},{25,17},{2,10},{10... | collective-permute-start | bytes 3145736 | tf_op jit(solution)/shard_map/ppermute | solution.py:947
  373.2 42.4 %collective-permute-start.16 = (bf16[256,2048]{1,0:T(8,128)(2,1)S(1)}, bf16[256,2048]{1,0:T(8,128)(2,1)}, u32[]{:S(2)}, u32[]{:S(2)}) collective-permute-start(bf16[256,2048]{1,0:T(8,128)(2,1)S(1)} %copy-done.59), channel_id=1, source_target_pairs={{0,16},{8,24},{16,0},{24,8},{1,17},{9,25},{17,1},{25,9},{2,18},{10... | collective-permute-start | bytes 3145736 | tf_op jit(solution)/shard_map/ppermute | solution.py:947
  374.2 47.2 %collective-permute-start.17 = (bf16[256,2048]{1,0:T(8,128)(2,1)S(1)}, bf16[256,2048]{1,0:T(8,128)(2,1)}, u32[]{:S(2)}, u32[]{:S(2)}) collective-permute-start(bf16[256,2048]{1,0:T(8,128)(2,1)S(1)} %copy-done.61), channel_id=1, source_target_pairs={{0,24},{8,16},{16,8},{24,0},{1,25},{9,17},{17,9},{25,1},{2,26},{10... | collective-permute-start | bytes 3145736 | tf_op jit(solution)/shard_map/ppermute | solution.py:947
  412.1 50.0 %collective-permute-start.13 = (bf16[256,2048]{1,0:T(8,128)(2,1)S(1)}, bf16[256,2048]{1,0:T(8,128)(2,1)S(1)}, u32[]{:S(2)}, u32[]{:S(2)}) collective-permute-start(bf16[256,2048]{1,0:T(8,128)(2,1)S(1)} %get-tuple-element.97), channel_id=1, source_target_pairs={{0,16},{8,24},{16,0},{24,8},{1,17},{9,25},{17,1},{25,9},{2,18},{10... | collective-permute-start | bytes 3145736 | tf_op jit(solution)/shard_map/ppermute | solution.py:947
  413.1 50.0 %collective-permute-start.14 = (bf16[256,2048]{1,0:T(8,128)(2,1)S(1)}, bf16[256,2048]{1,0:T(8,128)(2,1)S(1)}, u32[]{:S(2)}, u32[]{:S(2)}) collective-permute-start(bf16[256,2048]{1,0:T(8,128)(2,1)S(1)} %get-tuple-element.98), channel_id=1, source_target_pairs={{0,24},{8,16},{16,8},{24,0},{1,25},{9,17},{17,9},{25,1},{2,26},{10... | collective-permute-start | bytes 3145736 | tf_op jit(solution)/shard_map/ppermute | solution.py:947
  469.0 47.2 %collective-permute-start.19 = (bf16[256,2048]{1,0:T(8,128)(2,1)S(1)}, bf16[256,2048]{1,0:T(8,128)(2,1)S(1)}, u32[]{:S(2)}, u32[]{:S(2)}) collective-permute-start(bf16[256,2048]{1,0:T(8,128)(2,1)S(1)} %get-tuple-element.102.refs_0_), channel_id=1, source_target_pairs={{0,16},{8,24},{16,0},{24,8},{1,17},{9,25},{17,1},{25,9},{2,18},{10... | collective-permute-start | bytes 3145736 | tf_op jit(solution)/shard_map/ppermute | solution.py:947
  470.2 46.1 %collective-permute-start.20 = (bf16[256,2048]{1,0:T(8,128)(2,1)S(1)}, bf16[256,2048]{1,0:T(8,128)(2,1)S(1)}, u32[]{:S(2)}, u32[]{:S(2)}) collective-permute-start(bf16[256,2048]{1,0:T(8,128)(2,1)S(1)} %get-tuple-element.102.refs_0_), channel_id=1, source_target_pairs={{0,24},{8,16},{16,8},{24,0},{1,25},{9,17},{17,9},{25,1},{2,26},{10... | collective-permute-start | bytes 3145736 | tf_op jit(solution)/shard_map/ppermute | solution.py:947
  518.7 69.4 %collective-permute-start.21 = (bf16[256,2048]{1,0:T(8,128)(2,1)}, bf16[256,2048]{1,0:T(8,128)(2,1)}, u32[]{:S(2)}, u32[]{:S(2)}) collective-permute-start(bf16[256,2048]{1,0:T(8,128)(2,1)} %after.50.refs_0_), channel_id=1, source_target_pairs={{0,8},{8,0},{16,24},{24,16},{1,9},{9,1},{17,25},{25,17},{2,10},{10... | collective-permute-start | bytes 3145736 | tf_op jit(solution)/shard_map/ppermute | solution.py:947
  519.3 90.2 %collective-permute-start.22 = (bf16[256,2048]{1,0:T(8,128)(2,1)}, bf16[256,2048]{1,0:T(8,128)(2,1)}, u32[]{:S(2)}, u32[]{:S(2)}) collective-permute-start(bf16[256,2048]{1,0:T(8,128)(2,1)} %after.50.refs_0_), channel_id=1, source_target_pairs={{0,16},{8,24},{16,0},{24,8},{1,17},{9,25},{17,1},{25,9},{2,18},{10... | collective-permute-start | bytes 3145736 | tf_op jit(solution)/shard_map/ppermute | solution.py:947
  520.5 89.1 %collective-permute-start.23 = (bf16[256,2048]{1,0:T(8,128)(2,1)}, bf16[256,2048]{1,0:T(8,128)(2,1)}, u32[]{:S(2)}, u32[]{:S(2)}) collective-permute-start(bf16[256,2048]{1,0:T(8,128)(2,1)} %after.50.refs_0_), channel_id=1, source_target_pairs={{0,24},{8,16},{16,8},{24,0},{1,25},{9,17},{17,9},{25,1},{2,26},{10... | collective-permute-start | bytes 3145736 | tf_op jit(solution)/shard_map/ppermute | solution.py:947
  523.4 89.8 %collective-permute-start.24 = (bf16[256,2048]{1,0:T(8,128)(2,1)S(1)}, bf16[256,2048]{1,0:T(8,128)(2,1)}, u32[]{:S(2)}, u32[]{:S(2)}) collective-permute-start(bf16[256,2048]{1,0:T(8,128)(2,1)S(1)} %copy-done.7), channel_id=1, source_target_pairs={{0,8},{8,0},{16,24},{24,16},{1,9},{9,1},{17,25},{25,17},{2,10},{10... | collective-permute-start | bytes 3145736 | tf_op jit(solution)/shard_map/ppermute | solution.py:947
  524.0 89.3 %collective-permute-start.25 = (bf16[256,2048]{1,0:T(8,128)(2,1)S(1)}, bf16[256,2048]{1,0:T(8,128)(2,1)}, u32[]{:S(2)}, u32[]{:S(2)}) collective-permute-start(bf16[256,2048]{1,0:T(8,128)(2,1)S(1)} %copy-done.7), channel_id=1, source_target_pairs={{0,16},{8,24},{16,0},{24,8},{1,17},{9,25},{17,1},{25,9},{2,18},{10... | collective-permute-start | bytes 3145736 | tf_op jit(solution)/shard_map/ppermute | solution.py:947
  616.6 42.3 %collective-permute-start.27 = (bf16[256,2048]{1,0:T(8,128)(2,1)}, bf16[256,2048]{1,0:T(8,128)(2,1)}, u32[]{:S(2)}, u32[]{:S(2)}) collective-permute-start(bf16[256,2048]{1,0:T(8,128)(2,1)} %after.52), channel_id=1, source_target_pairs={{0,8},{8,0},{16,24},{24,16},{1,9},{9,1},{17,25},{25,17},{2,10},{10... | collective-permute-start | bytes 3145736 | tf_op jit(solution)/shard_map/ppermute | solution.py:947
  617.8 44.4 %collective-permute-start.28 = (bf16[256,2048]{1,0:T(8,128)(2,1)S(1)}, bf16[256,2048]{1,0:T(8,128)(2,1)}, u32[]{:S(2)}, u32[]{:S(2)}) collective-permute-start(bf16[256,2048]{1,0:T(8,128)(2,1)S(1)} %copy-done.25), channel_id=1, source_target_pairs={{0,16},{8,24},{16,0},{24,8},{1,17},{9,25},{17,1},{25,9},{2,18},{10... | collective-permute-start | bytes 3145736 | tf_op jit(solution)/shard_map/ppermute | solution.py:947
  618.9 43.3 %collective-permute-start.29 = (bf16[256,2048]{1,0:T(8,128)(2,1)S(1)}, bf16[256,2048]{1,0:T(8,128)(2,1)}, u32[]{:S(2)}, u32[]{:S(2)}) collective-permute-start(bf16[256,2048]{1,0:T(8,128)(2,1)S(1)} %copy-done.27), channel_id=1, source_target_pairs={{0,24},{8,16},{16,8},{24,0},{1,25},{9,17},{17,9},{25,1},{2,26},{10... | collective-permute-start | bytes 3145736 | tf_op jit(solution)/shard_map/ppermute | solution.py:947
  683.0 193.6 %reduce-scatter.8.cloned.1.call-start = ((), (), s32[]{:S(2)}) async-start(), calls=%async_computation.17 | async-start | bytes 4718592 | tf_op jit(solution)/shard_map/reduce_scatter | solution.py:993
  684.5 43.0 %collective-permute-start.31 = (bf16[256,2048]{1,0:T(8,128)(2,1)S(1)}, bf16[256,2048]{1,0:T(8,128)(2,1)S(1)}, u32[]{:S(2)}, u32[]{:S(2)}) collective-permute-start(bf16[256,2048]{1,0:T(8,128)(2,1)S(1)} %copy-done.85), channel_id=1, source_target_pairs={{0,16},{8,24},{16,0},{24,8},{1,17},{9,25},{17,1},{25,9},{2,18},{10... | collective-permute-start | bytes 3145736 | tf_op jit(solution)/shard_map/ppermute | solution.py:947
  685.4 42.1 %collective-permute-start.32 = (bf16[256,2048]{1,0:T(8,128)(2,1)S(1)}, bf16[256,2048]{1,0:T(8,128)(2,1)S(1)}, u32[]{:S(2)}, u32[]{:S(2)}) collective-permute-start(bf16[256,2048]{1,0:T(8,128)(2,1)S(1)} %get-tuple-element.118), channel_id=1, source_target_pairs={{0,24},{8,16},{16,8},{24,0},{1,25},{9,17},{17,9},{25,1},{2,26},{10... | collective-permute-start | bytes 3145736 | tf_op jit(solution)/shard_map/ppermute | solution.py:947
  741.3 184.0 %reduce-scatter.10.cloned.1.call-start = ((), (), s32[]{:S(2)}) async-start(), calls=%async_computation.18 | async-start | bytes 4718592 | tf_op jit(solution)/shard_map/reduce_scatter | solution.py:993
  742.4 42.2 %collective-permute-start.34 = (bf16[256,2048]{1,0:T(8,128)(2,1)S(1)}, bf16[256,2048]{1,0:T(8,128)(2,1)S(1)}, u32[]{:S(2)}, u32[]{:S(2)}) collective-permute-start(bf16[256,2048]{1,0:T(8,128)(2,1)S(1)} %get-tuple-element.119.refs_3_.refs_0_), channel_id=1, source_target_pairs={{0,16},{8,24},{16,0},{24,8},{1,17},{9,25},{17,1},{25,9},{2,18},{10... | collective-permute-start | bytes 3145736 | tf_op jit(solution)/shard_map/ppermute | solution.py:947
  743.9 40.8 %collective-permute-start.35 = (bf16[256,2048]{1,0:T(8,128)(2,1)S(1)}, bf16[256,2048]{1,0:T(8,128)(2,1)S(1)}, u32[]{:S(2)}, u32[]{:S(2)}) collective-permute-start(bf16[256,2048]{1,0:T(8,128)(2,1)S(1)} %get-tuple-element.119.refs_3_.refs_0_), channel_id=1, source_target_pairs={{0,24},{8,16},{16,8},{24,0},{1,25},{9,17},{17,9},{25,1},{2,26},{10... | collective-permute-start | bytes 3145736 | tf_op jit(solution)/shard_map/ppermute | solution.py:947
  807.0 216.6 %reduce-scatter.12.cloned.1.call-start = ((), (), s32[]{:S(2)}) async-start(), calls=%async_computation.19 | async-start | bytes 5898240 | tf_op jit(solution)/shard_map/reduce_scatter | solution.py:993
  807.4 41.1 %collective-permute-start.37 = (bf16[256,2048]{1,0:T(8,128)(2,1)}, bf16[256,2048]{1,0:T(8,128)(2,1)S(1)}, u32[]{:S(2)}, u32[]{:S(2)}) collective-permute-start(bf16[256,2048]{1,0:T(8,128)(2,1)} %after.58), channel_id=1, source_target_pairs={{0,16},{8,24},{16,0},{24,8},{1,17},{9,25},{17,1},{25,9},{2,18},{10... | collective-permute-start | bytes 3145736 | tf_op jit(solution)/shard_map/ppermute | solution.py:947
  808.8 39.7 %collective-permute-start.38 = (bf16[256,2048]{1,0:T(8,128)(2,1)}, bf16[256,2048]{1,0:T(8,128)(2,1)}, u32[]{:S(2)}, u32[]{:S(2)}) collective-permute-start(bf16[256,2048]{1,0:T(8,128)(2,1)} %after.59), channel_id=1, source_target_pairs={{0,24},{8,16},{16,8},{24,0},{1,25},{9,17},{17,9},{25,1},{2,26},{10... | collective-permute-start | bytes 3145736 | tf_op jit(solution)/shard_map/ppermute | solution.py:947
  868.8 40.1 %collective-permute-start.39 = (bf16[256,2048]{1,0:T(8,128)(2,1)S(1)}, bf16[256,2048]{1,0:T(8,128)(2,1)}, u32[]{:S(2)}, u32[]{:S(2)}) collective-permute-start(bf16[256,2048]{1,0:T(8,128)(2,1)S(1)} %copy-done.45), channel_id=1, source_target_pairs={{0,8},{8,0},{16,24},{24,16},{1,9},{9,1},{17,25},{25,17},{2,10},{10... | collective-permute-start | bytes 3145736 | tf_op jit(solution)/shard_map/ppermute | solution.py:947
  870.4 48.9 %collective-permute-start.40 = (bf16[256,2048]{1,0:T(8,128)(2,1)S(1)}, bf16[256,2048]{1,0:T(8,128)(2,1)}, u32[]{:S(2)}, u32[]{:S(2)}) collective-permute-start(bf16[256,2048]{1,0:T(8,128)(2,1)S(1)} %copy-done.47), channel_id=1, source_target_pairs={{0,16},{8,24},{16,0},{24,8},{1,17},{9,25},{17,1},{25,9},{2,18},{10... | collective-permute-start | bytes 3145736 | tf_op jit(solution)/shard_map/ppermute | solution.py:947
  871.0 48.3 %collective-permute-start.41 = (bf16[256,2048]{1,0:T(8,128)(2,1)S(1)}, bf16[256,2048]{1,0:T(8,128)(2,1)}, u32[]{:S(2)}, u32[]{:S(2)}) collective-permute-start(bf16[256,2048]{1,0:T(8,128)(2,1)S(1)} %copy-done.49), channel_id=1, source_target_pairs={{0,24},{8,16},{16,8},{24,0},{1,25},{9,17},{17,9},{25,1},{2,26},{10... | collective-permute-start | bytes 3145736 | tf_op jit(solution)/shard_map/ppermute | solution.py:947
  872.3 51.2 %all-to-all-start.2 = ((bf16[4,64,2048]{2,1,0:T(8,128)(2,1)}), bf16[4,64,2048]{2,1,0:T(8,128)(2,1)}, u32[]{:S(2)}, u32[]{:S(2)}) async-start(bf16[4,64,2048]{2,1,0:T(8,128)(2,1)} %bitcast.214), calls=%async_computation.4 | async-start | bytes 2097152 | tf_op jit(solution)/shard_map/all_to_all | solution.py:985
  876.6 159.2 %reduce-scatter.14.cloned.1.call-start = ((), (), s32[]{:S(2)}) async-start(), calls=%async_computation.20 | async-start | bytes 6488064 | tf_op jit(solution)/shard_map/reduce_scatter | solution.py:993
  963.6 43.1 %collective-permute-start.42 = (bf16[256,2048]{1,0:T(8,128)(2,1)}, bf16[256,2048]{1,0:T(8,128)(2,1)}, u32[]{:S(2)}, u32[]{:S(2)}) collective-permute-start(bf16[256,2048]{1,0:T(8,128)(2,1)} %get-tuple-element.134), channel_id=1, source_target_pairs={{0,8},{8,0},{16,24},{24,16},{1,9},{9,1},{17,25},{25,17},{2,10},{10... | collective-permute-start | bytes 3145736 | tf_op jit(solution)/shard_map/ppermute | solution.py:947
  963.6 43.1 %collective-permute-start.43 = (bf16[256,2048]{1,0:T(8,128)(2,1)}, bf16[256,2048]{1,0:T(8,128)(2,1)}, u32[]{:S(2)}, u32[]{:S(2)}) collective-permute-start(bf16[256,2048]{1,0:T(8,128)(2,1)} %get-tuple-element.135), channel_id=1, source_target_pairs={{0,16},{8,24},{16,0},{24,8},{1,17},{9,25},{17,1},{25,9},{2,18},{10... | collective-permute-start | bytes 3145736 | tf_op jit(solution)/shard_map/ppermute | solution.py:947
  963.8 42.9 %collective-permute-start.44 = (bf16[256,2048]{1,0:T(8,128)(2,1)}, bf16[256,2048]{1,0:T(8,128)(2,1)}, u32[]{:S(2)}, u32[]{:S(2)}) collective-permute-start(bf16[256,2048]{1,0:T(8,128)(2,1)} %get-tuple-element.136), channel_id=1, source_target_pairs={{0,24},{8,16},{16,8},{24,0},{1,25},{9,17},{17,9},{25,1},{2,26},{10... | collective-permute-start | bytes 3145736 | tf_op jit(solution)/shard_map/ppermute | solution.py:947
  (166 other events, 2136.5 us)
Sparse Core Ops, SparseCore 0:
  32.3 33.5 all-gather.6
  68.1 59.4 all-gather.8
  131.1 37.9 all-gather.10
  171.2 46.0 all-gather.12
  218.7 45.8 all-gather.16
  266.1 80.7 all-gather.14
  683.2 89.4 reduce-scatter.5
  774.9 48.3 reduce-scatter.7
  825.6 48.1 reduce-scatter.9
  875.9 58.0 reduce-scatter.11
  945.0 66.4 reduce-scatter.13

commit v5 on v4

--- a/solution.py
+++ b/solution.py
@@ -359,7 +359,7 @@
         compiler_params=pltpu.CompilerParams(
             dimension_semantics=("arbitrary",), vmem_limit_bytes=VMEM_BYTES
         ),
-        cost_estimate=work(15),
+        cost_estimate=work(0),
         name="ssd_forward",
     )(order, first, aux, seg_rows, conv, head, skip)
 
@@ -651,13 +651,6 @@
     outs[0][...] = total.astype(jnp.bfloat16)
     if keep_wide:
         outs[1][...] = total
-    gain_grad = outs[-1]
-
-    @pl.when(pl.program_id(0) == 0)
-    def _():
-        gain_grad[...] = jnp.zeros(gain_grad.shape, jnp.float32)
-
-    gain_grad[0:1, :] += jnp.sum(normed * grads, axis=0, keepdims=True)
 
 
 def add_rows_kernel(count, own, rows, gain, *refs):
@@ -751,36 +744,42 @@
     )(*pieces)
 
 
-def start_rows_kernel(places, halves, rows, cot, out):
-    @pl.when(pl.program_id(0) < halves)
+def start_rows_kernel(places, halves, rows, *refs):
+    cots, out = refs[:-1], refs[-1]
+    part = pl.program_id(0) // halves
+
+    @pl.when(part == 0)
     def _():
         moved = to_gathered_tiles(tiles_of(rows[...].astype(jnp.float32)), *places)
         out[...] = jnp.concatenate(moved, axis=1).astype(out.dtype)
 
-    @pl.when(pl.program_id(0) >= halves)
-    def _():
-        out[...] = cot[...]
-
-
-def start_rows(rows, cot, places):
+    for place, cot in enumerate(cots):
+
+        @pl.when(part == place + 1)
+        def _(cot=cot):
+            out[...] = cot[...]
+
+
+def start_rows(rows, cots, places):
     tokens, width = rows.shape
     halves = tokens // SPAN
+    parts = 1 + len(cots)
+
+    def block(part):
+        return pl.BlockSpec((SPAN, width), lambda i: (jnp.clip(i - part * halves, 0, halves - 1), 0))
 
     return pl.pallas_call(
         functools.partial(start_rows_kernel, places, halves),
-        grid=(2 * halves,),
-        in_specs=[
-            pl.BlockSpec((SPAN, width), lambda i: (jnp.minimum(i, halves - 1), 0)),
-            pl.BlockSpec((SPAN, width), lambda i: (jnp.maximum(i - halves, 0), 0)),
-        ],
+        grid=(parts * halves,),
+        in_specs=[block(part) for part in range(parts)],
         out_specs=pl.BlockSpec((SPAN, width), lambda i: (i, 0)),
-        out_shape=jax.ShapeDtypeStruct((2 * tokens, width), rows.dtype),
+        out_shape=jax.ShapeDtypeStruct((parts * tokens, width), rows.dtype),
         compiler_params=pltpu.CompilerParams(
             dimension_semantics=("arbitrary",), vmem_limit_bytes=VMEM_BYTES
         ),
         cost_estimate=work(2),
         name="start_rows",
-    )(rows, cot)
+    )(rows, *cots)
 
 
 def product_kernel(back, pairs, skip, sets, *refs):
@@ -799,7 +798,7 @@
             outs[out][place * SPAN : (place + 1) * SPAN, :] = part.astype(outs[out].dtype)
 
 
-def product_rows(lefts, rights, back, sets, dtypes, deps=()):
+def product_rows(lefts, rights, back, sets, dtypes, deps=(), weight=1):
     length = lefts[0].shape[0]
     width = rights[0].shape[0 if back else 1]
     slab = 512
@@ -820,7 +819,7 @@
         compiler_params=pltpu.CompilerParams(
             dimension_semantics=("arbitrary",), vmem_limit_bytes=VMEM_BYTES
         ),
-        cost_estimate=work(sum(2 * length * left.shape[1] * width for left in lefts) / 0.66e9),
+        cost_estimate=work(weight * sum(2 * length * left.shape[1] * width for left in lefts) / 0.66e9),
         name="product_rows",
     )(*lefts, *rights, *deps)
 
@@ -961,23 +960,22 @@
     return [rows] + [swap(rows, flip) for flip in range(1, lax.axis_size("seq"))]
 
 
-def scatter_tokens(lefts, rights, back, tokens, hold=(), deps=()):
+def scatter_tokens(lefts, rights, back, tokens, hold=(), deps=(), weight=1):
     f32, bf16 = jnp.float32, jnp.bfloat16
     halves = tokens // SPAN
     count = lax.axis_size("seq")
     sets = tuple(tuple(range(flip * halves, (flip + 1) * halves)) for flip in range(count))
-    own, *parts = product_rows(lefts, rights, back, sets, (f32,) + (bf16,) * (count - 1), deps)
+    own, *parts = product_rows(lefts, rights, back, sets, (f32,) + (bf16,) * (count - 1), deps, weight)
     arrived = [swap(after(part, *hold) if hold else part, flip + 1) for flip, part in enumerate(parts)]
     return own, tuple(arrived), tuple(parts)
 
 
-def add_small(vector):
-    for axis in ("fsdp", "seq"):
-        count = lax.axis_size(axis)
-        flip = 1
-        while flip < count:
-            vector = vector + lax.ppermute(vector, axis, peers(count, flip))
-            flip *= 2
+def add_over(vector, axis):
+    count = lax.axis_size(axis)
+    flip = 1
+    while flip < count:
+        vector = vector + lax.ppermute(vector, axis, peers(count, flip))
+        flip *= 2
     return vector
 
 
@@ -1141,21 +1139,19 @@
 
     def mixer_out(m, deps, hold=()):
         mixeds.append(
-            scatter_tokens([gateds[m], attendeds[m]], [ssm_out_w, attn_out_w], False, tokens, hold, deps)
+            scatter_tokens([gateds[m], attendeds[m]], [ssm_out_w, attn_out_w], False, tokens, hold, deps, m)
         )
 
-    def fetch_cotangent(m, deps):
-        cot_alls.append(assemble(fetch_tokens(after(cotangent[m, 0], *deps)), spots))
-
-    mixer_start(0)
-    later_mine = trade(after(later_send, attendeds[0]))
-    pieces.append(fetch_tokens(after(start_rows(inputs[1, 0], cotangent[0, 0], places), later_mine)))
+    later_mine = trade(after(later_send, *pieces[0][1:]))
+    mixer_start(0, [later_mine])
+    start_second = start_rows(inputs[1, 0], [cotangent[m, 0] for m in micro], places)
+    pieces.append(fetch_tokens(after(start_second, later_mine)))
     z_mine, ffn_mine = later_mine[:, :, :inner], later_mine[:, :, inner:]
     z_w = gather_weights(z_mine)
     out_send = after(out_send, z_mine)
     out_w = gather_weights(out_send)
     gate_up_w = gather_weights(after(ffn_mine, out_send))
-    mixer_scan(0, [attendeds[0], later_mine])
+    mixer_scan(0, [attendeds[0], later_mine, start_second])
     down_w = gather_weights(after(w_down, firsts[0]))
     out_w = out_w.reshape(fsdp, -1, out_w.shape[1])
     ssm_out_w, attn_out_w = out_w[:, :out_rows].reshape(inner, -1), out_w[:, out_rows:].reshape(q_width, -1)
@@ -1163,11 +1159,11 @@
     mixer_gate(0, [ys[0]])
     mixer_out(0, [gateds[0]])
     mixer_start(1, [mixeds[0][0]])
-    cot_alls.append(assemble(pieces[1], [(flip, half + halves) for flip, half in spots]))
-    mixer_scan(1, [attendeds[1]])
+    for m in micro:
+        cot_alls.append(assemble(pieces[1], [(flip, half + (1 + m) * halves) for flip, half in spots]))
 
     middles, ffn_hiddens, activateds, grad_gus, grad_hiddens = [], [], [], [], []
-    grad_middles, lows, gain_ffn_grads, grads_mixed = [], [], [], []
+    grad_middles, lows, grads_mixed = [], [], []
 
     def middle_forward(m, deps, hold=()):
         own, arrived, parts = mixeds[m]
@@ -1196,20 +1192,19 @@
 
     def middle_back(m, deps):
         own, arrived, parts = grad_hiddens[m]
-        low, wide, gain_grad = rows_call(
+        low, wide = rows_call(
             functools.partial(norm_back_kernel, places, len(arrived), len(deps), True),
             tokens,
             width,
             [own, middles[m], cotangent[m, 0]],
             gain_ffn,
             arrived,
-            [((tokens, width), bf16), ((tokens, width), f32), ((8, width), f32)],
+            [((tokens, width), bf16), ((tokens, width), f32)],
             deps,
             "middle_back",
         )
         grad_middles.append(wide)
         lows.append(low)
-        gain_ffn_grads.append(gain_grad[0])
         grads_mixed.append(assemble(fetch_tokens(low), spots))
 
     grad_ys, grad_sides, outs, back, in_backs, outputs = [], [], [], [], [], []
@@ -1245,18 +1240,17 @@
 
     def finish_input(m, deps=()):
         own, arrived, parts = in_backs[m]
-        low, gain_grad = rows_call(
+        return rows_call(
             functools.partial(norm_back_kernel, places, len(arrived), len(deps), False),
             tokens,
             width,
             [own, inputs[m, 0], grad_middles[m]],
             gain_in,
             arrived,
-            [((tokens, width), bf16), ((8, width), f32)],
+            [((tokens, width), bf16)],
             deps,
             "input_back",
-        )
-        return low, gain_grad[0]
+        )[0]
 
     def finish_output(m, deps=()):
         own, arrived, parts = outs[m]
@@ -1278,8 +1272,9 @@
     def back_to_rows(part):
         return trade(part.reshape(seq, rows, -1)).astype(f32)
 
-    middle_forward(0, [ys[1]])
-    mixer_gate(1, [middles[0]])
+    middle_forward(0, [attendeds[1]])
+    mixer_scan(1, [middles[0]])
+    mixer_gate(1, [ys[1]])
     mixer_out(1, [gateds[1]])
     mixeds[1] = (
         mixeds[1][0],
@@ -1291,44 +1286,38 @@
     down_sum = weight_sums(activateds[:1], cot_alls[:1], f32, None, [gate_up_sum])
     middle_back(0, [down_sum])
     middle_forward(1, (), [grads_mixed[0]])
-    fetch_cotangent(1, [grads_mixed[0]])
     heads_back(0, ())
-    output_rows(0, grad_sides, [ffn_hiddens[1], cot_alls[1]])
-    scan_back(0, [outs[0][0]])
-    hidden_back(0, ())
-    feed_forward(1, [in_backs[0][0]])
+    output_rows(0, grad_sides, [ffn_hiddens[1]])
+    feed_forward(1, [outs[0][0]])
     outputs.append(finish_output(0, [grad_hiddens[1][0]]))
     gate_up_sum = weight_sums(ffn_hiddens[1:], grad_gus[1:], bf16, gate_up_sum, [outputs[0]])
     gate_up_part = spread_sums(gate_up_sum)
-    middle_back(1, [gate_up_sum])
-
-    def send_late(scattered):
-        late = [swap(after(part, grads_mixed[1]), flip + 1) for flip, part in enumerate(scattered[2])]
-        return scattered[0], tuple(late), ()
+    scan_back(0, [gate_up_sum])
+    side_sum = weight_sums(hiddens[:1], grad_sides[:1], f32, None, [back[0][0]])
+    ssm_out_sum = weight_sums(gateds[:1], grads_mixed[:1], f32, None, [side_sum])
+    attn_out_sum = weight_sums(attendeds[:1], grads_mixed[:1], f32, None, [ssm_out_sum])
+    middle_back(1, [attn_out_sum])
 
     down_sum = weight_sums(activateds[1:], cot_alls[1:], bf16, down_sum, [lows[1]])
     down_part = spread_sums(down_sum)
-    in_backs[0] = send_late(in_backs[0])
-    output_rows(1, [down_sum], [grads_mixed[1]])
-    ssm_out_sum = weight_sums(gateds, grads_mixed, bf16, None, [outs[1][0]])
-    attn_out_sum = weight_sums(attendeds, grads_mixed, bf16, None, [ssm_out_sum])
+    hidden_back(0, [down_sum], [grads_mixed[1]])
+    output_rows(1, [in_backs[0][0]], [grads_mixed[1]])
+    first_sum = weight_sums(hiddens[:1], [back[0][0]], f32, None, [outs[1][0]])
+    ssm_out_sum = weight_sums(gateds[1:], grads_mixed[1:], bf16, ssm_out_sum, [first_sum])
+    attn_out_sum = weight_sums(attendeds[1:], grads_mixed[1:], bf16, attn_out_sum, [ssm_out_sum])
     out_sum = jnp.concatenate(
         [ssm_out_sum.reshape(fsdp, -1, width), attn_out_sum.reshape(fsdp, -1, width)], axis=1
     ).reshape(inner + q_width, width)
     out_part = spread_sums(out_sum)
-    heads_back(1, [out_sum, gate_up_part])
+    heads_back(1, [out_sum])
     outputs.append(finish_output(1, [grad_sides[1]]))
-    side_sum = weight_sums(hiddens, grad_sides, bf16, None, [outputs[1]])
+    side_sum = weight_sums(hiddens[1:], grad_sides[1:], bf16, side_sum, [outputs[1], gate_up_part])
     side_part = spread_sums(side_sum)
     gate_up_back = back_to_rows(gate_up_part)
     side_back = back_to_rows(side_part)
     scan_back(1, [side_sum, down_part])
-    low, gain_grad = finish_input(0, [back[1][0]])
-    input_grads, gain_in_grads = [low], [gain_grad]
-    first_sum = weight_sums(hiddens, [b[0] for b in back], bf16, None, [low, gate_up_back, out_part])
-    first_part = spread_sums(first_sum)
-    hidden_back(1, [first_sum])
-    first_back = back_to_rows(first_part)
+    low = finish_input(0, [back[1][0]])
+    input_grads = [low]
     conv_grad = (back[0][1] + back[1][1])[: CONV + 1]
     head_grad = back[0][2] + back[1][2]
     skip_sum = jnp.sum((back[0][3] + back[1][3])[0].reshape(heads, SSM_DIM), axis=1)
@@ -1338,16 +1327,19 @@
     head_sums = lax.dynamic_update_slice_in_dim(
         jnp.zeros((3, SSM_HEADS), f32), jnp.stack([head_grad[0, :heads], head_grad[1, :heads], skip_sum]), head_start, 1
     )
-    small_sums = [conv_whole.reshape(-1), head_sums.reshape(-1), gain_ffn_grads[0] + gain_ffn_grads[1]]
+    small_sums = [conv_whole.reshape(-1), head_sums.reshape(-1)]
     ends = [0]
     for piece in small_sums:
         ends.append(ends[-1] + piece.shape[0])
-    total = add_small(after(jnp.concatenate(small_sums), in_backs[1][0]))
-    low, gain_grad = finish_input(1, [total])
-    input_grads.append(low)
-    gain_in_total = add_small(gain_in_grads[0] + gain_grad)
-
-    out_part = after(out_part, first_back).astype(f32)
+    total = add_over(jnp.concatenate(small_sums), "seq")
+    first_sum = weight_sums(hiddens[1:], [back[1][0]], bf16, first_sum, [low, gate_up_back, out_part, total])
+    first_part = spread_sums(first_sum)
+    first_back = back_to_rows(first_part)
+    hidden_back(1, [first_sum])
+    total = add_over(after(total, in_backs[1][0]), "fsdp")
+    input_grads.append(finish_input(1))
+
+    out_part = after(out_part, in_backs[1][0]).astype(f32)
 
     def own_columns(block):
         return jnp.swapaxes(block, 0, 1).reshape(rows, -1)
@@ -1377,14 +1369,18 @@
         axis=1,
     )
 
-    conv_total, head_total, gain_ffn_total = (total[a:b] for a, b in zip(ends[:-1], ends[1:]))
+    conv_total, head_total = (total[a:b] for a, b in zip(ends[:-1], ends[1:]))
+    def gain_grad(gain, *pairs):
+        total = sum(jnp.sum(weight.astype(f32) * grad, axis=1) for weight, grad in pairs)
+        return total / gain.astype(f32)
+
     place = index * fsdp + lax.axis_index("fsdp")
     conv_total = lax.dynamic_slice_in_dim(conv_total.reshape(CONV + 1, CONV_CH), place * channels, channels, 1)
     head_total = head_total.reshape(3, SSM_HEADS)
     return (
         jnp.stack(outputs)[:, None],
         jnp.stack(input_grads)[:, None],
-        lax.dynamic_slice_in_dim(gain_in_total, place * rows, rows),
+        gain_grad(norm_in, (ssm_in, ssm_in_grad), (attn_in, attn_in_grad)),
         ssm_in_grad,
         attn_in_grad,
         conv_total[:CONV],
@@ -1394,10 +1390,10 @@
         head_total[2],
         out_part[:out_rows],
         out_part[out_rows:],
-        lax.dynamic_slice_in_dim(gain_ffn_total, place * rows, rows),
+        gain_grad(norm_ffn, (w_gate, gate_grad), (w_up, up_grad)),
         gate_grad,
         up_grad,
-        after(down_part, first_back).astype(f32),
+        after(down_part, in_backs[1][0]).astype(f32),
     )
 
 

time: 1080 us -> 1050 us (0.972); the launches traced: 1060 us -> 1050 us
  Pallas kernels: 404 us -> 424 us
  blocking collectives: 39.1 us -> 19.1 us
    ppermute x45 -> x42, waiting for transfers between devices: 239 us -> 198 us  [swap(): return lax.ppermute(value, 'seq', peers(lax.axis_size('seq'), flip))]
    all_gather x6, waiting for transfers between devices: 44.6 us -> 68.4 us  [gather_weights(): lax.all_gather(rows.reshape(-1, rows.shape[-1]), 'fsdp', axis=0, tiled=True)]
    all_to_all x3 -> x4, waiting for transfers between devices: 7.62 us -> 28.6 us  [trade(): lax.all_to_all(stacked, 'seq', split_axis=0, concat_axis=0, tiled=True)]
    all_to_all x2 -> x1, blocking collectives: 39.1 us -> 19.1 us  [trade(): lax.all_to_all(stacked, 'seq', split_axis=0, concat_axis=0, tiled=True)]
    pallas_call x8 -> x12, Pallas kernels: 98.3 us -> 113 us  [weight_sums(): pl.pallas_call(functools.partial(sums_kernel, len(lefts), len(extra), len...]
    ppermute x10 -> x5, waiting for transfers between devices: 35.3 us -> 26.4 us  [add_over(): vector = vector + lax.ppermute(vector, axis, peers(count, flip))]
    unnamed x298 -> x292, local copies, waits for them, and re-layouts: 58.6 us -> 52.8 us
    ppermute x45 -> x42, starting transfers between devices: 52.9 us -> 49.3 us  [swap(): return lax.ppermute(value, 'seq', peers(lax.axis_size('seq'), flip))]
  transfers between devices with their start and end apart: 69 -> 62, of which waited for: 30 -> 30; matrix products, arithmetic and copies ran while one was open for 12% -> 13% of each run, Pallas kernels for 35% -> 38%
where the time goes in v5:
time: 1050 us
  Pallas kernels  424 us (40%)
  waiting for transfers between devices  322 us (31%)
  local copies, waits for them, and re-layouts  84.2 us (8%)
  matrix products  74.2 us (7%)
  starting transfers between devices  71.3 us (7%)
  other arithmetic  33.8 us (3%)
  blocking collectives  19.1 us (2%)
  between operations  16.2 us (2%)
    ppermute x42, waiting for transfers between devices, swap(): return lax.ppermute(value, 'seq', peers(lax.axis_size('seq'), flip))  198 us
    pallas_call x12, Pallas kernels, weight_sums(): pl.pallas_call(functools.partial(sums_kernel, len(lefts), len(extra), len...  113 us
    pallas_call x8, Pallas kernels, product_rows(): pl.pallas_call(functools.partial(product_kernel, back, len(lefts), len(de...  93.6 us
    all_gather x6, waiting for transfers between devices, gather_weights(): lax.all_gather(rows.reshape(-1, rows.shape[-1]), 'fsdp', axis=0, tiled=True)  68.4 us
    pallas_call x2, Pallas kernels, ssd_backward(): pl.pallas_call(functools.partial(ssd_backward_kernel, heads), grid_spec=p...  56.8 us
    unnamed x292, local copies, waits for them, and re-layouts  52.8 us
    dot_general x6, matrix products, matmul_rows(): jnp.einsum('tc,cd->td', left, right, preferred_element_type=jnp.float32)  51.8 us
    ppermute x42, starting transfers between devices, swap(): return lax.ppermute(value, 'seq', peers(lax.axis_size('seq'), flip))  49.3 us
  transfers between devices with their start and end apart: 62, of which 30 were waited for; matrix products, arithmetic and copies ran while one was open for 13% of the time, Pallas kernels for 38%

profile of v5, /device:TPU:0, one launch (start us, length us, event | category | flops | bytes accessed | tf_op | source)
XLA Modules:
  0.0 1045.1 jit_solution(14996821937593332080)
XLA Ops:
  12.2 19.1 %all_to_all.25.refs_1_ = bf16[4,64,2048]{2,1,0:T(8,128)(2,1)S(1)} all-to-all(bf16[4,64,2048]{2,1,0:T(8,128)(2,1)S(1)} %pad_dynamic-update-slice_fusion), channel_id=1, replica_groups=mesh['seq'=4,'fsdp'=8] {'seq'}, dimensions={0} | all-to-all | bytes 2097152 | tf_op jit(solution)/shard_map/all_to_all | solution.py:983
  41.2 22.4 %collective-permute-done.2.refs_3_.refs_6_.refs_7_ = bf16[256,2048]{1,0:T(8,128)(2,1)S(1)} collective-permute-done((bf16[256,2048]{1,0:T(8,128)(2,1)}, bf16[256,2048]{1,0:T(8,128)(2,1)S(1)}, u32[]{:S(2)}, u32[]{:S(2)}) %collective-permute-start.2) | collective-permute-done | bytes 1048608 | tf_op jit(solution)/shard_map/ppermute | solution.py:946
  63.6 19.8 %collective-permute-done.1.refs_2_.refs_4_.refs_5_ = bf16[256,2048]{1,0:T(8,128)(2,1)} collective-permute-done((bf16[256,2048]{1,0:T(8,128)(2,1)}, bf16[256,2048]{1,0:T(8,128)(2,1)}, u32[]{:S(2)}, u32[]{:S(2)}) %collective-permute-start.1) | collective-permute-done | bytes 1048608 | tf_op jit(solution)/shard_map/ppermute | solution.py:946
  87.9 17.4 %all-to-all-done.1.refs_1_.refs_2_ = bf16[4,64,2816]{2,1,0:T(8,128)(2,1)S(1)} async-done(((bf16[4,64,2816]{2,1,0:T(8,128)(2,1)}), bf16[4,64,2816]{2,1,0:T(8,128)(2,1)S(1)}, u32[]{:S(2)}, u32[]{:S(2)}) %all-to-all-start.1) | async-done | bytes 1441824 | tf_op jit(solution)/shard_map/all_to_all | solution.py:983
  160.3 54.9 %all-gather.9.cloned.1.call-done.refs_2_ = bf16[2048,1408]{1,0:T(8,128)(2,1)} async-done(((bf16[256,1408]{1,0:T(8,128)(2,1)}), bf16[2048,1408]{1,0:T(8,128)(2,1)}) %all-gather.9.cloned.1.call-update) | async-done | bytes 5767184 | tf_op jit(solution)/shard_map/all_gather | solution.py:987
  215.2 11.5 %convolution_convert_fusion.1.first_ref.refs_1_.before_ref = bf16[1024,1408]{1,0:T(8,128)(2,1)} fusion(bf16[1024,2048]{1,0:T(8,128)(2,1)} %after.37.refs_0_, bf16[2048,1408]{1,0:T(8,128)(2,1)} %all-gather.9.cloned.1.call-done.refs_2_), kind=kOutput, calls=%fused_computation.7 | convolution fusion | flops 5907021824 | bytes 12845056 | tf_op jit(solution)/shard_map/tc,cd->td/dot_general | solution.py:930
  230.2 13.5 %ssd_forward.2 = (bf16[1024,768]{1,0:T(8,128)(2,1)S(1)}, bf16[8,256,768]{2,1,0:T(8,128)(2,1)}) custom-call(s32[8]{0:T(128)S(1)} %copy-done.85, bf16[1024,1408]{1,0:T(8,128)(2,1)S(1)} %copy-done.8, f32[1024,16]{1,0:T(8,128)S(1)} %copy-done.25, f32[8,1,128]{2,1,0:T(1,128)S(1)} %get-tuple-element.226.seg_ref, f32[8,1280]{1,0:T(8,128)S(1)} %select_maximum_fusion.conv_ref, ...), custom_call_target="tpu_custom_call" | custom-call | tf_op jit(solution)/shard_map/ssd_forward/pallas_call | solution.py:339
  244.9 9.3 all-gather.11.cloned.1.call-done
  254.2 9.4 fusion
  263.7 8.2 product_rows.8
  284.1 6.5 norm_pieces.3.refs_0_
  305.5 19.8 %collective-permute-done.5.refs_2_ = bf16[256,2048]{1,0:T(8,128)(2,1)} collective-permute-done((bf16[256,2048]{1,0:T(8,128)(2,1)}, bf16[256,2048]{1,0:T(8,128)(2,1)}, u32[]{:S(2)}, u32[]{:S(2)}) %collective-permute-start.5) | collective-permute-done | bytes 1048608 | tf_op jit(solution)/shard_map/ppermute | solution.py:946
  332.9 10.3 convolution_convert_fusion.first_ref.before_ref
  343.2 13.5 %ssd_forward.3 = (bf16[1024,768]{1,0:T(8,128)(2,1)S(1)}, bf16[8,256,768]{2,1,0:T(8,128)(2,1)}) custom-call(s32[8]{0:T(128)S(1)} %copy-done.86, bf16[1024,1408]{1,0:T(8,128)(2,1)S(1)} %convolution_convert_fusion.first_ref.before_ref, f32[1024,16]{1,0:T(8,128)S(1)} %copy.218.aux_ref, f32[8,1,128]{2,1,0:T(1,128)S(1)} %get-tuple-element.223.seg_ref, ...), custom_call_target="tpu_custom_call" | custom-call | tf_op jit(solution)/shard_map/ssd_forward/pallas_call | solution.py:339
  360.8 9.2 fusion.4
  370.0 7.5 product_rows.10
  387.7 21.6 %feed_products.2 = (bf16[1024,1024]{1,0:T(8,128)(2,1)S(1)}, bf16[1024,2048]{1,0:T(8,128)(2,1)}) custom-call(bf16[1024,2048]{1,0:T(8,128)(2,1)} %after.42.hidden.refs_0_, bf16[1024,2048]{1,0:T(8,128)(2,1)} %assemble.7.cot.refs_1_, bf16[2048,2048]{1,0:T(8,128)(2,1)} %all-gather.15.cloned.1.call-done.gate_w.up_w.refs_1_, ...), custom_call_target="tpu_custom_call" | custom-call | flops 24696061952 | tf_op jit(solution)/shard_map/feed_products/pallas_call | solution.py:848
  409.3 13.4 %product_rows.9 = (f32[256,2048]{1,0:T(8,128)S(1)}, bf16[256,2048]{1,0:T(8,128)(2,1)S(1)}, bf16[256,2048]{1,0:T(8,128)(2,1)S(1)}, bf16[256,2048]{1,0:T(8,128)(2,1)S(1)}) custom-call(bf16[1024,2048]{1,0:T(8,128)(2,1)} %get-tuple-element.86.refs_0_.refs_1_, bf16[2048,2048]{1,0:T(8,128)(2,1)} %all-gather.15.cloned.1.call-done.gate_w.up_w.refs_1_), custom_call_target="tpu_custom_call" | custom-call | flops 14967310336 | tf_op jit(solution)/shard_map/product_rows/pallas_call | solution.py:811
  434.0 16.1 %weight_sums.12.refs_2_ = f32[2048,2048]{1,0:T(8,128)} custom-call(bf16[1024,2048]{1,0:T(8,128)(2,1)} %after.42.hidden.refs_0_, bf16[1024,2048]{1,0:T(8,128)(2,1)} %get-tuple-element.86.refs_0_.refs_1_, f32[256,2048]{1,0:T(8,128)S(1)} %get-tuple-element.87.refs_2_.own, bf16[256,2048]{1,0:T(8,128)(2,1)} %collective-permute-done.15.refs_3_.refs_0_, ...), custom_call_target="tpu_custom_call" | custom-call | flops 14967310336 | tf_op jit(solution)/shard_map/weight_sums/pallas_call | solution.py:890
  450.1 8.5 weight_sums.13.refs_3_.refs_2_
  458.6 16.8 %collective-permute-done.14.refs_2_ = bf16[256,2048]{1,0:T(8,128)(2,1)} collective-permute-done((bf16[256,2048]{1,0:T(8,128)(2,1)S(1)}, bf16[256,2048]{1,0:T(8,128)(2,1)}, u32[]{:S(2)}, u32[]{:S(2)}) %collective-permute-start.14) | collective-permute-done | bytes 1048608 | tf_op jit(solution)/shard_map/ppermute | solution.py:946
  491.5 15.5 %collective-permute-done.20.refs_3_ = bf16[256,2048]{1,0:T(8,128)(2,1)S(1)} collective-permute-done((bf16[256,2048]{1,0:T(8,128)(2,1)S(1)}, bf16[256,2048]{1,0:T(8,128)(2,1)S(1)}, u32[]{:S(2)}, u32[]{:S(2)}) %collective-permute-start.20) | collective-permute-done | bytes 1048608 | tf_op jit(solution)/shard_map/ppermute | solution.py:946
  506.9 18.0 %collective-permute-done.19.refs_2_ = bf16[256,2048]{1,0:T(8,128)(2,1)S(1)} collective-permute-done((bf16[256,2048]{1,0:T(8,128)(2,1)S(1)}, bf16[256,2048]{1,0:T(8,128)(2,1)S(1)}, u32[]{:S(2)}, u32[]{:S(2)}) %collective-permute-start.19) | collective-permute-done | bytes 1048608 | tf_op jit(solution)/shard_map/ppermute | solution.py:946
  535.9 7.8 multiply_convert_fusion.1
  543.8 6.9 attend_backward.2
  552.3 7.3 product_rows.11
  562.9 14.0 %collective-permute-done.22.refs_2_ = bf16[256,2048]{1,0:T(8,128)(2,1)S(1)} collective-permute-done((bf16[256,2048]{1,0:T(8,128)(2,1)S(1)}, bf16[256,2048]{1,0:T(8,128)(2,1)S(1)}, u32[]{:S(2)}, u32[]{:S(2)}) %collective-permute-start.22) | collective-permute-done | bytes 1048608 | tf_op jit(solution)/shard_map/ppermute | solution.py:946
  583.4 21.5 %feed_products.3 = (bf16[1024,1024]{1,0:T(8,128)(2,1)S(1)}, bf16[1024,2048]{1,0:T(8,128)(2,1)}) custom-call(bf16[1024,2048]{1,0:T(8,128)(2,1)} %after.55.hidden.refs_0_, bf16[1024,2048]{1,0:T(8,128)(2,1)} %assemble.10.cot.refs_1_, bf16[2048,2048]{1,0:T(8,128)(2,1)} %all-gather.15.cloned.1.call-done.gate_w.up_w.refs_1_, ...), custom_call_target="tpu_custom_call" | custom-call | flops 24696061952 | tf_op jit(solution)/shard_map/feed_products/pallas_call | solution.py:848
  606.2 13.5 %product_rows.12 = (f32[256,2048]{1,0:T(8,128)S(1)}, bf16[256,2048]{1,0:T(8,128)(2,1)}, bf16[256,2048]{1,0:T(8,128)(2,1)}, bf16[256,2048]{1,0:T(8,128)(2,1)}) custom-call(bf16[1024,2048]{1,0:T(8,128)(2,1)} %get-tuple-element.103.refs_0_.refs_1_, bf16[2048,2048]{1,0:T(8,128)(2,1)} %all-gather.15.cloned.1.call-done.gate_w.up_w.refs_1_), custom_call_target="tpu_custom_call" | custom-call | flops 14967310336 | tf_op jit(solution)/shard_map/product_rows/pallas_call | solution.py:811
  621.0 7.2 collective-permute-done.25.refs_1_
  633.0 15.5 %weight_sums.14.refs_1_ = bf16[2048,2048]{1,0:T(8,128)(2,1)} custom-call(bf16[1024,2048]{1,0:T(8,128)(2,1)S(1)} %copy-done.2, bf16[1024,2048]{1,0:T(8,128)(2,1)} %get-tuple-element.103.refs_0_.refs_1_, f32[2048,2048]{1,0:T(8,128)} %weight_sums.12.refs_2_, bf16[256,2048]{1,0:T(8,128)(2,1)S(1)} %output_rows.2.refs_3_), custom_call_target="tpu_custom_call" | custom-call | flops 14967310336 | tf_op jit(solution)/shard_map/weight_sums/pallas_call | solution.py:890
  655.5 28.6 %ssd_backward.2 = (bf16[1024,1408]{1,0:T(8,128)(2,1)S(1)}, f32[8,1280]{1,0:T(8,128)S(1)}, f32[8,128]{1,0:T(8,128)S(1)}, f32[8,768]{1,0:T(8,128)S(1)}) custom-call(s32[8]{0:T(128)S(1)} %copy-done.87, bf16[1024,1408]{1,0:T(8,128)(2,1)} %convolution_convert_fusion.1.first_ref.refs_1_.before_ref, ...), custom_call_target="tpu_custom_call" | custom-call | flops 60949999616 | tf_op jit(solution)/shard_map/ssd_backward/pallas_call | solution.py:388
  684.2 10.7 %weight_sums.15.refs_2_ = f32[2048,1280]{1,0:T(8,128)} custom-call(bf16[1024,2048]{1,0:T(8,128)(2,1)} %after.38.refs_0_, bf16[1024,1280]{1,0:T(8,128)(2,1)S(1)} %copy-done.20, bf16[1024,1408]{1,0:T(8,128)(2,1)S(1)} %get-tuple-element.107.refs_2_.refs_0_.refs_1_), custom_call_target="tpu_custom_call" | custom-call | flops 9354568704 | tf_op jit(solution)/shard_map/weight_sums/pallas_call | solution.py:890
  710.4 9.1 weight_sums.18.refs_4_
  729.1 17.4 %product_rows.13 = (f32[256,2048]{1,0:T(8,128)S(1)}, bf16[256,2048]{1,0:T(8,128)(2,1)}, bf16[256,2048]{1,0:T(8,128)(2,1)}, bf16[256,2048]{1,0:T(8,128)(2,1)S(1)}) custom-call(bf16[1024,1408]{1,0:T(8,128)(2,1)} %copy-done.95, bf16[1024,1280]{1,0:T(8,128)(2,1)} %pad_maximum_fusion.2.refs_2_.refs_1_, bf16[2048,1408]{1,0:T(8,128)(2,1)} %all-gather.9.cloned.1.call-done.refs_2_, ...), custom_call_target="tpu_custom_call" | custom-call | flops 19644594176 | tf_op jit(solution)/shard_map/product_rows/pallas_call | solution.py:811
  748.9 8.3 product_rows.14
  758.1 11.1 %weight_sums.19.refs_3_.refs_2_ = f32[2048,1408]{1,0:T(8,128)} custom-call(bf16[1024,2048]{1,0:T(8,128)(2,1)} %after.38.refs_0_, bf16[1024,1408]{1,0:T(8,128)(2,1)S(1)} %copy-done.96, f32[256,2048]{1,0:T(8,128)S(1)} %get-tuple-element.114.refs_2_.own), custom_call_target="tpu_custom_call" | custom-call | flops 10290025472 | tf_op jit(solution)/shard_map/weight_sums/pallas_call | solution.py:890
  775.4 6.6 weight_sums.20.refs_3_
  800.3 7.5 multiply_convert_fusion
  807.8 6.8 attend_backward.3
  818.9 21.2 %collective-permute-done.34.refs_1_ = bf16[256,2048]{1,0:T(8,128)(2,1)} collective-permute-done((bf16[256,2048]{1,0:T(8,128)(2,1)}, bf16[256,2048]{1,0:T(8,128)(2,1)}, u32[]{:S(2)}, u32[]{:S(2)}) %collective-permute-start.34) | collective-permute-done | bytes 1048608 | tf_op jit(solution)/shard_map/ppermute | solution.py:946
  846.1 10.7 %weight_sums.22.refs_1_ = bf16[2048,1280]{1,0:T(8,128)(2,1)} custom-call(bf16[1024,2048]{1,0:T(8,128)(2,1)} %after.46.refs_0_, bf16[1024,1280]{1,0:T(8,128)(2,1)S(1)} %copy-done.19, f32[2048,1280]{1,0:T(8,128)} %weight_sums.15.refs_2_, bf16[256,2048]{1,0:T(8,128)(2,1)S(1)} %copy-done.52, bf16[256,2048]{1,0:T(8,128)(2,1)} %reduce-scatter.6.cloned.1.call-done.refs_4_), custom_call_target="tpu_custom_call" | custom-call | flops 9354568704 | tf_op jit(solution)/shard_map/weight_sums/pallas_call | solution.py:890
  867.3 28.2 %ssd_backward.3 = (bf16[1024,1408]{1,0:T(8,128)(2,1)S(1)}, f32[8,1280]{1,0:T(8,128)S(1)}, f32[8,128]{1,0:T(8,128)S(1)}, f32[8,768]{1,0:T(8,128)S(1)}) custom-call(s32[8]{0:T(128)S(1)} %copy-done.87, bf16[1024,1408]{1,0:T(8,128)(2,1)} %copy-done.18, bf16[1024,1408]{1,0:T(8,128)(2,1)} %copy-done.18, f32[1024,16]{1,0:T(8,128)S(1)} %copy-done.23, ...), custom_call_target="tpu_custom_call" | custom-call | flops 60949999616 | tf_op jit(solution)/shard_map/ssd_backward/pallas_call | solution.py:388
  899.8 19.5 %collective-permute-done.39 = f32[18064]{0:T(1024)S(1)} collective-permute-done((f32[18064]{0:T(1024)S(1)}, f32[18064]{0:T(1024)S(1)}, u32[]{:S(2)}, u32[]{:S(2)}) %collective-permute-start.39) | collective-permute-done | bytes 72288 | tf_op jit(solution)/shard_map/ppermute | solution.py:977
  926.6 12.5 %weight_sums.23.refs_4_ = bf16[2048,1408]{1,0:T(8,128)(2,1)} custom-call(bf16[1024,2048]{1,0:T(8,128)(2,1)} %after.46.refs_0_, bf16[1024,1408]{1,0:T(8,128)(2,1)} %copy-done.89, f32[2048,1408]{1,0:T(8,128)} %weight_sums.19.refs_3_.refs_2_, bf16[256,2048]{1,0:T(8,128)(2,1)S(1)} %input_back.2.refs_3_, f32[4,64,2048]{2,1,0:T(8,128)S(1)} %convert_element_type.341.refs_4_, ...), custom_call_target="tpu_custom_call" | custom-call | flops 10290025472 | tf_op jit(solution)/shard_map/weight_sums/pallas_call | solution.py:890
  944.4 18.0 %product_rows.15 = (f32[256,2048]{1,0:T(8,128)S(1)}, bf16[256,2048]{1,0:T(8,128)(2,1)}, bf16[256,2048]{1,0:T(8,128)(2,1)S(1)}, bf16[256,2048]{1,0:T(8,128)(2,1)S(1)}) custom-call(bf16[1024,1408]{1,0:T(8,128)(2,1)} %copy-done.89, bf16[1024,1280]{1,0:T(8,128)(2,1)} %pad_maximum_fusion.3.refs_3_.refs_1_, ...), custom_call_target="tpu_custom_call" | custom-call | flops 19644594176 | tf_op jit(solution)/shard_map/product_rows/pallas_call | solution.py:811
  992.9 20.9 %collective-permute-done.43.refs_2_ = bf16[256,2048]{1,0:T(8,128)(2,1)} collective-permute-done((bf16[256,2048]{1,0:T(8,128)(2,1)S(1)}, bf16[256,2048]{1,0:T(8,128)(2,1)}, u32[]{:S(2)}, u32[]{:S(2)}) %collective-permute-start.43) | collective-permute-done | bytes 1048608 | tf_op jit(solution)/shard_map/ppermute | solution.py:946
  1025.5 10.3 all-to-all-done.4
  (617 shorter events, 325.5 us)
Async XLA Ops:
  7.3 113.4 %all-gather.7.cloned.1.call-start = ((), (), s32[]{:S(2)}) async-start(), calls=%async_computation.10 | async-start | bytes 2949120 | tf_op jit(solution)/shard_map/all_gather | solution.py:987
  37.3 46.1 %collective-permute-start.1 = (bf16[256,2048]{1,0:T(8,128)(2,1)}, bf16[256,2048]{1,0:T(8,128)(2,1)}, u32[]{:S(2)}, u32[]{:S(2)}) collective-permute-start(bf16[256,2048]{1,0:T(8,128)(2,1)} %after.34.refs_0_), channel_id=1, source_target_pairs={{0,16},{8,24},{16,0},{24,8},{1,17},{9,25},{17,1},{25,9},{2,18},{10... | collective-permute-start | bytes 3145736 | tf_op jit(solution)/shard_map/ppermute | solution.py:946
  38.8 44.7 %collective-permute-start = (bf16[256,2048]{1,0:T(8,128)(2,1)}, bf16[256,2048]{1,0:T(8,128)(2,1)}, u32[]{:S(2)}, u32[]{:S(2)}) collective-permute-start(bf16[256,2048]{1,0:T(8,128)(2,1)} %after.34.refs_0_), channel_id=1, source_target_pairs={{0,8},{8,0},{16,24},{24,16},{1,9},{9,1},{17,25},{25,17},{2,10},{10... | collective-permute-start | bytes 3145736 | tf_op jit(solution)/shard_map/ppermute | solution.py:946
  87.0 67.0 %all-gather.13.cloned.1.call-start = ((), (), s32[]{:S(2)}) async-start(), calls=%async_computation.13 | async-start | bytes 4718592 | tf_op jit(solution)/shard_map/all_gather | solution.py:987
  106.1 109.0 %all-gather.9.cloned.1.call-start = ((), (), s32[]{:S(2)}) async-start(), calls=%async_computation.11 | async-start | bytes 6488064 | tf_op jit(solution)/shard_map/all_gather | solution.py:987
  108.3 146.0 %all-gather.11.cloned.1.call-start = ((), (), s32[]{:S(2)}) async-start(), calls=%async_computation.12 | async-start | bytes 3538944 | tf_op jit(solution)/shard_map/all_gather | solution.py:987
  108.8 278.8 %all-gather.15.cloned.1.call-start = ((), (), s32[]{:S(2)}) async-start(), calls=%async_computation.14 | async-start | bytes 9437184 | tf_op jit(solution)/shard_map/all_gather | solution.py:987
  110.0 277.6 %all-gather.17.cloned.1.call-start = ((), (), s32[]{:S(2)}) async-start(), calls=%async_computation.15 | async-start | bytes 4718592 | tf_op jit(solution)/shard_map/all_gather | solution.py:987
  142.5 132.4 %collective-permute-start.8 = (bf16[768,2048]{1,0:T(8,128)(2,1)}, bf16[768,2048]{1,0:T(8,128)(2,1)}, u32[]{:S(2)}, u32[]{:S(2)}) collective-permute-start(bf16[768,2048]{1,0:T(8,128)(2,1)} %after.40.refs_0_), channel_id=1, source_target_pairs={{0,24},{8,16},{16,8},{24,0},{1,25},{9,17},{17,9},{25,1},{2,26},{10... | collective-permute-start | bytes 9437192 | tf_op jit(solution)/shard_map/ppermute | solution.py:946
  143.9 136.5 %collective-permute-start.7 = (bf16[768,2048]{1,0:T(8,128)(2,1)}, bf16[768,2048]{1,0:T(8,128)(2,1)}, u32[]{:S(2)}, u32[]{:S(2)}) collective-permute-start(bf16[768,2048]{1,0:T(8,128)(2,1)} %after.40.refs_0_), channel_id=1, source_target_pairs={{0,16},{8,24},{16,0},{24,8},{1,17},{9,25},{17,1},{25,9},{2,18},{10... | collective-permute-start | bytes 9437192 | tf_op jit(solution)/shard_map/ppermute | solution.py:946
  145.4 136.8 %collective-permute-start.6 = (bf16[768,2048]{1,0:T(8,128)(2,1)}, bf16[768,2048]{1,0:T(8,128)(2,1)}, u32[]{:S(2)}, u32[]{:S(2)}) collective-permute-start(bf16[768,2048]{1,0:T(8,128)(2,1)} %after.40.refs_0_), channel_id=1, source_target_pairs={{0,8},{8,0},{16,24},{24,16},{1,9},{9,1},{17,25},{25,17},{2,10},{10... | collective-permute-start | bytes 9437192 | tf_op jit(solution)/shard_map/ppermute | solution.py:946
  244.9 600.0 %reduce-scatter.6.cloned.1.call-start = ((), (), s32[]{:S(2)}) async-start(), calls=%async_computation.16 | async-start | bytes 9437184 | tf_op jit(solution)/shard_map/reduce_scatter | solution.py:991
  271.9 33.6 %collective-permute-start.3 = (bf16[256,2048]{1,0:T(8,128)(2,1)}, bf16[256,2048]{1,0:T(8,128)(2,1)}, u32[]{:S(2)}, u32[]{:S(2)}) collective-permute-start(bf16[256,2048]{1,0:T(8,128)(2,1)} %get-tuple-element.79), channel_id=1, source_target_pairs={{0,8},{8,0},{16,24},{24,16},{1,9},{9,1},{17,25},{25,17},{2,10},{10... | collective-permute-start | bytes 3145736 | tf_op jit(solution)/shard_map/ppermute | solution.py:946
  274.9 50.3 %collective-permute-start.5 = (bf16[256,2048]{1,0:T(8,128)(2,1)}, bf16[256,2048]{1,0:T(8,128)(2,1)}, u32[]{:S(2)}, u32[]{:S(2)}) collective-permute-start(bf16[256,2048]{1,0:T(8,128)(2,1)} %get-tuple-element.81), channel_id=1, source_target_pairs={{0,24},{8,16},{16,8},{24,0},{1,25},{9,17},{17,9},{25,1},{2,26},{10... | collective-permute-start | bytes 3145736 | tf_op jit(solution)/shard_map/ppermute | solution.py:946
  329.3 51.1 %collective-permute-start.11 = (bf16[256,2048]{1,0:T(8,128)(2,1)}, bf16[256,2048]{1,0:T(8,128)(2,1)}, u32[]{:S(2)}, u32[]{:S(2)}) collective-permute-start(bf16[256,2048]{1,0:T(8,128)(2,1)} %get-tuple-element.83.refs_0_), channel_id=1, source_target_pairs={{0,24},{8,16},{16,8},{24,0},{1,25},{9,17},{17,9},{25,1},{2,26},{10... | collective-permute-start | bytes 3145736 | tf_op jit(solution)/shard_map/ppermute | solution.py:946
  330.8 49.6 %collective-permute-start.10 = (bf16[256,2048]{1,0:T(8,128)(2,1)}, bf16[256,2048]{1,0:T(8,128)(2,1)}, u32[]{:S(2)}, u32[]{:S(2)}) collective-permute-start(bf16[256,2048]{1,0:T(8,128)(2,1)} %get-tuple-element.83.refs_0_), channel_id=1, source_target_pairs={{0,16},{8,24},{16,0},{24,8},{1,17},{9,25},{17,1},{25,9},{2,18},{10... | collective-permute-start | bytes 3145736 | tf_op jit(solution)/shard_map/ppermute | solution.py:946
  332.3 48.2 %collective-permute-start.9 = (bf16[256,2048]{1,0:T(8,128)(2,1)}, bf16[256,2048]{1,0:T(8,128)(2,1)}, u32[]{:S(2)}, u32[]{:S(2)}) collective-permute-start(bf16[256,2048]{1,0:T(8,128)(2,1)} %get-tuple-element.83.refs_0_), channel_id=1, source_target_pairs={{0,8},{8,0},{16,24},{24,16},{1,9},{9,1},{17,25},{25,17},{2,10},{10... | collective-permute-start | bytes 3145736 | tf_op jit(solution)/shard_map/ppermute | solution.py:946
  384.1 40.9 %collective-permute-start.17 = (bf16[256,2048]{1,0:T(8,128)(2,1)}, bf16[256,2048]{1,0:T(8,128)(2,1)}, u32[]{:S(2)}, u32[]{:S(2)}) collective-permute-start(bf16[256,2048]{1,0:T(8,128)(2,1)} %after.49), channel_id=1, source_target_pairs={{0,24},{8,16},{16,8},{24,0},{1,25},{9,17},{17,9},{25,1},{2,26},{10... | collective-permute-start | bytes 3145736 | tf_op jit(solution)/shard_map/ppermute | solution.py:946
  385.9 44.7 %collective-permute-start.16 = (bf16[256,2048]{1,0:T(8,128)(2,1)S(1)}, bf16[256,2048]{1,0:T(8,128)(2,1)}, u32[]{:S(2)}, u32[]{:S(2)}) collective-permute-start(bf16[256,2048]{1,0:T(8,128)(2,1)S(1)} %copy-done.65), channel_id=1, source_target_pairs={{0,16},{8,24},{16,0},{24,8},{1,17},{9,25},{17,1},{25,9},{2,18},{10... | collective-permute-start | bytes 3145736 | tf_op jit(solution)/shard_map/ppermute | solution.py:946
  387.1 46.9 %collective-permute-start.15 = (bf16[256,2048]{1,0:T(8,128)(2,1)}, bf16[256,2048]{1,0:T(8,128)(2,1)}, u32[]{:S(2)}, u32[]{:S(2)}) collective-permute-start(bf16[256,2048]{1,0:T(8,128)(2,1)} %after.47), channel_id=1, source_target_pairs={{0,8},{8,0},{16,24},{24,16},{1,9},{9,1},{17,25},{25,17},{2,10},{10... | collective-permute-start | bytes 3145736 | tf_op jit(solution)/shard_map/ppermute | solution.py:946
  422.7 35.9 %collective-permute-start.12 = (bf16[256,2048]{1,0:T(8,128)(2,1)S(1)}, bf16[256,2048]{1,0:T(8,128)(2,1)S(1)}, u32[]{:S(2)}, u32[]{:S(2)}) collective-permute-start(bf16[256,2048]{1,0:T(8,128)(2,1)S(1)} %get-tuple-element.89), channel_id=1, source_target_pairs={{0,8},{8,0},{16,24},{24,16},{1,9},{9,1},{17,25},{25,17},{2,10},{10... | collective-permute-start | bytes 3145736 | tf_op jit(solution)/shard_map/ppermute | solution.py:946
  424.2 34.5 %collective-permute-start.13 = (bf16[256,2048]{1,0:T(8,128)(2,1)S(1)}, bf16[256,2048]{1,0:T(8,128)(2,1)S(1)}, u32[]{:S(2)}, u32[]{:S(2)}) collective-permute-start(bf16[256,2048]{1,0:T(8,128)(2,1)S(1)} %get-tuple-element.90), channel_id=1, source_target_pairs={{0,16},{8,24},{16,0},{24,8},{1,17},{9,25},{17,1},{25,9},{2,18},{10... | collective-permute-start | bytes 3145736 | tf_op jit(solution)/shard_map/ppermute | solution.py:946
  425.0 50.4 %collective-permute-start.14 = (bf16[256,2048]{1,0:T(8,128)(2,1)S(1)}, bf16[256,2048]{1,0:T(8,128)(2,1)}, u32[]{:S(2)}, u32[]{:S(2)}) collective-permute-start(bf16[256,2048]{1,0:T(8,128)(2,1)S(1)} %get-tuple-element.91), channel_id=1, source_target_pairs={{0,24},{8,16},{16,8},{24,0},{1,25},{9,17},{17,9},{25,1},{2,26},{10... | collective-permute-start | bytes 3145736 | tf_op jit(solution)/shard_map/ppermute | solution.py:946
  481.2 43.7 %collective-permute-start.19 = (bf16[256,2048]{1,0:T(8,128)(2,1)S(1)}, bf16[256,2048]{1,0:T(8,128)(2,1)S(1)}, u32[]{:S(2)}, u32[]{:S(2)}) collective-permute-start(bf16[256,2048]{1,0:T(8,128)(2,1)S(1)} %get-tuple-element.96.refs_0_), channel_id=1, source_target_pairs={{0,16},{8,24},{16,0},{24,8},{1,17},{9,25},{17,1},{25,9},{2,18},{10... | collective-permute-start | bytes 3145736 | tf_op jit(solution)/shard_map/ppermute | solution.py:946
  482.8 42.4 %collective-permute-start.18 = (bf16[256,2048]{1,0:T(8,128)(2,1)S(1)}, bf16[256,2048]{1,0:T(8,128)(2,1)S(1)}, u32[]{:S(2)}, u32[]{:S(2)}) collective-permute-start(bf16[256,2048]{1,0:T(8,128)(2,1)S(1)} %get-tuple-element.96.refs_0_), channel_id=1, source_target_pairs={{0,8},{8,0},{16,24},{24,16},{1,9},{9,1},{17,25},{25,17},{2,10},{10... | collective-permute-start | bytes 3145736 | tf_op jit(solution)/shard_map/ppermute | solution.py:946
  528.9 34.0 %collective-permute-start.23 = (bf16[256,2048]{1,0:T(8,128)(2,1)S(1)}, bf16[256,2048]{1,0:T(8,128)(2,1)S(1)}, u32[]{:S(2)}, u32[]{:S(2)}) collective-permute-start(bf16[256,2048]{1,0:T(8,128)(2,1)S(1)} %copy-done.61), channel_id=1, source_target_pairs={{0,24},{8,16},{16,8},{24,0},{1,25},{9,17},{17,9},{25,1},{2,26},{10... | collective-permute-start | bytes 3145736 | tf_op jit(solution)/shard_map/ppermute | solution.py:946
  530.1 46.8 %collective-permute-start.22 = (bf16[256,2048]{1,0:T(8,128)(2,1)S(1)}, bf16[256,2048]{1,0:T(8,128)(2,1)S(1)}, u32[]{:S(2)}, u32[]{:S(2)}) collective-permute-start(bf16[256,2048]{1,0:T(8,128)(2,1)S(1)} %copy-done.61), channel_id=1, source_target_pairs={{0,16},{8,24},{16,0},{24,8},{1,17},{9,25},{17,1},{25,9},{2,18},{10... | collective-permute-start | bytes 3145736 | tf_op jit(solution)/shard_map/ppermute | solution.py:946
  531.5 45.8 %collective-permute-start.21 = (bf16[256,2048]{1,0:T(8,128)(2,1)S(1)}, bf16[256,2048]{1,0:T(8,128)(2,1)S(1)}, u32[]{:S(2)}, u32[]{:S(2)}) collective-permute-start(bf16[256,2048]{1,0:T(8,128)(2,1)S(1)} %copy-done.61), channel_id=1, source_target_pairs={{0,8},{8,0},{16,24},{24,16},{1,9},{9,1},{17,25},{25,17},{2,10},{10... | collective-permute-start | bytes 3145736 | tf_op jit(solution)/shard_map/ppermute | solution.py:946
  579.8 41.2 %collective-permute-start.26 = (bf16[256,2048]{1,0:T(8,128)(2,1)}, bf16[256,2048]{1,0:T(8,128)(2,1)}, u32[]{:S(2)}, u32[]{:S(2)}) collective-permute-start(bf16[256,2048]{1,0:T(8,128)(2,1)} %after.54), channel_id=1, source_target_pairs={{0,24},{8,16},{16,8},{24,0},{1,25},{9,17},{17,9},{25,1},{2,26},{10... | collective-permute-start | bytes 3145736 | tf_op jit(solution)/shard_map/ppermute | solution.py:946
  581.1 47.1 %collective-permute-start.25 = (bf16[256,2048]{1,0:T(8,128)(2,1)S(1)}, bf16[256,2048]{1,0:T(8,128)(2,1)}, u32[]{:S(2)}, u32[]{:S(2)}) collective-permute-start(bf16[256,2048]{1,0:T(8,128)(2,1)S(1)} %copy-done.63), channel_id=1, source_target_pairs={{0,16},{8,24},{16,0},{24,8},{1,17},{9,25},{17,1},{25,9},{2,18},{10... | collective-permute-start | bytes 3145736 | tf_op jit(solution)/shard_map/ppermute | solution.py:946
  582.5 46.1 %collective-permute-start.24 = (bf16[256,2048]{1,0:T(8,128)(2,1)S(1)}, bf16[256,2048]{1,0:T(8,128)(2,1)}, u32[]{:S(2)}, u32[]{:S(2)}) collective-permute-start(bf16[256,2048]{1,0:T(8,128)(2,1)S(1)} %copy-done.67), channel_id=1, source_target_pairs={{0,8},{8,0},{16,24},{24,16},{1,9},{9,1},{17,25},{25,17},{2,10},{10... | collective-permute-start | bytes 3145736 | tf_op jit(solution)/shard_map/ppermute | solution.py:946
  649.5 216.4 %reduce-scatter.8.cloned.1.call-start = ((), (), s32[]{:S(2)}) async-start(), calls=%async_computation.17 | async-start | bytes 4718592 | tf_op jit(solution)/shard_map/reduce_scatter | solution.py:991
  649.5 55.7 %collective-permute-start.27 = (bf16[256,2048]{1,0:T(8,128)(2,1)}, bf16[256,2048]{1,0:T(8,128)(2,1)}, u32[]{:S(2)}, u32[]{:S(2)}) collective-permute-start(bf16[256,2048]{1,0:T(8,128)(2,1)} %get-tuple-element.109), channel_id=1, source_target_pairs={{0,8},{8,0},{16,24},{24,16},{1,9},{9,1},{17,25},{25,17},{2,10},{10... | collective-permute-start | bytes 3145736 | tf_op jit(solution)/shard_map/ppermute | solution.py:946
  650.8 54.4 %collective-permute-start.28 = (bf16[256,2048]{1,0:T(8,128)(2,1)}, bf16[256,2048]{1,0:T(8,128)(2,1)}, u32[]{:S(2)}, u32[]{:S(2)}) collective-permute-start(bf16[256,2048]{1,0:T(8,128)(2,1)} %get-tuple-element.110), channel_id=1, source_target_pairs={{0,16},{8,24},{16,0},{24,8},{1,17},{9,25},{17,1},{25,9},{2,18},{10... | collective-permute-start | bytes 3145736 | tf_op jit(solution)/shard_map/ppermute | solution.py:946
  651.4 53.8 %collective-permute-start.29 = (bf16[256,2048]{1,0:T(8,128)(2,1)}, bf16[256,2048]{1,0:T(8,128)(2,1)}, u32[]{:S(2)}, u32[]{:S(2)}) collective-permute-start(bf16[256,2048]{1,0:T(8,128)(2,1)} %get-tuple-element.111), channel_id=1, source_target_pairs={{0,24},{8,16},{16,8},{24,0},{1,25},{9,17},{17,9},{25,1},{2,26},{10... | collective-permute-start | bytes 3145736 | tf_op jit(solution)/shard_map/ppermute | solution.py:946
  719.5 206.1 %reduce-scatter.10.cloned.1.call-start = ((), (), s32[]{:S(2)}) async-start(), calls=%async_computation.18 | async-start | bytes 4718592 | tf_op jit(solution)/shard_map/reduce_scatter | solution.py:991
  725.6 43.5 %collective-permute-start.32 = (bf16[256,2048]{1,0:T(8,128)(2,1)S(1)}, bf16[256,2048]{1,0:T(8,128)(2,1)S(1)}, u32[]{:S(2)}, u32[]{:S(2)}) collective-permute-start(bf16[256,2048]{1,0:T(8,128)(2,1)S(1)} %get-tuple-element.112.refs_3_.refs_0_), channel_id=1, source_target_pairs={{0,24},{8,16},{16,8},{24,0},{1,25},{9,17},{17,9},{25,1},{2,26},{10... | collective-permute-start | bytes 3145736 | tf_op jit(solution)/shard_map/ppermute | solution.py:946
  726.5 46.1 %collective-permute-start.31 = (bf16[256,2048]{1,0:T(8,128)(2,1)S(1)}, bf16[256,2048]{1,0:T(8,128)(2,1)S(1)}, u32[]{:S(2)}, u32[]{:S(2)}) collective-permute-start(bf16[256,2048]{1,0:T(8,128)(2,1)S(1)} %get-tuple-element.112.refs_3_.refs_0_), channel_id=1, source_target_pairs={{0,16},{8,24},{16,0},{24,8},{1,17},{9,25},{17,1},{25,9},{2,18},{10... | collective-permute-start | bytes 3145736 | tf_op jit(solution)/shard_map/ppermute | solution.py:946
  728.7 44.2 %collective-permute-start.30 = (bf16[256,2048]{1,0:T(8,128)(2,1)S(1)}, bf16[256,2048]{1,0:T(8,128)(2,1)S(1)}, u32[]{:S(2)}, u32[]{:S(2)}) collective-permute-start(bf16[256,2048]{1,0:T(8,128)(2,1)S(1)} %get-tuple-element.112.refs_3_.refs_0_), channel_id=1, source_target_pairs={{0,8},{8,0},{16,24},{24,16},{1,9},{9,1},{17,25},{25,17},{2,10},{10... | collective-permute-start | bytes 3145736 | tf_op jit(solution)/shard_map/ppermute | solution.py:946
  791.4 197.4 %reduce-scatter.12.cloned.1.call-start = ((), (), s32[]{:S(2)}) async-start(), calls=%async_computation.19 | async-start | bytes 5898240 | tf_op jit(solution)/shard_map/reduce_scatter | solution.py:991
  792.8 47.3 %collective-permute-start.34 = (bf16[256,2048]{1,0:T(8,128)(2,1)}, bf16[256,2048]{1,0:T(8,128)(2,1)}, u32[]{:S(2)}, u32[]{:S(2)}) collective-permute-start(bf16[256,2048]{1,0:T(8,128)(2,1)} %after.58), channel_id=1, source_target_pairs={{0,16},{8,24},{16,0},{24,8},{1,17},{9,25},{17,1},{25,9},{2,18},{10... | collective-permute-start | bytes 3145736 | tf_op jit(solution)/shard_map/ppermute | solution.py:946
  794.2 46.2 %collective-permute-start.33 = (bf16[256,2048]{1,0:T(8,128)(2,1)}, bf16[256,2048]{1,0:T(8,128)(2,1)}, u32[]{:S(2)}, u32[]{:S(2)}) collective-permute-start(bf16[256,2048]{1,0:T(8,128)(2,1)} %after.57), channel_id=1, source_target_pairs={{0,8},{8,0},{16,24},{24,16},{1,9},{9,1},{17,25},{25,17},{2,10},{10... | collective-permute-start | bytes 3145736 | tf_op jit(solution)/shard_map/ppermute | solution.py:946
  858.0 61.7 %collective-permute-start.38 = (bf16[256,2048]{1,0:T(8,128)(2,1)S(1)}, bf16[256,2048]{1,0:T(8,128)(2,1)}, u32[]{:S(2)}, u32[]{:S(2)}) collective-permute-start(bf16[256,2048]{1,0:T(8,128)(2,1)S(1)} %copy-done.56), channel_id=1, source_target_pairs={{0,24},{8,16},{16,8},{24,0},{1,25},{9,17},{17,9},{25,1},{2,26},{10... | collective-permute-start | bytes 3145736 | tf_op jit(solution)/shard_map/ppermute | solution.py:946
  859.2 60.5 %collective-permute-start.37 = (bf16[256,2048]{1,0:T(8,128)(2,1)}, bf16[256,2048]{1,0:T(8,128)(2,1)}, u32[]{:S(2)}, u32[]{:S(2)}) collective-permute-start(bf16[256,2048]{1,0:T(8,128)(2,1)} %after.62), channel_id=1, source_target_pairs={{0,16},{8,24},{16,0},{24,8},{1,17},{9,25},{17,1},{25,9},{2,18},{10... | collective-permute-start | bytes 3145736 | tf_op jit(solution)/shard_map/ppermute | solution.py:946
  860.6 59.0 %collective-permute-start.36 = (bf16[256,2048]{1,0:T(8,128)(2,1)}, bf16[256,2048]{1,0:T(8,128)(2,1)}, u32[]{:S(2)}, u32[]{:S(2)}) collective-permute-start(bf16[256,2048]{1,0:T(8,128)(2,1)} %after.61), channel_id=1, source_target_pairs={{0,8},{8,0},{16,24},{24,16},{1,9},{9,1},{17,25},{25,17},{2,10},{10... | collective-permute-start | bytes 3145736 | tf_op jit(solution)/shard_map/ppermute | solution.py:946
  861.5 62.3 %all-to-all-start.2 = ((bf16[4,64,2048]{2,1,0:T(8,128)(2,1)}), bf16[4,64,2048]{2,1,0:T(8,128)(2,1)}, u32[]{:S(2)}, u32[]{:S(2)}) async-start(bf16[4,64,2048]{2,1,0:T(8,128)(2,1)} %bitcast.67), calls=%async_computation.4 | async-start | bytes 2097152 | tf_op jit(solution)/shard_map/all_to_all | solution.py:983
  865.8 156.0 %reduce-scatter.14.cloned.1.call-start = ((), (), s32[]{:S(2)}) async-start(), calls=%async_computation.20 | async-start | bytes 6488064 | tf_op jit(solution)/shard_map/reduce_scatter | solution.py:991
  965.7 48.2 %collective-permute-start.43 = (bf16[256,2048]{1,0:T(8,128)(2,1)S(1)}, bf16[256,2048]{1,0:T(8,128)(2,1)}, u32[]{:S(2)}, u32[]{:S(2)}) collective-permute-start(bf16[256,2048]{1,0:T(8,128)(2,1)S(1)} %get-tuple-element.135), channel_id=1, source_target_pairs={{0,24},{8,16},{16,8},{24,0},{1,25},{9,17},{17,9},{25,1},{2,26},{10... | collective-permute-start | bytes 3145736 | tf_op jit(solution)/shard_map/ppermute | solution.py:946
  (156 other events, 1745.1 us)
Sparse Core Ops, SparseCore 0:
  32.3 33.5 all-gather.6
  106.2 47.7 all-gather.12
  156.2 58.9 all-gather.8
  217.2 36.9 all-gather.10
  255.7 80.9 all-gather.14
  338.1 45.6 all-gather.16
  649.6 90.0 reduce-scatter.5
  742.0 48.3 reduce-scatter.7
  792.7 49.7 reduce-scatter.9
  856.9 60.8 reduce-scatter.11
  939.3 69.2 reduce-scatter.13

commit v6 on v5

--- a/solution.py
+++ b/solution.py
@@ -1311,11 +1311,11 @@
     out_part = spread_sums(out_sum)
     heads_back(1, [out_sum])
     outputs.append(finish_output(1, [grad_sides[1]]))
-    side_sum = weight_sums(hiddens[1:], grad_sides[1:], bf16, side_sum, [outputs[1], gate_up_part])
+    side_sum = weight_sums(hiddens[1:], grad_sides[1:], bf16, side_sum, [outputs[1]])
     side_part = spread_sums(side_sum)
     gate_up_back = back_to_rows(gate_up_part)
     side_back = back_to_rows(side_part)
-    scan_back(1, [side_sum, down_part])
+    scan_back(1, [side_sum, gate_up_part])
     low = finish_input(0, [back[1][0]])
     input_grads = [low]
     conv_grad = (back[0][1] + back[1][1])[: CONV + 1]
@@ -1332,7 +1332,7 @@
     for piece in small_sums:
         ends.append(ends[-1] + piece.shape[0])
     total = add_over(jnp.concatenate(small_sums), "seq")
-    first_sum = weight_sums(hiddens[1:], [back[1][0]], bf16, first_sum, [low, gate_up_back, out_part, total])
+    first_sum = weight_sums(hiddens[1:], [back[1][0]], bf16, first_sum, [low, gate_up_back, down_part, out_part, total])
     first_part = spread_sums(first_sum)
     first_back = back_to_rows(first_part)
     hidden_back(1, [first_sum])

time: 1050 us -> 1050 us (level)
    unnamed x292 -> x302, local copies, waits for them, and re-layouts: 52.8 us -> 54.2 us
  transfers between devices with their start and end apart: 62 -> 62, of which waited for: 30 -> 32; matrix products, arithmetic and copies ran while one was open for 13% -> 13% of each run, Pallas kernels for 38% -> 38%
where the time goes in v6:
time: 1050 us; the launch traced here: 1040 us
  Pallas kernels  422 us (40%)
  waiting for transfers between devices  318 us (30%)
  local copies, waits for them, and re-layouts  86.6 us (8%)
  matrix products  74.1 us (7%)
  starting transfers between devices  71.9 us (7%)
  other arithmetic  35.3 us (3%)
  blocking collectives  19.1 us (2%)
  between operations  16.3 us (2%)
    ppermute x42, waiting for transfers between devices, swap(): return lax.ppermute(value, 'seq', peers(lax.axis_size('seq'), flip))  190 us
    pallas_call x12, Pallas kernels, weight_sums(): pl.pallas_call(functools.partial(sums_kernel, len(lefts), len(extra), len...  113 us
    pallas_call x8, Pallas kernels, product_rows(): pl.pallas_call(functools.partial(product_kernel, back, len(lefts), len(de...  92.3 us
    all_gather x6, waiting for transfers between devices, gather_weights(): lax.all_gather(rows.reshape(-1, rows.shape[-1]), 'fsdp', axis=0, tiled=True)  68.2 us
    pallas_call x2, Pallas kernels, ssd_backward(): pl.pallas_call(functools.partial(ssd_backward_kernel, heads), grid_spec=p...  56.7 us
    unnamed x302, local copies, waits for them, and re-layouts  54.2 us
    dot_general x6, matrix products, matmul_rows(): jnp.einsum('tc,cd->td', left, right, preferred_element_type=jnp.float32)  51.7 us
    ppermute x42, starting transfers between devices, swap(): return lax.ppermute(value, 'seq', peers(lax.axis_size('seq'), flip))  49.3 us
  transfers between devices with their start and end apart: 62, of which 32 were waited for; matrix products, arithmetic and copies ran while one was open for 13% of the time, Pallas kernels for 38%

profile of v6, /device:TPU:0, one launch (start us, length us, event | category | flops | bytes accessed | tf_op | source)
XLA Modules:
  0.0 1043.3 jit_solution(3429559391368328004)
XLA Ops:
  12.2 19.1 %all_to_all.25.refs_1_ = bf16[4,64,2048]{2,1,0:T(8,128)(2,1)S(1)} all-to-all(bf16[4,64,2048]{2,1,0:T(8,128)(2,1)S(1)} %pad_dynamic-update-slice_fusion), channel_id=1, replica_groups=mesh['seq'=4,'fsdp'=8] {'seq'}, dimensions={0} | all-to-all | bytes 2097152 | tf_op jit(solution)/shard_map/all_to_all | solution.py:983
  41.2 22.4 %collective-permute-done.2.refs_3_.refs_6_.refs_7_ = bf16[256,2048]{1,0:T(8,128)(2,1)S(1)} collective-permute-done((bf16[256,2048]{1,0:T(8,128)(2,1)}, bf16[256,2048]{1,0:T(8,128)(2,1)S(1)}, u32[]{:S(2)}, u32[]{:S(2)}) %collective-permute-start.2) | collective-permute-done | bytes 1048608 | tf_op jit(solution)/shard_map/ppermute | solution.py:946
  63.6 19.8 %collective-permute-done.1.refs_2_.refs_4_.refs_5_ = bf16[256,2048]{1,0:T(8,128)(2,1)} collective-permute-done((bf16[256,2048]{1,0:T(8,128)(2,1)}, bf16[256,2048]{1,0:T(8,128)(2,1)}, u32[]{:S(2)}, u32[]{:S(2)}) %collective-permute-start.1) | collective-permute-done | bytes 1048608 | tf_op jit(solution)/shard_map/ppermute | solution.py:946
  87.9 17.4 %all-to-all-done.1.refs_1_.refs_2_ = bf16[4,64,2816]{2,1,0:T(8,128)(2,1)S(1)} async-done(((bf16[4,64,2816]{2,1,0:T(8,128)(2,1)}), bf16[4,64,2816]{2,1,0:T(8,128)(2,1)S(1)}, u32[]{:S(2)}, u32[]{:S(2)}) %all-to-all-start.1) | async-done | bytes 1441824 | tf_op jit(solution)/shard_map/all_to_all | solution.py:983
  160.3 54.7 %all-gather.9.cloned.1.call-done.refs_2_ = bf16[2048,1408]{1,0:T(8,128)(2,1)} async-done(((bf16[256,1408]{1,0:T(8,128)(2,1)}), bf16[2048,1408]{1,0:T(8,128)(2,1)}) %all-gather.9.cloned.1.call-update) | async-done | bytes 5767184 | tf_op jit(solution)/shard_map/all_gather | solution.py:987
  215.0 11.4 %convolution_convert_fusion.1.first_ref.refs_1_.before_ref = bf16[1024,1408]{1,0:T(8,128)(2,1)} fusion(bf16[1024,2048]{1,0:T(8,128)(2,1)} %after.37.refs_0_, bf16[2048,1408]{1,0:T(8,128)(2,1)} %all-gather.9.cloned.1.call-done.refs_2_), kind=kOutput, calls=%fused_computation.7 | convolution fusion | flops 5907021824 | bytes 12845056 | tf_op jit(solution)/shard_map/tc,cd->td/dot_general | solution.py:930
  230.0 13.5 %ssd_forward.2 = (bf16[1024,768]{1,0:T(8,128)(2,1)S(1)}, bf16[8,256,768]{2,1,0:T(8,128)(2,1)}) custom-call(s32[8]{0:T(128)S(1)} %copy-done.89, bf16[1024,1408]{1,0:T(8,128)(2,1)S(1)} %copy-done.8, f32[1024,16]{1,0:T(8,128)S(1)} %copy-done.26, f32[8,1,128]{2,1,0:T(1,128)S(1)} %get-tuple-element.226.seg_ref, f32[8,1280]{1,0:T(8,128)S(1)} %select_maximum_fusion.conv_ref, ...), custom_call_target="tpu_custom_call" | custom-call | tf_op jit(solution)/shard_map/ssd_forward/pallas_call | solution.py:339
  244.7 9.3 all-gather.11.cloned.1.call-done
  254.1 9.4 fusion
  263.5 8.2 product_rows.8
  284.2 6.5 norm_pieces.3.refs_0_
  305.5 19.8 %collective-permute-done.5.refs_2_ = bf16[256,2048]{1,0:T(8,128)(2,1)} collective-permute-done((bf16[256,2048]{1,0:T(8,128)(2,1)}, bf16[256,2048]{1,0:T(8,128)(2,1)}, u32[]{:S(2)}, u32[]{:S(2)}) %collective-permute-start.5) | collective-permute-done | bytes 1048608 | tf_op jit(solution)/shard_map/ppermute | solution.py:946
  332.9 10.3 convolution_convert_fusion.first_ref.before_ref
  343.3 13.5 %ssd_forward.3 = (bf16[1024,768]{1,0:T(8,128)(2,1)S(1)}, bf16[8,256,768]{2,1,0:T(8,128)(2,1)}) custom-call(s32[8]{0:T(128)S(1)} %copy-done.90, bf16[1024,1408]{1,0:T(8,128)(2,1)S(1)} %convolution_convert_fusion.first_ref.before_ref, f32[1024,16]{1,0:T(8,128)S(1)} %copy.218.aux_ref, f32[8,1,128]{2,1,0:T(1,128)S(1)} %get-tuple-element.223.seg_ref, ...), custom_call_target="tpu_custom_call" | custom-call | tf_op jit(solution)/shard_map/ssd_forward/pallas_call | solution.py:339
  360.9 9.1 fusion.4
  370.0 7.5 product_rows.10
  387.6 21.4 %feed_products.2 = (bf16[1024,1024]{1,0:T(8,128)(2,1)S(1)}, bf16[1024,2048]{1,0:T(8,128)(2,1)}) custom-call(bf16[1024,2048]{1,0:T(8,128)(2,1)} %after.42.hidden.refs_0_, bf16[1024,2048]{1,0:T(8,128)(2,1)} %assemble.7.cot.refs_1_, bf16[2048,2048]{1,0:T(8,128)(2,1)} %all-gather.15.cloned.1.call-done.gate_w.up_w.refs_1_, ...), custom_call_target="tpu_custom_call" | custom-call | flops 24696061952 | tf_op jit(solution)/shard_map/feed_products/pallas_call | solution.py:848
  409.0 13.4 %product_rows.9 = (f32[256,2048]{1,0:T(8,128)S(1)}, bf16[256,2048]{1,0:T(8,128)(2,1)S(1)}, bf16[256,2048]{1,0:T(8,128)(2,1)S(1)}, bf16[256,2048]{1,0:T(8,128)(2,1)S(1)}) custom-call(bf16[1024,2048]{1,0:T(8,128)(2,1)} %get-tuple-element.86.refs_0_.refs_1_, bf16[2048,2048]{1,0:T(8,128)(2,1)} %all-gather.15.cloned.1.call-done.gate_w.up_w.refs_1_), custom_call_target="tpu_custom_call" | custom-call | flops 14967310336 | tf_op jit(solution)/shard_map/product_rows/pallas_call | solution.py:811
  433.9 16.0 %weight_sums.12.refs_2_ = f32[2048,2048]{1,0:T(8,128)} custom-call(bf16[1024,2048]{1,0:T(8,128)(2,1)} %after.42.hidden.refs_0_, bf16[1024,2048]{1,0:T(8,128)(2,1)} %get-tuple-element.86.refs_0_.refs_1_, f32[256,2048]{1,0:T(8,128)S(1)} %get-tuple-element.87.refs_2_.own, bf16[256,2048]{1,0:T(8,128)(2,1)} %collective-permute-done.15.refs_3_.refs_0_, ...), custom_call_target="tpu_custom_call" | custom-call | flops 14967310336 | tf_op jit(solution)/shard_map/weight_sums/pallas_call | solution.py:890
  449.9 8.6 weight_sums.13.refs_3_.refs_2_
  458.5 16.9 %collective-permute-done.14.refs_2_ = bf16[256,2048]{1,0:T(8,128)(2,1)} collective-permute-done((bf16[256,2048]{1,0:T(8,128)(2,1)S(1)}, bf16[256,2048]{1,0:T(8,128)(2,1)}, u32[]{:S(2)}, u32[]{:S(2)}) %collective-permute-start.14) | collective-permute-done | bytes 1048608 | tf_op jit(solution)/shard_map/ppermute | solution.py:946
  491.5 15.4 %collective-permute-done.20.refs_3_ = bf16[256,2048]{1,0:T(8,128)(2,1)S(1)} collective-permute-done((bf16[256,2048]{1,0:T(8,128)(2,1)S(1)}, bf16[256,2048]{1,0:T(8,128)(2,1)S(1)}, u32[]{:S(2)}, u32[]{:S(2)}) %collective-permute-start.20) | collective-permute-done | bytes 1048608 | tf_op jit(solution)/shard_map/ppermute | solution.py:946
  506.9 18.2 %collective-permute-done.19.refs_2_ = bf16[256,2048]{1,0:T(8,128)(2,1)S(1)} collective-permute-done((bf16[256,2048]{1,0:T(8,128)(2,1)S(1)}, bf16[256,2048]{1,0:T(8,128)(2,1)S(1)}, u32[]{:S(2)}, u32[]{:S(2)}) %collective-permute-start.19) | collective-permute-done | bytes 1048608 | tf_op jit(solution)/shard_map/ppermute | solution.py:946
  535.9 7.8 multiply_convert_fusion.1
  543.8 6.9 attend_backward.2
  552.5 7.3 product_rows.11
  563.1 14.1 %collective-permute-done.22.refs_2_ = bf16[256,2048]{1,0:T(8,128)(2,1)S(1)} collective-permute-done((bf16[256,2048]{1,0:T(8,128)(2,1)S(1)}, bf16[256,2048]{1,0:T(8,128)(2,1)S(1)}, u32[]{:S(2)}, u32[]{:S(2)}) %collective-permute-start.22) | collective-permute-done | bytes 1048608 | tf_op jit(solution)/shard_map/ppermute | solution.py:946
  583.3 21.4 %feed_products.3 = (bf16[1024,1024]{1,0:T(8,128)(2,1)S(1)}, bf16[1024,2048]{1,0:T(8,128)(2,1)}) custom-call(bf16[1024,2048]{1,0:T(8,128)(2,1)} %after.55.hidden.refs_0_, bf16[1024,2048]{1,0:T(8,128)(2,1)} %assemble.10.cot.refs_1_, bf16[2048,2048]{1,0:T(8,128)(2,1)} %all-gather.15.cloned.1.call-done.gate_w.up_w.refs_1_, ...), custom_call_target="tpu_custom_call" | custom-call | flops 24696061952 | tf_op jit(solution)/shard_map/feed_products/pallas_call | solution.py:848
  606.0 13.5 %product_rows.12 = (f32[256,2048]{1,0:T(8,128)S(1)}, bf16[256,2048]{1,0:T(8,128)(2,1)}, bf16[256,2048]{1,0:T(8,128)(2,1)}, bf16[256,2048]{1,0:T(8,128)(2,1)}) custom-call(bf16[1024,2048]{1,0:T(8,128)(2,1)} %get-tuple-element.103.refs_0_.refs_1_, bf16[2048,2048]{1,0:T(8,128)(2,1)} %all-gather.15.cloned.1.call-done.gate_w.up_w.refs_1_), custom_call_target="tpu_custom_call" | custom-call | flops 14967310336 | tf_op jit(solution)/shard_map/product_rows/pallas_call | solution.py:811
  620.9 7.6 collective-permute-done.25.refs_1_
  632.9 15.5 %weight_sums.14.refs_1_ = bf16[2048,2048]{1,0:T(8,128)(2,1)} custom-call(bf16[1024,2048]{1,0:T(8,128)(2,1)S(1)} %copy-done.2, bf16[1024,2048]{1,0:T(8,128)(2,1)} %get-tuple-element.103.refs_0_.refs_1_, f32[2048,2048]{1,0:T(8,128)} %weight_sums.12.refs_2_, bf16[256,2048]{1,0:T(8,128)(2,1)S(1)} %output_rows.2.refs_3_), custom_call_target="tpu_custom_call" | custom-call | flops 14967310336 | tf_op jit(solution)/shard_map/weight_sums/pallas_call | solution.py:890
  655.5 28.5 %ssd_backward.2 = (bf16[1024,1408]{1,0:T(8,128)(2,1)S(1)}, f32[8,1280]{1,0:T(8,128)S(1)}, f32[8,128]{1,0:T(8,128)S(1)}, f32[8,768]{1,0:T(8,128)S(1)}) custom-call(s32[8]{0:T(128)S(1)} %copy-done.91, bf16[1024,1408]{1,0:T(8,128)(2,1)} %convolution_convert_fusion.1.first_ref.refs_1_.before_ref, ...), custom_call_target="tpu_custom_call" | custom-call | flops 60949999616 | tf_op jit(solution)/shard_map/ssd_backward/pallas_call | solution.py:388
  684.1 10.6 %weight_sums.15.refs_2_ = f32[2048,1280]{1,0:T(8,128)} custom-call(bf16[1024,2048]{1,0:T(8,128)(2,1)} %after.38.refs_0_, bf16[1024,1280]{1,0:T(8,128)(2,1)S(1)} %copy-done.20, bf16[1024,1408]{1,0:T(8,128)(2,1)S(1)} %get-tuple-element.107.refs_2_.refs_0_.refs_1_), custom_call_target="tpu_custom_call" | custom-call | flops 9354568704 | tf_op jit(solution)/shard_map/weight_sums/pallas_call | solution.py:890
  710.2 9.0 weight_sums.18.refs_4_
  729.0 17.4 %product_rows.13 = (f32[256,2048]{1,0:T(8,128)S(1)}, bf16[256,2048]{1,0:T(8,128)(2,1)}, bf16[256,2048]{1,0:T(8,128)(2,1)}, bf16[256,2048]{1,0:T(8,128)(2,1)S(1)}) custom-call(bf16[1024,1408]{1,0:T(8,128)(2,1)} %copy-done.99, bf16[1024,1280]{1,0:T(8,128)(2,1)} %pad_maximum_fusion.2.refs_2_.refs_1_, bf16[2048,1408]{1,0:T(8,128)(2,1)} %all-gather.9.cloned.1.call-done.refs_2_, ...), custom_call_target="tpu_custom_call" | custom-call | flops 19644594176 | tf_op jit(solution)/shard_map/product_rows/pallas_call | solution.py:811
  748.7 7.4 product_rows.14
  759.1 11.1 %weight_sums.19.refs_3_.refs_2_ = f32[2048,1408]{1,0:T(8,128)} custom-call(bf16[1024,2048]{1,0:T(8,128)(2,1)} %after.38.refs_0_, bf16[1024,1408]{1,0:T(8,128)(2,1)S(1)} %copy-done.100, f32[256,2048]{1,0:T(8,128)S(1)} %get-tuple-element.114.refs_2_.own), custom_call_target="tpu_custom_call" | custom-call | flops 10290025472 | tf_op jit(solution)/shard_map/weight_sums/pallas_call | solution.py:890
  775.5 6.6 weight_sums.20.refs_3_
  800.5 7.5 multiply_convert_fusion
  808.1 6.8 attend_backward.3
  819.1 21.3 %collective-permute-done.34.refs_1_ = bf16[256,2048]{1,0:T(8,128)(2,1)} collective-permute-done((bf16[256,2048]{1,0:T(8,128)(2,1)S(1)}, bf16[256,2048]{1,0:T(8,128)(2,1)}, u32[]{:S(2)}, u32[]{:S(2)}) %collective-permute-start.34) | collective-permute-done | bytes 1048608 | tf_op jit(solution)/shard_map/ppermute | solution.py:946
  844.1 10.7 %weight_sums.22.refs_1_ = bf16[2048,1280]{1,0:T(8,128)(2,1)} custom-call(bf16[1024,2048]{1,0:T(8,128)(2,1)} %after.46.refs_0_, bf16[1024,1280]{1,0:T(8,128)(2,1)S(1)} %copy-done.19, f32[2048,1280]{1,0:T(8,128)} %weight_sums.15.refs_2_, bf16[256,2048]{1,0:T(8,128)(2,1)S(1)} %output_rows.3.refs_3_), custom_call_target="tpu_custom_call" | custom-call | flops 9354568704 | tf_op jit(solution)/shard_map/weight_sums/pallas_call | solution.py:890
  866.2 28.2 %ssd_backward.3 = (bf16[1024,1408]{1,0:T(8,128)(2,1)S(1)}, f32[8,1280]{1,0:T(8,128)S(1)}, f32[8,128]{1,0:T(8,128)S(1)}, f32[8,768]{1,0:T(8,128)S(1)}) custom-call(s32[8]{0:T(128)S(1)} %copy-done.91, bf16[1024,1408]{1,0:T(8,128)(2,1)} %copy-done.18, bf16[1024,1408]{1,0:T(8,128)(2,1)} %copy-done.18, f32[1024,16]{1,0:T(8,128)S(1)} %copy-done.24, ...), custom_call_target="tpu_custom_call" | custom-call | flops 60949999616 | tf_op jit(solution)/shard_map/ssd_backward/pallas_call | solution.py:388
  898.8 19.4 %collective-permute-done.39 = f32[18064]{0:T(1024)S(1)} collective-permute-done((f32[18064]{0:T(1024)S(1)}, f32[18064]{0:T(1024)S(1)}, u32[]{:S(2)}, u32[]{:S(2)}) %collective-permute-start.39) | collective-permute-done | bytes 72288 | tf_op jit(solution)/shard_map/ppermute | solution.py:977
  926.6 12.5 %weight_sums.23.refs_4_ = bf16[2048,1408]{1,0:T(8,128)(2,1)} custom-call(bf16[1024,2048]{1,0:T(8,128)(2,1)} %after.46.refs_0_, bf16[1024,1408]{1,0:T(8,128)(2,1)} %copy-done.93, f32[2048,1408]{1,0:T(8,128)} %weight_sums.19.refs_3_.refs_2_, bf16[256,2048]{1,0:T(8,128)(2,1)S(1)} %input_back.2.refs_3_, f32[4,64,2048]{2,1,0:T(8,128)S(1)} %convert_element_type.341.refs_4_, ...), custom_call_target="tpu_custom_call" | custom-call | flops 10290025472 | tf_op jit(solution)/shard_map/weight_sums/pallas_call | solution.py:890
  957.0 17.6 %product_rows.15 = (f32[256,2048]{1,0:T(8,128)S(1)}, bf16[256,2048]{1,0:T(8,128)(2,1)}, bf16[256,2048]{1,0:T(8,128)(2,1)S(1)}, bf16[256,2048]{1,0:T(8,128)(2,1)S(1)}) custom-call(bf16[1024,1408]{1,0:T(8,128)(2,1)} %copy-done.93, bf16[1024,1280]{1,0:T(8,128)(2,1)} %pad_maximum_fusion.3.refs_3_.refs_1_, ...), custom_call_target="tpu_custom_call" | custom-call | flops 19644594176 | tf_op jit(solution)/shard_map/product_rows/pallas_call | solution.py:811
  1000.8 7.6 reduce-scatter.14.cloned.1.call-done
  1012.5 13.2 %collective-permute-done.43.refs_2_ = bf16[256,2048]{1,0:T(8,128)(2,1)} collective-permute-done((bf16[256,2048]{1,0:T(8,128)(2,1)S(1)}, bf16[256,2048]{1,0:T(8,128)(2,1)}, u32[]{:S(2)}, u32[]{:S(2)}) %collective-permute-start.43) | collective-permute-done | bytes 1048608 | tf_op jit(solution)/shard_map/ppermute | solution.py:946
  (627 shorter events, 335.6 us)
Async XLA Ops:
  7.3 113.4 %all-gather.7.cloned.1.call-start = ((), (), s32[]{:S(2)}) async-start(), calls=%async_computation.10 | async-start | bytes 2949120 | tf_op jit(solution)/shard_map/all_gather | solution.py:987
  37.3 46.1 %collective-permute-start.1 = (bf16[256,2048]{1,0:T(8,128)(2,1)}, bf16[256,2048]{1,0:T(8,128)(2,1)}, u32[]{:S(2)}, u32[]{:S(2)}) collective-permute-start(bf16[256,2048]{1,0:T(8,128)(2,1)} %after.34.refs_0_), channel_id=1, source_target_pairs={{0,16},{8,24},{16,0},{24,8},{1,17},{9,25},{17,1},{25,9},{2,18},{10... | collective-permute-start | bytes 3145736 | tf_op jit(solution)/shard_map/ppermute | solution.py:946
  38.8 44.7 %collective-permute-start = (bf16[256,2048]{1,0:T(8,128)(2,1)}, bf16[256,2048]{1,0:T(8,128)(2,1)}, u32[]{:S(2)}, u32[]{:S(2)}) collective-permute-start(bf16[256,2048]{1,0:T(8,128)(2,1)} %after.34.refs_0_), channel_id=1, source_target_pairs={{0,8},{8,0},{16,24},{24,16},{1,9},{9,1},{17,25},{25,17},{2,10},{10... | collective-permute-start | bytes 3145736 | tf_op jit(solution)/shard_map/ppermute | solution.py:946
  87.0 67.0 %all-gather.13.cloned.1.call-start = ((), (), s32[]{:S(2)}) async-start(), calls=%async_computation.13 | async-start | bytes 4718592 | tf_op jit(solution)/shard_map/all_gather | solution.py:987
  106.1 108.9 %all-gather.9.cloned.1.call-start = ((), (), s32[]{:S(2)}) async-start(), calls=%async_computation.11 | async-start | bytes 6488064 | tf_op jit(solution)/shard_map/all_gather | solution.py:987
  108.3 145.8 %all-gather.11.cloned.1.call-start = ((), (), s32[]{:S(2)}) async-start(), calls=%async_computation.12 | async-start | bytes 3538944 | tf_op jit(solution)/shard_map/all_gather | solution.py:987
  108.9 278.7 %all-gather.15.cloned.1.call-start = ((), (), s32[]{:S(2)}) async-start(), calls=%async_computation.14 | async-start | bytes 9437184 | tf_op jit(solution)/shard_map/all_gather | solution.py:987
  110.0 277.5 %all-gather.17.cloned.1.call-start = ((), (), s32[]{:S(2)}) async-start(), calls=%async_computation.15 | async-start | bytes 4718592 | tf_op jit(solution)/shard_map/all_gather | solution.py:987
  142.5 132.2 %collective-permute-start.8 = (bf16[768,2048]{1,0:T(8,128)(2,1)}, bf16[768,2048]{1,0:T(8,128)(2,1)}, u32[]{:S(2)}, u32[]{:S(2)}) collective-permute-start(bf16[768,2048]{1,0:T(8,128)(2,1)} %after.40.refs_0_), channel_id=1, source_target_pairs={{0,24},{8,16},{16,8},{24,0},{1,25},{9,17},{17,9},{25,1},{2,26},{10... | collective-permute-start | bytes 9437192 | tf_op jit(solution)/shard_map/ppermute | solution.py:946
  144.0 136.5 %collective-permute-start.7 = (bf16[768,2048]{1,0:T(8,128)(2,1)}, bf16[768,2048]{1,0:T(8,128)(2,1)}, u32[]{:S(2)}, u32[]{:S(2)}) collective-permute-start(bf16[768,2048]{1,0:T(8,128)(2,1)} %after.40.refs_0_), channel_id=1, source_target_pairs={{0,16},{8,24},{16,0},{24,8},{1,17},{9,25},{17,1},{25,9},{2,18},{10... | collective-permute-start | bytes 9437192 | tf_op jit(solution)/shard_map/ppermute | solution.py:946
  145.4 136.8 %collective-permute-start.6 = (bf16[768,2048]{1,0:T(8,128)(2,1)}, bf16[768,2048]{1,0:T(8,128)(2,1)}, u32[]{:S(2)}, u32[]{:S(2)}) collective-permute-start(bf16[768,2048]{1,0:T(8,128)(2,1)} %after.40.refs_0_), channel_id=1, source_target_pairs={{0,8},{8,0},{16,24},{24,16},{1,9},{9,1},{17,25},{25,17},{2,10},{10... | collective-permute-start | bytes 9437192 | tf_op jit(solution)/shard_map/ppermute | solution.py:946
  244.7 615.8 %reduce-scatter.6.cloned.1.call-start = ((), (), s32[]{:S(2)}) async-start(), calls=%async_computation.16 | async-start | bytes 9437184 | tf_op jit(solution)/shard_map/reduce_scatter | solution.py:991
  274.8 50.6 %collective-permute-start.5 = (bf16[256,2048]{1,0:T(8,128)(2,1)}, bf16[256,2048]{1,0:T(8,128)(2,1)}, u32[]{:S(2)}, u32[]{:S(2)}) collective-permute-start(bf16[256,2048]{1,0:T(8,128)(2,1)} %get-tuple-element.81), channel_id=1, source_target_pairs={{0,24},{8,16},{16,8},{24,0},{1,25},{9,17},{17,9},{25,1},{2,26},{10... | collective-permute-start | bytes 3145736 | tf_op jit(solution)/shard_map/ppermute | solution.py:946
  329.4 51.0 %collective-permute-start.11 = (bf16[256,2048]{1,0:T(8,128)(2,1)}, bf16[256,2048]{1,0:T(8,128)(2,1)}, u32[]{:S(2)}, u32[]{:S(2)}) collective-permute-start(bf16[256,2048]{1,0:T(8,128)(2,1)} %get-tuple-element.83.refs_0_), channel_id=1, source_target_pairs={{0,24},{8,16},{16,8},{24,0},{1,25},{9,17},{17,9},{25,1},{2,26},{10... | collective-permute-start | bytes 3145736 | tf_op jit(solution)/shard_map/ppermute | solution.py:946
  330.9 49.4 %collective-permute-start.10 = (bf16[256,2048]{1,0:T(8,128)(2,1)}, bf16[256,2048]{1,0:T(8,128)(2,1)}, u32[]{:S(2)}, u32[]{:S(2)}) collective-permute-start(bf16[256,2048]{1,0:T(8,128)(2,1)} %get-tuple-element.83.refs_0_), channel_id=1, source_target_pairs={{0,16},{8,24},{16,0},{24,8},{1,17},{9,25},{17,1},{25,9},{2,18},{10... | collective-permute-start | bytes 3145736 | tf_op jit(solution)/shard_map/ppermute | solution.py:946
  332.3 48.0 %collective-permute-start.9 = (bf16[256,2048]{1,0:T(8,128)(2,1)}, bf16[256,2048]{1,0:T(8,128)(2,1)}, u32[]{:S(2)}, u32[]{:S(2)}) collective-permute-start(bf16[256,2048]{1,0:T(8,128)(2,1)} %get-tuple-element.83.refs_0_), channel_id=1, source_target_pairs={{0,8},{8,0},{16,24},{24,16},{1,9},{9,1},{17,25},{25,17},{2,10},{10... | collective-permute-start | bytes 3145736 | tf_op jit(solution)/shard_map/ppermute | solution.py:946
  384.0 40.7 %collective-permute-start.17 = (bf16[256,2048]{1,0:T(8,128)(2,1)}, bf16[256,2048]{1,0:T(8,128)(2,1)}, u32[]{:S(2)}, u32[]{:S(2)}) collective-permute-start(bf16[256,2048]{1,0:T(8,128)(2,1)} %after.49), channel_id=1, source_target_pairs={{0,24},{8,16},{16,8},{24,0},{1,25},{9,17},{17,9},{25,1},{2,26},{10... | collective-permute-start | bytes 3145736 | tf_op jit(solution)/shard_map/ppermute | solution.py:946
  385.7 44.8 %collective-permute-start.16 = (bf16[256,2048]{1,0:T(8,128)(2,1)S(1)}, bf16[256,2048]{1,0:T(8,128)(2,1)}, u32[]{:S(2)}, u32[]{:S(2)}) collective-permute-start(bf16[256,2048]{1,0:T(8,128)(2,1)S(1)} %copy-done.69), channel_id=1, source_target_pairs={{0,16},{8,24},{16,0},{24,8},{1,17},{9,25},{17,1},{25,9},{2,18},{10... | collective-permute-start | bytes 3145736 | tf_op jit(solution)/shard_map/ppermute | solution.py:946
  387.0 46.9 %collective-permute-start.15 = (bf16[256,2048]{1,0:T(8,128)(2,1)}, bf16[256,2048]{1,0:T(8,128)(2,1)}, u32[]{:S(2)}, u32[]{:S(2)}) collective-permute-start(bf16[256,2048]{1,0:T(8,128)(2,1)} %after.47), channel_id=1, source_target_pairs={{0,8},{8,0},{16,24},{24,16},{1,9},{9,1},{17,25},{25,17},{2,10},{10... | collective-permute-start | bytes 3145736 | tf_op jit(solution)/shard_map/ppermute | solution.py:946
  422.4 36.1 %collective-permute-start.12 = (bf16[256,2048]{1,0:T(8,128)(2,1)S(1)}, bf16[256,2048]{1,0:T(8,128)(2,1)S(1)}, u32[]{:S(2)}, u32[]{:S(2)}) collective-permute-start(bf16[256,2048]{1,0:T(8,128)(2,1)S(1)} %get-tuple-element.89), channel_id=1, source_target_pairs={{0,8},{8,0},{16,24},{24,16},{1,9},{9,1},{17,25},{25,17},{2,10},{10... | collective-permute-start | bytes 3145736 | tf_op jit(solution)/shard_map/ppermute | solution.py:946
  423.9 34.6 %collective-permute-start.13 = (bf16[256,2048]{1,0:T(8,128)(2,1)S(1)}, bf16[256,2048]{1,0:T(8,128)(2,1)S(1)}, u32[]{:S(2)}, u32[]{:S(2)}) collective-permute-start(bf16[256,2048]{1,0:T(8,128)(2,1)S(1)} %get-tuple-element.90), channel_id=1, source_target_pairs={{0,16},{8,24},{16,0},{24,8},{1,17},{9,25},{17,1},{25,9},{2,18},{10... | collective-permute-start | bytes 3145736 | tf_op jit(solution)/shard_map/ppermute | solution.py:946
  424.7 50.7 %collective-permute-start.14 = (bf16[256,2048]{1,0:T(8,128)(2,1)S(1)}, bf16[256,2048]{1,0:T(8,128)(2,1)}, u32[]{:S(2)}, u32[]{:S(2)}) collective-permute-start(bf16[256,2048]{1,0:T(8,128)(2,1)S(1)} %get-tuple-element.91), channel_id=1, source_target_pairs={{0,24},{8,16},{16,8},{24,0},{1,25},{9,17},{17,9},{25,1},{2,26},{10... | collective-permute-start | bytes 3145736 | tf_op jit(solution)/shard_map/ppermute | solution.py:946
  481.2 43.9 %collective-permute-start.19 = (bf16[256,2048]{1,0:T(8,128)(2,1)S(1)}, bf16[256,2048]{1,0:T(8,128)(2,1)S(1)}, u32[]{:S(2)}, u32[]{:S(2)}) collective-permute-start(bf16[256,2048]{1,0:T(8,128)(2,1)S(1)} %get-tuple-element.96.refs_0_), channel_id=1, source_target_pairs={{0,16},{8,24},{16,0},{24,8},{1,17},{9,25},{17,1},{25,9},{2,18},{10... | collective-permute-start | bytes 3145736 | tf_op jit(solution)/shard_map/ppermute | solution.py:946
  482.8 42.3 %collective-permute-start.18 = (bf16[256,2048]{1,0:T(8,128)(2,1)S(1)}, bf16[256,2048]{1,0:T(8,128)(2,1)S(1)}, u32[]{:S(2)}, u32[]{:S(2)}) collective-permute-start(bf16[256,2048]{1,0:T(8,128)(2,1)S(1)} %get-tuple-element.96.refs_0_), channel_id=1, source_target_pairs={{0,8},{8,0},{16,24},{24,16},{1,9},{9,1},{17,25},{25,17},{2,10},{10... | collective-permute-start | bytes 3145736 | tf_op jit(solution)/shard_map/ppermute | solution.py:946
  530.3 46.9 %collective-permute-start.22 = (bf16[256,2048]{1,0:T(8,128)(2,1)S(1)}, bf16[256,2048]{1,0:T(8,128)(2,1)S(1)}, u32[]{:S(2)}, u32[]{:S(2)}) collective-permute-start(bf16[256,2048]{1,0:T(8,128)(2,1)S(1)} %copy-done.65), channel_id=1, source_target_pairs={{0,16},{8,24},{16,0},{24,8},{1,17},{9,25},{17,1},{25,9},{2,18},{10... | collective-permute-start | bytes 3145736 | tf_op jit(solution)/shard_map/ppermute | solution.py:946
  531.7 45.6 %collective-permute-start.21 = (bf16[256,2048]{1,0:T(8,128)(2,1)S(1)}, bf16[256,2048]{1,0:T(8,128)(2,1)S(1)}, u32[]{:S(2)}, u32[]{:S(2)}) collective-permute-start(bf16[256,2048]{1,0:T(8,128)(2,1)S(1)} %copy-done.65), channel_id=1, source_target_pairs={{0,8},{8,0},{16,24},{24,16},{1,9},{9,1},{17,25},{25,17},{2,10},{10... | collective-permute-start | bytes 3145736 | tf_op jit(solution)/shard_map/ppermute | solution.py:946
  579.7 41.1 %collective-permute-start.26 = (bf16[256,2048]{1,0:T(8,128)(2,1)}, bf16[256,2048]{1,0:T(8,128)(2,1)}, u32[]{:S(2)}, u32[]{:S(2)}) collective-permute-start(bf16[256,2048]{1,0:T(8,128)(2,1)} %after.54), channel_id=1, source_target_pairs={{0,24},{8,16},{16,8},{24,0},{1,25},{9,17},{17,9},{25,1},{2,26},{10... | collective-permute-start | bytes 3145736 | tf_op jit(solution)/shard_map/ppermute | solution.py:946
  581.2 47.2 %collective-permute-start.25 = (bf16[256,2048]{1,0:T(8,128)(2,1)S(1)}, bf16[256,2048]{1,0:T(8,128)(2,1)}, u32[]{:S(2)}, u32[]{:S(2)}) collective-permute-start(bf16[256,2048]{1,0:T(8,128)(2,1)S(1)} %copy-done.67), channel_id=1, source_target_pairs={{0,16},{8,24},{16,0},{24,8},{1,17},{9,25},{17,1},{25,9},{2,18},{10... | collective-permute-start | bytes 3145736 | tf_op jit(solution)/shard_map/ppermute | solution.py:946
  582.7 45.9 %collective-permute-start.24 = (bf16[256,2048]{1,0:T(8,128)(2,1)S(1)}, bf16[256,2048]{1,0:T(8,128)(2,1)}, u32[]{:S(2)}, u32[]{:S(2)}) collective-permute-start(bf16[256,2048]{1,0:T(8,128)(2,1)S(1)} %copy-done.71), channel_id=1, source_target_pairs={{0,8},{8,0},{16,24},{24,16},{1,9},{9,1},{17,25},{25,17},{2,10},{10... | collective-permute-start | bytes 3145736 | tf_op jit(solution)/shard_map/ppermute | solution.py:946
  649.5 275.0 %reduce-scatter.8.cloned.1.call-start = ((), (), s32[]{:S(2)}) async-start(), calls=%async_computation.17 | async-start | bytes 4718592 | tf_op jit(solution)/shard_map/reduce_scatter | solution.py:991
  649.5 55.5 %collective-permute-start.27 = (bf16[256,2048]{1,0:T(8,128)(2,1)}, bf16[256,2048]{1,0:T(8,128)(2,1)}, u32[]{:S(2)}, u32[]{:S(2)}) collective-permute-start(bf16[256,2048]{1,0:T(8,128)(2,1)} %get-tuple-element.109), channel_id=1, source_target_pairs={{0,8},{8,0},{16,24},{24,16},{1,9},{9,1},{17,25},{25,17},{2,10},{10... | collective-permute-start | bytes 3145736 | tf_op jit(solution)/shard_map/ppermute | solution.py:946
  651.0 54.0 %collective-permute-start.28 = (bf16[256,2048]{1,0:T(8,128)(2,1)}, bf16[256,2048]{1,0:T(8,128)(2,1)}, u32[]{:S(2)}, u32[]{:S(2)}) collective-permute-start(bf16[256,2048]{1,0:T(8,128)(2,1)} %get-tuple-element.110), channel_id=1, source_target_pairs={{0,16},{8,24},{16,0},{24,8},{1,17},{9,25},{17,1},{25,9},{2,18},{10... | collective-permute-start | bytes 3145736 | tf_op jit(solution)/shard_map/ppermute | solution.py:946
  651.6 53.4 %collective-permute-start.29 = (bf16[256,2048]{1,0:T(8,128)(2,1)}, bf16[256,2048]{1,0:T(8,128)(2,1)}, u32[]{:S(2)}, u32[]{:S(2)}) collective-permute-start(bf16[256,2048]{1,0:T(8,128)(2,1)} %get-tuple-element.111), channel_id=1, source_target_pairs={{0,24},{8,16},{16,8},{24,0},{1,25},{9,17},{17,9},{25,1},{2,26},{10... | collective-permute-start | bytes 3145736 | tf_op jit(solution)/shard_map/ppermute | solution.py:946
  719.3 205.2 %reduce-scatter.10.cloned.1.call-start = ((), (), s32[]{:S(2)}) async-start(), calls=%async_computation.18 | async-start | bytes 4718592 | tf_op jit(solution)/shard_map/reduce_scatter | solution.py:991
  725.5 44.7 %collective-permute-start.32 = (bf16[256,2048]{1,0:T(8,128)(2,1)S(1)}, bf16[256,2048]{1,0:T(8,128)(2,1)S(1)}, u32[]{:S(2)}, u32[]{:S(2)}) collective-permute-start(bf16[256,2048]{1,0:T(8,128)(2,1)S(1)} %get-tuple-element.112.refs_3_.refs_0_), channel_id=1, source_target_pairs={{0,24},{8,16},{16,8},{24,0},{1,25},{9,17},{17,9},{25,1},{2,26},{10... | collective-permute-start | bytes 3145736 | tf_op jit(solution)/shard_map/ppermute | solution.py:946
  727.0 45.9 %collective-permute-start.31 = (bf16[256,2048]{1,0:T(8,128)(2,1)S(1)}, bf16[256,2048]{1,0:T(8,128)(2,1)S(1)}, u32[]{:S(2)}, u32[]{:S(2)}) collective-permute-start(bf16[256,2048]{1,0:T(8,128)(2,1)S(1)} %get-tuple-element.112.refs_3_.refs_0_), channel_id=1, source_target_pairs={{0,16},{8,24},{16,0},{24,8},{1,17},{9,25},{17,1},{25,9},{2,18},{10... | collective-permute-start | bytes 3145736 | tf_op jit(solution)/shard_map/ppermute | solution.py:946
  728.6 44.4 %collective-permute-start.30 = (bf16[256,2048]{1,0:T(8,128)(2,1)S(1)}, bf16[256,2048]{1,0:T(8,128)(2,1)S(1)}, u32[]{:S(2)}, u32[]{:S(2)}) collective-permute-start(bf16[256,2048]{1,0:T(8,128)(2,1)S(1)} %get-tuple-element.112.refs_3_.refs_0_), channel_id=1, source_target_pairs={{0,8},{8,0},{16,24},{24,16},{1,9},{9,1},{17,25},{25,17},{2,10},{10... | collective-permute-start | bytes 3145736 | tf_op jit(solution)/shard_map/ppermute | solution.py:946
  791.5 147.7 %reduce-scatter.12.cloned.1.call-start = ((), (), s32[]{:S(2)}) async-start(), calls=%async_computation.19 | async-start | bytes 5898240 | tf_op jit(solution)/shard_map/reduce_scatter | solution.py:991
  793.2 47.1 %collective-permute-start.34 = (bf16[256,2048]{1,0:T(8,128)(2,1)S(1)}, bf16[256,2048]{1,0:T(8,128)(2,1)}, u32[]{:S(2)}, u32[]{:S(2)}) collective-permute-start(bf16[256,2048]{1,0:T(8,128)(2,1)S(1)} %copy-done.59), channel_id=1, source_target_pairs={{0,16},{8,24},{16,0},{24,8},{1,17},{9,25},{17,1},{25,9},{2,18},{10... | collective-permute-start | bytes 3145736 | tf_op jit(solution)/shard_map/ppermute | solution.py:946
  794.6 46.0 %collective-permute-start.33 = (bf16[256,2048]{1,0:T(8,128)(2,1)S(1)}, bf16[256,2048]{1,0:T(8,128)(2,1)}, u32[]{:S(2)}, u32[]{:S(2)}) collective-permute-start(bf16[256,2048]{1,0:T(8,128)(2,1)S(1)} %copy-done.61), channel_id=1, source_target_pairs={{0,8},{8,0},{16,24},{24,16},{1,9},{9,1},{17,25},{25,17},{2,10},{10... | collective-permute-start | bytes 3145736 | tf_op jit(solution)/shard_map/ppermute | solution.py:946
  856.9 61.6 %collective-permute-start.38 = (bf16[256,2048]{1,0:T(8,128)(2,1)S(1)}, bf16[256,2048]{1,0:T(8,128)(2,1)}, u32[]{:S(2)}, u32[]{:S(2)}) collective-permute-start(bf16[256,2048]{1,0:T(8,128)(2,1)S(1)} %copy-done.56), channel_id=1, source_target_pairs={{0,24},{8,16},{16,8},{24,0},{1,25},{9,17},{17,9},{25,1},{2,26},{10... | collective-permute-start | bytes 3145736 | tf_op jit(solution)/shard_map/ppermute | solution.py:946
  858.4 60.2 %collective-permute-start.37 = (bf16[256,2048]{1,0:T(8,128)(2,1)}, bf16[256,2048]{1,0:T(8,128)(2,1)}, u32[]{:S(2)}, u32[]{:S(2)}) collective-permute-start(bf16[256,2048]{1,0:T(8,128)(2,1)} %after.62), channel_id=1, source_target_pairs={{0,16},{8,24},{16,0},{24,8},{1,17},{9,25},{17,1},{25,9},{2,18},{10... | collective-permute-start | bytes 3145736 | tf_op jit(solution)/shard_map/ppermute | solution.py:946
  859.8 58.8 %collective-permute-start.36 = (bf16[256,2048]{1,0:T(8,128)(2,1)}, bf16[256,2048]{1,0:T(8,128)(2,1)}, u32[]{:S(2)}, u32[]{:S(2)}) collective-permute-start(bf16[256,2048]{1,0:T(8,128)(2,1)} %after.61), channel_id=1, source_target_pairs={{0,8},{8,0},{16,24},{24,16},{1,9},{9,1},{17,25},{25,17},{2,10},{10... | collective-permute-start | bytes 3145736 | tf_op jit(solution)/shard_map/ppermute | solution.py:946
  860.4 62.2 %all-to-all-start.2 = ((bf16[4,64,2048]{2,1,0:T(8,128)(2,1)}), bf16[4,64,2048]{2,1,0:T(8,128)(2,1)}, u32[]{:S(2)}, u32[]{:S(2)}) async-start(bf16[4,64,2048]{2,1,0:T(8,128)(2,1)} %bitcast.215), calls=%async_computation.3 | async-start | bytes 2097152 | tf_op jit(solution)/shard_map/all_to_all | solution.py:983
  864.7 143.6 %reduce-scatter.14.cloned.1.call-start = ((), (), s32[]{:S(2)}) async-start(), calls=%async_computation.20 | async-start | bytes 6488064 | tf_op jit(solution)/shard_map/reduce_scatter | solution.py:991
  975.9 36.6 %collective-permute-start.41 = (bf16[256,2048]{1,0:T(8,128)(2,1)}, bf16[256,2048]{1,0:T(8,128)(2,1)}, u32[]{:S(2)}, u32[]{:S(2)}) collective-permute-start(bf16[256,2048]{1,0:T(8,128)(2,1)} %get-tuple-element.133), channel_id=1, source_target_pairs={{0,8},{8,0},{16,24},{24,16},{1,9},{9,1},{17,25},{25,17},{2,10},{10... | collective-permute-start | bytes 3145736 | tf_op jit(solution)/shard_map/ppermute | solution.py:946
  977.4 35.2 %collective-permute-start.42 = (bf16[256,2048]{1,0:T(8,128)(2,1)S(1)}, bf16[256,2048]{1,0:T(8,128)(2,1)}, u32[]{:S(2)}, u32[]{:S(2)}) collective-permute-start(bf16[256,2048]{1,0:T(8,128)(2,1)S(1)} %get-tuple-element.134), channel_id=1, source_target_pairs={{0,16},{8,24},{16,0},{24,8},{1,17},{9,25},{17,1},{25,9},{2,18},{10... | collective-permute-start | bytes 3145736 | tf_op jit(solution)/shard_map/ppermute | solution.py:946
  977.9 47.8 %collective-permute-start.43 = (bf16[256,2048]{1,0:T(8,128)(2,1)S(1)}, bf16[256,2048]{1,0:T(8,128)(2,1)}, u32[]{:S(2)}, u32[]{:S(2)}) collective-permute-start(bf16[256,2048]{1,0:T(8,128)(2,1)S(1)} %get-tuple-element.135), channel_id=1, source_target_pairs={{0,24},{8,16},{16,8},{24,0},{1,25},{9,17},{17,9},{25,1},{2,26},{10... | collective-permute-start | bytes 3145736 | tf_op jit(solution)/shard_map/ppermute | solution.py:946
  (161 other events, 1763.1 us)
Sparse Core Ops, SparseCore 0:
  32.3 33.5 all-gather.6
  106.3 47.6 all-gather.12
  156.2 58.7 all-gather.8
  217.1 36.9 all-gather.10
  255.5 80.9 all-gather.14
  337.9 45.6 all-gather.16
  649.6 89.8 reduce-scatter.5
  741.8 48.3 reduce-scatter.7
  792.5 49.8 reduce-scatter.9
  855.9 60.5 reduce-scatter.11
  939.3 68.9 reduce-scatter.13
